TPU v7x, 32 devices: a whole 2x2x4 slice. The times are simulated.
32 devices in a mesh: seq: 4 (over y, core), fsdp: 2 (over x), batch: 4 (over z).
Axes of the slice: x: 2, y: 2, z: 4, core: 2. Of those that a mesh axis runs over, the one named last changes fastest.
Arguments:
- hidden: bfloat16 [8, 512, 2048], P(('fsdp', 'batch'), 'seq'), may hold values from -6 to 6
- in_weight: bfloat16 [2048, 2208], P(('fsdp', 'batch')), may hold values from -0.125 to 0.125
- read_starts: int32 [8, 4], P(('fsdp', 'batch')), may hold values from 1 to 511
- conv_weight: float32 [2, 4, 2176], replicated, may hold values from -3 to 3
- conv_bias: float32 [2, 2176], replicated, may hold values from -0.5 to 0.5
- dt_bias: float32 [2, 32], replicated, may hold values from -4.5 to -2.5
- decay: float32 [2, 32], replicated, may hold values from 9.765625e-05 to 0.7
- skip: float32 [2, 32], replicated, may hold values from 0.5 to 1.5
- norm_gain: float32 [2, 2048], replicated, may hold values from 0.5 to 1.5
Outputs:
- mixed: bfloat16 [8, 512, 2048], P(('fsdp', 'batch'), 'seq')
All inputs are finite; a program needn't handle non-finite values.
Results may differ from a plain program's by a relative error of at most 0.0051.
Values may be sent and summed in bfloat16 or wider, within the bound.
No kernel may reach another device: no remote copies, remote signals or barrier semaphores. Data moves between devices by JAX's collectives and lax.ppermute only.
A program may use at most 128 MiB of HBM per device.

v0:
```python
import jax
import jax.numpy as jnp
from jax import lax
from jax.sharding import PartitionSpec as P

HEADS = 32
HEAD_DIM = 64
STATE = 64
KERNEL = 4
BLOCK = 128
INNER = 2048
CONV_CH = 2176


def prefix(value, axis, join, neutral, backward):
    count, mine = (lax.axis_size(axis), lax.axis_index(axis))
    pieces = jax.tree.map(lambda part: lax.all_gather(part, axis), value)
    if backward:
        pieces = jax.tree.map(lambda part: part[::-1], pieces)
        mine = count - 1 - mine
    running = jax.tree.map(
        lambda part, zero: jnp.full_like(part, 0) + jnp.asarray(zero, part.dtype), value, neutral
    )

    def turn(position, running):
        longer = join(running, jax.tree.map(lambda part: part[position], pieces))
        return jax.tree.map(lambda new, old: jnp.where(position < mine, new, old), longer, running)

    return lax.fori_loop(0, count - 1, turn, running)


def extended_2(value, sides, width):
    for axis, dim in sides:
        size, length = (lax.axis_size(axis), value.shape[dim])
        up = [(i, (i + 1) % size) for i in range(size - 1)]
        down = [(j, i) for i, j in up]
        last = lax.slice_in_dim(value, length - width, length, axis=dim)
        initial = lax.slice_in_dim(value, 0, width, axis=dim)
        before = lax.ppermute(last, axis, up)
        after = lax.ppermute(initial, axis, down)
        value = jnp.concatenate([before, value, after], axis=dim)
    return value


def conv_silu(padded, weight, bias):
    length = padded.shape[0] - weight.shape[0] + 1
    total = jnp.broadcast_to(bias[None, :], (length, bias.shape[0]))
    for tap in range(weight.shape[0]):
        total = total + weight[tap][None, :] * padded[tap : tap + length].astype(jnp.float32)
    return jax.nn.silu(total).astype(jnp.bfloat16)


def block_parts(x_part, b_part, c_part, step_size, log_rate, resets):
    length = x_part.shape[0]
    running = jnp.cumsum(log_rate, axis=0)
    running_heads = running.T
    step_heads = step_size.T
    resets_seen = jnp.cumsum(resets)
    scores = jnp.dot(c_part, b_part.T, preferred_element_type=jnp.float32)
    positions = jnp.arange(length)
    allowed = (positions[:, None] >= positions[None, :]) & (
        resets_seen[:, None] == resets_seen[None, :]
    )
    log_gaps = jnp.minimum(running_heads[:, :, None] - running_heads[:, None, :], 0.0)
    weights = (
        jnp.where(allowed[None, :, :], jnp.exp(log_gaps), 0.0)
        * scores[None, :, :]
        * step_heads[:, None, :]
    )
    weights = weights.astype(jnp.bfloat16)
    values = x_part.reshape(length, HEADS, HEAD_DIM)
    inner_part = jnp.einsum("hts,shp->thp", weights, values, preferred_element_type=jnp.float32)
    last_same = resets_seen == resets_seen[-1]
    tail_weight = (
        jnp.where(last_same[:, None], jnp.exp(running[-1][None, :] - running), 0.0) * step_size
    )
    inputs = (tail_weight[:, :, None] * values.astype(jnp.float32)).astype(jnp.bfloat16)
    local_end = jnp.einsum("shp,sn->hpn", inputs, b_part, preferred_element_type=jnp.float32)
    lead_fade = jnp.where((resets_seen == 0)[:, None], jnp.exp(running), 0.0)
    block_fade = jnp.where(resets_seen[-1] == 0, jnp.exp(running[-1]), 0.0)
    return (inner_part, local_end, lead_fade, block_fade)


def chain_combine(earlier, later):
    return (earlier[0] * later[0], later[0][:, None] * earlier[1] + later[1])


def direction(conv_out, step_cols, resets, bias_step, rates, direct, gains, backward):
    length = conv_out.shape[0]
    blocks = length // BLOCK
    x_part = conv_out[:, :INNER]
    b_part = conv_out[:, INNER : INNER + STATE]
    c_part = conv_out[:, INNER + STATE :]
    step_size = jax.nn.softplus(step_cols.astype(jnp.float32) + bias_step[None, :])
    log_rate = -step_size * rates[None, :]
    inner_part, local_end, lead_fade, block_fade = jax.vmap(block_parts)(
        x_part.reshape(blocks, BLOCK, INNER),
        b_part.reshape(blocks, BLOCK, STATE),
        c_part.reshape(blocks, BLOCK, STATE),
        step_size.reshape(blocks, BLOCK, HEADS),
        log_rate.reshape(blocks, BLOCK, HEADS),
        resets.reshape(blocks, BLOCK),
    )
    carried_state = jnp.zeros((HEADS, HEAD_DIM, STATE), jnp.float32)
    carried_fade = jnp.ones((HEADS,), jnp.float32)
    entering = carried_state
    fades_before = carried_fade
    carried_state = block_fade[0][:, None, None] * carried_state + local_end[0]
    carried_fade = block_fade[0] * carried_fade
    summary = (carried_fade, carried_state.reshape(HEADS, HEAD_DIM * STATE))
    identity = (jnp.ones((HEADS,), jnp.float32), jnp.zeros((HEADS, HEAD_DIM * STATE), jnp.float32))
    if backward:
        incoming = prefix(summary, "seq", chain_combine, identity, True)
    else:
        incoming = prefix(summary, "seq", chain_combine, identity, False)
    incoming_state = incoming[1].reshape(HEADS, HEAD_DIM, STATE)
    states = jnp.stack([fades_before[:, None, None] * incoming_state + entering])
    rounded = states.astype(jnp.bfloat16)
    carried = jnp.einsum(
        "btn,bhpn->bthp",
        c_part.reshape(blocks, BLOCK, STATE),
        rounded,
        preferred_element_type=jnp.float32,
    )
    direct_part = direct[None, None, :, None] * x_part.reshape(
        blocks, BLOCK, HEADS, HEAD_DIM
    ).astype(jnp.float32)
    result = (inner_part + lead_fade[..., None] * carried + direct_part).reshape(
        length, HEADS, HEAD_DIM
    )
    scale = lax.rsqrt(jnp.mean(result * result, axis=-1, keepdims=True) + 1e-05)
    return (result * scale * gains.reshape(HEADS, HEAD_DIM)).reshape(length, INNER)


def project(rows_in, in_weight):
    total = jnp.dot(
        rows_in,
        lax.all_gather(in_weight, ("fsdp", "batch"), axis=0, tiled=True),
        preferred_element_type=jnp.float32,
    )
    return total.astype(jnp.bfloat16)


def on_device(
    hidden, in_weight, read_starts, conv_weight, conv_bias, dt_bias, decay, skip, norm_gain
):
    tokens = hidden[0]
    length = tokens.shape[0]
    margin = KERNEL - 1
    projected = project(tokens, in_weight)
    extended = extended_2(projected[:, :CONV_CH], (("seq", 0),), margin)
    forward_in = conv_silu(extended[: length + margin], conv_weight[0], conv_bias[0])
    backward_in = conv_silu(jnp.flip(extended[margin:], 0), conv_weight[1], conv_bias[1])
    step_cols = projected[:, CONV_CH:]
    positions = lax.axis_index("seq") * length + jnp.arange(length, dtype=jnp.int32)
    marks = read_starts[0]
    starts_here = jnp.any(positions[:, None] == marks[None, :], axis=1).astype(jnp.float32)
    starts_next = jnp.any((positions + 1)[:, None] == marks[None, :], axis=1).astype(jnp.float32)
    forward_out = direction(
        forward_in, step_cols, starts_here, dt_bias[0], decay[0], skip[0], norm_gain[0], False
    )
    backward_out = direction(
        backward_in,
        jnp.flip(step_cols, 0),
        jnp.flip(starts_next, 0),
        dt_bias[1],
        decay[1],
        skip[1],
        norm_gain[1],
        True,
    )
    mixed = forward_out + jnp.flip(backward_out, 0)
    return mixed.astype(jnp.bfloat16)[None]


def solution(mesh):
    in_specs = (
        P(("fsdp", "batch"), "seq", None),
        P(("fsdp", "batch"), None),
        P(("fsdp", "batch"), None),
        P(),
        P(),
        P(),
        P(),
        P(),
        P(),
    )
    out_specs = P(("fsdp", "batch"), "seq", None)
    return jax.shard_map(
        on_device, mesh=mesh, in_specs=in_specs, out_specs=out_specs, check_vma=False
    )
```

profile of v0, /device:TPU:0, one launch (start us, length us, event | category | flops | bytes accessed | tf_op | source)
XLA Modules:
  0.0 266.7 jit_solution(13821560791026674322)
XLA Ops:
  16.6 128.9 %all-gather.6.cloned.1.call-done = bf16[2048,2208]{0,1:T(8,128)(2,1)} async-done(((bf16[256,2208]{0,1:T(8,128)(2,1)}), bf16[2048,2208]{0,1:T(8,128)(2,1)}) %all-gather.6.cloned.1.call-update) | async-done | bytes 9043984 | tf_op jit(solution)/shard_map/all_gather | solution.py:138
  145.5 6.1 %convolution_convert_fusion = bf16[128,2208]{0,1:T(8,128)(2,1)S(1)} fusion(bf16[2048,2208]{0,1:T(8,128)(2,1)} %all-gather.6.cloned.1.call-done, bf16[1,128,2048]{2,1,0:T(8,128)(2,1)S(1)} %copy-done), kind=kOutput, calls=%fused_computation.6 | convolution fusion | flops 1157910528 | bytes 10133504 | tf_op jit(solution)/shard_map/dot_general | solution.py:136
  158.0 1.3 collective-permute-start.1
  159.3 1.4 fusion.62
  160.7 1.3 fusion.36
  162.7 6.2 %slice.189 = bf16[128,2176]{0,1:T(8,128)(2,1)} reverse(bf16[128,2176]{0,1:T(8,128)(2,1)S(1)} %slice.200), dimensions={0} | reverse | bytes 1114112 | tf_op jit(solution)/shard_map/slice | solution.py:49
  169.0 7.5 %all-gather.1 = f32[4,1,32]{2,1,0:T(1,128)S(1)} all-gather(f32[1,1,32]{2,1,0:T(1,128)S(1)} %copy-done.26), channel_id=3, replica_groups=mesh['seq'=4,'fsdp'=2,'batch'=4] {'seq'}, dimensions={0}, use_global_device_ids=true | all-gather | bytes 640 | tf_op jit(solution)/shard_map/all_gather | solution.py:17
  177.1 5.3 %all-gather = f32[4,1,32]{2,1,0:T(1,128)S(1)} all-gather(f32[1,1,32]{2,1,0:T(1,128)S(1)} %copy-done.27), channel_id=2, replica_groups=mesh['seq'=4,'fsdp'=2,'batch'=4] {'seq'}, dimensions={0}, use_global_device_ids=true | all-gather | bytes 640 | tf_op jit(solution)/shard_map/all_gather | solution.py:17
  182.8 2.6 multiply_convert_fusion.3
  186.8 1.6 squeeze.41
  189.5 1.8 copy.49
  191.3 3.6 %fusion.27 = (bf16[128,2176]{0,1:T(8,128)(2,1)}, bf16[128,2176]{0,1:T(8,128)(2,1)S(1)}, bf16[128,2176]{0,1:T(8,128)(2,1)}) fusion(bf16[128,2176]{0,1:T(8,128)(2,1)S(1)} %slice.200, bf16[3,2176]{0,1:T(8,128)(2,1)} %copy.49), kind=kLoop, calls=%fused_computation.54 | loop fusion | flops 3342336 | bytes 2241280 | tf_op jit(solution)/shard_map/concatenate | solution.py:41
  194.9 9.0 %slice.181 = bf16[128,2176]{0,1:T(8,128)(2,1)} reverse(bf16[128,2176]{0,1:T(8,128)(2,1)} %get-tuple-element.263), dimensions={0} | reverse | bytes 1114112 | tf_op jit(solution)/shard_map/slice | solution.py:49
  203.9 9.0 %slice.184 = bf16[128,2176]{0,1:T(8,128)(2,1)} reverse(bf16[128,2176]{0,1:T(8,128)(2,1)} %get-tuple-element.265), dimensions={0} | reverse | bytes 1114112 | tf_op jit(solution)/shard_map/slice | solution.py:49
  212.9 6.2 %slice.187 = bf16[128,2176]{0,1:T(8,128)(2,1)} reverse(bf16[128,2176]{0,1:T(8,128)(2,1)S(1)} %get-tuple-element.264), dimensions={0} | reverse | bytes 1114112 | tf_op jit(solution)/shard_map/slice | solution.py:49
  219.1 3.6 %multiply_convert_fusion.2 = bf16[128,2176]{0,1:T(8,128)(2,1)S(1)} fusion(bf16[128,2176]{0,1:T(8,128)(2,1)S(1)} %copy-done.2, bf16[128,2176]{0,1:T(8,128)(2,1)} %slice.187, bf16[128,2176]{0,1:T(8,128)(2,1)} %slice.184, bf16[128,2176]{0,1:T(8,128)(2,1)} %slice.181, f32[2176]{0:T(1024)S(1)} %get-tuple-element.237, f32[2176]{0:T(1024)S(1)} %copy-done.8, ...), kind=kLoop, calls=%fused_computation.27 | loop fusion | flops 4734976 | bytes 2828800 | tf_op jit(solution)/shard_map/convert_element_type | solution.py:50
  224.1 1.6 squeeze.43
  226.1 1.3 slice_convert_fusion.1
  229.6 3.6 %while.28 = (s32[]{:T(128)}, f32[32,4096]{1,0:T(8,128)S(1)}, s32[]{:T(128)}, f32[4,32]{1,0:T(4,128)S(1)}, f32[4,32,4096]{2,1,0:T(8,128)}, /*index=5*/s32[]{:T(128)}, s32[]{:T(128)}) while((s32[]{:T(128)}, f32[32,4096]{1,0:T(8,128)S(1)}, s32[]{:T(128)}, f32[4,32]{1,0:T(4,128)S(1)}, f32[4,32,4096]{2,1,0:T(8,128)}, ...), condition=%wide.region_4.5_spmd.clone, body=%wide.region_3.4_spmd.clone.sunk | while | flops 524292 | bytes 1573353 | solution.py:29
  235.4 2.0 multiply_reduce_fusion.1
  237.4 13.4 %all-gather.10.cloned.1.call-done = f32[4,32,4096]{2,1,0:T(8,128)} async-done(((f32[1,32,4096]{2,1,0:T(8,128)}), f32[4,32,4096]{2,1,0:T(8,128)}) %all-gather.10.cloned.1.call-update) | async-done | bytes 2097168 | tf_op jit(solution)/shard_map/all_gather | solution.py:17
  250.8 1.7 rev.23
  256.2 1.4 rev.24
  257.6 1.6 fusion.12
  (157 shorter events, 33.5 us)
Async XLA Ops:
  6.5 139.0 %copy-start = (bf16[1,128,2048]{2,1,0:T(8,128)(2,1)S(1)}, bf16[1,128,2048]{2,1,0:T(8,128)(2,1)}, u32[]{:S(2)}) copy-start(bf16[1,128,2048]{2,1,0:T(8,128)(2,1)} %param.13) | copy-start | bytes 1572868
  6.5 4.2 %copy-start.15 = (f32[2,2176]{1,0:T(2,128)S(1)}, f32[2,2176]{1,0:T(2,128)}, u32[]{:S(2)}) copy-start(f32[2,2176]{1,0:T(2,128)} %param.17) | copy-start | bytes 52228
  6.5 4.3 %copy-start.7 = (f32[2,4,2176]{2,1,0:T(4,128)S(1)}, f32[2,4,2176]{2,1,0:T(4,128)}, u32[]{:S(2)}) copy-start(f32[2,4,2176]{2,1,0:T(4,128)} %param.16) | copy-start | bytes 208900
  6.5 7.5 %copy-start.28 = (f32[2,32]{1,0:T(2,128)S(1)}, f32[2,32]{1,0:T(2,128)}, u32[]{:S(2)}) copy-start(f32[2,32]{1,0:T(2,128)} %param.18) | copy-start | bytes 772
  6.5 7.5 %copy-start.29 = (f32[2,32]{1,0:T(2,128)S(1)}, f32[2,32]{1,0:T(2,128)}, u32[]{:S(2)}) copy-start(f32[2,32]{1,0:T(2,128)} %param.19) | copy-start | bytes 772
  6.6 7.5 %copy-start.30 = (f32[2,32]{1,0:T(2,128)S(1)}, f32[2,32]{1,0:T(2,128)}, u32[]{:S(2)}) copy-start(f32[2,32]{1,0:T(2,128)} %param.20) | copy-start | bytes 772
  6.6 9.4 %copy-start.20 = (f32[2,2048]{1,0:T(2,128)S(1)}, f32[2,2048]{1,0:T(2,128)}, u32[]{:S(2)}) copy-start(f32[2,2048]{1,0:T(2,128)} %param.21) | copy-start | bytes 49156
  6.6 139.0 %all-gather.6.cloned.1.call-start = ((), (), s32[]{:S(2)}) async-start(), calls=%async_computation | async-start | bytes 10174464 | tf_op jit(solution)/shard_map/all_gather | solution.py:138
  7.3 222.3 %all-gather.8.cloned.1.call-start = ((), (), s32[]{:S(2)}) async-start(), calls=%async_computation.1 | async-start | bytes 2621440 | tf_op jit(solution)/shard_map/all_gather | solution.py:17
  14.0 138.0 %copy-start.23 = (f32[32]{0:T(128)}, f32[32]{0:T(128)S(1)}, u32[]{:S(2)}) copy-start(f32[32]{0:T(128)S(1)} %get-tuple-element.286) | copy-start | bytes 388
  153.6 5.8 %copy-start.24 = (f32[32]{0:T(128)S(1)}, f32[32]{0:T(128)}, u32[]{:S(2)}) copy-start(f32[32]{0:T(128)} %copy-done.23) | copy-start | bytes 388
  153.6 7.1 %copy-start.25 = (f32[32]{0:T(128)S(1)}, f32[32]{0:T(128)}, u32[]{:S(2)}) copy-start(f32[32]{0:T(128)} %get-tuple-element.276) | copy-start | bytes 388
  155.2 27.2 %collective-permute-start = (bf16[3,2176]{1,0:T(4,128)(2,1)}, bf16[3,2176]{1,0:T(4,128)(2,1)S(1)}, u32[]{:S(2)}, u32[]{:S(2)}) collective-permute-start(bf16[3,2176]{1,0:T(4,128)(2,1)} %copy.42), channel_id=1, source_target_pairs={{0,8},{8,16},{16,24},{1,9},{9,17},{17,25},{2,10},{10,18},{18,26},{... | collective-permute-start | bytes 39176 | tf_op jit(solution)/shard_map/ppermute | solution.py:39
  158.0 31.4 %collective-permute-start.1 = (bf16[3,2176]{1,0:T(4,128)(2,1)}, bf16[3,2176]{1,0:T(4,128)(2,1)}, u32[]{:S(2)}, u32[]{:S(2)}) collective-permute-start(bf16[3,2176]{1,0:T(4,128)(2,1)} %copy.48), channel_id=1, source_target_pairs={{8,0},{16,8},{24,16},{9,1},{17,9},{25,17},{10,2},{18,10},{26,18},{... | collective-permute-start | bytes 39176 | tf_op jit(solution)/shard_map/ppermute | solution.py:40
  162.6 6.3 %copy-start.26 = (f32[1,1,32]{2,1,0:T(1,128)S(1)}, f32[1,1,32]{2,1,0:T(1,128)}, u32[]{:S(2)}) copy-start(f32[1,1,32]{2,1,0:T(1,128)} %get-tuple-element.277) | copy-start | bytes 388
  162.6 14.5 %copy-start.27 = (f32[1,1,32]{2,1,0:T(1,128)S(1)}, f32[1,1,32]{2,1,0:T(1,128)}, u32[]{:S(2)}) copy-start(f32[1,1,32]{2,1,0:T(1,128)} %get-tuple-element.275) | copy-start | bytes 388
  162.7 20.1 %copy-start.9 = (f32[2176]{0:T(1024)S(1)}, f32[2176]{0:T(1024)}, u32[]{:S(2)}) copy-start(f32[2176]{0:T(1024)} %get-tuple-element.231) | copy-start | bytes 26116
  162.7 20.1 %copy-start.10 = (f32[2176]{0:T(1024)S(1)}, f32[2176]{0:T(1024)}, u32[]{:S(2)}) copy-start(f32[2176]{0:T(1024)} %get-tuple-element.234) | copy-start | bytes 26116
  162.7 20.1 %copy-start.11 = (f32[2176]{0:T(1024)S(1)}, f32[2176]{0:T(1024)}, u32[]{:S(2)}) copy-start(f32[2176]{0:T(1024)} %get-tuple-element.235) | copy-start | bytes 26116
  162.7 20.1 %copy-start.12 = (f32[2176]{0:T(1024)S(1)}, f32[2176]{0:T(1024)}, u32[]{:S(2)}) copy-start(f32[2176]{0:T(1024)} %get-tuple-element.236) | copy-start | bytes 26116
  189.3 61.6 %all-gather.10.cloned.1.call-start = ((), (), s32[]{:S(2)}) async-start(), calls=%async_computation.2 | async-start | bytes 2621440 | tf_op jit(solution)/shard_map/all_gather | solution.py:17
  203.8 15.3 %copy-start.2 = (bf16[128,2176]{0,1:T(8,128)(2,1)S(1)}, bf16[128,2176]{0,1:T(8,128)(2,1)}, u32[]{:S(2)}) copy-start(bf16[128,2176]{0,1:T(8,128)(2,1)} %slice.189) | copy-start | bytes 1671172
  203.8 15.3 %copy-start.8 = (f32[2176]{0:T(1024)S(1)}, f32[2176]{0:T(1024)}, u32[]{:S(2)}) copy-start(f32[2176]{0:T(1024)} %get-tuple-element.238) | copy-start | bytes 26116
  222.8 4.6 %copy-start.1 = (bf16[128,2176]{0,1:T(8,128)(2,1)}, bf16[128,2176]{0,1:T(8,128)(2,1)S(1)}, u32[]{:S(2)}) copy-start(bf16[128,2176]{0,1:T(8,128)(2,1)S(1)} %multiply_convert_fusion.2) | copy-start | bytes 1671172
  (17 other events, 22.2 us)
Sparse Core Ops, SparseCore 0:
  9.4 136.0 all-gather.5
  189.4 21.0 all-gather.7
  229.7 21.0 all-gather.9
where the time goes:
time: 269 us; the launch traced here: 267 us
  waiting for transfers between devices  143 us (53%)
  local copies, waits for them, and re-layouts  49.4 us (18%)
  other arithmetic  30.1 us (11%)
  between operations  15 us (6%)
  matrix products  13.2 us (5%)
  blocking collectives  12.8 us (5%)
  starting transfers between devices  2.86 us (1%)
    all_gather x1, waiting for transfers between devices, project(): lax.all_gather(in_weight, ('fsdp', 'batch'), axis=0, tiled=True)  129 us
    slice x4, local copies, waits for them, and re-layouts, conv_silu(): padded[tap:tap + length].astype(jnp.float32)  30.5 us
    all_gather x2, waiting for transfers between devices, prefix(): pieces = jax.tree.map(lambda part: lax.all_gather(part, axis), value)  13.5 us
    all_gather x2, blocking collectives, prefix(): pieces = jax.tree.map(lambda part: lax.all_gather(part, axis), value)  12.8 us
    convert_element_type x2, other arithmetic, conv_silu(): return jax.nn.silu(total).astype(jnp.bfloat16)  6.24 us
    dot_general x1, matrix products, project(): jnp.dot(rows_in, lax.all_gather(in_weight, ('fsdp', 'batch'), axis=0, til...  6.09 us
  transfers between devices with their start and end apart: 5, of which 2 were waited for; matrix products, arithmetic and copies ran while one was open for 27% of the time, Pallas kernels for 0%

commit v1 on v0

--- a/solution.py
+++ b/solution.py
@@ -1,6 +1,10 @@
+import functools
+
 import jax
 import jax.numpy as jnp
 from jax import lax
+from jax.experimental import pallas as pl
+from jax.experimental.pallas import tpu as pltpu
 from jax.sharding import PartitionSpec as P
 
 HEADS = 32
@@ -141,7 +145,7 @@
     return total.astype(jnp.bfloat16)
 
 
-def on_device(
+def on_sections(
     hidden, in_weight, read_starts, conv_weight, conv_bias, dt_bias, decay, skip, norm_gain
 ):
     tokens = hidden[0]
@@ -173,6 +177,320 @@
     return mixed.astype(jnp.bfloat16)[None]
 
 
+LANES = 128
+SIDE = 256
+EDGE = 8
+
+
+def split_two(value):
+    high = value.astype(jnp.bfloat16)
+    low = (value - high.astype(jnp.float32)).astype(jnp.bfloat16)
+    return high, low
+
+
+def mixer_kernel(
+    heads,
+    shards,
+    ids,
+    marks,
+    *refs,
+):
+    pieces, refs = refs[:4], refs[4:]
+    weights, refs = refs[:shards], refs[shards:]
+    sides, refs = refs[:4], refs[4:]
+    conv_w, conv_b, step_bias, rates, direct, gains = refs[:6]
+    outs, refs = refs[6:10], refs[10:]
+    rows_in, w_own, w_side, padded, xs, cs, bs, steps, cums, tails, leads, fades, turned, total, state, sems = refs
+    seq, fsdp, batch = ids[0], ids[1], ids[2]
+    ring = shards // 2
+    depth = w_own.shape[0] // shards
+    part = depth // 4
+    columns = heads * HEAD_DIM
+    chunks = columns // LANES
+    length = rows_in.shape[0]
+    blocks = length // BLOCK
+
+    copies = []
+    for mask in range(4):
+        place = pl.multiple_of((seq ^ mask) * BLOCK, BLOCK)
+        copies.append((pieces[mask], rows_in.at[pl.ds(place, BLOCK)]))
+    for side in range(2):
+        for turn in range(ring):
+            shard = (fsdp ^ side) * ring + lax.rem(batch + ring - turn, ring)
+            place = pl.multiple_of(shard * depth, depth)
+            at = side * ring + turn
+            copies.append((weights[at], w_own.at[pl.ds(place, depth)]))
+            for mask in range(4):
+                place_side = pl.multiple_of(shard * depth + (seq ^ mask) * part, part)
+                copies.append((sides[mask].at[at], w_side.at[pl.ds(place_side, part)]))
+    copies = [pltpu.make_async_copy(a, b, sems.at[i]) for i, (a, b) in enumerate(copies)]
+    for copy in copies:
+        copy.start()
+    lane = lax.broadcasted_iota(jnp.int32, (BLOCK, LANES), 1)
+    row = lax.broadcasted_iota(jnp.int32, (BLOCK, LANES), 0)
+    edge = jnp.zeros((EDGE, LANES), jnp.float32)
+    for c in range(chunks + 1):
+        padded[c, 0:EDGE, :] = edge
+        padded[c, EDGE + length :, :] = edge
+    total[...] = jnp.zeros_like(total)
+    state[...] = jnp.zeros_like(state)
+    for copy in copies:
+        copy.wait()
+
+    side_out = jnp.dot(rows_in[...], w_side[...], preferred_element_type=jnp.float32)
+    side_out = side_out.astype(jnp.bfloat16).astype(jnp.float32)
+    padded[chunks, EDGE : EDGE + length, :] = side_out[:, :LANES]
+    steps[...] = side_out[:, LANES:]
+    for n in range(columns // SIDE):
+        part_out = jnp.dot(
+            rows_in[...], w_own[:, n * SIDE : (n + 1) * SIDE], preferred_element_type=jnp.float32
+        )
+        part_out = part_out.astype(jnp.bfloat16).astype(jnp.float32)
+        for k in range(SIDE // LANES):
+            padded[n * (SIDE // LANES) + k, EDGE : EDGE + length, :] = part_out[
+                :, k * LANES : (k + 1) * LANES
+            ]
+
+    own_at = pl.multiple_of(seq * columns, columns)
+    short = 64
+
+    def conv_rows(i, carry):
+        at = pl.multiple_of(i * short, short)
+        for c in range(chunks + 1):
+            taps = [padded[c, pl.ds(at + EDGE - 3 + k, short), :] for k in range(7)]
+            if c < chunks:
+                lanes = pl.ds(pl.multiple_of(own_at + c * LANES, LANES), LANES)
+            else:
+                lanes = pl.ds(INNER, LANES)
+            for d in range(2):
+                acc = conv_b[d : d + 1, lanes] + conv_w[d, 0:1, lanes] * taps[0 if d == 0 else 6]
+                for k in range(1, KERNEL):
+                    acc = acc + conv_w[d, k : k + 1, lanes] * taps[k if d == 0 else 6 - k]
+                half = 0.5 * acc
+                value = half + half * jnp.tanh(half)
+                if c < chunks:
+                    xs[d, pl.ds(at, short), c * LANES : (c + 1) * LANES] = value.astype(jnp.bfloat16)
+                else:
+                    upper = lax.broadcasted_iota(jnp.int32, (short, LANES), 1) >= STATE
+                    cs[d, pl.ds(at, short), :] = jnp.where(upper, value, 0.0).astype(jnp.bfloat16)
+                    bs[d, pl.ds(at, short), :] = jnp.where(
+                        upper, pltpu.roll(value, STATE, 1), 0.0
+                    ).astype(jnp.bfloat16)
+        return carry
+
+    lax.fori_loop(0, length // short, conv_rows, 0)
+
+    backward_lane = ((lane >= heads) & (lane < 2 * heads)) | (lane == 2 * heads + 1)
+    head_lane = lane < 2 * heads
+    lower = jnp.where(row >= lane, 1.0, 0.0)
+    upper_sum = jnp.where(row <= lane, 1.0, 0.0)
+
+    def decays(b, carry):
+        at = pl.multiple_of(b * BLOCK, BLOCK)
+        columns_in = steps[pl.ds(at, BLOCK), :]
+        mine = pltpu.roll(columns_in, lax.rem(LANES - seq * heads, LANES), 1)
+        both = jnp.where(lane < heads, mine, pltpu.roll(mine, heads, 1)) + step_bias[...]
+        step = jnp.maximum(both, 0.0) + jnp.log1p(jnp.exp(-jnp.abs(both)))
+        rate = -step * rates[...]
+        position = row + b * BLOCK
+        here = position == marks[0]
+        after = position + 1 == marks[0]
+        for m in range(1, 4):
+            here = here | (position == marks[m])
+            after = after | (position + 1 == marks[m])
+        here = jnp.where(here, 1.0, 0.0)
+        after = jnp.where(after, 1.0, 0.0)
+        rate = jnp.where(
+            head_lane, rate, jnp.where(lane == 2 * heads, here, jnp.where(lane == 2 * heads + 1, after, 0.0))
+        )
+        ahead = jnp.dot(lower, rate, precision=lax.Precision.HIGHEST, preferred_element_type=jnp.float32)
+        behind = jnp.dot(upper_sum, rate, precision=lax.Precision.HIGHEST, preferred_element_type=jnp.float32)
+        cum = jnp.where(backward_lane, behind, ahead)
+        seen = jnp.where(
+            backward_lane,
+            jnp.broadcast_to(cum[:, 2 * heads + 1 : 2 * heads + 2], (BLOCK, LANES)),
+            jnp.broadcast_to(cum[:, 2 * heads : 2 * heads + 1], (BLOCK, LANES)),
+        )
+        last = jnp.where(backward_lane[:1], cum[:1], cum[BLOCK - 1 :])
+        seen_last = jnp.where(backward_lane[:1], seen[:1], seen[BLOCK - 1 :])
+        tail = jnp.where((seen == seen_last) & head_lane, jnp.exp(last - cum) * step, 0.0)
+        lead = jnp.where((seen == 0.0) & head_lane, jnp.exp(cum), 0.0)
+        fade = jnp.where((seen_last == 0.0) & head_lane[:1], jnp.exp(last), 0.0)
+        cums[b] = cum
+        tails[b] = tail
+        leads[b] = lead
+        fades[b] = jnp.broadcast_to(fade, (8, LANES))
+        turned[b] = jnp.where(head_lane, jnp.log(step) - cum, cum).T
+        return carry
+
+    lax.fori_loop(0, blocks, decays, 0)
+
+    own_lanes = pl.ds(own_at, columns)
+    spread_row = lax.broadcasted_iota(jnp.int32, (LANES, columns), 0)
+    spread_head = lax.broadcasted_iota(jnp.int32, (LANES, columns), 1) // HEAD_DIM
+    spreads = [
+        jnp.where(spread_row == spread_head + d * heads, 1.0, 0.0).astype(jnp.bfloat16) for d in range(2)
+    ]
+    same = jnp.where(row // HEAD_DIM == lane // HEAD_DIM, 1.0 / HEAD_DIM, 0.0).astype(jnp.bfloat16)
+    left = lane < HEAD_DIM
+
+    def widen(value, d):
+        high, low = split_two(value)
+        return jnp.dot(high, spreads[d], preferred_element_type=jnp.float32) + jnp.dot(
+            low, spreads[d], preferred_element_type=jnp.float32
+        )
+
+    def scan_step(i, carry):
+        for d in range(2):
+            b = i if d == 0 else blocks - 1 - i
+            at = pl.ds(pl.multiple_of(b * BLOCK, BLOCK), BLOCK)
+            c_part = cs[d, at, :]
+            b_part = bs[d, at, :]
+            scores = lax.dot_general(
+                c_part, b_part, (((1,), (1,)), ((), ())), preferred_element_type=jnp.float32
+            )
+            cum = cums[b]
+            seen_at = 2 * heads + d
+            ordered = (row >= lane) if d == 0 else (row <= lane)
+            allowed = ordered & (cum[:, seen_at : seen_at + 1] == turned[b, seen_at : seen_at + 1, :])
+            barred = jnp.where(allowed, 0.0, -1e30)
+            before = state[d]
+            carried = jnp.dot(c_part, before.astype(jnp.bfloat16), preferred_element_type=jnp.float32)
+            lead = widen(leads[b], d)
+            tail = widen(tails[b], d)
+            fade = widen(fades[b], d)[:1]
+            x_all = xs[d, at, :]
+            x_wide = x_all.astype(jnp.float32)
+            inputs = (tail * x_wide).astype(jnp.bfloat16)
+            local_end = lax.dot_general(
+                b_part, inputs, (((0,), (0,)), ((), ())), preferred_element_type=jnp.float32
+            )
+            state[d] = fade * before + local_end
+            for p in range(chunks):
+                pair = []
+                for h in (2 * p + d * heads, 2 * p + 1 + d * heads):
+                    gap = cum[:, h : h + 1] + (turned[b, h : h + 1, :] + barred)
+                    pair.append((jnp.exp(gap) * scores).astype(jnp.bfloat16))
+                lanes = slice(p * LANES, (p + 1) * LANES)
+                x_pair = x_wide[:, lanes]
+                x_two = jnp.concatenate(
+                    [
+                        jnp.where(left, x_pair, 0.0).astype(jnp.bfloat16),
+                        jnp.where(left, 0.0, x_pair).astype(jnp.bfloat16),
+                    ],
+                    axis=0,
+                )
+                inner = jnp.dot(jnp.concatenate(pair, axis=1), x_two, preferred_element_type=jnp.float32)
+                at_lanes = pl.ds(pl.multiple_of(own_at + p * LANES, LANES), LANES)
+                y = inner + lead[:, lanes] * carried[:, lanes] + direct[d : d + 1, at_lanes] * x_pair
+                high, low = split_two(y * y)
+                mean = jnp.dot(high, same, preferred_element_type=jnp.float32) + jnp.dot(
+                    low, same, preferred_element_type=jnp.float32
+                )
+                scale = lax.rsqrt(mean + 1e-05)
+                total[at, lanes] += y * scale * gains[d : d + 1, at_lanes]
+        return carry
+
+    lax.fori_loop(0, blocks, scan_step, 0)
+    for mask in range(4):
+        at = pl.ds(pl.multiple_of((seq ^ mask) * BLOCK, BLOCK), BLOCK)
+        outs[mask][...] = total[at, :].astype(jnp.bfloat16)
+
+
+def ring_up(value, axis):
+    count = lax.axis_size(axis)
+    return lax.ppermute(value, axis, [(i, (i + 1) % count) for i in range(count)])
+
+
+def swap(value, axis, mask):
+    count = lax.axis_size(axis)
+    return lax.ppermute(value, axis, [(i, i ^ mask) for i in range(count)])
+
+
+def gather_rows(piece):
+    mine = [piece]
+    for _ in range(lax.axis_size("batch") - 1):
+        mine.append(ring_up(mine[-1], "batch"))
+    return mine + [swap(part, "fsdp", 1) for part in mine]
+
+
+def on_heads(
+    hidden, in_weight, read_starts, conv_weight, conv_bias, dt_bias, decay, skip, norm_gain
+):
+    tokens = hidden[0]
+    section = tokens.shape[0]
+    count = lax.axis_size("seq")
+    seq = lax.axis_index("seq")
+    heads = HEADS // count
+    columns = heads * HEAD_DIM
+    depth = in_weight.shape[0]
+    part = depth // count
+    shards = lax.axis_size("fsdp") * lax.axis_size("batch")
+    side = lax.dynamic_slice(in_weight, (seq * part, INNER), (part, in_weight.shape[1] - INNER))
+    side = jnp.pad(side, ((0, 0), (0, SIDE - side.shape[1])))
+    own = lax.dynamic_slice(in_weight, (0, seq * columns), (depth, columns))
+    side_mine = jnp.stack(gather_rows(side))
+    across = swap(tokens, "seq", 2)
+    pieces = [tokens, swap(tokens, "seq", 1), across, swap(across, "seq", 1)]
+    side_across = swap(side_mine, "seq", 2)
+    sides = [side_mine, swap(side_mine, "seq", 1), side_across, swap(side_across, "seq", 1)]
+    weights = gather_rows(own)
+
+    def for_lanes(value):
+        mine = lax.dynamic_slice(value, (0, seq * heads), (2, heads)).reshape(1, 2 * heads)
+        return jnp.pad(mine, ((0, 0), (0, LANES - 2 * heads)))
+
+    length = section * count
+    blocks = length // BLOCK
+    ids = jnp.stack([seq, lax.axis_index("fsdp"), lax.axis_index("batch")]).astype(jnp.int32)
+    in_smem = pl.BlockSpec(memory_space=pltpu.SMEM)
+    in_vmem = pl.BlockSpec(memory_space=pltpu.VMEM)
+    anywhere = pl.BlockSpec(memory_space=pl.ANY)
+    chunks = columns // LANES
+    results = pl.pallas_call(
+        functools.partial(mixer_kernel, heads, shards),
+        out_shape=[jax.ShapeDtypeStruct((section, columns), jnp.bfloat16)] * count,
+        in_specs=[in_smem] * 2 + [anywhere] * (count + shards + count) + [in_vmem] * 6,
+        out_specs=[in_vmem] * count,
+        scratch_shapes=[
+            pltpu.VMEM((length, tokens.shape[1]), jnp.bfloat16),
+            pltpu.VMEM((depth * shards, columns), jnp.bfloat16),
+            pltpu.VMEM((depth * shards, SIDE), jnp.bfloat16),
+            pltpu.VMEM((chunks + 1, length + 2 * EDGE, LANES), jnp.float32),
+            pltpu.VMEM((2, length, columns), jnp.bfloat16),
+            pltpu.VMEM((2, length, LANES), jnp.bfloat16),
+            pltpu.VMEM((2, length, LANES), jnp.bfloat16),
+            pltpu.VMEM((length, LANES), jnp.float32),
+            pltpu.VMEM((blocks, BLOCK, LANES), jnp.float32),
+            pltpu.VMEM((blocks, BLOCK, LANES), jnp.float32),
+            pltpu.VMEM((blocks, BLOCK, LANES), jnp.float32),
+            pltpu.VMEM((blocks, 8, LANES), jnp.float32),
+            pltpu.VMEM((blocks, BLOCK, LANES), jnp.float32),
+            pltpu.VMEM((length, columns), jnp.float32),
+            pltpu.VMEM((2, LANES, columns), jnp.float32),
+            pltpu.SemaphoreType.DMA((count + shards + count * shards,)),
+        ],
+        compiler_params=pltpu.CompilerParams(vmem_limit_bytes=40 * 1024 * 1024),
+    )(
+        ids,
+        read_starts[0],
+        *pieces,
+        *weights,
+        *sides,
+        conv_weight,
+        conv_bias,
+        for_lanes(dt_bias),
+        for_lanes(decay),
+        jnp.repeat(skip, HEAD_DIM, axis=1),
+        norm_gain,
+    )
+    received = [results[0]] + [swap(results[mask], "seq", mask) for mask in range(1, count)]
+    mixed = jnp.zeros((section, INNER), jnp.bfloat16)
+    for mask in range(count):
+        mixed = lax.dynamic_update_slice(mixed, received[mask], (0, (seq ^ mask) * columns))
+    return mixed[None]
+
+
 def solution(mesh):
     in_specs = (
         P(("fsdp", "batch"), "seq", None),
@@ -186,6 +504,16 @@
         P(),
     )
     out_specs = P(("fsdp", "batch"), "seq", None)
-    return jax.shard_map(
-        on_device, mesh=mesh, in_specs=in_specs, out_specs=out_specs, check_vma=False
-    )
+    by_heads = mesh.shape["seq"] == 4 and mesh.shape["fsdp"] == 2
+
+    def mixer(hidden, *rest):
+        whole = by_heads and hidden.shape[1] == mesh.shape["seq"] * BLOCK
+        return jax.shard_map(
+            on_heads if whole else on_sections,
+            mesh=mesh,
+            in_specs=in_specs,
+            out_specs=out_specs,
+            check_vma=False,
+        )(hidden, *rest)
+
+    return mixer

time: 269 us -> 84.9 us (0.32)
  waiting for transfers between devices: 143 us -> 37.8 us
  local copies, waits for them, and re-layouts: 49.4 us -> 13.3 us
  other arithmetic: 30.1 us -> 0.08 us
  starting transfers between devices: 2.86 us -> 19.3 us
  between operations: 15 us -> 0.29 us
  Pallas kernels: 0 us -> 13.7 us
  matrix products: 13.2 us -> 0 us
  blocking collectives: 12.8 us -> 0 us
    all_gather x3 -> x0, waiting for transfers between devices: 142 us -> none  [the longest x1 129 us: project(): lax.all_gather(in_weight, ('fsdp', 'batch'), axis=0, tiled=True)]
    ppermute x2 -> x23, waiting for transfers between devices: 0.01 us -> 37.8 us  [the longest x17 21.2 us: swap(): return lax.ppermute(value, axis, [(i, i ^ mask) for i in range(count)])]
    slice x14 -> x0, local copies, waits for them, and re-layouts: 35.1 us -> none  [the longest x4 30.5 us: conv_silu(): padded[tap:tap + length].astype(jnp.float32)]
    ppermute x2 -> x23, starting transfers between devices: 2.56 us -> 19.3 us  [the longest x17 13 us: swap(): return lax.ppermute(value, axis, [(i, i ^ mask) for i in range(count)])]
    pallas_call x0 -> x1, Pallas kernels: none -> 13.7 us  [on_heads(): pl.pallas_call(functools.partial(mixer_kernel, heads, shards), out_shape=...]
    dot_general x9 -> x0, matrix products: 13.2 us -> none  [the longest x1 6.09 us: project(): jnp.dot(rows_in, lax.all_gather(in_weight, ('fsdp', 'batch'), axis=0, til...]
    all_gather x2 -> x0, blocking collectives: 12.8 us -> none  [prefix(): pieces = jax.tree.map(lambda part: lax.all_gather(part, axis), value)]
    convert_element_type x11 -> x0, other arithmetic: 10.6 us -> none  [the longest x2 6.24 us: conv_silu(): return jax.nn.silu(total).astype(jnp.bfloat16)]
  transfers between devices with their start and end apart: 5 -> 23, of which waited for: 2 -> 12; matrix products, arithmetic and copies ran while one was open for 27% -> 3% of each run, Pallas kernels for 0% -> 0%
where the time goes in v1:
time: 84.9 us; the launch traced here: 84.5 us
  waiting for transfers between devices  37.8 us (45%)
  starting transfers between devices  19.3 us (23%)
  Pallas kernels  13.7 us (16%)
  local copies, waits for them, and re-layouts  13.3 us (16%)
    ppermute x17, waiting for transfers between devices, swap(): return lax.ppermute(value, axis, [(i, i ^ mask) for i in range(count)])  21.2 us
    ppermute x6, waiting for transfers between devices, ring_up(): lax.ppermute(value, axis, [(i, (i + 1) % count) for i in range(count)])  16.6 us
    pallas_call x1, Pallas kernels, on_heads(): pl.pallas_call(functools.partial(mixer_kernel, heads, shards), out_shape=...  13.7 us
    ppermute x17, starting transfers between devices, swap(): return lax.ppermute(value, axis, [(i, i ^ mask) for i in range(count)])  13 us
    unnamed x49, local copies, waits for them, and re-layouts  10.6 us
    ppermute x6, starting transfers between devices, ring_up(): lax.ppermute(value, axis, [(i, (i + 1) % count) for i in range(count)])  6.34 us
  transfers between devices with their start and end apart: 23, of which 12 were waited for; matrix products, arithmetic and copies ran while one was open for 3% of the time, Pallas kernels for 0%

profile of v1, /device:TPU:0, one launch (start us, length us, event | category | flops | bytes accessed | tf_op | source)
XLA Modules:
  0.0 84.5 jit_solution(4410462157752230049)
XLA Ops:
  0.1 1.2 %copy-done = bf16[256,2208]{0,1:T(8,128)(2,1)S(1)} copy-done((bf16[256,2208]{0,1:T(8,128)(2,1)S(1)}, bf16[256,2208]{0,1:T(8,128)(2,1)}, u32[]{:S(2)}) %copy-start) | copy-done | bytes 1130520
  1.5 3.1 %collective-permute-start.10 = (bf16[64,256]{1,0:T(8,128)(2,1)S(1)}, bf16[64,256]{1,0:T(8,128)(2,1)S(1)}, u32[]{:S(2)}, u32[]{:S(2)}) collective-permute-start(bf16[64,256]{1,0:T(8,128)(2,1)S(1)} %pad.11), channel_id=1, source_target_pairs={{0,1},{1,2},{2,3},{3,0},{4,5},{5,6},{6,7},{7,4},{8,9},{9,10},{10,1... | collective-permute-start | bytes 98312 | tf_op jit(solution)/shard_map/ppermute | solution.py:402
  4.5 1.5 %collective-permute-start.13 = (bf16[64,256]{1,0:T(8,128)(2,1)S(1)}, bf16[64,256]{1,0:T(8,128)(2,1)S(1)}, u32[]{:S(2)}, u32[]{:S(2)}) collective-permute-start(bf16[64,256]{1,0:T(8,128)(2,1)S(1)} %pad.11), channel_id=1, source_target_pairs={{0,4},{4,0},{1,5},{5,1},{2,6},{6,2},{3,7},{7,3},{8,12},{12,8},{9,1... | collective-permute-start | bytes 98312 | tf_op jit(solution)/shard_map/ppermute | solution.py:407
  6.2 1.6 %collective-permute-start.3 = (bf16[256,512]{1,0:T(8,128)(2,1)S(1)}, bf16[256,512]{1,0:T(8,128)(2,1)S(1)}, u32[]{:S(2)}, u32[]{:S(2)}) collective-permute-start(bf16[256,512]{1,0:T(8,128)(2,1)S(1)} %copy.12.refs_4_), channel_id=1, source_target_pairs={{0,1},{1,2},{2,3},{3,0},{4,5},{5,6},{6,7},{7,4},{8,9},{9,10},{10,1... | collective-permute-start | bytes 786440 | tf_op jit(solution)/shard_map/ppermute | solution.py:402
  8.4 1.5 %collective-permute-start.1 = (bf16[128,2048]{1,0:T(8,128)(2,1)S(1)}, bf16[128,2048]{1,0:T(8,128)(2,1)S(1)}, u32[]{:S(2)}, u32[]{:S(2)}) collective-permute-start(bf16[128,2048]{1,0:T(8,128)(2,1)S(1)} %bitcast.29), channel_id=1, source_target_pairs={{0,16},{8,24},{16,0},{24,8},{1,17},{9,25},{17,1},{25,9},{2,18},{10... | collective-permute-start | bytes 1572872 | tf_op jit(solution)/shard_map/ppermute | solution.py:407
  9.9 1.6 %collective-permute-start.11 = (bf16[64,256]{1,0:T(8,128)(2,1)S(1)}, bf16[64,256]{1,0:T(8,128)(2,1)S(1)}, u32[]{:S(2)}, u32[]{:S(2)}) collective-permute-start(bf16[64,256]{1,0:T(8,128)(2,1)S(1)} %collective-permute-done.10), channel_id=1, source_target_pairs={{0,1},{1,2},{2,3},{3,0},{4,5},{5,6},{6,7},{7,4},{8,9},{9,10},{10,1... | collective-permute-start | bytes 98312 | tf_op jit(solution)/shard_map/ppermute | solution.py:402
  11.5 4.7 %collective-permute-done.11 = bf16[64,256]{1,0:T(8,128)(2,1)S(1)} collective-permute-done((bf16[64,256]{1,0:T(8,128)(2,1)S(1)}, bf16[64,256]{1,0:T(8,128)(2,1)S(1)}, u32[]{:S(2)}, u32[]{:S(2)}) %collective-permute-start.11) | collective-permute-done | bytes 32800 | tf_op jit(solution)/shard_map/ppermute | solution.py:402
  16.2 5.7 %collective-permute-done.12 = bf16[64,256]{1,0:T(8,128)(2,1)S(1)} collective-permute-done((bf16[64,256]{1,0:T(8,128)(2,1)S(1)}, bf16[64,256]{1,0:T(8,128)(2,1)S(1)}, u32[]{:S(2)}, u32[]{:S(2)}) %collective-permute-start.12) | collective-permute-done | bytes 32800 | tf_op jit(solution)/shard_map/ppermute | solution.py:402
  22.9 1.1 %collective-permute-start.15 = (bf16[64,256]{1,0:T(8,128)(2,1)S(1)}, bf16[64,256]{1,0:T(8,128)(2,1)S(1)}, u32[]{:S(2)}, u32[]{:S(2)}) collective-permute-start(bf16[64,256]{1,0:T(8,128)(2,1)S(1)} %collective-permute-done.11), channel_id=1, source_target_pairs={{0,4},{4,0},{1,5},{5,1},{2,6},{6,2},{3,7},{7,3},{8,12},{12,8},{9,1... | collective-permute-start | bytes 98312 | tf_op jit(solution)/shard_map/ppermute | solution.py:407
  24.0 1.9 %collective-permute-done.14 = bf16[64,256]{1,0:T(8,128)(2,1)S(1)} collective-permute-done((bf16[64,256]{1,0:T(8,128)(2,1)S(1)}, bf16[64,256]{1,0:T(8,128)(2,1)S(1)}, u32[]{:S(2)}, u32[]{:S(2)}) %collective-permute-start.14) | collective-permute-done | bytes 32800 | tf_op jit(solution)/shard_map/ppermute | solution.py:407
  26.8 3.0 %collective-permute-done.16 = bf16[64,256]{1,0:T(8,128)(2,1)S(1)} collective-permute-done((bf16[64,256]{1,0:T(8,128)(2,1)S(1)}, bf16[64,256]{1,0:T(8,128)(2,1)S(1)}, u32[]{:S(2)}, u32[]{:S(2)}) %collective-permute-start.16) | collective-permute-done | bytes 32800 | tf_op jit(solution)/shard_map/ppermute | solution.py:407
  29.8 1.5 %collective-permute-start.18 = (bf16[8,64,256]{2,1,0:T(8,128)(2,1)S(1)}, bf16[8,64,256]{2,1,0:T(8,128)(2,1)}, u32[]{:S(2)}, u32[]{:S(2)}) collective-permute-start(bf16[8,64,256]{2,1,0:T(8,128)(2,1)S(1)} %bitcast_dynamic-update-slice_fusion.4.refs_12_), channel_id=1, source_target_pairs={{0,16},{8,24},{16,0},{24,8},{1,17},{9,25},{17,1},{25,9},{2,18},{10... | collective-permute-start | bytes 786440 | tf_op jit(solution)/shard_map/ppermute | solution.py:407
  33.2 3.0 %collective-permute-done.18.refs_14_ = bf16[8,64,256]{2,1,0:T(8,128)(2,1)} collective-permute-done((bf16[8,64,256]{2,1,0:T(8,128)(2,1)S(1)}, bf16[8,64,256]{2,1,0:T(8,128)(2,1)}, u32[]{:S(2)}, u32[]{:S(2)}) %collective-permute-start.18) | collective-permute-done | bytes 262176 | tf_op jit(solution)/shard_map/ppermute | solution.py:407
  37.9 2.0 %collective-permute-done.4.refs_6_ = bf16[256,512]{1,0:T(8,128)(2,1)} collective-permute-done((bf16[256,512]{1,0:T(8,128)(2,1)S(1)}, bf16[256,512]{1,0:T(8,128)(2,1)}, u32[]{:S(2)}, u32[]{:S(2)}) %collective-permute-start.4) | collective-permute-done | bytes 262176 | tf_op jit(solution)/shard_map/ppermute | solution.py:402
  41.2 1.5 %collective-permute-done.7.refs_9_ = bf16[256,512]{1,0:T(8,128)(2,1)S(1)} collective-permute-done((bf16[256,512]{1,0:T(8,128)(2,1)S(1)}, bf16[256,512]{1,0:T(8,128)(2,1)S(1)}, u32[]{:S(2)}, u32[]{:S(2)}) %collective-permute-start.7) | collective-permute-done | bytes 262176 | tf_op jit(solution)/shard_map/ppermute | solution.py:407
  44.3 4.1 %collective-permute-done.5.refs_7_ = bf16[256,512]{1,0:T(8,128)(2,1)} collective-permute-done((bf16[256,512]{1,0:T(8,128)(2,1)}, bf16[256,512]{1,0:T(8,128)(2,1)}, u32[]{:S(2)}, u32[]{:S(2)}) %collective-permute-start.5) | collective-permute-done | bytes 262176 | tf_op jit(solution)/shard_map/ppermute | solution.py:402
  50.5 2.4 %collective-permute-done.8.refs_10_ = bf16[256,512]{1,0:T(8,128)(2,1)} collective-permute-done((bf16[256,512]{1,0:T(8,128)(2,1)}, bf16[256,512]{1,0:T(8,128)(2,1)}, u32[]{:S(2)}, u32[]{:S(2)}) %collective-permute-start.8) | collective-permute-done | bytes 262176 | tf_op jit(solution)/shard_map/ppermute | solution.py:407
  52.9 3.1 %collective-permute-done.9.refs_11_ = bf16[256,512]{1,0:T(8,128)(2,1)} collective-permute-done((bf16[256,512]{1,0:T(8,128)(2,1)}, bf16[256,512]{1,0:T(8,128)(2,1)}, u32[]{:S(2)}, u32[]{:S(2)}) %collective-permute-start.9) | collective-permute-done | bytes 262176 | tf_op jit(solution)/shard_map/ppermute | solution.py:407
  57.0 0.9 %copy-done.5 = bf16[256,512]{1,0:T(8,128)(2,1)S(1)} copy-done((bf16[256,512]{1,0:T(8,128)(2,1)S(1)}, bf16[256,512]{1,0:T(8,128)(2,1)}, u32[]{:S(2)}) %copy-start.5) | copy-done | bytes 262168
  58.0 0.9 %copy-done.7 = bf16[256,512]{1,0:T(8,128)(2,1)S(1)} copy-done((bf16[256,512]{1,0:T(8,128)(2,1)S(1)}, bf16[256,512]{1,0:T(8,128)(2,1)}, u32[]{:S(2)}) %copy-start.7) | copy-done | bytes 262168
  61.7 13.7 %shard_map.91 = (bf16[128,512]{1,0:T(8,128)(2,1)S(1)}, bf16[128,512]{1,0:T(8,128)(2,1)S(1)}, bf16[128,512]{1,0:T(8,128)(2,1)S(1)}, bf16[128,512]{1,0:T(8,128)(2,1)S(1)}) custom-call(s32[3]{0:T(128)S(1)} %pad_add_fusion.ids, s32[4]{0:T(128)S(1)} %bitcast.32, bf16[128,2048]{1,0:T(8,128)(2,1)S(1)} %bitcast.31, ...), custom_call_target="tpu_custom_call" | custom-call | tf_op jit(solution)/shard_map/pallas_call | solution.py:450
  75.7 1.6 %collective-permute-start.22 = (bf16[128,512]{1,0:T(8,128)(2,1)S(1)}, bf16[128,512]{1,0:T(8,128)(2,1)S(1)}, u32[]{:S(2)}, u32[]{:S(2)}) collective-permute-start(bf16[128,512]{1,0:T(8,128)(2,1)S(1)} %get-tuple-element.12), channel_id=1, source_target_pairs={{0,24},{8,16},{16,8},{24,0},{1,25},{9,17},{17,9},{25,1},{2,26},{10... | collective-permute-start | bytes 393224 | tf_op jit(solution)/shard_map/ppermute | solution.py:407
  77.5 4.4 %collective-permute-done.21 = bf16[128,512]{1,0:T(8,128)(2,1)S(1)} collective-permute-done((bf16[128,512]{1,0:T(8,128)(2,1)S(1)}, bf16[128,512]{1,0:T(8,128)(2,1)S(1)}, u32[]{:S(2)}, u32[]{:S(2)}) %collective-permute-start.21) | collective-permute-done | bytes 131104 | tf_op jit(solution)/shard_map/ppermute | solution.py:407
  81.9 1.9 %collective-permute-done.22 = bf16[128,512]{1,0:T(8,128)(2,1)S(1)} collective-permute-done((bf16[128,512]{1,0:T(8,128)(2,1)S(1)}, bf16[128,512]{1,0:T(8,128)(2,1)S(1)}, u32[]{:S(2)}, u32[]{:S(2)}) %collective-permute-start.22) | collective-permute-done | bytes 131104 | tf_op jit(solution)/shard_map/ppermute | solution.py:407
  (89 shorter events, 16.0 us)
Async XLA Ops:
  0.0 56.0 %copy-start.15 = (s32[1,4]{1,0:T(1,128)S(1)}, s32[1,4]{1,0:T(1,128)}, u32[]{:S(2)}) copy-start(s32[1,4]{1,0:T(1,128)} %param.11) | copy-start | bytes 52
  1.5 8.4 %collective-permute-start.10 = (bf16[64,256]{1,0:T(8,128)(2,1)S(1)}, bf16[64,256]{1,0:T(8,128)(2,1)S(1)}, u32[]{:S(2)}, u32[]{:S(2)}) collective-permute-start(bf16[64,256]{1,0:T(8,128)(2,1)S(1)} %pad.11), channel_id=1, source_target_pairs={{0,1},{1,2},{2,3},{3,0},{4,5},{5,6},{6,7},{7,4},{8,9},{9,10},{10,1... | collective-permute-start | bytes 98312 | tf_op jit(solution)/shard_map/ppermute | solution.py:402
  4.5 18.3 %collective-permute-start.13 = (bf16[64,256]{1,0:T(8,128)(2,1)S(1)}, bf16[64,256]{1,0:T(8,128)(2,1)S(1)}, u32[]{:S(2)}, u32[]{:S(2)}) collective-permute-start(bf16[64,256]{1,0:T(8,128)(2,1)S(1)} %pad.11), channel_id=1, source_target_pairs={{0,4},{4,0},{1,5},{5,1},{2,6},{6,2},{3,7},{7,3},{8,12},{12,8},{9,1... | collective-permute-start | bytes 98312 | tf_op jit(solution)/shard_map/ppermute | solution.py:407
  6.2 25.1 %collective-permute-start.3 = (bf16[256,512]{1,0:T(8,128)(2,1)S(1)}, bf16[256,512]{1,0:T(8,128)(2,1)S(1)}, u32[]{:S(2)}, u32[]{:S(2)}) collective-permute-start(bf16[256,512]{1,0:T(8,128)(2,1)S(1)} %copy.12.refs_4_), channel_id=1, source_target_pairs={{0,1},{1,2},{2,3},{3,0},{4,5},{5,6},{6,7},{7,4},{8,9},{9,10},{10,1... | collective-permute-start | bytes 786440 | tf_op jit(solution)/shard_map/ppermute | solution.py:402
  7.8 23.5 %collective-permute-start.6 = (bf16[256,512]{1,0:T(8,128)(2,1)S(1)}, bf16[256,512]{1,0:T(8,128)(2,1)S(1)}, u32[]{:S(2)}, u32[]{:S(2)}) collective-permute-start(bf16[256,512]{1,0:T(8,128)(2,1)S(1)} %copy.12.refs_4_), channel_id=1, source_target_pairs={{0,4},{4,0},{1,5},{5,1},{2,6},{6,2},{3,7},{7,3},{8,12},{12,8},{9,1... | collective-permute-start | bytes 786440 | tf_op jit(solution)/shard_map/ppermute | solution.py:407
  8.4 31.6 %collective-permute-start.1 = (bf16[128,2048]{1,0:T(8,128)(2,1)S(1)}, bf16[128,2048]{1,0:T(8,128)(2,1)S(1)}, u32[]{:S(2)}, u32[]{:S(2)}) collective-permute-start(bf16[128,2048]{1,0:T(8,128)(2,1)S(1)} %bitcast.29), channel_id=1, source_target_pairs={{0,16},{8,24},{16,0},{24,8},{1,17},{9,25},{17,1},{25,9},{2,18},{10... | collective-permute-start | bytes 1572872 | tf_op jit(solution)/shard_map/ppermute | solution.py:407
  9.9 6.3 %collective-permute-start.11 = (bf16[64,256]{1,0:T(8,128)(2,1)S(1)}, bf16[64,256]{1,0:T(8,128)(2,1)S(1)}, u32[]{:S(2)}, u32[]{:S(2)}) collective-permute-start(bf16[64,256]{1,0:T(8,128)(2,1)S(1)} %collective-permute-done.10), channel_id=1, source_target_pairs={{0,1},{1,2},{2,3},{3,0},{4,5},{5,6},{6,7},{7,4},{8,9},{9,10},{10,1... | collective-permute-start | bytes 98312 | tf_op jit(solution)/shard_map/ppermute | solution.py:402
  16.2 5.7 %collective-permute-start.12 = (bf16[64,256]{1,0:T(8,128)(2,1)S(1)}, bf16[64,256]{1,0:T(8,128)(2,1)S(1)}, u32[]{:S(2)}, u32[]{:S(2)}) collective-permute-start(bf16[64,256]{1,0:T(8,128)(2,1)S(1)} %collective-permute-done.11), channel_id=1, source_target_pairs={{0,1},{1,2},{2,3},{3,0},{4,5},{5,6},{6,7},{7,4},{8,9},{9,10},{10,1... | collective-permute-start | bytes 98312 | tf_op jit(solution)/shard_map/ppermute | solution.py:402
  21.9 3.9 %collective-permute-start.14 = (bf16[64,256]{1,0:T(8,128)(2,1)S(1)}, bf16[64,256]{1,0:T(8,128)(2,1)S(1)}, u32[]{:S(2)}, u32[]{:S(2)}) collective-permute-start(bf16[64,256]{1,0:T(8,128)(2,1)S(1)} %collective-permute-done.10), channel_id=1, source_target_pairs={{0,4},{4,0},{1,5},{5,1},{2,6},{6,2},{3,7},{7,3},{8,12},{12,8},{9,1... | collective-permute-start | bytes 98312 | tf_op jit(solution)/shard_map/ppermute | solution.py:407
  22.9 3.9 %collective-permute-start.15 = (bf16[64,256]{1,0:T(8,128)(2,1)S(1)}, bf16[64,256]{1,0:T(8,128)(2,1)S(1)}, u32[]{:S(2)}, u32[]{:S(2)}) collective-permute-start(bf16[64,256]{1,0:T(8,128)(2,1)S(1)} %collective-permute-done.11), channel_id=1, source_target_pairs={{0,4},{4,0},{1,5},{5,1},{2,6},{6,2},{3,7},{7,3},{8,12},{12,8},{9,1... | collective-permute-start | bytes 98312 | tf_op jit(solution)/shard_map/ppermute | solution.py:407
  25.9 3.9 %collective-permute-start.16 = (bf16[64,256]{1,0:T(8,128)(2,1)S(1)}, bf16[64,256]{1,0:T(8,128)(2,1)S(1)}, u32[]{:S(2)}, u32[]{:S(2)}) collective-permute-start(bf16[64,256]{1,0:T(8,128)(2,1)S(1)} %collective-permute-done.12), channel_id=1, source_target_pairs={{0,4},{4,0},{1,5},{5,1},{2,6},{6,2},{3,7},{7,3},{8,12},{12,8},{9,1... | collective-permute-start | bytes 98312 | tf_op jit(solution)/shard_map/ppermute | solution.py:407
  29.8 6.5 %collective-permute-start.18 = (bf16[8,64,256]{2,1,0:T(8,128)(2,1)S(1)}, bf16[8,64,256]{2,1,0:T(8,128)(2,1)}, u32[]{:S(2)}, u32[]{:S(2)}) collective-permute-start(bf16[8,64,256]{2,1,0:T(8,128)(2,1)S(1)} %bitcast_dynamic-update-slice_fusion.4.refs_12_), channel_id=1, source_target_pairs={{0,16},{8,24},{16,0},{24,8},{1,17},{9,25},{17,1},{25,9},{2,18},{10... | collective-permute-start | bytes 786440 | tf_op jit(solution)/shard_map/ppermute | solution.py:407
  31.3 8.6 %collective-permute-start.4 = (bf16[256,512]{1,0:T(8,128)(2,1)S(1)}, bf16[256,512]{1,0:T(8,128)(2,1)}, u32[]{:S(2)}, u32[]{:S(2)}) collective-permute-start(bf16[256,512]{1,0:T(8,128)(2,1)S(1)} %collective-permute-done.3.refs_5_), channel_id=1, source_target_pairs={{0,1},{1,2},{2,3},{3,0},{4,5},{5,6},{6,7},{7,4},{8,9},{9,10},{10,1... | collective-permute-start | bytes 786440 | tf_op jit(solution)/shard_map/ppermute | solution.py:402
  31.3 19.2 %collective-permute-start = (bf16[128,2048]{1,0:T(8,128)(2,1)S(1)}, bf16[128,2048]{1,0:T(8,128)(2,1)S(1)}, u32[]{:S(2)}, u32[]{:S(2)}) collective-permute-start(bf16[128,2048]{1,0:T(8,128)(2,1)S(1)} %bitcast.30), channel_id=1, source_target_pairs={{0,8},{8,0},{16,24},{24,16},{1,9},{9,1},{17,25},{25,17},{2,10},{10... | collective-permute-start | bytes 1572872 | tf_op jit(solution)/shard_map/ppermute | solution.py:407
  32.0 7.9 %collective-permute-start.17 = (bf16[8,64,256]{2,1,0:T(8,128)(2,1)S(1)}, bf16[8,64,256]{2,1,0:T(8,128)(2,1)S(1)}, u32[]{:S(2)}, u32[]{:S(2)}) collective-permute-start(bf16[8,64,256]{2,1,0:T(8,128)(2,1)S(1)} %bitcast_dynamic-update-slice_fusion.4.refs_12_), channel_id=1, source_target_pairs={{0,8},{8,0},{16,24},{24,16},{1,9},{9,1},{17,25},{25,17},{2,10},{10... | collective-permute-start | bytes 786440 | tf_op jit(solution)/shard_map/ppermute | solution.py:407
  36.3 6.4 %collective-permute-start.7 = (bf16[256,512]{1,0:T(8,128)(2,1)S(1)}, bf16[256,512]{1,0:T(8,128)(2,1)S(1)}, u32[]{:S(2)}, u32[]{:S(2)}) collective-permute-start(bf16[256,512]{1,0:T(8,128)(2,1)S(1)} %collective-permute-done.3.refs_5_), channel_id=1, source_target_pairs={{0,4},{4,0},{1,5},{5,1},{2,6},{6,2},{3,7},{7,3},{8,12},{12,8},{9,1... | collective-permute-start | bytes 786440 | tf_op jit(solution)/shard_map/ppermute | solution.py:407
  39.9 8.5 %collective-permute-start.5 = (bf16[256,512]{1,0:T(8,128)(2,1)}, bf16[256,512]{1,0:T(8,128)(2,1)}, u32[]{:S(2)}, u32[]{:S(2)}) collective-permute-start(bf16[256,512]{1,0:T(8,128)(2,1)} %collective-permute-done.4.refs_6_), channel_id=1, source_target_pairs={{0,1},{1,2},{2,3},{3,0},{4,5},{5,6},{6,7},{7,4},{8,9},{9,10},{10,1... | collective-permute-start | bytes 786440 | tf_op jit(solution)/shard_map/ppermute | solution.py:402
  39.9 16.1 %collective-permute-start.2 = (bf16[128,2048]{1,0:T(8,128)(2,1)S(1)}, bf16[128,2048]{1,0:T(8,128)(2,1)S(1)}, u32[]{:S(2)}, u32[]{:S(2)}) collective-permute-start(bf16[128,2048]{1,0:T(8,128)(2,1)S(1)} %collective-permute-done.1.refs_2_), channel_id=1, source_target_pairs={{0,8},{8,0},{16,24},{24,16},{1,9},{9,1},{17,25},{25,17},{2,10},{10... | collective-permute-start | bytes 1572872 | tf_op jit(solution)/shard_map/ppermute | solution.py:407
  40.7 9.8 %collective-permute-start.19 = (bf16[8,64,256]{2,1,0:T(8,128)(2,1)}, bf16[8,64,256]{2,1,0:T(8,128)(2,1)}, u32[]{:S(2)}, u32[]{:S(2)}) collective-permute-start(bf16[8,64,256]{2,1,0:T(8,128)(2,1)} %collective-permute-done.18.refs_14_), channel_id=1, source_target_pairs={{0,8},{8,0},{16,24},{24,16},{1,9},{9,1},{17,25},{25,17},{2,10},{10... | collective-permute-start | bytes 786440 | tf_op jit(solution)/shard_map/ppermute | solution.py:407
  43.4 9.6 %collective-permute-start.8 = (bf16[256,512]{1,0:T(8,128)(2,1)}, bf16[256,512]{1,0:T(8,128)(2,1)}, u32[]{:S(2)}, u32[]{:S(2)}) collective-permute-start(bf16[256,512]{1,0:T(8,128)(2,1)} %collective-permute-done.4.refs_6_), channel_id=1, source_target_pairs={{0,4},{4,0},{1,5},{5,1},{2,6},{6,2},{3,7},{7,3},{8,12},{12,8},{9,1... | collective-permute-start | bytes 786440 | tf_op jit(solution)/shard_map/ppermute | solution.py:407
  48.4 7.6 %collective-permute-start.9 = (bf16[256,512]{1,0:T(8,128)(2,1)}, bf16[256,512]{1,0:T(8,128)(2,1)}, u32[]{:S(2)}, u32[]{:S(2)}) collective-permute-start(bf16[256,512]{1,0:T(8,128)(2,1)} %collective-permute-done.5.refs_7_), channel_id=1, source_target_pairs={{0,4},{4,0},{1,5},{5,1},{2,6},{6,2},{3,7},{7,3},{8,12},{12,8},{9,1... | collective-permute-start | bytes 786440 | tf_op jit(solution)/shard_map/ppermute | solution.py:407
  75.4 2.0 %collective-permute-start.20 = (bf16[128,512]{1,0:T(8,128)(2,1)S(1)}, bf16[128,512]{1,0:T(8,128)(2,1)S(1)}, u32[]{:S(2)}, u32[]{:S(2)}) collective-permute-start(bf16[128,512]{1,0:T(8,128)(2,1)S(1)} %get-tuple-element.10), channel_id=1, source_target_pairs={{0,8},{8,0},{16,24},{24,16},{1,9},{9,1},{17,25},{25,17},{2,10},{10... | collective-permute-start | bytes 393224 | tf_op jit(solution)/shard_map/ppermute | solution.py:407
  75.5 6.4 %collective-permute-start.21 = (bf16[128,512]{1,0:T(8,128)(2,1)S(1)}, bf16[128,512]{1,0:T(8,128)(2,1)S(1)}, u32[]{:S(2)}, u32[]{:S(2)}) collective-permute-start(bf16[128,512]{1,0:T(8,128)(2,1)S(1)} %get-tuple-element.11), channel_id=1, source_target_pairs={{0,16},{8,24},{16,0},{24,8},{1,17},{9,25},{17,1},{25,9},{2,18},{10... | collective-permute-start | bytes 393224 | tf_op jit(solution)/shard_map/ppermute | solution.py:407
  75.7 8.0 %collective-permute-start.22 = (bf16[128,512]{1,0:T(8,128)(2,1)S(1)}, bf16[128,512]{1,0:T(8,128)(2,1)S(1)}, u32[]{:S(2)}, u32[]{:S(2)}) collective-permute-start(bf16[128,512]{1,0:T(8,128)(2,1)S(1)} %get-tuple-element.12), channel_id=1, source_target_pairs={{0,24},{8,16},{16,8},{24,0},{1,25},{9,17},{17,9},{25,1},{2,26},{10... | collective-permute-start | bytes 393224 | tf_op jit(solution)/shard_map/ppermute | solution.py:407
  (19 other events, 278.8 us)

commit v2 on v0

--- a/solution.py
+++ b/solution.py
@@ -1,6 +1,10 @@
+import functools
+
 import jax
 import jax.numpy as jnp
 from jax import lax
+from jax.experimental import pallas as pl
+from jax.experimental.pallas import tpu as pltpu
 from jax.sharding import PartitionSpec as P
 
 HEADS = 32
@@ -141,7 +145,7 @@
     return total.astype(jnp.bfloat16)
 
 
-def on_device(
+def on_sections(
     hidden, in_weight, read_starts, conv_weight, conv_bias, dt_bias, decay, skip, norm_gain
 ):
     tokens = hidden[0]
@@ -173,6 +177,345 @@
     return mixed.astype(jnp.bfloat16)[None]
 
 
+LANES = 128
+SIDE = 256
+EDGE = 8
+
+
+def ring_order(count):
+    return [i if i < count else 3 * count - 1 - i for i in range(2 * count)]
+
+
+def split_three(value):
+    parts = []
+    for _ in range(3):
+        parts.append(value.astype(jnp.bfloat16))
+        value = value - parts[-1].astype(jnp.float32)
+    return parts
+
+
+def mixer_kernel(heads, shards, ids, marks, *refs):
+    pieces, refs = refs[:4], refs[4:]
+    weights, refs = refs[: shards - 1], refs[shards - 1 :]
+    ends, refs = refs[:2], refs[2:]
+    own_side, refs = refs[0], refs[1:]
+    swapped, refs = refs[: shards // 2], refs[shards // 2 :]
+    conv_w, conv_b, step_bias, rates, direct, gains = refs[:6]
+    outs, refs = refs[6:10], refs[10:]
+    rows_in, w_own, w_side, padded, xs, cs, bs, steps, refs = (*refs[:8], refs[8:])
+    cums, tails, leads, fades, turned, barred, spread, columns_of, total, state = refs
+    seq, core = ids[0], ids[1]
+    columns = heads * HEAD_DIM
+    depth = own_side.shape[1]
+    side_rows = own_side.shape[0]
+    half_side = side_rows // 2
+    chunks = columns // LANES
+    length = rows_in.shape[0]
+    blocks = length // BLOCK
+    cut = ends[0].shape[0]
+
+    lane = lax.broadcasted_iota(jnp.int32, (BLOCK, LANES), 1)
+    row = lax.broadcasted_iota(jnp.int32, (BLOCK, LANES), 0)
+
+    for mask in range(4):
+        rows_in[mask * BLOCK : (mask + 1) * BLOCK, :] = pieces[mask][...]
+    mine = pl.ds(pl.multiple_of(core * half_side, 16), half_side)
+    other = pl.ds(pl.multiple_of((1 - core) * half_side, 16), half_side)
+    w_side[side_rows:, :] = jnp.zeros((SIDE - side_rows, w_side.shape[1]), jnp.bfloat16)
+    for n in range(shards):
+        at = pl.ds(pl.multiple_of(ids[2 + n] * depth, depth), depth)
+        if n < shards - 1:
+            w_own[:, at] = weights[n][:columns, :]
+            if n:
+                w_side[mine, at] = weights[n][columns:, :]
+        else:
+            w_own[:cut, at] = ends[0][...]
+            w_own[cut:, at] = ends[1][: columns - cut, :]
+            w_side[mine, at] = ends[1][columns - cut :, :]
+        if n:
+            w_side[other, at] = swapped[(n - 1) // 2][pl.ds((n - 1) % 2 * half_side, half_side), :]
+        else:
+            w_side[:side_rows, at] = own_side[...]
+    edge = jnp.zeros((EDGE, LANES), jnp.float32)
+    for c in range(chunks + 1):
+        padded[c, 0:EDGE, :] = edge
+        padded[c, EDGE + length :, :] = edge
+
+    def project_in(weight):
+        out = lax.dot_general(
+            rows_in[...], weight, (((1,), (1,)), ((), ())), preferred_element_type=jnp.float32
+        )
+        return out.astype(jnp.bfloat16).astype(jnp.float32)
+
+    def keep(c, value):
+        for mask in range(4):
+            place = pl.multiple_of((seq ^ mask) * BLOCK, BLOCK)
+            padded[c, pl.ds(EDGE + place, BLOCK), :] = value[mask * BLOCK : (mask + 1) * BLOCK, :]
+
+    side_out = project_in(w_side[...])
+    keep(chunks, side_out[:, :LANES])
+    for mask in range(4):
+        place = pl.multiple_of((seq ^ mask) * BLOCK, BLOCK)
+        steps[pl.ds(place, BLOCK), :] = side_out[mask * BLOCK : (mask + 1) * BLOCK, LANES:]
+    for n in range(columns // SIDE):
+        part_out = project_in(w_own[n * SIDE : (n + 1) * SIDE, :])
+        for k in range(SIDE // LANES):
+            keep(n * (SIDE // LANES) + k, part_out[:, k * LANES : (k + 1) * LANES])
+
+    own_at = pl.multiple_of(seq * columns, columns)
+    short = 64
+
+    def conv_rows(i, carry):
+        at = pl.multiple_of(i * short, short)
+        for c in range(chunks + 1):
+            taps = [padded[c, pl.ds(at + EDGE - 3 + k, short), :] for k in range(7)]
+            if c < chunks:
+                lanes = pl.ds(pl.multiple_of(own_at + c * LANES, LANES), LANES)
+            else:
+                lanes = pl.ds(INNER, LANES)
+            for d in range(2):
+                acc = conv_b[d : d + 1, lanes] + conv_w[d, 0:1, lanes] * taps[0 if d == 0 else 6]
+                for k in range(1, KERNEL):
+                    acc = acc + conv_w[d, k : k + 1, lanes] * taps[k if d == 0 else 6 - k]
+                half = 0.5 * acc
+                value = half + half * jnp.tanh(half)
+                if c < chunks:
+                    xs[d, pl.ds(at, short), c * LANES : (c + 1) * LANES] = value.astype(jnp.bfloat16)
+                else:
+                    upper = lax.broadcasted_iota(jnp.int32, (short, LANES), 1) >= STATE
+                    cs[d, pl.ds(at, short), :] = jnp.where(upper, value, 0.0).astype(jnp.bfloat16)
+                    bs[d, pl.ds(at, short), :] = jnp.where(
+                        upper, pltpu.roll(value, STATE, 1), 0.0
+                    ).astype(jnp.bfloat16)
+        return carry
+
+    lax.fori_loop(0, length // short, conv_rows, 0)
+
+    backward_lane = ((lane >= heads) & (lane < 2 * heads)) | (lane == 2 * heads + 1)
+    head_lane = lane < 2 * heads
+    lower = jnp.where(row >= lane, 1.0, 0.0).astype(jnp.bfloat16)
+    upper_sum = jnp.where(row <= lane, 1.0, 0.0).astype(jnp.bfloat16)
+
+    def decays(b, carry):
+        at = pl.multiple_of(b * BLOCK, BLOCK)
+        columns_in = steps[pl.ds(at, BLOCK), :]
+        mine = pltpu.roll(columns_in, lax.rem(LANES - seq * heads, LANES), 1)
+        both = jnp.where(lane < heads, mine, pltpu.roll(mine, heads, 1)) + step_bias[...]
+        step = jnp.maximum(both, 0.0) + jnp.log1p(jnp.exp(-jnp.abs(both)))
+        rate = -step * rates[...]
+        position = row + b * BLOCK
+        here = position == marks[0]
+        after = position + 1 == marks[0]
+        for m in range(1, 4):
+            here = here | (position == marks[m])
+            after = after | (position + 1 == marks[m])
+        here = jnp.where(here, 1.0, 0.0)
+        after = jnp.where(after, 1.0, 0.0)
+        rate = jnp.where(
+            head_lane, rate, jnp.where(lane == 2 * heads, here, jnp.where(lane == 2 * heads + 1, after, 0.0))
+        )
+        parts = split_three(rate)
+        ahead = sum(jnp.dot(lower, p, preferred_element_type=jnp.float32) for p in parts)
+        behind = sum(jnp.dot(upper_sum, p, preferred_element_type=jnp.float32) for p in parts)
+        cum = jnp.where(backward_lane, behind, ahead)
+        seen = jnp.where(
+            backward_lane,
+            jnp.broadcast_to(cum[:, 2 * heads + 1 : 2 * heads + 2], (BLOCK, LANES)),
+            jnp.broadcast_to(cum[:, 2 * heads : 2 * heads + 1], (BLOCK, LANES)),
+        )
+        last = jnp.where(backward_lane[:1], cum[:1], cum[BLOCK - 1 :])
+        seen_last = jnp.where(backward_lane[:1], seen[:1], seen[BLOCK - 1 :])
+        tail = jnp.where((seen == seen_last) & head_lane, jnp.exp(last - cum) * step, 0.0)
+        lead = jnp.where((seen == 0.0) & head_lane, jnp.exp(cum), 0.0)
+        fade = jnp.where((seen_last == 0.0) & head_lane[:1], jnp.exp(last), 0.0)
+        parts = split_three(jnp.where(head_lane, cum, 0.0))
+        joined = parts[0].astype(jnp.float32)
+        for k in range(1, 3):
+            joined = joined + pltpu.roll(parts[k].astype(jnp.float32), 2 * heads * k, 1)
+        cums[b] = joined.astype(jnp.bfloat16)
+        tails[b] = tail.astype(jnp.bfloat16)
+        leads[b] = lead.astype(jnp.bfloat16)
+        high = fade.astype(jnp.bfloat16).astype(jnp.float32)
+        fades[b] = jnp.broadcast_to(high + pltpu.roll(fade - high, 2 * heads, 1), (16, LANES)).astype(
+            jnp.bfloat16
+        )
+        shown = jnp.where(head_lane, jnp.log(step) - cum, cum).T
+        turned[b] = shown
+        for d in range(2):
+            ordered = (row >= lane) if d == 0 else (row <= lane)
+            seen_at = 2 * heads + d
+            allowed = ordered & (cum[:, seen_at : seen_at + 1] == shown[seen_at : seen_at + 1, :])
+            barred[d, b] = jnp.where(allowed, 0.0, -1e30)
+        return carry
+
+    lax.fori_loop(0, blocks, decays, 0)
+
+    def head_columns(width, group, d):
+        at_row = lax.broadcasted_iota(jnp.int32, (LANES, width), 0)
+        head = lax.broadcasted_iota(jnp.int32, (LANES, width), 1) // group + d * heads
+        hit = (at_row == head) | (at_row == head + 2 * heads) | (at_row == head + 4 * heads)
+        return jnp.where(hit, 1.0, 0.0).astype(jnp.bfloat16)
+
+    for d in range(2):
+        spread[d] = head_columns(columns, HEAD_DIM, d)
+        columns_of[d] = head_columns(heads * LANES, LANES, d)
+    total[...] = jnp.zeros_like(total)
+    state[...] = jnp.zeros_like(state)
+    same = jnp.where(row // HEAD_DIM == lane // HEAD_DIM, 1.0 / HEAD_DIM, 0.0).astype(jnp.bfloat16)
+    left = lane < HEAD_DIM
+
+    def scan_step(i, carry):
+        for d in range(2):
+            b = i if d == 0 else blocks - 1 - i
+            at = pl.ds(pl.multiple_of(b * BLOCK, BLOCK), BLOCK)
+            c_part = cs[d, at, :]
+            b_part = bs[d, at, :]
+            scores = lax.dot_general(
+                c_part, b_part, (((1,), (1,)), ((), ())), preferred_element_type=jnp.float32
+            )
+            bar = barred[d, b]
+            before = state[d]
+            carried = jnp.dot(c_part, before.astype(jnp.bfloat16), preferred_element_type=jnp.float32)
+            lead = jnp.dot(leads[b], spread[d], preferred_element_type=jnp.float32)
+            tail = jnp.dot(tails[b], spread[d], preferred_element_type=jnp.float32)
+            fade = jnp.dot(fades[b], spread[d], preferred_element_type=jnp.float32)[:1]
+            shown = jnp.dot(cums[b], columns_of[d], preferred_element_type=jnp.float32)
+            x_all = xs[d, at, :]
+            x_wide = x_all.astype(jnp.float32)
+            inputs = (tail * x_wide).astype(jnp.bfloat16)
+            local_end = lax.dot_general(
+                b_part, inputs, (((0,), (0,)), ((), ())), preferred_element_type=jnp.float32
+            )
+            state[d] = fade * before + local_end
+            for p in range(chunks):
+                pair = []
+                for h in (2 * p, 2 * p + 1):
+                    at_row = d * heads + h
+                    gap = shown[:, h * LANES : (h + 1) * LANES] + (turned[b, at_row : at_row + 1, :] + bar)
+                    pair.append((jnp.exp(gap) * scores).astype(jnp.bfloat16))
+                lanes = slice(p * LANES, (p + 1) * LANES)
+                x_pair = x_all[:, lanes]
+                none = jnp.zeros_like(x_pair)
+                x_two = jnp.concatenate([jnp.where(left, x_pair, none), jnp.where(left, none, x_pair)], axis=0)
+                inner = jnp.dot(jnp.concatenate(pair, axis=1), x_two, preferred_element_type=jnp.float32)
+                at_lanes = pl.ds(pl.multiple_of(own_at + p * LANES, LANES), LANES)
+                y = inner + lead[:, lanes] * carried[:, lanes] + direct[d : d + 1, at_lanes] * x_wide[:, lanes]
+                mean = jnp.dot((y * y).astype(jnp.bfloat16), same, preferred_element_type=jnp.float32)
+                scale = lax.rsqrt(mean + 1e-05)
+                total[at, lanes] += y * scale * gains[d : d + 1, at_lanes]
+        return carry
+
+    lax.fori_loop(0, blocks, scan_step, 0)
+    for mask in range(4):
+        at = pl.ds(pl.multiple_of((seq ^ mask) * BLOCK, BLOCK), BLOCK)
+        outs[mask][...] = total[at, :].astype(jnp.bfloat16)
+
+
+def mix(heads, ids, marks, pieces, weights, ends, own_side, swapped, params):
+    conv_weight, conv_bias, dt_bias, decay, skip, norm_gain = params
+    shards = len(weights) + 1
+    section, width = pieces[0].shape
+    columns = heads * HEAD_DIM
+    length = section * len(pieces)
+    blocks = length // BLOCK
+    chunks = columns // LANES
+    in_smem = pl.BlockSpec(memory_space=pltpu.SMEM)
+    in_vmem = pl.BlockSpec(memory_space=pltpu.VMEM)
+    operands = (*pieces, *weights, *ends, own_side, *swapped, conv_weight, conv_bias, dt_bias, decay, skip, norm_gain)
+    scratch = [
+        ((length, width), jnp.bfloat16),
+        ((columns, width), jnp.bfloat16),
+        ((SIDE, width), jnp.bfloat16),
+        ((chunks + 1, length + 2 * EDGE, LANES), jnp.float32),
+        ((2, length, columns), jnp.bfloat16),
+        ((2, length, LANES), jnp.bfloat16),
+        ((2, length, LANES), jnp.bfloat16),
+        ((length, LANES), jnp.float32),
+        ((blocks, BLOCK, LANES), jnp.bfloat16),
+        ((blocks, BLOCK, LANES), jnp.bfloat16),
+        ((blocks, BLOCK, LANES), jnp.bfloat16),
+        ((blocks, 16, LANES), jnp.bfloat16),
+        ((blocks, BLOCK, LANES), jnp.float32),
+        ((2, blocks, BLOCK, LANES), jnp.float32),
+        ((2, LANES, columns), jnp.bfloat16),
+        ((2, LANES, heads * LANES), jnp.bfloat16),
+        ((length, columns), jnp.float32),
+        ((2, LANES, columns), jnp.float32),
+    ]
+    return pl.pallas_call(
+        functools.partial(mixer_kernel, heads, shards),
+        out_shape=[jax.ShapeDtypeStruct((section, columns), jnp.bfloat16)] * len(pieces),
+        in_specs=[in_smem] * 2 + [in_vmem] * len(operands),
+        out_specs=[in_vmem] * len(pieces),
+        scratch_shapes=[pltpu.VMEM(*one) for one in scratch],
+        compiler_params=pltpu.CompilerParams(vmem_limit_bytes=32 * 1024 * 1024),
+    )(ids, marks, *operands)
+
+
+def turn(value, way):
+    order = ring_order(lax.axis_size("batch"))
+    count = len(order)
+    return lax.ppermute(value, ("fsdp", "batch"), [(order[i], order[(i + way) % count]) for i in range(count)])
+
+
+def swap(value, axis, mask):
+    return lax.ppermute(value, axis, [(i, i ^ mask) for i in range(lax.axis_size(axis))])
+
+
+def on_heads(hidden, in_weight, read_starts, conv_weight, conv_bias, dt_bias, decay, skip, norm_gain):
+    tokens = hidden[0]
+    count = lax.axis_size("seq")
+    seq = lax.axis_index("seq")
+    core = seq % 2
+    heads = HEADS // count
+    columns = heads * HEAD_DIM
+    by_column = in_weight.T
+    side_rows = by_column.shape[0] - INNER
+    half_side = side_rows // 2
+    own_side = by_column[INNER:]
+    own = lax.dynamic_slice_in_dim(by_column, seq * columns, columns, axis=0)
+    own = jnp.concatenate([own, lax.dynamic_slice_in_dim(own_side, core * half_side, half_side, axis=0)])
+
+    order = ring_order(lax.axis_size("batch"))
+    shards = len(order)
+    up, down = [own], [own]
+    for _ in range(shards // 2 - 1):
+        up.append(turn(up[-1], 1))
+        down.append(turn(down[-1], -1))
+    cut = own.shape[0] // 32 * 16 + 16
+    ends = [turn(up[-1][:cut], 1), turn(down[-1][cut:], -1)]
+    weights = [own]
+    for a, b in zip(up[1:], down[1:]):
+        weights += [a, b]
+    sides = [one[columns:] for one in weights[1:]] + [ends[1][columns - cut :]]
+    swapped = [swap(jnp.concatenate(sides[i : i + 2]), "seq", 1) for i in range(0, shards - 1, 2)]
+    across = swap(tokens, "seq", 2)
+    pieces = [tokens, swap(tokens, "seq", 1), across, swap(across, "seq", 1)]
+
+    place = jnp.asarray([order.index(i) for i in range(shards)], jnp.int32)[
+        lax.axis_index("fsdp") * lax.axis_size("batch") + lax.axis_index("batch")
+    ]
+    steps = [0]
+    for i in range(1, shards // 2):
+        steps += [-i, i]
+    steps.append(shards // 2)
+    shard_ids = jnp.asarray(order, jnp.int32)[(place + jnp.asarray(steps, jnp.int32)) % shards]
+    ids = jnp.concatenate([jnp.stack([seq, core]).astype(jnp.int32), shard_ids])
+
+    def for_lanes(value):
+        mine = lax.dynamic_slice(value, (0, seq * heads), (2, heads)).reshape(1, 2 * heads)
+        return jnp.pad(mine, ((0, 0), (0, LANES - 2 * heads)))
+
+    wide_skip = jnp.repeat(skip, HEAD_DIM, axis=1)
+    params = (conv_weight, conv_bias, for_lanes(dt_bias), for_lanes(decay), wide_skip, norm_gain)
+    results = mix(heads, ids, read_starts[0], pieces, weights, ends, own_side, swapped, params)
+    received = [results[0]] + [swap(results[mask], "seq", mask) for mask in range(1, count)]
+    mixed = jnp.zeros((tokens.shape[0], INNER), jnp.bfloat16)
+    for mask in range(count):
+        mixed = lax.dynamic_update_slice(mixed, received[mask], (0, (seq ^ mask) * columns))
+    return mixed[None]
+
+
 def solution(mesh):
     in_specs = (
         P(("fsdp", "batch"), "seq", None),
@@ -186,6 +529,16 @@
         P(),
     )
     out_specs = P(("fsdp", "batch"), "seq", None)
-    return jax.shard_map(
-        on_device, mesh=mesh, in_specs=in_specs, out_specs=out_specs, check_vma=False
-    )
+    by_heads = mesh.shape["seq"] == 4 and mesh.shape["fsdp"] == 2
+
+    def mixer(hidden, *rest):
+        whole = by_heads and hidden.shape[1] == mesh.shape["seq"] * BLOCK
+        return jax.shard_map(
+            on_heads if whole else on_sections,
+            mesh=mesh,
+            in_specs=in_specs,
+            out_specs=out_specs,
+            check_vma=False,
+        )(hidden, *rest)
+
+    return mixer

time: 269 us -> 71.4 us (0.27)
  waiting for transfers between devices: 143 us -> 22 us
  local copies, waits for them, and re-layouts: 49.4 us -> 17.6 us
  other arithmetic: 30.1 us -> 2.5 us
  Pallas kernels: 0 us -> 15 us
  between operations: 15 us -> 0.25 us
  matrix products: 13.2 us -> 0 us
  blocking collectives: 12.8 us -> 0 us
  starting transfers between devices: 2.86 us -> 13.1 us
    all_gather x3 -> x0, waiting for transfers between devices: 142 us -> none  [the longest x1 129 us: project(): lax.all_gather(in_weight, ('fsdp', 'batch'), axis=0, tiled=True)]
    slice x14 -> x10, local copies, waits for them, and re-layouts: 35.1 us -> 4.62 us  [the longest x7 2.98 us: on_heads(): sides = [one[columns:] for one in weights[1:]] + [ends[1][columns - cut:]]]
    ppermute x2 -> x18, waiting for transfers between devices: 0.01 us -> 22 us  [the longest x8 16.3 us: turn(): lax.ppermute(value, ('fsdp', 'batch'), [(order[i], order[(i + way) % coun...]
    pallas_call x0 -> x1, Pallas kernels: none -> 15 us  [mix(): pl.pallas_call(functools.partial(mixer_kernel, heads, shards), out_shape=...]
    dot_general x9 -> x0, matrix products: 13.2 us -> none  [the longest x1 6.09 us: project(): jnp.dot(rows_in, lax.all_gather(in_weight, ('fsdp', 'batch'), axis=0, til...]
    all_gather x2 -> x0, blocking collectives: 12.8 us -> none  [prefix(): pieces = jax.tree.map(lambda part: lax.all_gather(part, axis), value)]
    convert_element_type x11 -> x0, other arithmetic: 10.6 us -> none  [the longest x2 6.24 us: conv_silu(): return jax.nn.silu(total).astype(jnp.bfloat16)]
    ppermute x2 -> x18, starting transfers between devices: 2.56 us -> 13.1 us  [the longest x8 8.33 us: turn(): lax.ppermute(value, ('fsdp', 'batch'), [(order[i], order[(i + way) % coun...]
  transfers between devices with their start and end apart: 5 -> 18, of which waited for: 2 -> 7; matrix products, arithmetic and copies ran while one was open for 27% -> 14% of each run, Pallas kernels for 0% -> 0%
where the time goes in v2:
time: 71.4 us; the launch traced here: 70.5 us
  waiting for transfers between devices  22 us (31%)
  local copies, waits for them, and re-layouts  17.6 us (25%)
  Pallas kernels  15 us (21%)
  starting transfers between devices  13.1 us (18%)
  other arithmetic  2.5 us (4%)
    ppermute x8, waiting for transfers between devices, turn(): lax.ppermute(value, ('fsdp', 'batch'), [(order[i], order[(i + way) % coun...  16.3 us
    pallas_call x1, Pallas kernels, mix(): pl.pallas_call(functools.partial(mixer_kernel, heads, shards), out_shape=...  15 us
    ppermute x8, starting transfers between devices, turn(): lax.ppermute(value, ('fsdp', 'batch'), [(order[i], order[(i + way) % coun...  8.33 us
    unnamed x36, local copies, waits for them, and re-layouts  7.29 us
    ppermute x10, waiting for transfers between devices, swap(): lax.ppermute(value, axis, [(i, i ^ mask) for i in range(lax.axis_size(axi...  5.68 us
    ppermute x10, starting transfers between devices, swap(): lax.ppermute(value, axis, [(i, i ^ mask) for i in range(lax.axis_size(axi...  4.8 us
    slice x7, local copies, waits for them, and re-layouts, on_heads(): sides = [one[columns:] for one in weights[1:]] + [ends[1][columns - cut:]]  2.98 us
  transfers between devices with their start and end apart: 18, of which 7 were waited for; matrix products, arithmetic and copies ran while one was open for 14% of the time, Pallas kernels for 0%

profile of v2, /device:TPU:0, one launch (start us, length us, event | category | flops | bytes accessed | tf_op | source)
XLA Modules:
  0.0 70.5 jit_solution(7790133302167171513)
XLA Ops:
  0.0 1.0 %slice.42.refs_13_ = bf16[160,256]{1,0:T(8,128)(2,1)S(1)} slice(bf16[2208,256]{1,0:T(8,128)(2,1)} %bitcast.20), slice={[2048:2208], [0:256]} | slice | bytes 163840 | tf_op jit(solution)/shard_map/slice | solution.py:475
  1.0 1.0 %dynamic-slice_bitcast_fusion = bf16[512,256]{1,0:T(8,128)(2,1)S(1)} fusion(bf16[256,2208]{0,1:T(8,128)(2,1)} %param.13, s32[]{:T(128)S(6)} %select_n.45), kind=kLoop, calls=%fused_computation.2 | loop fusion | bytes 524292 | tf_op jit(solution)/shard_map/dynamic_slice | solution.py:476
  2.0 3.0 %collective-permute-start.4 = (bf16[592,256]{1,0:T(8,128)(2,1)S(1)}, bf16[592,256]{1,0:T(8,128)(2,1)S(1)}, u32[]{:S(2)}, u32[]{:S(2)}) collective-permute-start(bf16[592,256]{1,0:T(8,128)(2,1)S(1)} %pad_maximum_fusion.refs_4_), channel_id=1, source_target_pairs={{0,4},{1,0},{2,1},{3,2},{7,3},{6,7},{5,6},{4,5},{8,12},{9,8},{10,9... | collective-permute-start | bytes 909320 | tf_op jit(solution)/shard_map/ppermute | solution.py:458
  5.2 1.9 %collective-permute-start.1 = (bf16[128,2048]{1,0:T(8,128)(2,1)S(1)}, bf16[128,2048]{1,0:T(8,128)(2,1)S(1)}, u32[]{:S(2)}, u32[]{:S(2)}) collective-permute-start(bf16[128,2048]{1,0:T(8,128)(2,1)S(1)} %bitcast.16), channel_id=1, source_target_pairs={{0,16},{8,24},{16,0},{24,8},{1,17},{9,25},{17,1},{25,9},{2,18},{10... | collective-permute-start | bytes 1572872 | tf_op jit(solution)/shard_map/ppermute | solution.py:462
  7.1 5.2 %collective-permute-done.4.refs_6_ = bf16[592,256]{1,0:T(8,128)(2,1)S(1)} collective-permute-done((bf16[592,256]{1,0:T(8,128)(2,1)S(1)}, bf16[592,256]{1,0:T(8,128)(2,1)S(1)}, u32[]{:S(2)}, u32[]{:S(2)}) %collective-permute-start.4) | collective-permute-done | bytes 303136 | tf_op jit(solution)/shard_map/ppermute | solution.py:458
  12.3 1.7 %collective-permute-start.6 = (bf16[592,256]{1,0:T(8,128)(2,1)S(1)}, bf16[592,256]{1,0:T(8,128)(2,1)}, u32[]{:S(2)}, u32[]{:S(2)}) collective-permute-start(bf16[592,256]{1,0:T(8,128)(2,1)S(1)} %collective-permute-done.4.refs_6_), channel_id=1, source_target_pairs={{0,4},{1,0},{2,1},{3,2},{7,3},{6,7},{5,6},{4,5},{8,12},{9,8},{10,9... | collective-permute-start | bytes 909320 | tf_op jit(solution)/shard_map/ppermute | solution.py:458
  15.5 5.3 %collective-permute-done.6.refs_8_ = bf16[592,256]{1,0:T(8,128)(2,1)} collective-permute-done((bf16[592,256]{1,0:T(8,128)(2,1)S(1)}, bf16[592,256]{1,0:T(8,128)(2,1)}, u32[]{:S(2)}, u32[]{:S(2)}) %collective-permute-start.6) | collective-permute-done | bytes 303136 | tf_op jit(solution)/shard_map/ppermute | solution.py:458
  20.8 1.3 %collective-permute-start.8 = (bf16[592,256]{1,0:T(8,128)(2,1)}, bf16[592,256]{1,0:T(8,128)(2,1)S(1)}, u32[]{:S(2)}, u32[]{:S(2)}) collective-permute-start(bf16[592,256]{1,0:T(8,128)(2,1)} %collective-permute-done.6.refs_8_), channel_id=1, source_target_pairs={{0,4},{1,0},{2,1},{3,2},{7,3},{6,7},{5,6},{4,5},{8,12},{9,8},{10,9... | collective-permute-start | bytes 909320 | tf_op jit(solution)/shard_map/ppermute | solution.py:458
  22.8 1.4 %collective-permute-done.5.refs_7_ = bf16[592,256]{1,0:T(8,128)(2,1)} collective-permute-done((bf16[592,256]{1,0:T(8,128)(2,1)S(1)}, bf16[592,256]{1,0:T(8,128)(2,1)}, u32[]{:S(2)}, u32[]{:S(2)}) %collective-permute-start.5) | collective-permute-done | bytes 303136 | tf_op jit(solution)/shard_map/ppermute | solution.py:458
  24.7 0.8 %slice.45 = bf16[80,256]{1,0:T(8,128)(2,1)S(1)} slice(bf16[592,256]{1,0:T(8,128)(2,1)} %copy-done.1), slice={[512:592], [0:256]} | slice | bytes 81920 | tf_op jit(solution)/shard_map/slice | solution.py:490
  25.6 0.8 %slice.47 = bf16[80,256]{1,0:T(8,128)(2,1)S(1)} slice(bf16[592,256]{1,0:T(8,128)(2,1)} %collective-permute-done.5.refs_7_), slice={[512:592], [0:256]} | slice | bytes 81920 | tf_op jit(solution)/shard_map/slice | solution.py:490
  26.3 0.8 %slice.48 = bf16[80,256]{1,0:T(8,128)(2,1)S(1)} slice(bf16[592,256]{1,0:T(8,128)(2,1)} %collective-permute-done.6.refs_8_), slice={[512:592], [0:256]} | slice | bytes 81920 | tf_op jit(solution)/shard_map/slice | solution.py:490
  27.1 1.3 %collective-permute-done.8.refs_10_ = bf16[592,256]{1,0:T(8,128)(2,1)S(1)} collective-permute-done((bf16[592,256]{1,0:T(8,128)(2,1)}, bf16[592,256]{1,0:T(8,128)(2,1)S(1)}, u32[]{:S(2)}, u32[]{:S(2)}) %collective-permute-start.8) | collective-permute-done | bytes 303136 | tf_op jit(solution)/shard_map/ppermute | solution.py:458
  28.4 1.1 %collective-permute-start.10 = (bf16[288,256]{1,0:T(8,128)(2,1)S(1)}, bf16[288,256]{1,0:T(8,128)(2,1)S(1)}, u32[]{:S(2)}, u32[]{:S(2)}) collective-permute-start(bf16[288,256]{1,0:T(8,128)(2,1)S(1)} %slice.44), channel_id=1, source_target_pairs={{0,4},{1,0},{2,1},{3,2},{7,3},{6,7},{5,6},{4,5},{8,12},{9,8},{10,9... | collective-permute-start | bytes 442376 | tf_op jit(solution)/shard_map/ppermute | solution.py:458
  30.1 3.1 %collective-permute-done.7.refs_9_ = bf16[592,256]{1,0:T(8,128)(2,1)S(1)} collective-permute-done((bf16[592,256]{1,0:T(8,128)(2,1)}, bf16[592,256]{1,0:T(8,128)(2,1)S(1)}, u32[]{:S(2)}, u32[]{:S(2)}) %collective-permute-start.7) | collective-permute-done | bytes 303136 | tf_op jit(solution)/shard_map/ppermute | solution.py:458
  39.2 0.8 %reshape.19.refs_22_ = f32[2,2048]{1,0:T(2,128)S(1)} reshape(f32[2,32,64]{2,1,0:T(8,128)} %broadcast_in_dim.20) | data formatting | bytes 32768 | tf_op jit(solution)/shard_map/reshape | solution.py:509
  40.1 1.0 %copy-done.2 = bf16[592,256]{1,0:T(8,128)(2,1)S(1)} copy-done((bf16[592,256]{1,0:T(8,128)(2,1)S(1)}, bf16[592,256]{1,0:T(8,128)(2,1)}, u32[]{:S(2)}) %copy-start.2) | copy-done | bytes 303128
  41.1 0.9 %copy-done.4 = bf16[160,256]{1,0:T(8,128)(2,1)S(1)} copy-done((bf16[160,256]{1,0:T(8,128)(2,1)S(1)}, bf16[160,256]{1,0:T(8,128)(2,1)}, u32[]{:S(2)}) %copy-start.4) | copy-done | bytes 81944
  42.0 0.9 %copy-done.5 = f32[2,4,2176]{2,1,0:T(4,128)S(1)} copy-done((f32[2,4,2176]{2,1,0:T(4,128)S(1)}, f32[2,4,2176]{2,1,0:T(4,128)}, u32[]{:S(2)}) %copy-start.5) | copy-done | bytes 69656
  42.9 0.7 %copy-done.6 = f32[2,2176]{1,0:T(2,128)S(1)} copy-done((f32[2,2176]{1,0:T(2,128)S(1)}, f32[2,2176]{1,0:T(2,128)}, u32[]{:S(2)}) %copy-start.6) | copy-done | bytes 17432
  46.8 15.0 %shard_map.118 = (bf16[128,512]{1,0:T(8,128)(2,1)S(1)}, bf16[128,512]{1,0:T(8,128)(2,1)S(1)}, bf16[128,512]{1,0:T(8,128)(2,1)S(1)}, bf16[128,512]{1,0:T(8,128)(2,1)S(1)}) custom-call(s32[10]{0:T(128)S(1)} %copy-done.8, s32[4]{0:T(128)S(1)} %bitcast.19, bf16[128,2048]{1,0:T(8,128)(2,1)S(1)} %bitcast.18, bf16[128,2048]{1,0:T(8,128)(2,1)S(1)} %collective-permute-done.refs_1_, ...), custom_call_target="tpu_custom_call" | custom-call | tf_op jit(solution)/shard_map/pallas_call | solution.py:445
  62.3 1.7 %collective-permute-start.16 = (bf16[128,512]{1,0:T(8,128)(2,1)S(1)}, bf16[128,512]{1,0:T(8,128)(2,1)S(1)}, u32[]{:S(2)}, u32[]{:S(2)}) collective-permute-start(bf16[128,512]{1,0:T(8,128)(2,1)S(1)} %get-tuple-element.11), channel_id=1, source_target_pairs={{0,16},{8,24},{16,0},{24,8},{1,17},{9,25},{17,1},{25,9},{2,18},{10... | collective-permute-start | bytes 393224 | tf_op jit(solution)/shard_map/ppermute | solution.py:462
  64.1 4.5 %collective-permute-done.16 = bf16[128,512]{1,0:T(8,128)(2,1)S(1)} collective-permute-done((bf16[128,512]{1,0:T(8,128)(2,1)S(1)}, bf16[128,512]{1,0:T(8,128)(2,1)S(1)}, u32[]{:S(2)}, u32[]{:S(2)}) %collective-permute-start.16) | collective-permute-done | bytes 131104 | tf_op jit(solution)/shard_map/ppermute | solution.py:462
  68.6 1.2 %collective-permute-done.17 = bf16[128,512]{1,0:T(8,128)(2,1)S(1)} collective-permute-done((bf16[128,512]{1,0:T(8,128)(2,1)S(1)}, bf16[128,512]{1,0:T(8,128)(2,1)S(1)}, u32[]{:S(2)}, u32[]{:S(2)}) %collective-permute-start.17) | collective-permute-done | bytes 131104 | tf_op jit(solution)/shard_map/ppermute | solution.py:462
  (82 shorter events, 14.1 us)
Async XLA Ops:
  0.0 13.9 %copy-start.12 = (s32[8]{0:T(128)S(1)}, s32[8]{0:T(128)}, u32[]{:S(2)}) copy-start(s32[8]{0:T(128)} %constant.71.clone) | copy-start | bytes 100
  0.0 14.9 %copy-start.17 = (s32[8]{0:T(128)S(1)}, s32[8]{0:T(128)}, u32[]{:S(2)}) copy-start(s32[8]{0:T(128)} %constant.72.clone) | copy-start | bytes 100
  0.0 24.6 %copy-start.16 = (f32[2,32]{1,0:T(2,128)S(1)}, f32[2,32]{1,0:T(2,128)}, u32[]{:S(2)}) copy-start(f32[2,32]{1,0:T(2,128)} %param.17) | copy-start | bytes 772
  0.0 24.6 %copy-start.15 = (f32[2,32]{1,0:T(2,128)S(1)}, f32[2,32]{1,0:T(2,128)}, u32[]{:S(2)}) copy-start(f32[2,32]{1,0:T(2,128)} %param.18) | copy-start | bytes 772
  2.0 10.3 %collective-permute-start.4 = (bf16[592,256]{1,0:T(8,128)(2,1)S(1)}, bf16[592,256]{1,0:T(8,128)(2,1)S(1)}, u32[]{:S(2)}, u32[]{:S(2)}) collective-permute-start(bf16[592,256]{1,0:T(8,128)(2,1)S(1)} %pad_maximum_fusion.refs_4_), channel_id=1, source_target_pairs={{0,4},{1,0},{2,1},{3,2},{7,3},{6,7},{5,6},{4,5},{8,12},{9,8},{10,9... | collective-permute-start | bytes 909320 | tf_op jit(solution)/shard_map/ppermute | solution.py:458
  5.0 9.5 %collective-permute-start.3 = (bf16[592,256]{1,0:T(8,128)(2,1)S(1)}, bf16[592,256]{1,0:T(8,128)(2,1)S(1)}, u32[]{:S(2)}, u32[]{:S(2)}) collective-permute-start(bf16[592,256]{1,0:T(8,128)(2,1)S(1)} %pad_maximum_fusion.refs_4_), channel_id=1, source_target_pairs={{0,1},{1,2},{2,3},{3,7},{7,6},{6,5},{5,4},{4,0},{8,9},{9,10},{10,1... | collective-permute-start | bytes 909320 | tf_op jit(solution)/shard_map/ppermute | solution.py:458
  5.2 17.6 %collective-permute-start.1 = (bf16[128,2048]{1,0:T(8,128)(2,1)S(1)}, bf16[128,2048]{1,0:T(8,128)(2,1)S(1)}, u32[]{:S(2)}, u32[]{:S(2)}) collective-permute-start(bf16[128,2048]{1,0:T(8,128)(2,1)S(1)} %bitcast.16), channel_id=1, source_target_pairs={{0,16},{8,24},{16,0},{24,8},{1,17},{9,25},{17,1},{25,9},{2,18},{10... | collective-permute-start | bytes 1572872 | tf_op jit(solution)/shard_map/ppermute | solution.py:462
  12.3 8.5 %collective-permute-start.6 = (bf16[592,256]{1,0:T(8,128)(2,1)S(1)}, bf16[592,256]{1,0:T(8,128)(2,1)}, u32[]{:S(2)}, u32[]{:S(2)}) collective-permute-start(bf16[592,256]{1,0:T(8,128)(2,1)S(1)} %collective-permute-done.4.refs_6_), channel_id=1, source_target_pairs={{0,4},{1,0},{2,1},{3,2},{7,3},{6,7},{5,6},{4,5},{8,12},{9,8},{10,9... | collective-permute-start | bytes 909320 | tf_op jit(solution)/shard_map/ppermute | solution.py:458
  13.9 22.8 %collective-permute-start = (bf16[128,2048]{1,0:T(8,128)(2,1)S(1)}, bf16[128,2048]{1,0:T(8,128)(2,1)S(1)}, u32[]{:S(2)}, u32[]{:S(2)}) collective-permute-start(bf16[128,2048]{1,0:T(8,128)(2,1)S(1)} %bitcast.17), channel_id=1, source_target_pairs={{0,8},{8,0},{16,24},{24,16},{1,9},{9,1},{17,25},{25,17},{2,10},{10... | collective-permute-start | bytes 1572872 | tf_op jit(solution)/shard_map/ppermute | solution.py:462
  13.9 24.6 %copy-start.14 = (f32[2,32]{1,0:T(2,128)S(1)}, f32[2,32]{1,0:T(2,128)}, u32[]{:S(2)}) copy-start(f32[2,32]{1,0:T(2,128)} %param.19) | copy-start | bytes 772
  14.5 8.3 %copy-start.1 = (bf16[592,256]{1,0:T(8,128)(2,1)}, bf16[592,256]{1,0:T(8,128)(2,1)S(1)}, u32[]{:S(2)}) copy-start(bf16[592,256]{1,0:T(8,128)(2,1)S(1)} %collective-permute-done.3.refs_5_) | copy-start | bytes 909316
  14.5 9.7 %collective-permute-start.5 = (bf16[592,256]{1,0:T(8,128)(2,1)S(1)}, bf16[592,256]{1,0:T(8,128)(2,1)}, u32[]{:S(2)}, u32[]{:S(2)}) collective-permute-start(bf16[592,256]{1,0:T(8,128)(2,1)S(1)} %collective-permute-done.3.refs_5_), channel_id=1, source_target_pairs={{0,1},{1,2},{2,3},{3,7},{7,6},{6,5},{5,4},{4,0},{8,9},{9,10},{10,1... | collective-permute-start | bytes 909320 | tf_op jit(solution)/shard_map/ppermute | solution.py:458
  20.8 7.7 %collective-permute-start.8 = (bf16[592,256]{1,0:T(8,128)(2,1)}, bf16[592,256]{1,0:T(8,128)(2,1)S(1)}, u32[]{:S(2)}, u32[]{:S(2)}) collective-permute-start(bf16[592,256]{1,0:T(8,128)(2,1)} %collective-permute-done.6.refs_8_), channel_id=1, source_target_pairs={{0,4},{1,0},{2,1},{3,2},{7,3},{6,7},{5,6},{4,5},{8,12},{9,8},{10,9... | collective-permute-start | bytes 909320 | tf_op jit(solution)/shard_map/ppermute | solution.py:458
  22.7 17.3 %collective-permute-start.2 = (bf16[128,2048]{1,0:T(8,128)(2,1)S(1)}, bf16[128,2048]{1,0:T(8,128)(2,1)S(1)}, u32[]{:S(2)}, u32[]{:S(2)}) collective-permute-start(bf16[128,2048]{1,0:T(8,128)(2,1)S(1)} %collective-permute-done.1.refs_2_), channel_id=1, source_target_pairs={{0,8},{8,0},{16,24},{24,16},{1,9},{9,1},{17,25},{25,17},{2,10},{10... | collective-permute-start | bytes 1572872 | tf_op jit(solution)/shard_map/ppermute | solution.py:462
  24.2 9.0 %collective-permute-start.7 = (bf16[592,256]{1,0:T(8,128)(2,1)}, bf16[592,256]{1,0:T(8,128)(2,1)S(1)}, u32[]{:S(2)}, u32[]{:S(2)}) collective-permute-start(bf16[592,256]{1,0:T(8,128)(2,1)} %collective-permute-done.5.refs_7_), channel_id=1, source_target_pairs={{0,1},{1,2},{2,3},{3,7},{7,6},{6,5},{5,4},{4,0},{8,9},{9,10},{10,1... | collective-permute-start | bytes 909320 | tf_op jit(solution)/shard_map/ppermute | solution.py:458
  25.5 10.1 %collective-permute-start.11 = (bf16[160,256]{1,0:T(8,128)(2,1)S(1)}, bf16[160,256]{1,0:T(8,128)(2,1)S(1)}, u32[]{:S(2)}, u32[]{:S(2)}) collective-permute-start(bf16[160,256]{1,0:T(8,128)(2,1)S(1)} %pad_maximum_fusion.1), channel_id=1, source_target_pairs={{0,8},{8,0},{16,24},{24,16},{1,9},{9,1},{17,25},{25,17},{2,10},{10... | collective-permute-start | bytes 245768 | tf_op jit(solution)/shard_map/ppermute | solution.py:462
  28.4 6.5 %collective-permute-start.10 = (bf16[288,256]{1,0:T(8,128)(2,1)S(1)}, bf16[288,256]{1,0:T(8,128)(2,1)S(1)}, u32[]{:S(2)}, u32[]{:S(2)}) collective-permute-start(bf16[288,256]{1,0:T(8,128)(2,1)S(1)} %slice.44), channel_id=1, source_target_pairs={{0,4},{1,0},{2,1},{3,2},{7,3},{6,7},{5,6},{4,5},{8,12},{9,8},{10,9... | collective-permute-start | bytes 442376 | tf_op jit(solution)/shard_map/ppermute | solution.py:458
  33.9 6.2 %collective-permute-start.9 = (bf16[304,256]{1,0:T(8,128)(2,1)}, bf16[304,256]{1,0:T(8,128)(2,1)}, u32[]{:S(2)}, u32[]{:S(2)}) collective-permute-start(bf16[304,256]{1,0:T(8,128)(2,1)} %slice.43), channel_id=1, source_target_pairs={{0,1},{1,2},{2,3},{3,7},{7,6},{6,5},{5,4},{4,0},{8,9},{9,10},{10,1... | collective-permute-start | bytes 466952 | tf_op jit(solution)/shard_map/ppermute | solution.py:458
  35.0 5.1 %collective-permute-start.12 = (bf16[160,256]{1,0:T(8,128)(2,1)}, bf16[160,256]{1,0:T(8,128)(2,1)}, u32[]{:S(2)}, u32[]{:S(2)}) collective-permute-start(bf16[160,256]{1,0:T(8,128)(2,1)} %pad_maximum_fusion.2), channel_id=1, source_target_pairs={{0,8},{8,0},{16,24},{24,16},{1,9},{9,1},{17,25},{25,17},{2,10},{10... | collective-permute-start | bytes 245768 | tf_op jit(solution)/shard_map/ppermute | solution.py:462
  36.2 3.9 %collective-permute-start.13 = (bf16[160,256]{1,0:T(8,128)(2,1)}, bf16[160,256]{1,0:T(8,128)(2,1)}, u32[]{:S(2)}, u32[]{:S(2)}) collective-permute-start(bf16[160,256]{1,0:T(8,128)(2,1)} %pad_maximum_fusion.3), channel_id=1, source_target_pairs={{0,8},{8,0},{16,24},{24,16},{1,9},{9,1},{17,25},{25,17},{2,10},{10... | collective-permute-start | bytes 245768 | tf_op jit(solution)/shard_map/ppermute | solution.py:462
  36.7 3.4 %collective-permute-start.14 = (bf16[80,256]{1,0:T(8,128)(2,1)}, bf16[80,256]{1,0:T(8,128)(2,1)}, u32[]{:S(2)}, u32[]{:S(2)}) collective-permute-start(bf16[80,256]{1,0:T(8,128)(2,1)} %slice.51), channel_id=1, source_target_pairs={{0,8},{8,0},{16,24},{24,16},{1,9},{9,1},{17,25},{25,17},{2,10},{10... | collective-permute-start | bytes 122888 | tf_op jit(solution)/shard_map/ppermute | solution.py:462
  61.8 2.3 %collective-permute-start.15 = (bf16[128,512]{1,0:T(8,128)(2,1)S(1)}, bf16[128,512]{1,0:T(8,128)(2,1)S(1)}, u32[]{:S(2)}, u32[]{:S(2)}) collective-permute-start(bf16[128,512]{1,0:T(8,128)(2,1)S(1)} %get-tuple-element.10), channel_id=1, source_target_pairs={{0,8},{8,0},{16,24},{24,16},{1,9},{9,1},{17,25},{25,17},{2,10},{10... | collective-permute-start | bytes 393224 | tf_op jit(solution)/shard_map/ppermute | solution.py:462
  62.3 6.3 %collective-permute-start.16 = (bf16[128,512]{1,0:T(8,128)(2,1)S(1)}, bf16[128,512]{1,0:T(8,128)(2,1)S(1)}, u32[]{:S(2)}, u32[]{:S(2)}) collective-permute-start(bf16[128,512]{1,0:T(8,128)(2,1)S(1)} %get-tuple-element.11), channel_id=1, source_target_pairs={{0,16},{8,24},{16,0},{24,8},{1,17},{9,25},{17,1},{25,9},{2,18},{10... | collective-permute-start | bytes 393224 | tf_op jit(solution)/shard_map/ppermute | solution.py:462
  64.0 5.8 %collective-permute-start.17 = (bf16[128,512]{1,0:T(8,128)(2,1)S(1)}, bf16[128,512]{1,0:T(8,128)(2,1)S(1)}, u32[]{:S(2)}, u32[]{:S(2)}) collective-permute-start(bf16[128,512]{1,0:T(8,128)(2,1)S(1)} %get-tuple-element.12), channel_id=1, source_target_pairs={{0,24},{8,16},{16,8},{24,0},{1,25},{9,17},{17,9},{25,1},{2,26},{10... | collective-permute-start | bytes 393224 | tf_op jit(solution)/shard_map/ppermute | solution.py:462
  (12 other events, 13.6 us)

commit v3 on v0

--- a/solution.py
+++ b/solution.py
@@ -1,6 +1,10 @@
+import functools
+
 import jax
 import jax.numpy as jnp
 from jax import lax
+from jax.experimental import pallas as pl
+from jax.experimental.pallas import tpu as pltpu
 from jax.sharding import PartitionSpec as P
 
 HEADS = 32
@@ -141,7 +145,7 @@
     return total.astype(jnp.bfloat16)
 
 
-def on_device(
+def on_sections(
     hidden, in_weight, read_starts, conv_weight, conv_bias, dt_bias, decay, skip, norm_gain
 ):
     tokens = hidden[0]
@@ -173,6 +177,355 @@
     return mixed.astype(jnp.bfloat16)[None]
 
 
+LANES = 128
+SIDE = 256
+EDGE = 8
+
+
+def ring_order(count):
+    return [i if i < count else 3 * count - 1 - i for i in range(2 * count)]
+
+
+def split_parts(value, count):
+    parts = []
+    for _ in range(count):
+        parts.append(value.astype(jnp.bfloat16))
+        value = value - parts[-1].astype(jnp.float32)
+    return parts
+
+
+def mixer_kernel(heads, ring, *refs):
+    shards = 2 * ring
+    pieces, refs = refs[:4], refs[4:]
+    weights, refs = refs[: shards - 1], refs[shards - 1 :]
+    ends, refs = refs[:2], refs[2:]
+    marks_in, conv_w_in, conv_b_in, step_bias_in, decay_in, skip_in, gain_in = refs[:7]
+    outs, refs = refs[7:11], refs[11:]
+    conv_w, conv_b, per_head, gains, marks, sems = refs[:6]
+    rows_in, w_own, w_side, padded, xs, cs, bs, cums, leads, tails, turned, barred, fade_wide, state, ys, mixed = refs[6:]
+    seq, fsdp, batch = lax.axis_index("seq"), lax.axis_index("fsdp"), lax.axis_index("batch")
+    columns = heads * HEAD_DIM
+    depth = weights[0].shape[1]
+    side_rows = weights[0].shape[0] - columns
+    chunks = columns // LANES
+    length = rows_in.shape[0]
+    blocks = length // BLOCK
+    cut = ends[0].shape[0]
+    own_at = pl.multiple_of(seq * columns, columns)
+
+    own_lanes = pl.ds(own_at, columns)
+    side_lanes = pl.ds(INNER, LANES)
+    narrow = pl.ds(0, HEADS)
+    copies = [
+        (conv_w_in.at[:, :, own_lanes], conv_w.at[:, :, pl.ds(0, columns)]),
+        (conv_w_in.at[:, :, side_lanes], conv_w.at[:, :, pl.ds(columns, LANES)]),
+        (conv_b_in.at[:, own_lanes], conv_b.at[:, pl.ds(0, columns)]),
+        (conv_b_in.at[:, side_lanes], conv_b.at[:, pl.ds(columns, LANES)]),
+        (step_bias_in, per_head.at[0]),
+        (decay_in, per_head.at[1]),
+        (skip_in, per_head.at[2]),
+        (gain_in.at[:, own_lanes], gains),
+        (marks_in, marks),
+    ]
+    copies = [pltpu.make_async_copy(a, b, sems.at[i]) for i, (a, b) in enumerate(copies)]
+    for copy in copies:
+        copy.start()
+
+    lane = lax.broadcasted_iota(jnp.int32, (BLOCK, LANES), 1)
+    row = lax.broadcasted_iota(jnp.int32, (BLOCK, LANES), 0)
+
+    for mask in range(4):
+        rows_in[mask * BLOCK : (mask + 1) * BLOCK, :] = pieces[mask][...]
+    w_side[side_rows:, :] = jnp.zeros((SIDE - side_rows, w_side.shape[1]), jnp.bfloat16)
+    position = jnp.where(fsdp == 0, batch, shards - 1 - batch)
+    for n in range(shards):
+        away = 0 if n == 0 else (shards // 2 if n == shards - 1 else (-1) ** n * ((n + 1) // 2))
+        there = lax.rem(position + shards + away, shards)
+        shard = jnp.where(there < ring, there, 3 * ring - 1 - there)
+        at = pl.ds(pl.multiple_of(shard * depth, depth), depth)
+        if n < shards - 1:
+            w_own[:, at] = weights[n][:columns, :]
+            w_side[:side_rows, at] = weights[n][columns:, :]
+        else:
+            w_own[:cut, at] = ends[0][...]
+            w_own[cut:, at] = ends[1][: columns - cut, :]
+            w_side[:side_rows, at] = ends[1][columns - cut :, :]
+    edge = jnp.zeros((EDGE, LANES), jnp.float32)
+    for c in range(chunks + 1):
+        padded[c, 0:EDGE, :] = edge
+        padded[c, EDGE + length :, :] = edge
+    state[...] = jnp.zeros_like(state)
+
+    places = [pl.multiple_of((seq ^ mask) * BLOCK, BLOCK) for mask in range(4)]
+
+    def project_in(weight):
+        out = lax.dot_general(
+            rows_in[...], weight, (((1,), (1,)), ((), ())), preferred_element_type=jnp.float32
+        )
+        return out.astype(jnp.bfloat16).astype(jnp.float32)
+
+    def keep(c, value):
+        for mask in range(4):
+            padded[c, pl.ds(EDGE + places[mask], BLOCK), :] = value[mask * BLOCK : (mask + 1) * BLOCK, :]
+
+    side_out = project_in(w_side[...])
+    keep(chunks, side_out[:, :LANES])
+    for n in range(columns // SIDE):
+        part_out = project_in(w_own[n * SIDE : (n + 1) * SIDE, :])
+        for k in range(SIDE // LANES):
+            keep(n * (SIDE // LANES) + k, part_out[:, k * LANES : (k + 1) * LANES])
+    for copy in copies:
+        copy.wait()
+
+    backward_lane = ((lane >= heads) & (lane < 2 * heads)) | (lane == 2 * heads + 1)
+    head_lane = lane < 2 * heads
+    lower = jnp.where(row >= lane, 1.0, 0.0).astype(jnp.bfloat16)
+    upper = jnp.where(row <= lane, 1.0, 0.0).astype(jnp.bfloat16)
+    to_first = lax.rem(LANES - seq * heads, LANES)
+
+    def own_heads(k):
+        both = jnp.concatenate([per_head[k], jnp.zeros((2, LANES - HEADS), jnp.float32)], axis=1)
+        both = pltpu.roll(both, to_first, 1)
+        ahead, behind = both[0:1, :], pltpu.roll(both, heads, 1)[1:2, :]
+        value = jnp.where(lane[:1] < heads, ahead, behind)
+        return jnp.where(head_lane[:1], value, 0.0)
+
+    step_bias, rates, direct = own_heads(0), own_heads(1), own_heads(2)
+
+    def head_columns(d):
+        at_row = lax.broadcasted_iota(jnp.int32, (LANES, columns), 0)
+        head = lax.broadcasted_iota(jnp.int32, (LANES, columns), 1) // HEAD_DIM + d * heads
+        hit = (at_row == head) | (at_row == head + 2 * heads) | (at_row == head + 4 * heads)
+        return jnp.where(hit, 1.0, 0.0).astype(jnp.bfloat16)
+
+    spread = [head_columns(d) for d in range(2)]
+
+    def packed(value, count):
+        parts = split_parts(value, count)
+        joined = parts[0].astype(jnp.float32)
+        for k in range(1, count):
+            joined = joined + pltpu.roll(parts[k].astype(jnp.float32), 2 * heads * k, 1)
+        return joined
+
+    fades = []
+    for mask in range(4):
+        place = places[mask]
+        b = seq ^ mask
+        mine = pltpu.roll(side_out[mask * BLOCK : (mask + 1) * BLOCK, LANES:], to_first, 1)
+        both = jnp.where(lane < heads, mine, pltpu.roll(mine, heads, 1)) + step_bias
+        step = jnp.maximum(both, 0.0) + jnp.log1p(jnp.exp(-jnp.abs(both)))
+        rate = -step * rates
+        here_at = row + place
+        here = here_at == marks[:, 0:1]
+        after = here_at + 1 == marks[:, 0:1]
+        for m in range(1, marks.shape[1]):
+            here = here | (here_at == marks[:, m : m + 1])
+            after = after | (here_at + 1 == marks[:, m : m + 1])
+        start = (here & (lane == 2 * heads)) | (after & (lane == 2 * heads + 1))
+        rate = jnp.where(head_lane, rate, jnp.where(start, 1.0, 0.0))
+        parts = split_parts(rate, 3)
+        ahead = sum(jnp.dot(lower, p, preferred_element_type=jnp.float32) for p in parts)
+        behind = sum(jnp.dot(upper, p, preferred_element_type=jnp.float32) for p in parts)
+        cum = jnp.where(backward_lane, behind, ahead)
+        seen_ahead = jnp.broadcast_to(cum[:, 2 * heads : 2 * heads + 1], (BLOCK, LANES))
+        seen_behind = jnp.broadcast_to(cum[:, 2 * heads + 1 : 2 * heads + 2], (BLOCK, LANES))
+        seen = jnp.where(backward_lane, seen_behind, seen_ahead)
+        last = jnp.where(backward_lane[:1], cum[:1], cum[BLOCK - 1 :])
+        seen_last = jnp.where(backward_lane[:1], seen[:1], seen[BLOCK - 1 :])
+        tail = jnp.where((seen == seen_last) & head_lane, jnp.exp(last - cum) * step, 0.0)
+        lead = jnp.where((seen == 0.0) & head_lane, jnp.exp(cum), 0.0)
+        fade = jnp.where((seen_last == 0.0) & head_lane[:1], jnp.exp(last), 0.0)
+        fades.append(packed(jnp.broadcast_to(fade, (8, LANES)), 2)[:1])
+        at = pl.ds(place, BLOCK)
+        cums[at, :] = cum
+        for d in range(2):
+            leads[d, at, :] = jnp.dot(
+                lead.astype(jnp.bfloat16), spread[d], preferred_element_type=jnp.float32
+            ).astype(jnp.bfloat16)
+            tails[d, at, :] = jnp.dot(
+                tail.astype(jnp.bfloat16), spread[d], preferred_element_type=jnp.float32
+            ).astype(jnp.bfloat16)
+        shown = jnp.where(head_lane, jnp.log(step) - cum, cum).T
+        turned[b] = shown
+        for d in range(2):
+            ordered = (row >= lane) if d == 0 else (row <= lane)
+            seen_row = shown[2 * heads + d : 2 * heads + d + 1, :]
+            allowed = ordered & ((seen_ahead if d == 0 else seen_behind) == seen_row)
+            barred[d, b] = jnp.where(allowed, 0.0, -1e30)
+    fades.append(packed(jnp.broadcast_to(direct, (8, LANES)), 3)[:1])
+    rows_wide = jnp.concatenate(fades + [jnp.zeros((11, LANES), jnp.float32)], axis=0).astype(jnp.bfloat16)
+    wide = [jnp.dot(rows_wide, spread[d], preferred_element_type=jnp.float32) for d in range(2)]
+    for d in range(2):
+        for mask in range(4):
+            fade_wide[d, seq ^ mask] = jnp.broadcast_to(wide[d][mask : mask + 1, :], (8, columns))
+    skips = [wide[d][4:5, :] for d in range(2)]
+
+    short = 64
+
+    def conv_rows(i, carry):
+        at = pl.multiple_of(i * short, short)
+        for c in range(chunks + 1):
+            taps = [padded[c, pl.ds(at + EDGE - 3 + k, short), :] for k in range(7)]
+            lanes = slice(c * LANES, (c + 1) * LANES)
+            for d in range(2):
+                acc = conv_b[d : d + 1, lanes] + conv_w[d, 0:1, lanes] * taps[0 if d == 0 else 6]
+                for k in range(1, KERNEL):
+                    acc = acc + conv_w[d, k : k + 1, lanes] * taps[k if d == 0 else 6 - k]
+                half = 0.5 * acc
+                value = half + half * jnp.tanh(half)
+                if c < chunks:
+                    xs[d, pl.ds(at, short), lanes] = value.astype(jnp.bfloat16)
+                else:
+                    high = lax.broadcasted_iota(jnp.int32, (short, LANES), 1) >= STATE
+                    cs[d, pl.ds(at, short), :] = jnp.where(high, value, 0.0).astype(jnp.bfloat16)
+                    bs[d, pl.ds(at, short), :] = jnp.where(
+                        high, pltpu.roll(value, STATE, 1), 0.0
+                    ).astype(jnp.bfloat16)
+        return carry
+
+    lax.fori_loop(0, length // short, conv_rows, 0)
+
+    group = SIDE // HEAD_DIM
+    lane_head = lax.broadcasted_iota(jnp.int32, (BLOCK, SIDE), 1) // HEAD_DIM
+
+    def scan_step(i, carry):
+        for d in range(2):
+            b = i if d == 0 else blocks - 1 - i
+            at = pl.ds(pl.multiple_of(b * BLOCK, BLOCK), BLOCK)
+            c_part = cs[d, at, :]
+            b_part = bs[d, at, :]
+            scores = lax.dot_general(
+                c_part, b_part, (((1,), (1,)), ((), ())), preferred_element_type=jnp.float32
+            )
+            bar = barred[d, b]
+            before = state[d]
+            carried = jnp.dot(c_part, before.astype(jnp.bfloat16), preferred_element_type=jnp.float32)
+            x_all = xs[d, at, :]
+            inputs = tails[d, at, :] * x_all
+            local_end = lax.dot_general(
+                b_part, inputs, (((0,), (0,)), ((), ())), preferred_element_type=jnp.float32
+            )
+            state[d] = fade_wide[d, b][:1] * before + local_end
+            for q in range(columns // SIDE):
+                some = []
+                for h in range(q * group, (q + 1) * group):
+                    at_row = d * heads + h
+                    gap = cums[at, at_row : at_row + 1] + (turned[b, at_row : at_row + 1, :] + bar)
+                    some.append((jnp.exp(gap) * scores).astype(jnp.bfloat16))
+                lanes = slice(q * SIDE, (q + 1) * SIDE)
+                x_part = x_all[:, lanes]
+                none = jnp.zeros_like(x_part)
+                spaced = jnp.concatenate([jnp.where(lane_head == h, x_part, none) for h in range(group)], axis=0)
+                inner = jnp.dot(jnp.concatenate(some, axis=1), spaced, preferred_element_type=jnp.float32)
+                ys[d, at, lanes] = (
+                    inner
+                    + leads[d, at, lanes].astype(jnp.float32) * carried[:, lanes]
+                    + skips[d][:, lanes] * x_part.astype(jnp.float32)
+                )
+        return carry
+
+    lax.fori_loop(0, blocks, scan_step, 0)
+
+    head_row = lax.broadcasted_iota(jnp.int32, (SIDE, SIDE), 0) // HEAD_DIM
+    head_col = lax.broadcasted_iota(jnp.int32, (SIDE, SIDE), 1) // HEAD_DIM
+    same = jnp.where(head_row == head_col, 1.0 / HEAD_DIM, 0.0).astype(jnp.bfloat16)
+    for q in range(columns // SIDE):
+        lanes = slice(q * SIDE, (q + 1) * SIDE)
+        both = 0.0
+        for d in range(2):
+            y = ys[d, :, lanes]
+            mean = jnp.dot((y * y).astype(jnp.bfloat16), same, preferred_element_type=jnp.float32)
+            both = both + y * lax.rsqrt(mean + 1e-05) * gains[d : d + 1, lanes]
+        mixed[:, lanes] = both.astype(jnp.bfloat16)
+    for mask in range(4):
+        outs[mask][...] = mixed[pl.ds(places[mask], BLOCK), :]
+
+
+def mix(heads, ring, pieces, weights, ends, params):
+    section, width = pieces[0].shape
+    columns = heads * HEAD_DIM
+    length = section * len(pieces)
+    blocks = length // BLOCK
+    chunks = columns // LANES
+    in_hbm = pl.BlockSpec(memory_space=pltpu.HBM)
+    in_vmem = pl.BlockSpec(memory_space=pltpu.VMEM)
+    operands = (*pieces, *weights, *ends)
+    scratch = [
+        pltpu.VMEM((2, KERNEL, columns + LANES), jnp.float32),
+        pltpu.VMEM((2, columns + LANES), jnp.float32),
+        pltpu.VMEM((3, 2, HEADS), jnp.float32),
+        pltpu.VMEM((2, columns), jnp.float32),
+        pltpu.VMEM(params[0].shape, jnp.int32),
+        pltpu.SemaphoreType.DMA((9,)),
+        pltpu.VMEM((length, width), jnp.bfloat16),
+        pltpu.VMEM((columns, width), jnp.bfloat16),
+        pltpu.VMEM((SIDE, width), jnp.bfloat16),
+        pltpu.VMEM((chunks + 1, length + 2 * EDGE, LANES), jnp.float32),
+        pltpu.VMEM((2, length, columns), jnp.bfloat16),
+        pltpu.VMEM((2, length, LANES), jnp.bfloat16),
+        pltpu.VMEM((2, length, LANES), jnp.bfloat16),
+        pltpu.VMEM((length, LANES), jnp.float32),
+        pltpu.VMEM((2, length, columns), jnp.bfloat16),
+        pltpu.VMEM((2, length, columns), jnp.bfloat16),
+        pltpu.VMEM((blocks, BLOCK, LANES), jnp.float32),
+        pltpu.VMEM((2, blocks, BLOCK, LANES), jnp.float32),
+        pltpu.VMEM((2, blocks, 8, columns), jnp.float32),
+        pltpu.VMEM((2, LANES, columns), jnp.float32),
+        pltpu.VMEM((2, length, columns), jnp.float32),
+        pltpu.VMEM((length, columns), jnp.bfloat16),
+    ]
+    return pl.pallas_call(
+        functools.partial(mixer_kernel, heads, ring),
+        out_shape=[jax.ShapeDtypeStruct((section, columns), jnp.bfloat16)] * len(pieces),
+        in_specs=[in_vmem] * len(operands) + [in_hbm] * len(params),
+        out_specs=[in_vmem] * len(pieces),
+        scratch_shapes=scratch,
+        compiler_params=pltpu.CompilerParams(vmem_limit_bytes=36 * 1024 * 1024),
+    )(*operands, *params)
+
+
+def turn(value, way):
+    order = ring_order(lax.axis_size("batch"))
+    count = len(order)
+    return lax.ppermute(value, ("fsdp", "batch"), [(order[i], order[(i + way) % count]) for i in range(count)])
+
+
+def swap(value, axis, mask):
+    return lax.ppermute(value, axis, [(i, i ^ mask) for i in range(lax.axis_size(axis))])
+
+
+def on_heads(hidden, in_weight, read_starts, conv_weight, conv_bias, dt_bias, decay, skip, norm_gain):
+    tokens = hidden[0]
+    count = lax.axis_size("seq")
+    seq = lax.axis_index("seq")
+    heads = HEADS // count
+    columns = heads * HEAD_DIM
+    by_column = in_weight.T
+    own = jnp.concatenate(
+        [lax.dynamic_slice_in_dim(by_column, seq * columns, columns, axis=0), by_column[INNER:]]
+    )
+
+    ring = lax.axis_size("batch")
+    up, down = [own], [own]
+    for _ in range(ring - 1):
+        up.append(turn(up[-1], 1))
+        down.append(turn(down[-1], -1))
+    cut = own.shape[0] // 32 * 16
+    ends = [turn(up[-1][:cut], 1), turn(down[-1][cut:], -1)]
+    weights = [own]
+    for a, b in zip(up[1:], down[1:]):
+        weights += [a, b]
+    across = swap(tokens, "seq", 2)
+    pieces = [tokens, swap(tokens, "seq", 1), across, swap(across, "seq", 1)]
+    params = (read_starts, conv_weight, conv_bias, dt_bias, decay, skip, norm_gain)
+    results = mix(heads, ring, pieces, weights, ends, params)
+    received = [results[0]] + [swap(results[mask], "seq", mask) for mask in range(1, count)]
+    mixed = jnp.zeros((tokens.shape[0], INNER), jnp.bfloat16)
+    for mask in range(count):
+        mixed = lax.dynamic_update_slice(mixed, received[mask], (0, (seq ^ mask) * columns))
+    return mixed[None]
+
+
 def solution(mesh):
     in_specs = (
         P(("fsdp", "batch"), "seq", None),
@@ -186,6 +539,16 @@
         P(),
     )
     out_specs = P(("fsdp", "batch"), "seq", None)
-    return jax.shard_map(
-        on_device, mesh=mesh, in_specs=in_specs, out_specs=out_specs, check_vma=False
-    )
+    by_heads = mesh.shape["seq"] == 4 and mesh.shape["fsdp"] == 2
+
+    def mixer(hidden, *rest):
+        whole = by_heads and hidden.shape[1] == mesh.shape["seq"] * BLOCK
+        return jax.shard_map(
+            on_heads if whole else on_sections,
+            mesh=mesh,
+            in_specs=in_specs,
+            out_specs=out_specs,
+            check_vma=False,
+        )(hidden, *rest)
+
+    return mixer

time: 269 us -> 64.6 us (0.24)
  waiting for transfers between devices: 143 us -> 29.1 us
  local copies, waits for them, and re-layouts: 49.4 us -> 10.5 us
  other arithmetic: 30.1 us -> 0.02 us
  between operations: 15 us -> 0.12 us
  matrix products: 13.2 us -> 0 us
  blocking collectives: 12.8 us -> 0 us
  Pallas kernels: 0 us -> 11.3 us
  starting transfers between devices: 2.86 us -> 13.1 us
    all_gather x3 -> x0, waiting for transfers between devices: 142 us -> none  [the longest x1 129 us: project(): lax.all_gather(in_weight, ('fsdp', 'batch'), axis=0, tiled=True)]
    slice x14 -> x3, local copies, waits for them, and re-layouts: 35.1 us -> 2.25 us  [the longest x2 1.35 us: on_heads(): ends = [turn(up[-1][:cut], 1), turn(down[-1][cut:], -1)]]
    ppermute x2 -> x14, waiting for transfers between devices: 0.01 us -> 29.1 us  [the longest x8 20.2 us: turn(): lax.ppermute(value, ('fsdp', 'batch'), [(order[i], order[(i + way) % coun...]
    dot_general x9 -> x0, matrix products: 13.2 us -> none  [the longest x1 6.09 us: project(): jnp.dot(rows_in, lax.all_gather(in_weight, ('fsdp', 'batch'), axis=0, til...]
    all_gather x2 -> x0, blocking collectives: 12.8 us -> none  [prefix(): pieces = jax.tree.map(lambda part: lax.all_gather(part, axis), value)]
    pallas_call x0 -> x1, Pallas kernels: none -> 11.3 us  [mix(): pl.pallas_call(functools.partial(mixer_kernel, heads, ring), out_shape=[j...]
    convert_element_type x11 -> x0, other arithmetic: 10.6 us -> none  [the longest x2 6.24 us: conv_silu(): return jax.nn.silu(total).astype(jnp.bfloat16)]
    ppermute x2 -> x14, starting transfers between devices: 2.56 us -> 13.1 us  [the longest x8 9.23 us: turn(): lax.ppermute(value, ('fsdp', 'batch'), [(order[i], order[(i + way) % coun...]
  transfers between devices with their start and end apart: 5 -> 14, of which waited for: 2 -> 8; matrix products, arithmetic and copies ran while one was open for 27% -> 2% of each run, Pallas kernels for 0% -> 0%
where the time goes in v3:
time: 64.6 us; the launch traced here: 64.2 us
  waiting for transfers between devices  29.1 us (45%)
  starting transfers between devices  13.1 us (20%)
  Pallas kernels  11.3 us (17%)
  local copies, waits for them, and re-layouts  10.5 us (16%)
    ppermute x8, waiting for transfers between devices, turn(): lax.ppermute(value, ('fsdp', 'batch'), [(order[i], order[(i + way) % coun...  20.2 us
    pallas_call x1, Pallas kernels, mix(): pl.pallas_call(functools.partial(mixer_kernel, heads, ring), out_shape=[j...  11.3 us
    ppermute x8, starting transfers between devices, turn(): lax.ppermute(value, ('fsdp', 'batch'), [(order[i], order[(i + way) % coun...  9.23 us
    ppermute x6, waiting for transfers between devices, swap(): lax.ppermute(value, axis, [(i, i ^ mask) for i in range(lax.axis_size(axi...  8.9 us
    unnamed x30, local copies, waits for them, and re-layouts  6.51 us
    ppermute x6, starting transfers between devices, swap(): lax.ppermute(value, axis, [(i, i ^ mask) for i in range(lax.axis_size(axi...  3.84 us
    slice x2, local copies, waits for them, and re-layouts, on_heads(): ends = [turn(up[-1][:cut], 1), turn(down[-1][cut:], -1)]  1.35 us
  transfers between devices with their start and end apart: 14, of which 8 were waited for; matrix products, arithmetic and copies ran while one was open for 2% of the time, Pallas kernels for 0%

profile of v3, /device:TPU:0, one launch (start us, length us, event | category | flops | bytes accessed | tf_op | source)
XLA Modules:
  0.0 64.2 jit_solution(11039867826949992474)
XLA Ops:
  0.0 1.0 %dynamic-slice_bitcast_fusion = bf16[512,256]{1,0:T(8,128)(2,1)S(1)} fusion(bf16[256,2208]{0,1:T(8,128)(2,1)} %param.10, s32[]{:T(128)S(6)} %select_n.15), kind=kLoop, calls=%fused_computation.1 | loop fusion | bytes 524292 | tf_op jit(solution)/shard_map/dynamic_slice | solution.py:505
  1.1 0.9 %slice.12 = bf16[160,256]{1,0:T(8,128)(2,1)S(1)} slice(bf16[2208,256]{1,0:T(8,128)(2,1)} %bitcast.15), slice={[2048:2208], [0:256]} | slice | bytes 163840 | tf_op jit(solution)/shard_map/slice | solution.py:505
  2.0 3.0 %collective-permute-start.4 = (bf16[672,256]{1,0:T(8,128)(2,1)S(1)}, bf16[672,256]{1,0:T(8,128)(2,1)S(1)}, u32[]{:S(2)}, u32[]{:S(2)}) collective-permute-start(bf16[672,256]{1,0:T(8,128)(2,1)S(1)} %pad_maximum_fusion.refs_4_), channel_id=1, source_target_pairs={{0,4},{1,0},{2,1},{3,2},{7,3},{6,7},{5,6},{4,5},{8,12},{9,8},{10,9... | collective-permute-start | bytes 1032200 | tf_op jit(solution)/shard_map/ppermute | solution.py:490
  5.1 1.9 %collective-permute-start.1 = (bf16[128,2048]{1,0:T(8,128)(2,1)S(1)}, bf16[128,2048]{1,0:T(8,128)(2,1)S(1)}, u32[]{:S(2)}, u32[]{:S(2)}) collective-permute-start(bf16[128,2048]{1,0:T(8,128)(2,1)S(1)} %bitcast.12), channel_id=1, source_target_pairs={{0,16},{8,24},{16,0},{24,8},{1,17},{9,25},{17,1},{25,9},{2,18},{10... | collective-permute-start | bytes 1572872 | tf_op jit(solution)/shard_map/ppermute | solution.py:494
  7.0 6.1 %collective-permute-done.4.refs_6_ = bf16[672,256]{1,0:T(8,128)(2,1)S(1)} collective-permute-done((bf16[672,256]{1,0:T(8,128)(2,1)S(1)}, bf16[672,256]{1,0:T(8,128)(2,1)S(1)}, u32[]{:S(2)}, u32[]{:S(2)}) %collective-permute-start.4) | collective-permute-done | bytes 344096 | tf_op jit(solution)/shard_map/ppermute | solution.py:490
  13.1 1.7 %collective-permute-start.6 = (bf16[672,256]{1,0:T(8,128)(2,1)S(1)}, bf16[672,256]{1,0:T(8,128)(2,1)S(1)}, u32[]{:S(2)}, u32[]{:S(2)}) collective-permute-start(bf16[672,256]{1,0:T(8,128)(2,1)S(1)} %collective-permute-done.4.refs_6_), channel_id=1, source_target_pairs={{0,4},{1,0},{2,1},{3,2},{7,3},{6,7},{5,6},{4,5},{8,12},{9,8},{10,9... | collective-permute-start | bytes 1032200 | tf_op jit(solution)/shard_map/ppermute | solution.py:490
  15.2 0.7 %copy-done.1 = bf16[672,256]{1,0:T(8,128)(2,1)} copy-done((bf16[672,256]{1,0:T(8,128)(2,1)}, bf16[672,256]{1,0:T(8,128)(2,1)S(1)}, u32[]{:S(2)}) %copy-start.1) | copy-done | bytes 344088
  15.9 2.6 %collective-permute-done.1.refs_2_ = bf16[128,2048]{1,0:T(8,128)(2,1)S(1)} collective-permute-done((bf16[128,2048]{1,0:T(8,128)(2,1)S(1)}, bf16[128,2048]{1,0:T(8,128)(2,1)S(1)}, u32[]{:S(2)}, u32[]{:S(2)}) %collective-permute-start.1) | collective-permute-done | bytes 524320 | tf_op jit(solution)/shard_map/ppermute | solution.py:494
  18.5 3.9 %collective-permute-done.6.refs_8_ = bf16[672,256]{1,0:T(8,128)(2,1)S(1)} collective-permute-done((bf16[672,256]{1,0:T(8,128)(2,1)S(1)}, bf16[672,256]{1,0:T(8,128)(2,1)S(1)}, u32[]{:S(2)}, u32[]{:S(2)}) %collective-permute-start.6) | collective-permute-done | bytes 344096 | tf_op jit(solution)/shard_map/ppermute | solution.py:490
  22.4 1.3 %collective-permute-start.8 = (bf16[672,256]{1,0:T(8,128)(2,1)S(1)}, bf16[672,256]{1,0:T(8,128)(2,1)S(1)}, u32[]{:S(2)}, u32[]{:S(2)}) collective-permute-start(bf16[672,256]{1,0:T(8,128)(2,1)S(1)} %collective-permute-done.6.refs_8_), channel_id=1, source_target_pairs={{0,4},{1,0},{2,1},{3,2},{7,3},{6,7},{5,6},{4,5},{8,12},{9,8},{10,9... | collective-permute-start | bytes 1032200 | tf_op jit(solution)/shard_map/ppermute | solution.py:490
  23.7 0.7 %copy-done.3 = bf16[672,256]{1,0:T(8,128)(2,1)} copy-done((bf16[672,256]{1,0:T(8,128)(2,1)}, bf16[672,256]{1,0:T(8,128)(2,1)S(1)}, u32[]{:S(2)}) %copy-start.3) | copy-done | bytes 344088
  25.1 5.6 %collective-permute-done.8.refs_10_ = bf16[672,256]{1,0:T(8,128)(2,1)S(1)} collective-permute-done((bf16[672,256]{1,0:T(8,128)(2,1)S(1)}, bf16[672,256]{1,0:T(8,128)(2,1)S(1)}, u32[]{:S(2)}, u32[]{:S(2)}) %collective-permute-start.8) | collective-permute-done | bytes 344096 | tf_op jit(solution)/shard_map/ppermute | solution.py:490
  31.4 1.0 %collective-permute-start.10 = (bf16[336,256]{1,0:T(8,128)(2,1)}, bf16[336,256]{1,0:T(8,128)(2,1)}, u32[]{:S(2)}, u32[]{:S(2)}) collective-permute-start(bf16[336,256]{1,0:T(8,128)(2,1)} %slice.14), channel_id=1, source_target_pairs={{0,4},{1,0},{2,1},{3,2},{7,3},{6,7},{5,6},{4,5},{8,12},{9,8},{10,9... | collective-permute-start | bytes 516104 | tf_op jit(solution)/shard_map/ppermute | solution.py:490
  33.1 1.0 %collective-permute-start.9 = (bf16[336,256]{1,0:T(8,128)(2,1)}, bf16[336,256]{1,0:T(8,128)(2,1)}, u32[]{:S(2)}, u32[]{:S(2)}) collective-permute-start(bf16[336,256]{1,0:T(8,128)(2,1)} %slice.13), channel_id=1, source_target_pairs={{0,1},{1,2},{2,3},{3,7},{7,6},{6,5},{5,4},{4,0},{8,9},{9,10},{10,1... | collective-permute-start | bytes 516104 | tf_op jit(solution)/shard_map/ppermute | solution.py:490
  34.1 3.0 %collective-permute-done.10.refs_12_ = bf16[336,256]{1,0:T(8,128)(2,1)} collective-permute-done((bf16[336,256]{1,0:T(8,128)(2,1)}, bf16[336,256]{1,0:T(8,128)(2,1)}, u32[]{:S(2)}, u32[]{:S(2)}) %collective-permute-start.10) | collective-permute-done | bytes 172064 | tf_op jit(solution)/shard_map/ppermute | solution.py:490
  37.1 1.7 %collective-permute-done.9.refs_11_ = bf16[336,256]{1,0:T(8,128)(2,1)} collective-permute-done((bf16[336,256]{1,0:T(8,128)(2,1)}, bf16[336,256]{1,0:T(8,128)(2,1)}, u32[]{:S(2)}, u32[]{:S(2)}) %collective-permute-start.9) | collective-permute-done | bytes 172064 | tf_op jit(solution)/shard_map/ppermute | solution.py:490
  38.8 1.0 %copy-done.2 = bf16[672,256]{1,0:T(8,128)(2,1)S(1)} copy-done((bf16[672,256]{1,0:T(8,128)(2,1)S(1)}, bf16[672,256]{1,0:T(8,128)(2,1)}, u32[]{:S(2)}) %copy-start.2) | copy-done | bytes 344088
  39.8 1.0 %copy-done.4 = bf16[672,256]{1,0:T(8,128)(2,1)S(1)} copy-done((bf16[672,256]{1,0:T(8,128)(2,1)S(1)}, bf16[672,256]{1,0:T(8,128)(2,1)}, u32[]{:S(2)}) %copy-start.4) | copy-done | bytes 344088
  40.8 1.0 %copy-done.6 = bf16[672,256]{1,0:T(8,128)(2,1)S(1)} copy-done((bf16[672,256]{1,0:T(8,128)(2,1)S(1)}, bf16[672,256]{1,0:T(8,128)(2,1)}, u32[]{:S(2)}) %copy-start.6) | copy-done | bytes 344088
  41.8 0.7 %copy-done.8 = f32[2,2176]{1,0:T(2,128)S(1)} copy-done((f32[2,2176]{1,0:T(2,128)S(1)}, f32[2,2176]{1,0:T(2,128)}, u32[]{:S(2)}) %copy-start.8) | copy-done | bytes 17432
  43.9 11.3 %shard_map.91 = (bf16[128,512]{1,0:T(8,128)(2,1)S(1)}, bf16[128,512]{1,0:T(8,128)(2,1)S(1)}, bf16[128,512]{1,0:T(8,128)(2,1)S(1)}, bf16[128,512]{1,0:T(8,128)(2,1)S(1)}) custom-call(bf16[128,2048]{1,0:T(8,128)(2,1)S(1)} %bitcast.14, bf16[128,2048]{1,0:T(8,128)(2,1)S(1)} %collective-permute-done.refs_1_, ...), custom_call_target="tpu_custom_call" | custom-call | tf_op jit(solution)/shard_map/pallas_call | solution.py:477
  55.2 1.6 %collective-permute-start.12 = (bf16[128,512]{1,0:T(8,128)(2,1)S(1)}, bf16[128,512]{1,0:T(8,128)(2,1)S(1)}, u32[]{:S(2)}, u32[]{:S(2)}) collective-permute-start(bf16[128,512]{1,0:T(8,128)(2,1)S(1)} %get-tuple-element.11), channel_id=1, source_target_pairs={{0,16},{8,24},{16,0},{24,8},{1,17},{9,25},{17,1},{25,9},{2,18},{10... | collective-permute-start | bytes 393224 | tf_op jit(solution)/shard_map/ppermute | solution.py:494
  57.2 4.4 %collective-permute-done.12 = bf16[128,512]{1,0:T(8,128)(2,1)S(1)} collective-permute-done((bf16[128,512]{1,0:T(8,128)(2,1)S(1)}, bf16[128,512]{1,0:T(8,128)(2,1)S(1)}, u32[]{:S(2)}, u32[]{:S(2)}) %collective-permute-start.12) | collective-permute-done | bytes 131104 | tf_op jit(solution)/shard_map/ppermute | solution.py:494
  61.6 1.9 %collective-permute-done.13 = bf16[128,512]{1,0:T(8,128)(2,1)S(1)} collective-permute-done((bf16[128,512]{1,0:T(8,128)(2,1)S(1)}, bf16[128,512]{1,0:T(8,128)(2,1)S(1)}, u32[]{:S(2)}, u32[]{:S(2)}) %collective-permute-start.13) | collective-permute-done | bytes 131104 | tf_op jit(solution)/shard_map/ppermute | solution.py:494
  (45 shorter events, 5.1 us)
Async XLA Ops:
  0.0 5.1 %copy-start = (bf16[1,128,2048]{2,1,0:T(8,128)(2,1)S(1)}, bf16[1,128,2048]{2,1,0:T(8,128)(2,1)}, u32[]{:S(2)}) copy-start(bf16[1,128,2048]{2,1,0:T(8,128)(2,1)} %param.9) | copy-start | bytes 1572868
  0.0 38.8 %copy-start.7 = (f32[2,4,2176]{2,1,0:T(4,128)S(1)}, f32[2,4,2176]{2,1,0:T(4,128)}, u32[]{:S(2)}) copy-start(f32[2,4,2176]{2,1,0:T(4,128)} %refs_14_.1) | copy-start | bytes 208900
  0.0 38.8 %copy-start.10 = (f32[2,32]{1,0:T(2,128)S(1)}, f32[2,32]{1,0:T(2,128)}, u32[]{:S(2)}) copy-start(f32[2,32]{1,0:T(2,128)} %refs_16_.1) | copy-start | bytes 772
  0.0 38.8 %copy-start.11 = (f32[2,32]{1,0:T(2,128)S(1)}, f32[2,32]{1,0:T(2,128)}, u32[]{:S(2)}) copy-start(f32[2,32]{1,0:T(2,128)} %refs_17_.1) | copy-start | bytes 772
  0.0 38.8 %copy-start.12 = (f32[2,32]{1,0:T(2,128)S(1)}, f32[2,32]{1,0:T(2,128)}, u32[]{:S(2)}) copy-start(f32[2,32]{1,0:T(2,128)} %refs_18_.1) | copy-start | bytes 772
  2.0 11.1 %collective-permute-start.4 = (bf16[672,256]{1,0:T(8,128)(2,1)S(1)}, bf16[672,256]{1,0:T(8,128)(2,1)S(1)}, u32[]{:S(2)}, u32[]{:S(2)}) collective-permute-start(bf16[672,256]{1,0:T(8,128)(2,1)S(1)} %pad_maximum_fusion.refs_4_), channel_id=1, source_target_pairs={{0,4},{1,0},{2,1},{3,2},{7,3},{6,7},{5,6},{4,5},{8,12},{9,8},{10,9... | collective-permute-start | bytes 1032200 | tf_op jit(solution)/shard_map/ppermute | solution.py:490
  5.0 9.8 %collective-permute-start.3 = (bf16[672,256]{1,0:T(8,128)(2,1)S(1)}, bf16[672,256]{1,0:T(8,128)(2,1)S(1)}, u32[]{:S(2)}, u32[]{:S(2)}) collective-permute-start(bf16[672,256]{1,0:T(8,128)(2,1)S(1)} %pad_maximum_fusion.refs_4_), channel_id=1, source_target_pairs={{0,1},{1,2},{2,3},{3,7},{7,6},{6,5},{5,4},{4,0},{8,9},{9,10},{10,1... | collective-permute-start | bytes 1032200 | tf_op jit(solution)/shard_map/ppermute | solution.py:490
  5.1 13.4 %collective-permute-start.1 = (bf16[128,2048]{1,0:T(8,128)(2,1)S(1)}, bf16[128,2048]{1,0:T(8,128)(2,1)S(1)}, u32[]{:S(2)}, u32[]{:S(2)}) collective-permute-start(bf16[128,2048]{1,0:T(8,128)(2,1)S(1)} %bitcast.12), channel_id=1, source_target_pairs={{0,16},{8,24},{16,0},{24,8},{1,17},{9,25},{17,1},{25,9},{2,18},{10... | collective-permute-start | bytes 1572872 | tf_op jit(solution)/shard_map/ppermute | solution.py:494
  13.1 9.2 %collective-permute-start.6 = (bf16[672,256]{1,0:T(8,128)(2,1)S(1)}, bf16[672,256]{1,0:T(8,128)(2,1)S(1)}, u32[]{:S(2)}, u32[]{:S(2)}) collective-permute-start(bf16[672,256]{1,0:T(8,128)(2,1)S(1)} %collective-permute-done.4.refs_6_), channel_id=1, source_target_pairs={{0,4},{1,0},{2,1},{3,2},{7,3},{6,7},{5,6},{4,5},{8,12},{9,8},{10,9... | collective-permute-start | bytes 1032200 | tf_op jit(solution)/shard_map/ppermute | solution.py:490
  14.8 9.7 %collective-permute-start.5 = (bf16[672,256]{1,0:T(8,128)(2,1)S(1)}, bf16[672,256]{1,0:T(8,128)(2,1)S(1)}, u32[]{:S(2)}, u32[]{:S(2)}) collective-permute-start(bf16[672,256]{1,0:T(8,128)(2,1)S(1)} %collective-permute-done.3.refs_5_), channel_id=1, source_target_pairs={{0,1},{1,2},{2,3},{3,7},{7,6},{6,5},{5,4},{4,0},{8,9},{9,10},{10,1... | collective-permute-start | bytes 1032200 | tf_op jit(solution)/shard_map/ppermute | solution.py:490
  15.9 18.2 %collective-permute-start = (bf16[128,2048]{1,0:T(8,128)(2,1)S(1)}, bf16[128,2048]{1,0:T(8,128)(2,1)S(1)}, u32[]{:S(2)}, u32[]{:S(2)}) collective-permute-start(bf16[128,2048]{1,0:T(8,128)(2,1)S(1)} %bitcast.13), channel_id=1, source_target_pairs={{0,8},{8,0},{16,24},{24,16},{1,9},{9,1},{17,25},{25,17},{2,10},{10... | collective-permute-start | bytes 1572872 | tf_op jit(solution)/shard_map/ppermute | solution.py:494
  18.5 15.6 %collective-permute-start.2 = (bf16[128,2048]{1,0:T(8,128)(2,1)S(1)}, bf16[128,2048]{1,0:T(8,128)(2,1)S(1)}, u32[]{:S(2)}, u32[]{:S(2)}) collective-permute-start(bf16[128,2048]{1,0:T(8,128)(2,1)S(1)} %collective-permute-done.1.refs_2_), channel_id=1, source_target_pairs={{0,8},{8,0},{16,24},{24,16},{1,9},{9,1},{17,25},{25,17},{2,10},{10... | collective-permute-start | bytes 1572872 | tf_op jit(solution)/shard_map/ppermute | solution.py:494
  22.4 8.3 %collective-permute-start.8 = (bf16[672,256]{1,0:T(8,128)(2,1)S(1)}, bf16[672,256]{1,0:T(8,128)(2,1)S(1)}, u32[]{:S(2)}, u32[]{:S(2)}) collective-permute-start(bf16[672,256]{1,0:T(8,128)(2,1)S(1)} %collective-permute-done.6.refs_8_), channel_id=1, source_target_pairs={{0,4},{1,0},{2,1},{3,2},{7,3},{6,7},{5,6},{4,5},{8,12},{9,8},{10,9... | collective-permute-start | bytes 1032200 | tf_op jit(solution)/shard_map/ppermute | solution.py:490
  24.4 8.0 %copy-start.5 = (bf16[672,256]{1,0:T(8,128)(2,1)}, bf16[672,256]{1,0:T(8,128)(2,1)S(1)}, u32[]{:S(2)}) copy-start(bf16[672,256]{1,0:T(8,128)(2,1)S(1)} %collective-permute-done.5.refs_7_) | copy-start | bytes 1032196
  24.4 7.9 %collective-permute-start.7 = (bf16[672,256]{1,0:T(8,128)(2,1)S(1)}, bf16[672,256]{1,0:T(8,128)(2,1)S(1)}, u32[]{:S(2)}, u32[]{:S(2)}) collective-permute-start(bf16[672,256]{1,0:T(8,128)(2,1)S(1)} %collective-permute-done.5.refs_7_), channel_id=1, source_target_pairs={{0,1},{1,2},{2,3},{3,7},{7,6},{6,5},{5,4},{4,0},{8,9},{9,10},{10,1... | collective-permute-start | bytes 1032200 | tf_op jit(solution)/shard_map/ppermute | solution.py:490
  31.4 5.7 %collective-permute-start.10 = (bf16[336,256]{1,0:T(8,128)(2,1)}, bf16[336,256]{1,0:T(8,128)(2,1)}, u32[]{:S(2)}, u32[]{:S(2)}) collective-permute-start(bf16[336,256]{1,0:T(8,128)(2,1)} %slice.14), channel_id=1, source_target_pairs={{0,4},{1,0},{2,1},{3,2},{7,3},{6,7},{5,6},{4,5},{8,12},{9,8},{10,9... | collective-permute-start | bytes 516104 | tf_op jit(solution)/shard_map/ppermute | solution.py:490
  33.1 5.7 %collective-permute-start.9 = (bf16[336,256]{1,0:T(8,128)(2,1)}, bf16[336,256]{1,0:T(8,128)(2,1)}, u32[]{:S(2)}, u32[]{:S(2)}) collective-permute-start(bf16[336,256]{1,0:T(8,128)(2,1)} %slice.13), channel_id=1, source_target_pairs={{0,1},{1,2},{2,3},{3,7},{7,6},{6,5},{5,4},{4,0},{8,9},{9,10},{10,1... | collective-permute-start | bytes 516104 | tf_op jit(solution)/shard_map/ppermute | solution.py:490
  38.8 1.0 %copy-start.2 = (bf16[672,256]{1,0:T(8,128)(2,1)S(1)}, bf16[672,256]{1,0:T(8,128)(2,1)}, u32[]{:S(2)}) copy-start(bf16[672,256]{1,0:T(8,128)(2,1)} %copy-done.1) | copy-start | bytes 1032196
  39.8 1.0 %copy-start.4 = (bf16[672,256]{1,0:T(8,128)(2,1)S(1)}, bf16[672,256]{1,0:T(8,128)(2,1)}, u32[]{:S(2)}) copy-start(bf16[672,256]{1,0:T(8,128)(2,1)} %copy-done.3) | copy-start | bytes 1032196
  40.8 1.0 %copy-start.6 = (bf16[672,256]{1,0:T(8,128)(2,1)S(1)}, bf16[672,256]{1,0:T(8,128)(2,1)}, u32[]{:S(2)}) copy-start(bf16[672,256]{1,0:T(8,128)(2,1)} %copy-done.5) | copy-start | bytes 1032196
  55.1 2.0 %collective-permute-start.11 = (bf16[128,512]{1,0:T(8,128)(2,1)S(1)}, bf16[128,512]{1,0:T(8,128)(2,1)S(1)}, u32[]{:S(2)}, u32[]{:S(2)}) collective-permute-start(bf16[128,512]{1,0:T(8,128)(2,1)S(1)} %get-tuple-element.10), channel_id=1, source_target_pairs={{0,8},{8,0},{16,24},{24,16},{1,9},{9,1},{17,25},{25,17},{2,10},{10... | collective-permute-start | bytes 393224 | tf_op jit(solution)/shard_map/ppermute | solution.py:494
  55.2 6.4 %collective-permute-start.12 = (bf16[128,512]{1,0:T(8,128)(2,1)S(1)}, bf16[128,512]{1,0:T(8,128)(2,1)S(1)}, u32[]{:S(2)}, u32[]{:S(2)}) collective-permute-start(bf16[128,512]{1,0:T(8,128)(2,1)S(1)} %get-tuple-element.11), channel_id=1, source_target_pairs={{0,16},{8,24},{16,0},{24,8},{1,17},{9,25},{17,1},{25,9},{2,18},{10... | collective-permute-start | bytes 393224 | tf_op jit(solution)/shard_map/ppermute | solution.py:494
  56.8 6.7 %collective-permute-start.13 = (bf16[128,512]{1,0:T(8,128)(2,1)S(1)}, bf16[128,512]{1,0:T(8,128)(2,1)S(1)}, u32[]{:S(2)}, u32[]{:S(2)}) collective-permute-start(bf16[128,512]{1,0:T(8,128)(2,1)S(1)} %get-tuple-element.12), channel_id=1, source_target_pairs={{0,24},{8,16},{16,8},{24,0},{1,25},{9,17},{17,9},{25,1},{2,26},{10... | collective-permute-start | bytes 393224 | tf_op jit(solution)/shard_map/ppermute | solution.py:494
  61.6 1.9 %copy-start.14 = (bf16[1,128,2048]{2,1,0:T(8,128)(2,1)}, bf16[1,128,2048]{2,1,0:T(8,128)(2,1)S(1)}, u32[]{:S(2)}) copy-start(bf16[1,128,2048]{2,1,0:T(8,128)(2,1)S(1)} %bitcast_dynamic-update-slice_fusion.1) | copy-start | bytes 1572868
  (5 other events, 3.6 us)

commit v4 on v0

--- a/solution.py
+++ b/solution.py
@@ -1,6 +1,10 @@
+import functools
+
 import jax
 import jax.numpy as jnp
 from jax import lax
+from jax.experimental import pallas as pl
+from jax.experimental.pallas import tpu as pltpu
 from jax.sharding import PartitionSpec as P
 
 HEADS = 32
@@ -141,7 +145,7 @@
     return total.astype(jnp.bfloat16)
 
 
-def on_device(
+def on_sections(
     hidden, in_weight, read_starts, conv_weight, conv_bias, dt_bias, decay, skip, norm_gain
 ):
     tokens = hidden[0]
@@ -173,6 +177,448 @@
     return mixed.astype(jnp.bfloat16)[None]
 
 
+LANES = 128
+SIDE = 256
+EDGE = 8
+GROUP = 32
+
+
+def ring_order(count):
+    return [i if i < count else 3 * count - 1 - i for i in range(2 * count)]
+
+
+def split_parts(value, count):
+    parts = []
+    for _ in range(count):
+        parts.append(value.astype(jnp.bfloat16))
+        value = value - parts[-1].astype(jnp.float32)
+    return parts
+
+
+def lane_row():
+    lane = lax.broadcasted_iota(jnp.int32, (BLOCK, LANES), 1)
+    row = lax.broadcasted_iota(jnp.int32, (BLOCK, LANES), 0)
+    return lane, row
+
+
+def shard_at(away, ring):
+    fsdp, batch = lax.axis_index("fsdp"), lax.axis_index("batch")
+    position = jnp.where(fsdp == 0, batch, 2 * ring - 1 - batch)
+    there = lax.rem(position + 2 * ring + away, 2 * ring)
+    return jnp.where(there < ring, there, 3 * ring - 1 - there)
+
+
+def take_rows(pieces, ring, ways, rows_in):
+    depth = rows_in.shape[1] // len(ways)
+    for n, away in enumerate(ways):
+        at = pl.ds(pl.multiple_of(shard_at(away, ring) * depth, depth), depth)
+        for mask in range(4):
+            rows_in[mask * BLOCK : (mask + 1) * BLOCK, n * depth : (n + 1) * depth] = pieces[mask][:, at]
+
+
+def times_transposed(a, b):
+    return lax.dot_general(a, b, (((1,), (1,)), ((), ())), preferred_element_type=jnp.float32)
+
+
+def pack_kernel(columns, weight_in, own, sems):
+    at = pl.ds(pl.multiple_of(lax.axis_index("seq") * columns, columns), columns)
+    side_rows = own.shape[0] - columns
+    copies = [
+        pltpu.make_async_copy(weight_in.at[at], own.at[pl.ds(0, columns)], sems.at[0]),
+        pltpu.make_async_copy(weight_in.at[pl.ds(INNER, side_rows)], own.at[pl.ds(columns, side_rows)], sems.at[1]),
+    ]
+    for copy in copies:
+        copy.start()
+    for copy in copies:
+        copy.wait()
+
+
+def early_kernel(heads, ring, ways, *refs):
+    count = len(ways)
+    pieces, refs = refs[:4], refs[4:]
+    weights, refs = refs[:count], refs[count:]
+    marks_in, conv_w_in, conv_b_in, step_bias_in, decay_in, skip_in, gain_in = refs[:7]
+    partial, conv_w, conv_b, per_lane, skips, gains, spread, barred, flags, refs = (*refs[7:16], refs[16:])
+    per_head, marks, rows_in, w_in, sems = refs
+    seq = lax.axis_index("seq")
+    columns = heads * HEAD_DIM
+    depth = weights[0].shape[1]
+    rows = weights[0].shape[0]
+    own_lanes = pl.ds(pl.multiple_of(seq * columns, columns), columns)
+    side_lanes = pl.ds(INNER, LANES)
+    copies = [
+        (conv_w_in.at[:, :, own_lanes], conv_w.at[:, :, pl.ds(0, columns)]),
+        (conv_w_in.at[:, :, side_lanes], conv_w.at[:, :, pl.ds(columns, LANES)]),
+        (conv_b_in.at[:, own_lanes], conv_b.at[:, pl.ds(0, columns)]),
+        (conv_b_in.at[:, side_lanes], conv_b.at[:, pl.ds(columns, LANES)]),
+        (step_bias_in, per_head.at[0]),
+        (decay_in, per_head.at[1]),
+        (skip_in, per_head.at[2]),
+        (gain_in.at[:, own_lanes], gains),
+        (marks_in, marks),
+    ]
+    copies = [pltpu.make_async_copy(a, b, sems.at[i]) for i, (a, b) in enumerate(copies)]
+    for copy in copies:
+        copy.start()
+    take_rows(pieces, ring, ways, rows_in)
+    w_in[rows:, :] = jnp.zeros((w_in.shape[0] - rows, w_in.shape[1]), jnp.bfloat16)
+    for n in range(count):
+        w_in[:rows, n * depth : (n + 1) * depth] = weights[n][...]
+    for n in range(w_in.shape[0] // SIDE):
+        at = slice(n * SIDE, (n + 1) * SIDE)
+        partial[:, at] = times_transposed(rows_in[...], w_in[at, :])
+    for copy in copies:
+        copy.wait()
+
+    lane, row = lane_row()
+    within = lane % GROUP
+    head_lane = within < 2 * heads
+    to_first = lax.rem(LANES - seq * heads, LANES)
+
+    def own_heads(k):
+        both = jnp.concatenate([per_head[k], jnp.zeros((2, LANES - HEADS), jnp.float32)], axis=1)
+        both = pltpu.roll(both, to_first, 1)
+        behind = pltpu.roll(both, heads, 1)
+        value = jnp.where(lane[:1] < heads, both[0:1, :], behind[1:2, :])
+        return jnp.where(lane[:1] < 2 * heads, value, 0.0)
+
+    for k in range(2):
+        value = jnp.broadcast_to(own_heads(k), (8, LANES))
+        per_lane[k] = sum([pltpu.roll(value, g * GROUP, 1) for g in range(1, LANES // GROUP)], value)
+    at_row = lax.broadcasted_iota(jnp.int32, (LANES, columns), 0)
+    head = lax.broadcasted_iota(jnp.int32, (LANES, columns), 1) // HEAD_DIM
+    direct = jnp.broadcast_to(own_heads(2), (16, LANES))
+    for d in range(2):
+        hit = (at_row == head + d * heads) | (at_row == head + (d + 2) * heads) | (at_row == head + (d + 4) * heads)
+        spread[d] = jnp.where(hit, 1.0, 0.0).astype(jnp.bfloat16)
+        wide = jnp.dot(packed(direct, 3, heads), spread[d], preferred_element_type=jnp.float32)
+        skips[d] = wide[:8]
+
+    position = row + lane // GROUP * BLOCK
+    here = position == marks[:, 0:1]
+    after = position + 1 == marks[:, 0:1]
+    for m in range(1, marks.shape[1]):
+        here = here | (position == marks[:, m : m + 1])
+        after = after | (position + 1 == marks[:, m : m + 1])
+    forward_start, backward_start = within == 2 * heads, within == 2 * heads + 1
+    starts = jnp.where((here & forward_start) | (after & backward_start), 1.0, 0.0).astype(jnp.bfloat16)
+    backward_lane = ((within >= heads) & head_lane) | backward_start
+    lower = jnp.where(row >= lane, 1.0, 0.0).astype(jnp.bfloat16)
+    upper = jnp.where(row <= lane, 1.0, 0.0).astype(jnp.bfloat16)
+    ahead = jnp.dot(lower, starts, preferred_element_type=jnp.float32)
+    behind = jnp.dot(upper, starts, preferred_element_type=jnp.float32)
+    seen = jnp.where(backward_lane, behind, ahead)
+    wanted = lane - within + 2 * heads + jnp.where(backward_lane, 1, 0)
+    chosen = jnp.where(row == wanted, 1.0, 0.0).astype(jnp.bfloat16)
+    seen = jnp.dot(seen.astype(jnp.bfloat16), chosen, preferred_element_type=jnp.float32)
+    last = jnp.where(backward_lane[:1], seen[:1], seen[BLOCK - 1 :])
+    flags[0] = jnp.where((seen == last) & head_lane, 1.0, 0.0)
+    flags[1] = jnp.where((seen == 0.0) & head_lane, 1.0, 0.0)
+    flags[2] = jnp.where((jnp.broadcast_to(last, (BLOCK, LANES)) == 0.0) & head_lane, 1.0, 0.0)
+    turned = seen.T
+    for b in range(LANES // GROUP):
+        for d in range(2):
+            ordered = (row >= lane) if d == 0 else (row <= lane)
+            at = b * GROUP + d * heads
+            allowed = ordered & (seen[:, at : at + 1] == turned[at : at + 1, :])
+            barred[d, b] = jnp.where(allowed, 0.0, -1e30)
+
+
+def packed(value, count, heads):
+    parts = split_parts(value, count)
+    joined = parts[0].astype(jnp.float32)
+    for k in range(1, count):
+        joined = joined + pltpu.roll(parts[k].astype(jnp.float32), 2 * heads * k, 1)
+    return joined.astype(jnp.bfloat16)
+
+
+def mixer_kernel(heads, ring, ways, *refs):
+    count = len(ways)
+    pieces, refs = refs[:4], refs[4:]
+    weights, refs = refs[: count - 1], refs[count - 1 :]
+    ends, refs = refs[:2], refs[2:]
+    partial, conv_w, conv_b, per_lane, skips, gains, spread, barred, flags = refs[:9]
+    outs, refs = refs[9:13], refs[13:]
+    rows_in, w_in, padded, xs, cs, bs, widen_in, leads, tails, state, ys, mixed = refs
+    seq = lax.axis_index("seq")
+    columns = heads * HEAD_DIM
+    depth = weights[0].shape[1]
+    rows = weights[0].shape[0]
+    chunks = columns // LANES
+    length = rows_in.shape[0]
+    blocks = length // BLOCK
+    cut = ends[0].shape[0]
+    lane, row = lane_row()
+
+    take_rows(pieces, ring, ways, rows_in)
+    w_in[rows:, :] = jnp.zeros((w_in.shape[0] - rows, w_in.shape[1]), jnp.bfloat16)
+    for n in range(count - 1):
+        w_in[:rows, n * depth : (n + 1) * depth] = weights[n][...]
+    w_in[:cut, (count - 1) * depth :] = ends[0][...]
+    w_in[cut:rows, (count - 1) * depth :] = ends[1][...]
+    edge = jnp.zeros((EDGE, LANES), jnp.float32)
+    for c in range(chunks + 1):
+        padded[c, 0:EDGE, :] = edge
+        padded[c, EDGE + length :, :] = edge
+    state[...] = jnp.zeros_like(state)
+
+    places = [pl.multiple_of((seq ^ mask) * BLOCK, BLOCK) for mask in range(4)]
+
+    def project_in(n):
+        at = slice(n * SIDE, (n + 1) * SIDE)
+        out = partial[:, at] + times_transposed(rows_in[...], w_in[at, :])
+        return out.astype(jnp.bfloat16).astype(jnp.float32)
+
+    def keep(c, value):
+        for mask in range(4):
+            padded[c, pl.ds(EDGE + places[mask], BLOCK), :] = value[mask * BLOCK : (mask + 1) * BLOCK, :]
+
+    side_out = project_in(columns // SIDE)
+    keep(chunks, side_out[:, :LANES])
+    for n in range(columns // SIDE):
+        part_out = project_in(n)
+        for k in range(SIDE // LANES):
+            keep(n * (SIDE // LANES) + k, part_out[:, k * LANES : (k + 1) * LANES])
+
+    within = lane % GROUP
+    head_lane = within < 2 * heads
+    backward_lane = (within >= heads) & head_lane
+    to_first = lax.rem(LANES - seq * heads, LANES)
+    raw = jnp.zeros((BLOCK, LANES), jnp.float32)
+    for mask in range(4):
+        mine = pltpu.roll(side_out[mask * BLOCK : (mask + 1) * BLOCK, LANES:], to_first, 1)
+        mine = jnp.where(lane < heads, mine, 0.0)
+        raw = raw + pltpu.roll(mine + pltpu.roll(mine, heads, 1), (seq ^ mask) * GROUP, 1)
+    raw = raw + per_lane[0][:1]
+    step = jnp.maximum(raw, 0.0) + jnp.log1p(jnp.exp(-jnp.abs(raw)))
+    rate = -step * per_lane[1][:1]
+    two = jnp.concatenate(split_parts(rate, 2), axis=1)
+    lower = jnp.where(row >= lane, 1.0, 0.0).astype(jnp.bfloat16)
+    upper = jnp.where(row <= lane, 1.0, 0.0).astype(jnp.bfloat16)
+    sums = jnp.dot(jnp.concatenate([lower, upper], axis=0), two, preferred_element_type=jnp.float32)
+    sums = sums[:, :LANES] + sums[:, LANES:]
+    cum = jnp.where(backward_lane, sums[BLOCK:], sums[:BLOCK])
+    last = jnp.where(backward_lane[:1], cum[:1], cum[BLOCK - 1 :])
+    tail = flags[0] * jnp.exp(last - cum) * step
+    lead = flags[1] * jnp.exp(cum)
+    fade = flags[2][:8] * jnp.exp(jnp.broadcast_to(last, (8, LANES)))
+    shown = (jnp.log(step) - cum).T
+    fades = []
+    for b in range(blocks):
+        for k, value in enumerate((lead, tail)):
+            if b:
+                value = pltpu.roll(value, LANES - b * GROUP, 1)
+            at = (k * blocks + b) * BLOCK
+            widen_in[at : at + BLOCK, :] = jnp.where(lane < 2 * heads, value, 0.0).astype(jnp.bfloat16)
+        value = pltpu.roll(fade, LANES - b * GROUP, 1) if b else fade
+        fades.append(packed(jnp.where(lane[:8] < 2 * heads, value, 0.0), 2, heads)[:1])
+    fades = jnp.concatenate(fades + [jnp.zeros((16 - blocks, LANES), jnp.bfloat16)], axis=0)
+    fade_wide = []
+    for d in range(2):
+        wide = jnp.dot(widen_in[...], spread[d], preferred_element_type=jnp.float32).astype(jnp.bfloat16)
+        leads[d] = wide[:length]
+        tails[d] = wide[length:]
+        fade_wide.append(jnp.dot(fades, spread[d], preferred_element_type=jnp.float32))
+
+    short = 64
+
+    def conv_rows(i, carry):
+        at = pl.multiple_of(i * short, short)
+        for c in range(chunks + 1):
+            taps = [padded[c, pl.ds(at + EDGE - 3 + k, short), :] for k in range(7)]
+            lanes = slice(c * LANES, (c + 1) * LANES)
+            for d in range(2):
+                acc = conv_b[d : d + 1, lanes] + conv_w[d, 0:1, lanes] * taps[0 if d == 0 else 6]
+                for k in range(1, KERNEL):
+                    acc = acc + conv_w[d, k : k + 1, lanes] * taps[k if d == 0 else 6 - k]
+                half = 0.5 * acc
+                value = half + half * jnp.tanh(half)
+                if c < chunks:
+                    xs[d, pl.ds(at, short), lanes] = value.astype(jnp.bfloat16)
+                else:
+                    high = lax.broadcasted_iota(jnp.int32, (short, LANES), 1) >= STATE
+                    cs[d, pl.ds(at, short), :] = jnp.where(high, value, 0.0).astype(jnp.bfloat16)
+                    bs[d, pl.ds(at, short), :] = jnp.where(
+                        high, pltpu.roll(value, STATE, 1), 0.0
+                    ).astype(jnp.bfloat16)
+        return carry
+
+    lax.fori_loop(0, length // short, conv_rows, 0)
+
+    group = SIDE // HEAD_DIM
+    lane_head = lax.broadcasted_iota(jnp.int32, (BLOCK, SIDE), 1) // HEAD_DIM
+    for i in range(blocks):
+        for d in range(2):
+            b = i if d == 0 else blocks - 1 - i
+            at = slice(b * BLOCK, (b + 1) * BLOCK)
+            c_part = cs[d, at, :]
+            b_part = bs[d, at, :]
+            scores = times_transposed(c_part, b_part)
+            bar = barred[d, b]
+            before = state[d]
+            carried = jnp.dot(c_part, before.astype(jnp.bfloat16), preferred_element_type=jnp.float32)
+            x_all = xs[d, at, :]
+            local_end = lax.dot_general(
+                b_part, tails[d, at, :] * x_all, (((0,), (0,)), ((), ())), preferred_element_type=jnp.float32
+            )
+            state[d] = fade_wide[d][b : b + 1] * before + local_end
+            for q in range(columns // SIDE):
+                some = []
+                for h in range(q * group, (q + 1) * group):
+                    n = b * GROUP + d * heads + h
+                    gap = cum[:, n : n + 1] + (shown[n : n + 1, :] + bar)
+                    some.append((jnp.exp(gap) * scores).astype(jnp.bfloat16))
+                lanes = slice(q * SIDE, (q + 1) * SIDE)
+                x_part = x_all[:, lanes]
+                none = jnp.zeros_like(x_part)
+                spaced = jnp.concatenate([jnp.where(lane_head == h, x_part, none) for h in range(group)], axis=0)
+                inner = jnp.dot(jnp.concatenate(some, axis=1), spaced, preferred_element_type=jnp.float32)
+                ys[d, at, lanes] = (
+                    inner
+                    + leads[d, at, lanes].astype(jnp.float32) * carried[:, lanes]
+                    + skips[d, :1, lanes] * x_part.astype(jnp.float32)
+                )
+
+    head_row = lax.broadcasted_iota(jnp.int32, (SIDE, SIDE), 0) // HEAD_DIM
+    head_col = lax.broadcasted_iota(jnp.int32, (SIDE, SIDE), 1) // HEAD_DIM
+    same = jnp.where(head_row == head_col, 1.0 / HEAD_DIM, 0.0).astype(jnp.bfloat16)
+    for q in range(columns // SIDE):
+        lanes = slice(q * SIDE, (q + 1) * SIDE)
+        both = 0.0
+        for d in range(2):
+            y = ys[d, :, lanes]
+            mean = jnp.dot((y * y).astype(jnp.bfloat16), same, preferred_element_type=jnp.float32)
+            both = both + y * lax.rsqrt(mean + 1e-05) * gains[d : d + 1, lanes]
+        mixed[:, lanes] = both.astype(jnp.bfloat16)
+    for mask in range(4):
+        outs[mask][...] = mixed[pl.ds(places[mask], BLOCK), :]
+
+
+IN_VMEM = pl.BlockSpec(memory_space=pltpu.VMEM)
+IN_HBM = pl.BlockSpec(memory_space=pltpu.HBM)
+ROOM = 24 * 1024 * 1024
+
+
+def pack(weight, columns):
+    side_rows = weight.shape[0] - INNER
+    return pl.pallas_call(
+        functools.partial(pack_kernel, columns),
+        out_shape=jax.ShapeDtypeStruct((columns + side_rows, weight.shape[1]), weight.dtype),
+        in_specs=[IN_HBM],
+        out_specs=IN_VMEM,
+        scratch_shapes=[pltpu.SemaphoreType.DMA((2,))],
+        compiler_params=pltpu.CompilerParams(vmem_limit_bytes=ROOM),
+    )(weight)
+
+
+def early(heads, ring, ways, pieces, weights, params):
+    length = pieces[0].shape[0] * len(pieces)
+    columns = heads * HEAD_DIM
+    depth = weights[0].shape[1]
+    blocks = length // BLOCK
+    wide = columns + SIDE
+    known = depth * len(ways)
+    shapes = [
+        ((length, wide), jnp.float32),
+        ((2, KERNEL, columns + LANES), jnp.float32),
+        ((2, columns + LANES), jnp.float32),
+        ((2, 8, LANES), jnp.float32),
+        ((2, 8, columns), jnp.float32),
+        ((2, columns), jnp.float32),
+        ((2, LANES, columns), jnp.bfloat16),
+        ((2, blocks, BLOCK, LANES), jnp.float32),
+        ((3, BLOCK, LANES), jnp.float32),
+    ]
+    return pl.pallas_call(
+        functools.partial(early_kernel, heads, ring, ways),
+        out_shape=[jax.ShapeDtypeStruct(*one) for one in shapes],
+        in_specs=[IN_VMEM] * (len(pieces) + len(weights)) + [IN_HBM] * len(params),
+        out_specs=[IN_VMEM] * len(shapes),
+        scratch_shapes=[
+            pltpu.VMEM((3, 2, HEADS), jnp.float32),
+            pltpu.VMEM(params[0].shape, jnp.int32),
+            pltpu.VMEM((length, known), jnp.bfloat16),
+            pltpu.VMEM((wide, known), jnp.bfloat16),
+            pltpu.SemaphoreType.DMA((9,)),
+        ],
+        cost_estimate=pl.CostEstimate(flops=2 * length * wide * known, bytes_accessed=8 * 1024 * 1024, transcendentals=0),
+        compiler_params=pltpu.CompilerParams(vmem_limit_bytes=ROOM),
+    )(*pieces, *weights, *params)
+
+
+def mix(heads, ring, ways, pieces, weights, ends, prepared):
+    section = pieces[0].shape[0]
+    columns = heads * HEAD_DIM
+    length = section * len(pieces)
+    depth = weights[0].shape[1]
+    chunks = columns // LANES
+    known = depth * len(ways)
+    operands = (*pieces, *weights, *ends, *prepared)
+    scratch = [
+        ((length, known), jnp.bfloat16),
+        ((columns + SIDE, known), jnp.bfloat16),
+        ((chunks + 1, length + 2 * EDGE, LANES), jnp.float32),
+        ((2, length, columns), jnp.bfloat16),
+        ((2, length, LANES), jnp.bfloat16),
+        ((2, length, LANES), jnp.bfloat16),
+        ((2 * length, LANES), jnp.bfloat16),
+        ((2, length, columns), jnp.bfloat16),
+        ((2, length, columns), jnp.bfloat16),
+        ((2, LANES, columns), jnp.float32),
+        ((2, length, columns), jnp.float32),
+        ((length, columns), jnp.bfloat16),
+    ]
+    return pl.pallas_call(
+        functools.partial(mixer_kernel, heads, ring, ways),
+        out_shape=[jax.ShapeDtypeStruct((section, columns), jnp.bfloat16)] * len(pieces),
+        in_specs=[IN_VMEM] * len(operands),
+        out_specs=[IN_VMEM] * len(pieces),
+        scratch_shapes=[pltpu.VMEM(*one) for one in scratch],
+        compiler_params=pltpu.CompilerParams(vmem_limit_bytes=ROOM),
+    )(*operands)
+
+
+def turn(value, way):
+    order = ring_order(lax.axis_size("batch"))
+    count = len(order)
+    return lax.ppermute(value, ("fsdp", "batch"), [(order[i], order[(i + way) % count]) for i in range(count)])
+
+
+def swap(value, axis, mask):
+    return lax.ppermute(value, axis, [(i, i ^ mask) for i in range(lax.axis_size(axis))])
+
+
+def on_heads(hidden, in_weight, read_starts, conv_weight, conv_bias, dt_bias, decay, skip, norm_gain):
+    tokens = hidden[0]
+    count = lax.axis_size("seq")
+    seq = lax.axis_index("seq")
+    heads = HEADS // count
+    columns = heads * HEAD_DIM
+    own = pack(in_weight.T, columns)
+
+    ring = lax.axis_size("batch")
+    across = swap(tokens, "seq", 2)
+    pieces = [tokens, swap(tokens, "seq", 1), across, swap(across, "seq", 1)]
+    weights, ways = [own], [0]
+    up = down = own
+    for away in range(1, ring):
+        up, down = turn(up, 1), turn(down, -1)
+        weights += [up, down]
+        ways += [-away, away]
+    cut = own.shape[0] // 32 * 16
+    ends = [turn(up[:cut], 1), turn(down[cut:], -1)]
+    ways.append(ring)
+    params = (read_starts, conv_weight, conv_bias, dt_bias, decay, skip, norm_gain)
+    first = 2 * ring - 3
+    prepared = early(heads, ring, ways[:first], pieces, weights[:first], params)
+    results = mix(heads, ring, ways[first:], pieces, weights[first:], ends, prepared)
+    received = [results[0]] + [swap(results[mask], "seq", mask) for mask in range(1, count)]
+    mixed = jnp.zeros((tokens.shape[0], INNER), jnp.bfloat16)
+    for mask in range(count):
+        mixed = lax.dynamic_update_slice(mixed, received[mask], (0, (seq ^ mask) * columns))
+    return mixed[None]
+
+
 def solution(mesh):
     in_specs = (
         P(("fsdp", "batch"), "seq", None),
@@ -186,6 +632,16 @@
         P(),
     )
     out_specs = P(("fsdp", "batch"), "seq", None)
-    return jax.shard_map(
-        on_device, mesh=mesh, in_specs=in_specs, out_specs=out_specs, check_vma=False
-    )
+    by_heads = mesh.shape["seq"] == 4 and mesh.shape["fsdp"] == 2
+
+    def mixer(hidden, *rest):
+        whole = by_heads and hidden.shape[1] == mesh.shape["seq"] * BLOCK
+        return jax.shard_map(
+            on_heads if whole else on_sections,
+            mesh=mesh,
+            in_specs=in_specs,
+            out_specs=out_specs,
+            check_vma=False,
+        )(hidden, *rest)
+
+    return mixer

time: 269 us -> 57.5 us (0.21)
  waiting for transfers between devices: 143 us -> 24.4 us
  local copies, waits for them, and re-layouts: 49.4 us -> 9.92 us
  other arithmetic: 30.1 us -> 0 us
  between operations: 15 us -> 0.16 us
  matrix products: 13.2 us -> 0 us
  blocking collectives: 12.8 us -> 0 us
  starting transfers between devices: 2.86 us -> 13.1 us
  Pallas kernels: 0 us -> 9.53 us
    all_gather x3 -> x0, waiting for transfers between devices: 142 us -> none  [the longest x1 129 us: project(): lax.all_gather(in_weight, ('fsdp', 'batch'), axis=0, tiled=True)]
    slice x14 -> x2, local copies, waits for them, and re-layouts: 35.1 us -> 1.35 us  [on_heads(): ends = [turn(up[:cut], 1), turn(down[cut:], -1)]]
    ppermute x2 -> x14, waiting for transfers between devices: 0.01 us -> 24.4 us  [the longest x8 15.3 us: turn(): lax.ppermute(value, ('fsdp', 'batch'), [(order[i], order[(i + way) % coun...]
    dot_general x9 -> x0, matrix products: 13.2 us -> none  [the longest x1 6.09 us: project(): jnp.dot(rows_in, lax.all_gather(in_weight, ('fsdp', 'batch'), axis=0, til...]
    all_gather x2 -> x0, blocking collectives: 12.8 us -> none  [prefix(): pieces = jax.tree.map(lambda part: lax.all_gather(part, axis), value)]
    convert_element_type x11 -> x0, other arithmetic: 10.6 us -> none  [the longest x2 6.24 us: conv_silu(): return jax.nn.silu(total).astype(jnp.bfloat16)]
    ppermute x2 -> x14, starting transfers between devices: 2.56 us -> 13.1 us  [the longest x8 9.22 us: turn(): lax.ppermute(value, ('fsdp', 'batch'), [(order[i], order[(i + way) % coun...]
    pallas_call x0 -> x3, Pallas kernels: none -> 9.53 us  [the longest x1 7.1 us: mix(): pl.pallas_call(functools.partial(mixer_kernel, heads, ring, ways), out_sh...]
  transfers between devices with their start and end apart: 5 -> 14, of which waited for: 2 -> 6; matrix products, arithmetic and copies ran while one was open for 27% -> 3% of each run, Pallas kernels for 0% -> 4%
where the time goes in v4:
time: 57.5 us; the launch traced here: 57.1 us
  waiting for transfers between devices  24.4 us (42%)
  starting transfers between devices  13.1 us (23%)
  local copies, waits for them, and re-layouts  9.92 us (17%)
  Pallas kernels  9.53 us (17%)
    ppermute x8, waiting for transfers between devices, turn(): lax.ppermute(value, ('fsdp', 'batch'), [(order[i], order[(i + way) % coun...  15.3 us
    ppermute x8, starting transfers between devices, turn(): lax.ppermute(value, ('fsdp', 'batch'), [(order[i], order[(i + way) % coun...  9.22 us
    ppermute x6, waiting for transfers between devices, swap(): lax.ppermute(value, axis, [(i, i ^ mask) for i in range(lax.axis_size(axi...  9.11 us
    unnamed x32, local copies, waits for them, and re-layouts  7.81 us
    pallas_call x1, Pallas kernels, mix(): pl.pallas_call(functools.partial(mixer_kernel, heads, ring, ways), out_sh...  7.1 us
    ppermute x6, starting transfers between devices, swap(): lax.ppermute(value, axis, [(i, i ^ mask) for i in range(lax.axis_size(axi...  3.84 us
    pallas_call x1, Pallas kernels, early(): pl.pallas_call(functools.partial(early_kernel, heads, ring, ways), out_sh...  2.28 us
    slice x2, local copies, waits for them, and re-layouts, on_heads(): ends = [turn(up[:cut], 1), turn(down[cut:], -1)]  1.35 us
  transfers between devices with their start and end apart: 14, of which 6 were waited for; matrix products, arithmetic and copies ran while one was open for 3% of the time, Pallas kernels for 4%

profile of v4, /device:TPU:0, one launch (start us, length us, event | category | flops | bytes accessed | tf_op | source)
XLA Modules:
  0.0 57.1 jit_solution(1599004569258380862)
XLA Ops:
  0.0 1.3 %copy-done.1 = bf16[256,2208]{0,1:T(8,128)(2,1)S(1)} copy-done((bf16[256,2208]{0,1:T(8,128)(2,1)S(1)}, bf16[256,2208]{0,1:T(8,128)(2,1)}, u32[]{:S(2)}) %copy-start.1) | copy-done | bytes 1130520
  1.5 3.0 %collective-permute-start.6 = (bf16[672,256]{1,0:T(8,128)(2,1)S(1)}, bf16[672,256]{1,0:T(8,128)(2,1)S(1)}, u32[]{:S(2)}, u32[]{:S(2)}) collective-permute-start(bf16[672,256]{1,0:T(8,128)(2,1)S(1)} %shard_map.91.refs_4_), channel_id=1, source_target_pairs={{0,4},{1,0},{2,1},{3,2},{7,3},{6,7},{5,6},{4,5},{8,12},{9,8},{10,9... | collective-permute-start | bytes 1032200 | tf_op jit(solution)/shard_map/ppermute | solution.py:584
  4.6 1.9 %collective-permute-start.1 = (bf16[128,2048]{1,0:T(8,128)(2,1)}, bf16[128,2048]{1,0:T(8,128)(2,1)S(1)}, u32[]{:S(2)}, u32[]{:S(2)}) collective-permute-start(bf16[128,2048]{1,0:T(8,128)(2,1)} %bitcast.10), channel_id=1, source_target_pairs={{0,16},{8,24},{16,0},{24,8},{1,17},{9,25},{17,1},{25,9},{2,18},{10... | collective-permute-start | bytes 1572872 | tf_op jit(solution)/shard_map/ppermute | solution.py:588
  6.5 6.1 %collective-permute-done.6.refs_6_ = bf16[672,256]{1,0:T(8,128)(2,1)S(1)} collective-permute-done((bf16[672,256]{1,0:T(8,128)(2,1)S(1)}, bf16[672,256]{1,0:T(8,128)(2,1)S(1)}, u32[]{:S(2)}, u32[]{:S(2)}) %collective-permute-start.6) | collective-permute-done | bytes 344096 | tf_op jit(solution)/shard_map/ppermute | solution.py:584
  12.6 1.7 %collective-permute-start.7 = (bf16[672,256]{1,0:T(8,128)(2,1)S(1)}, bf16[672,256]{1,0:T(8,128)(2,1)S(1)}, u32[]{:S(2)}, u32[]{:S(2)}) collective-permute-start(bf16[672,256]{1,0:T(8,128)(2,1)S(1)} %collective-permute-done.6.refs_6_), channel_id=1, source_target_pairs={{0,4},{1,0},{2,1},{3,2},{7,3},{6,7},{5,6},{4,5},{8,12},{9,8},{10,9... | collective-permute-start | bytes 1032200 | tf_op jit(solution)/shard_map/ppermute | solution.py:584
  14.7 0.7 %copy-done.2 = bf16[672,256]{1,0:T(8,128)(2,1)} copy-done((bf16[672,256]{1,0:T(8,128)(2,1)}, bf16[672,256]{1,0:T(8,128)(2,1)S(1)}, u32[]{:S(2)}) %copy-start.2) | copy-done | bytes 344088
  15.4 2.8 %collective-permute-done.1.refs_2_ = bf16[128,2048]{1,0:T(8,128)(2,1)S(1)} collective-permute-done((bf16[128,2048]{1,0:T(8,128)(2,1)}, bf16[128,2048]{1,0:T(8,128)(2,1)S(1)}, u32[]{:S(2)}, u32[]{:S(2)}) %collective-permute-start.1) | collective-permute-done | bytes 524320 | tf_op jit(solution)/shard_map/ppermute | solution.py:588
  18.2 3.6 %collective-permute-done.7.refs_8_ = bf16[672,256]{1,0:T(8,128)(2,1)S(1)} collective-permute-done((bf16[672,256]{1,0:T(8,128)(2,1)S(1)}, bf16[672,256]{1,0:T(8,128)(2,1)S(1)}, u32[]{:S(2)}, u32[]{:S(2)}) %collective-permute-start.7) | collective-permute-done | bytes 344096 | tf_op jit(solution)/shard_map/ppermute | solution.py:584
  21.9 1.3 %collective-permute-start.8 = (bf16[672,256]{1,0:T(8,128)(2,1)S(1)}, bf16[672,256]{1,0:T(8,128)(2,1)S(1)}, u32[]{:S(2)}, u32[]{:S(2)}) collective-permute-start(bf16[672,256]{1,0:T(8,128)(2,1)S(1)} %collective-permute-done.7.refs_8_), channel_id=1, source_target_pairs={{0,4},{1,0},{2,1},{3,2},{7,3},{6,7},{5,6},{4,5},{8,12},{9,8},{10,9... | collective-permute-start | bytes 1032200 | tf_op jit(solution)/shard_map/ppermute | solution.py:584
  23.2 0.7 %copy-done.4 = bf16[672,256]{1,0:T(8,128)(2,1)} copy-done((bf16[672,256]{1,0:T(8,128)(2,1)}, bf16[672,256]{1,0:T(8,128)(2,1)S(1)}, u32[]{:S(2)}) %copy-start.4) | copy-done | bytes 344088
  24.6 5.6 %collective-permute-done.8.refs_5_ = bf16[672,256]{1,0:T(8,128)(2,1)S(1)} collective-permute-done((bf16[672,256]{1,0:T(8,128)(2,1)S(1)}, bf16[672,256]{1,0:T(8,128)(2,1)S(1)}, u32[]{:S(2)}, u32[]{:S(2)}) %collective-permute-start.8) | collective-permute-done | bytes 344096 | tf_op jit(solution)/shard_map/ppermute | solution.py:584
  30.9 1.0 %collective-permute-start.10 = (bf16[336,256]{1,0:T(8,128)(2,1)}, bf16[336,256]{1,0:T(8,128)(2,1)}, u32[]{:S(2)}, u32[]{:S(2)}) collective-permute-start(bf16[336,256]{1,0:T(8,128)(2,1)} %slice.9), channel_id=1, source_target_pairs={{0,4},{1,0},{2,1},{3,2},{7,3},{6,7},{5,6},{4,5},{8,12},{9,8},{10,9... | collective-permute-start | bytes 516104 | tf_op jit(solution)/shard_map/ppermute | solution.py:584
  32.6 1.0 %collective-permute-start.9 = (bf16[336,256]{1,0:T(8,128)(2,1)}, bf16[336,256]{1,0:T(8,128)(2,1)}, u32[]{:S(2)}, u32[]{:S(2)}) collective-permute-start(bf16[336,256]{1,0:T(8,128)(2,1)} %slice.8), channel_id=1, source_target_pairs={{0,1},{1,2},{2,3},{3,7},{7,6},{6,5},{5,4},{4,0},{8,9},{9,10},{10,1... | collective-permute-start | bytes 516104 | tf_op jit(solution)/shard_map/ppermute | solution.py:584
  33.7 1.0 %copy-done.3 = bf16[672,256]{1,0:T(8,128)(2,1)S(1)} copy-done((bf16[672,256]{1,0:T(8,128)(2,1)S(1)}, bf16[672,256]{1,0:T(8,128)(2,1)}, u32[]{:S(2)}) %copy-start.3) | copy-done | bytes 344088
  34.6 1.0 %copy-done.5 = bf16[672,256]{1,0:T(8,128)(2,1)S(1)} copy-done((bf16[672,256]{1,0:T(8,128)(2,1)S(1)}, bf16[672,256]{1,0:T(8,128)(2,1)}, u32[]{:S(2)}) %copy-start.5) | copy-done | bytes 344088
  35.6 1.0 %copy-done.7 = bf16[672,256]{1,0:T(8,128)(2,1)S(1)} copy-done((bf16[672,256]{1,0:T(8,128)(2,1)S(1)}, bf16[672,256]{1,0:T(8,128)(2,1)}, u32[]{:S(2)}) %copy-start.7) | copy-done | bytes 344088
  36.6 0.7 %copy-done.9 = f32[2,2176]{1,0:T(2,128)S(1)} copy-done((f32[2,2176]{1,0:T(2,128)S(1)}, f32[2,2176]{1,0:T(2,128)}, u32[]{:S(2)}) %copy-start.9) | copy-done | bytes 17432
  37.3 0.7 %copy-done.10 = f32[2,2048]{1,0:T(2,128)S(1)} copy-done((f32[2,2048]{1,0:T(2,128)S(1)}, f32[2,2048]{1,0:T(2,128)}, u32[]{:S(2)}) %copy-start.10) | copy-done | bytes 16408
  38.7 2.3 %shard_map.92 = (f32[512,768]{1,0:T(8,128)S(1)}, f32[2,4,640]{2,1,0:T(4,128)S(1)}, f32[2,640]{1,0:T(2,128)S(1)}, f32[2,8,128]{2,1,0:T(8,128)S(1)}, f32[2,8,512]{...) custom-call(bf16[128,2048]{1,0:T(8,128)(2,1)S(1)} %bitcast.12, ...), custom_call_target="tpu_custom_call" | custom-call | flops 1006632960 | bytes 8388608 | tf_op jit(solution)/shard_map/pallas_call | solution.py:532
  41.0 7.1 %shard_map.93 = (bf16[128,512]{1,0:T(8,128)(2,1)S(1)}, bf16[128,512]{1,0:T(8,128)(2,1)S(1)}, bf16[128,512]{1,0:T(8,128)(2,1)S(1)}, bf16[128,512]{1,0:T(8,128)(2,1)S(1)}) custom-call(bf16[128,2048]{1,0:T(8,128)(2,1)S(1)} %bitcast.13, bf16[128,2048]{1,0:T(8,128)(2,1)S(1)} %collective-permute-done.refs_1_, ...), custom_call_target="tpu_custom_call" | custom-call | tf_op jit(solution)/shard_map/pallas_call | solution.py:571
  48.2 1.1 %collective-permute-start.12 = (bf16[128,512]{1,0:T(8,128)(2,1)S(1)}, bf16[128,512]{1,0:T(8,128)(2,1)S(1)}, u32[]{:S(2)}, u32[]{:S(2)}) collective-permute-start(bf16[128,512]{1,0:T(8,128)(2,1)S(1)} %get-tuple-element.29), channel_id=1, source_target_pairs={{0,16},{8,24},{16,0},{24,8},{1,17},{9,25},{17,1},{25,9},{2,18},{10... | collective-permute-start | bytes 393224 | tf_op jit(solution)/shard_map/ppermute | solution.py:588
  49.3 0.7 %collective-permute-start.13 = (bf16[128,512]{1,0:T(8,128)(2,1)S(1)}, bf16[128,512]{1,0:T(8,128)(2,1)S(1)}, u32[]{:S(2)}, u32[]{:S(2)}) collective-permute-start(bf16[128,512]{1,0:T(8,128)(2,1)S(1)} %get-tuple-element.30), channel_id=1, source_target_pairs={{0,24},{8,16},{16,8},{24,0},{1,25},{9,17},{17,9},{25,1},{2,26},{10... | collective-permute-start | bytes 393224 | tf_op jit(solution)/shard_map/ppermute | solution.py:588
  50.1 4.4 %collective-permute-done.12 = bf16[128,512]{1,0:T(8,128)(2,1)S(1)} collective-permute-done((bf16[128,512]{1,0:T(8,128)(2,1)S(1)}, bf16[128,512]{1,0:T(8,128)(2,1)S(1)}, u32[]{:S(2)}, u32[]{:S(2)}) %collective-permute-start.12) | collective-permute-done | bytes 131104 | tf_op jit(solution)/shard_map/ppermute | solution.py:588
  54.6 1.9 %collective-permute-done.13 = bf16[128,512]{1,0:T(8,128)(2,1)S(1)} collective-permute-done((bf16[128,512]{1,0:T(8,128)(2,1)S(1)}, bf16[128,512]{1,0:T(8,128)(2,1)S(1)}, u32[]{:S(2)}, u32[]{:S(2)}) %collective-permute-start.13) | collective-permute-done | bytes 131104 | tf_op jit(solution)/shard_map/ppermute | solution.py:588
  (46 shorter events, 4.3 us)
Async XLA Ops:
  0.0 33.6 %copy-start = (bf16[1,128,2048]{2,1,0:T(8,128)(2,1)S(1)}, bf16[1,128,2048]{2,1,0:T(8,128)(2,1)}, u32[]{:S(2)}) copy-start(bf16[1,128,2048]{2,1,0:T(8,128)(2,1)} %param.9) | copy-start | bytes 1572868
  0.0 1.3 %copy-start.1 = (bf16[256,2208]{0,1:T(8,128)(2,1)S(1)}, bf16[256,2208]{0,1:T(8,128)(2,1)}, u32[]{:S(2)}) copy-start(bf16[256,2208]{0,1:T(8,128)(2,1)} %param.10) | copy-start | bytes 3391492
  1.3 32.3 %copy-start.8 = (f32[2,4,2176]{2,1,0:T(4,128)S(1)}, f32[2,4,2176]{2,1,0:T(4,128)}, u32[]{:S(2)}) copy-start(f32[2,4,2176]{2,1,0:T(4,128)} %refs_10_.1) | copy-start | bytes 208900
  1.3 32.3 %copy-start.11 = (f32[2,32]{1,0:T(2,128)S(1)}, f32[2,32]{1,0:T(2,128)}, u32[]{:S(2)}) copy-start(f32[2,32]{1,0:T(2,128)} %refs_12_.1) | copy-start | bytes 772
  1.3 32.3 %copy-start.12 = (f32[2,32]{1,0:T(2,128)S(1)}, f32[2,32]{1,0:T(2,128)}, u32[]{:S(2)}) copy-start(f32[2,32]{1,0:T(2,128)} %refs_13_.1) | copy-start | bytes 772
  1.3 32.3 %copy-start.13 = (f32[2,32]{1,0:T(2,128)S(1)}, f32[2,32]{1,0:T(2,128)}, u32[]{:S(2)}) copy-start(f32[2,32]{1,0:T(2,128)} %refs_14_.1) | copy-start | bytes 772
  1.5 11.1 %collective-permute-start.6 = (bf16[672,256]{1,0:T(8,128)(2,1)S(1)}, bf16[672,256]{1,0:T(8,128)(2,1)S(1)}, u32[]{:S(2)}, u32[]{:S(2)}) collective-permute-start(bf16[672,256]{1,0:T(8,128)(2,1)S(1)} %shard_map.91.refs_4_), channel_id=1, source_target_pairs={{0,4},{1,0},{2,1},{3,2},{7,3},{6,7},{5,6},{4,5},{8,12},{9,8},{10,9... | collective-permute-start | bytes 1032200 | tf_op jit(solution)/shard_map/ppermute | solution.py:584
  4.5 9.8 %collective-permute-start.3 = (bf16[672,256]{1,0:T(8,128)(2,1)S(1)}, bf16[672,256]{1,0:T(8,128)(2,1)S(1)}, u32[]{:S(2)}, u32[]{:S(2)}) collective-permute-start(bf16[672,256]{1,0:T(8,128)(2,1)S(1)} %shard_map.91.refs_4_), channel_id=1, source_target_pairs={{0,1},{1,2},{2,3},{3,7},{7,6},{6,5},{5,4},{4,0},{8,9},{9,10},{10,1... | collective-permute-start | bytes 1032200 | tf_op jit(solution)/shard_map/ppermute | solution.py:584
  4.6 13.6 %collective-permute-start.1 = (bf16[128,2048]{1,0:T(8,128)(2,1)}, bf16[128,2048]{1,0:T(8,128)(2,1)S(1)}, u32[]{:S(2)}, u32[]{:S(2)}) collective-permute-start(bf16[128,2048]{1,0:T(8,128)(2,1)} %bitcast.10), channel_id=1, source_target_pairs={{0,16},{8,24},{16,0},{24,8},{1,17},{9,25},{17,1},{25,9},{2,18},{10... | collective-permute-start | bytes 1572872 | tf_op jit(solution)/shard_map/ppermute | solution.py:588
  12.6 9.2 %collective-permute-start.7 = (bf16[672,256]{1,0:T(8,128)(2,1)S(1)}, bf16[672,256]{1,0:T(8,128)(2,1)S(1)}, u32[]{:S(2)}, u32[]{:S(2)}) collective-permute-start(bf16[672,256]{1,0:T(8,128)(2,1)S(1)} %collective-permute-done.6.refs_6_), channel_id=1, source_target_pairs={{0,4},{1,0},{2,1},{3,2},{7,3},{6,7},{5,6},{4,5},{8,12},{9,8},{10,9... | collective-permute-start | bytes 1032200 | tf_op jit(solution)/shard_map/ppermute | solution.py:584
  14.3 9.7 %collective-permute-start.4 = (bf16[672,256]{1,0:T(8,128)(2,1)S(1)}, bf16[672,256]{1,0:T(8,128)(2,1)S(1)}, u32[]{:S(2)}, u32[]{:S(2)}) collective-permute-start(bf16[672,256]{1,0:T(8,128)(2,1)S(1)} %collective-permute-done.3.refs_5_), channel_id=1, source_target_pairs={{0,1},{1,2},{2,3},{3,7},{7,6},{6,5},{5,4},{4,0},{8,9},{9,10},{10,1... | collective-permute-start | bytes 1032200 | tf_op jit(solution)/shard_map/ppermute | solution.py:584
  15.4 18.2 %collective-permute-start = (bf16[128,2048]{1,0:T(8,128)(2,1)}, bf16[128,2048]{1,0:T(8,128)(2,1)S(1)}, u32[]{:S(2)}, u32[]{:S(2)}) collective-permute-start(bf16[128,2048]{1,0:T(8,128)(2,1)} %bitcast.11), channel_id=1, source_target_pairs={{0,8},{8,0},{16,24},{24,16},{1,9},{9,1},{17,25},{25,17},{2,10},{10... | collective-permute-start | bytes 1572872 | tf_op jit(solution)/shard_map/ppermute | solution.py:588
  18.2 15.4 %collective-permute-start.2 = (bf16[128,2048]{1,0:T(8,128)(2,1)S(1)}, bf16[128,2048]{1,0:T(8,128)(2,1)S(1)}, u32[]{:S(2)}, u32[]{:S(2)}) collective-permute-start(bf16[128,2048]{1,0:T(8,128)(2,1)S(1)} %collective-permute-done.1.refs_2_), channel_id=1, source_target_pairs={{0,8},{8,0},{16,24},{24,16},{1,9},{9,1},{17,25},{25,17},{2,10},{10... | collective-permute-start | bytes 1572872 | tf_op jit(solution)/shard_map/ppermute | solution.py:588
  21.9 8.3 %collective-permute-start.8 = (bf16[672,256]{1,0:T(8,128)(2,1)S(1)}, bf16[672,256]{1,0:T(8,128)(2,1)S(1)}, u32[]{:S(2)}, u32[]{:S(2)}) collective-permute-start(bf16[672,256]{1,0:T(8,128)(2,1)S(1)} %collective-permute-done.7.refs_8_), channel_id=1, source_target_pairs={{0,4},{1,0},{2,1},{3,2},{7,3},{6,7},{5,6},{4,5},{8,12},{9,8},{10,9... | collective-permute-start | bytes 1032200 | tf_op jit(solution)/shard_map/ppermute | solution.py:584
  23.9 8.0 %copy-start.6 = (bf16[672,256]{1,0:T(8,128)(2,1)}, bf16[672,256]{1,0:T(8,128)(2,1)S(1)}, u32[]{:S(2)}) copy-start(bf16[672,256]{1,0:T(8,128)(2,1)S(1)} %collective-permute-done.4.refs_7_) | copy-start | bytes 1032196
  23.9 8.0 %collective-permute-start.5 = (bf16[672,256]{1,0:T(8,128)(2,1)S(1)}, bf16[672,256]{1,0:T(8,128)(2,1)S(1)}, u32[]{:S(2)}, u32[]{:S(2)}) collective-permute-start(bf16[672,256]{1,0:T(8,128)(2,1)S(1)} %collective-permute-done.4.refs_7_), channel_id=1, source_target_pairs={{0,1},{1,2},{2,3},{3,7},{7,6},{6,5},{5,4},{4,0},{8,9},{9,10},{10,1... | collective-permute-start | bytes 1032200 | tf_op jit(solution)/shard_map/ppermute | solution.py:584
  30.9 10.1 %collective-permute-start.10 = (bf16[336,256]{1,0:T(8,128)(2,1)}, bf16[336,256]{1,0:T(8,128)(2,1)}, u32[]{:S(2)}, u32[]{:S(2)}) collective-permute-start(bf16[336,256]{1,0:T(8,128)(2,1)} %slice.9), channel_id=1, source_target_pairs={{0,4},{1,0},{2,1},{3,2},{7,3},{6,7},{5,6},{4,5},{8,12},{9,8},{10,9... | collective-permute-start | bytes 516104 | tf_op jit(solution)/shard_map/ppermute | solution.py:584
  32.6 8.4 %collective-permute-start.9 = (bf16[336,256]{1,0:T(8,128)(2,1)}, bf16[336,256]{1,0:T(8,128)(2,1)}, u32[]{:S(2)}, u32[]{:S(2)}) collective-permute-start(bf16[336,256]{1,0:T(8,128)(2,1)} %slice.8), channel_id=1, source_target_pairs={{0,1},{1,2},{2,3},{3,7},{7,6},{6,5},{5,4},{4,0},{8,9},{9,10},{10,1... | collective-permute-start | bytes 516104 | tf_op jit(solution)/shard_map/ppermute | solution.py:584
  33.6 1.0 %copy-start.3 = (bf16[672,256]{1,0:T(8,128)(2,1)S(1)}, bf16[672,256]{1,0:T(8,128)(2,1)}, u32[]{:S(2)}) copy-start(bf16[672,256]{1,0:T(8,128)(2,1)} %copy-done.2) | copy-start | bytes 1032196
  34.6 1.0 %copy-start.5 = (bf16[672,256]{1,0:T(8,128)(2,1)S(1)}, bf16[672,256]{1,0:T(8,128)(2,1)}, u32[]{:S(2)}) copy-start(bf16[672,256]{1,0:T(8,128)(2,1)} %copy-done.4) | copy-start | bytes 1032196
  48.1 2.0 %collective-permute-start.11 = (bf16[128,512]{1,0:T(8,128)(2,1)S(1)}, bf16[128,512]{1,0:T(8,128)(2,1)S(1)}, u32[]{:S(2)}, u32[]{:S(2)}) collective-permute-start(bf16[128,512]{1,0:T(8,128)(2,1)S(1)} %get-tuple-element.28), channel_id=1, source_target_pairs={{0,8},{8,0},{16,24},{24,16},{1,9},{9,1},{17,25},{25,17},{2,10},{10... | collective-permute-start | bytes 393224 | tf_op jit(solution)/shard_map/ppermute | solution.py:588
  48.2 6.4 %collective-permute-start.12 = (bf16[128,512]{1,0:T(8,128)(2,1)S(1)}, bf16[128,512]{1,0:T(8,128)(2,1)S(1)}, u32[]{:S(2)}, u32[]{:S(2)}) collective-permute-start(bf16[128,512]{1,0:T(8,128)(2,1)S(1)} %get-tuple-element.29), channel_id=1, source_target_pairs={{0,16},{8,24},{16,0},{24,8},{1,17},{9,25},{17,1},{25,9},{2,18},{10... | collective-permute-start | bytes 393224 | tf_op jit(solution)/shard_map/ppermute | solution.py:588
  49.3 7.2 %collective-permute-start.13 = (bf16[128,512]{1,0:T(8,128)(2,1)S(1)}, bf16[128,512]{1,0:T(8,128)(2,1)S(1)}, u32[]{:S(2)}, u32[]{:S(2)}) collective-permute-start(bf16[128,512]{1,0:T(8,128)(2,1)S(1)} %get-tuple-element.30), channel_id=1, source_target_pairs={{0,24},{8,16},{16,8},{24,0},{1,25},{9,17},{17,9},{25,1},{2,26},{10... | collective-permute-start | bytes 393224 | tf_op jit(solution)/shard_map/ppermute | solution.py:588
  54.5 1.9 %copy-start.15 = (bf16[1,128,2048]{2,1,0:T(8,128)(2,1)}, bf16[1,128,2048]{2,1,0:T(8,128)(2,1)S(1)}, u32[]{:S(2)}) copy-start(bf16[1,128,2048]{2,1,0:T(8,128)(2,1)S(1)} %bitcast_dynamic-update-slice_fusion.1) | copy-start | bytes 1572868
  (6 other events, 4.5 us)

commit v5 on v4

--- a/solution.py
+++ b/solution.py
@@ -233,17 +233,25 @@
         copy.wait()
 
 
-def early_kernel(heads, ring, ways, *refs):
+def early_kernel(ring, ways, *refs):
     count = len(ways)
-    pieces, refs = refs[:4], refs[4:]
-    weights, refs = refs[:count], refs[count:]
+    pieces, weights, (partial, rows_in, w_in) = refs[:4], refs[4 : 4 + count], refs[4 + count :]
+    depth = weights[0].shape[1]
+    rows = weights[0].shape[0]
+    take_rows(pieces, ring, ways, rows_in)
+    w_in[rows:, :] = jnp.zeros((w_in.shape[0] - rows, w_in.shape[1]), jnp.bfloat16)
+    for n in range(count):
+        w_in[:rows, n * depth : (n + 1) * depth] = weights[n][...]
+    for n in range(w_in.shape[0] // SIDE):
+        at = slice(n * SIDE, (n + 1) * SIDE)
+        partial[:, at] = times_transposed(rows_in[...], w_in[at, :])
+
+
+def prepare_kernel(heads, *refs):
     marks_in, conv_w_in, conv_b_in, step_bias_in, decay_in, skip_in, gain_in = refs[:7]
-    partial, conv_w, conv_b, per_lane, skips, gains, spread, barred, flags, refs = (*refs[7:16], refs[16:])
-    per_head, marks, rows_in, w_in, sems = refs
+    conv_w, conv_b, per_lane, skips, gains, spread, barred, flags, per_head, marks, sems = refs[7:]
     seq = lax.axis_index("seq")
     columns = heads * HEAD_DIM
-    depth = weights[0].shape[1]
-    rows = weights[0].shape[0]
     own_lanes = pl.ds(pl.multiple_of(seq * columns, columns), columns)
     side_lanes = pl.ds(INNER, LANES)
     copies = [
@@ -260,13 +268,6 @@
     copies = [pltpu.make_async_copy(a, b, sems.at[i]) for i, (a, b) in enumerate(copies)]
     for copy in copies:
         copy.start()
-    take_rows(pieces, ring, ways, rows_in)
-    w_in[rows:, :] = jnp.zeros((w_in.shape[0] - rows, w_in.shape[1]), jnp.bfloat16)
-    for n in range(count):
-        w_in[:rows, n * depth : (n + 1) * depth] = weights[n][...]
-    for n in range(w_in.shape[0] // SIDE):
-        at = slice(n * SIDE, (n + 1) * SIDE)
-        partial[:, at] = times_transposed(rows_in[...], w_in[at, :])
     for copy in copies:
         copy.wait()
 
@@ -507,19 +508,28 @@
         in_specs=[IN_HBM],
         out_specs=IN_VMEM,
         scratch_shapes=[pltpu.SemaphoreType.DMA((2,))],
+        compiler_params=pltpu.CompilerParams(vmem_limit_bytes=63 * 1024 * 1024),
+    )(weight)
+
+
+def early(columns, ring, ways, pieces, weights):
+    length = pieces[0].shape[0] * len(pieces)
+    wide = columns + SIDE
+    known = weights[0].shape[1] * len(ways)
+    return pl.pallas_call(
+        functools.partial(early_kernel, ring, ways),
+        out_shape=jax.ShapeDtypeStruct((length, wide), jnp.float32),
+        in_specs=[IN_VMEM] * (len(pieces) + len(weights)),
+        out_specs=IN_VMEM,
+        scratch_shapes=[pltpu.VMEM((length, known), jnp.bfloat16), pltpu.VMEM((wide, known), jnp.bfloat16)],
+        cost_estimate=pl.CostEstimate(flops=2 * length * wide * known, bytes_accessed=8 * 1024 * 1024, transcendentals=0),
         compiler_params=pltpu.CompilerParams(vmem_limit_bytes=ROOM),
-    )(weight)
-
-
-def early(heads, ring, ways, pieces, weights, params):
-    length = pieces[0].shape[0] * len(pieces)
+    )(*pieces, *weights)
+
+
+def prepare(heads, blocks, params):
     columns = heads * HEAD_DIM
-    depth = weights[0].shape[1]
-    blocks = length // BLOCK
-    wide = columns + SIDE
-    known = depth * len(ways)
     shapes = [
-        ((length, wide), jnp.float32),
         ((2, KERNEL, columns + LANES), jnp.float32),
         ((2, columns + LANES), jnp.float32),
         ((2, 8, LANES), jnp.float32),
@@ -530,20 +540,18 @@
         ((3, BLOCK, LANES), jnp.float32),
     ]
     return pl.pallas_call(
-        functools.partial(early_kernel, heads, ring, ways),
+        functools.partial(prepare_kernel, heads),
         out_shape=[jax.ShapeDtypeStruct(*one) for one in shapes],
-        in_specs=[IN_VMEM] * (len(pieces) + len(weights)) + [IN_HBM] * len(params),
+        in_specs=[IN_HBM] * len(params),
         out_specs=[IN_VMEM] * len(shapes),
         scratch_shapes=[
             pltpu.VMEM((3, 2, HEADS), jnp.float32),
             pltpu.VMEM(params[0].shape, jnp.int32),
-            pltpu.VMEM((length, known), jnp.bfloat16),
-            pltpu.VMEM((wide, known), jnp.bfloat16),
             pltpu.SemaphoreType.DMA((9,)),
         ],
-        cost_estimate=pl.CostEstimate(flops=2 * length * wide * known, bytes_accessed=8 * 1024 * 1024, transcendentals=0),
+        cost_estimate=pl.CostEstimate(flops=10**9, bytes_accessed=4 * 1024 * 1024, transcendentals=0),
         compiler_params=pltpu.CompilerParams(vmem_limit_bytes=ROOM),
-    )(*pieces, *weights, *params)
+    )(*params)
 
 
 def mix(heads, ring, ways, pieces, weights, ends, prepared):
@@ -600,17 +608,22 @@
     across = swap(tokens, "seq", 2)
     pieces = [tokens, swap(tokens, "seq", 1), across, swap(across, "seq", 1)]
     weights, ways = [own], [0]
+    params = (read_starts, conv_weight, conv_bias, dt_bias, decay, skip, norm_gain)
+    prepared = prepare(heads, count * tokens.shape[0] // BLOCK, params)
     up = down = own
     for away in range(1, ring):
         up, down = turn(up, 1), turn(down, -1)
+        if away == ring - 2:
+            up, down, prepared = lax.optimization_barrier((up, down, prepared))
         weights += [up, down]
         ways += [-away, away]
+    first = 2 * ring - 3
+    partial = early(columns, ring, ways[:first], pieces, weights[:first])
+    up, down, partial = lax.optimization_barrier((up, down, partial))
     cut = own.shape[0] // 32 * 16
     ends = [turn(up[:cut], 1), turn(down[cut:], -1)]
     ways.append(ring)
-    params = (read_starts, conv_weight, conv_bias, dt_bias, decay, skip, norm_gain)
-    first = 2 * ring - 3
-    prepared = early(heads, ring, ways[:first], pieces, weights[:first], params)
+    prepared = (partial, *prepared)
     results = mix(heads, ring, ways[first:], pieces, weights[first:], ends, prepared)
     received = [results[0]] + [swap(results[mask], "seq", mask) for mask in range(1, count)]
     mixed = jnp.zeros((tokens.shape[0], INNER), jnp.bfloat16)

time: 57.5 us -> 67.5 us (1.17)
  local copies, waits for them, and re-layouts: 9.92 us -> 17.7 us
  waiting for transfers between devices: 24.4 us -> 25.3 us
    unnamed x32 -> x52, local copies, waits for them, and re-layouts: 7.81 us -> 15.6 us
    ppermute x8, waiting for transfers between devices: 15.3 us -> 19.1 us  [turn(): lax.ppermute(value, ('fsdp', 'batch'), [(order[i], order[(i + way) % coun...]
    ppermute x6, waiting for transfers between devices: 9.11 us -> 6.27 us  [swap(): lax.ppermute(value, axis, [(i, i ^ mask) for i in range(lax.axis_size(axi...]
    pallas_call x1, Pallas kernels: 0.16 us -> 1.73 us  [pack(): pl.pallas_call(functools.partial(pack_kernel, columns), out_shape=jax.Sha...]
    ppermute x6, starting transfers between devices: 3.84 us -> 5.41 us  [swap(): lax.ppermute(value, axis, [(i, i ^ mask) for i in range(lax.axis_size(axi...]
    ppermute x8, starting transfers between devices: 9.22 us -> 8.16 us  [turn(): lax.ppermute(value, ('fsdp', 'batch'), [(order[i], order[(i + way) % coun...]
    pallas_call x1, Pallas kernels: 7.1 us -> 6.12 us  [mix(): pl.pallas_call(functools.partial(mixer_kernel, heads, ring, ways), out_sh...]
    pallas_call x1 -> x2, Pallas kernels: 2.28 us -> 2.17 us  [the longest x1 1.22 us: early(): pl.pallas_call(functools.partial(early_kernel, ring, ways), out_shape=jax...]
  transfers between devices with their start and end apart: 14 -> 14, of which waited for: 6 -> 8; matrix products, arithmetic and copies ran while one was open for 3% -> 1% of each run, Pallas kernels for 4% -> 6%
where the time goes in v5:
time: 67.5 us; the launch traced here: 66.9 us
  waiting for transfers between devices  25.3 us (37%)
  local copies, waits for them, and re-layouts  17.7 us (26%)
  starting transfers between devices  13.6 us (20%)
  Pallas kernels  10 us (15%)
    ppermute x8, waiting for transfers between devices, turn(): lax.ppermute(value, ('fsdp', 'batch'), [(order[i], order[(i + way) % coun...  19.1 us
    unnamed x52, local copies, waits for them, and re-layouts  15.6 us
    ppermute x8, starting transfers between devices, turn(): lax.ppermute(value, ('fsdp', 'batch'), [(order[i], order[(i + way) % coun...  8.16 us
    ppermute x6, waiting for transfers between devices, swap(): lax.ppermute(value, axis, [(i, i ^ mask) for i in range(lax.axis_size(axi...  6.27 us
    pallas_call x1, Pallas kernels, mix(): pl.pallas_call(functools.partial(mixer_kernel, heads, ring, ways), out_sh...  6.12 us
    ppermute x6, starting transfers between devices, swap(): lax.ppermute(value, axis, [(i, i ^ mask) for i in range(lax.axis_size(axi...  5.41 us
    pallas_call x1, Pallas kernels, pack(): pl.pallas_call(functools.partial(pack_kernel, columns), out_shape=jax.Sha...  1.73 us
    slice x2, local copies, waits for them, and re-layouts, on_heads(): ends = [turn(up[:cut], 1), turn(down[cut:], -1)]  1.37 us
  transfers between devices with their start and end apart: 14, of which 8 were waited for; matrix products, arithmetic and copies ran while one was open for 1% of the time, Pallas kernels for 6%

profile of v5, /device:TPU:0, one launch (start us, length us, event | category | flops | bytes accessed | tf_op | source)
XLA Modules:
  0.0 66.9 jit_solution(13419887223027290798)
XLA Ops:
  0.0 3.0 %collective-permute-start.1 = (bf16[128,2048]{1,0:T(8,128)(2,1)}, bf16[128,2048]{1,0:T(8,128)(2,1)S(1)}, u32[]{:S(2)}, u32[]{:S(2)}) collective-permute-start(bf16[128,2048]{1,0:T(8,128)(2,1)} %bitcast.10), channel_id=1, source_target_pairs={{0,16},{8,24},{16,0},{24,8},{1,17},{9,25},{17,1},{25,9},{2,18},{10... | collective-permute-start | bytes 1572872 | tf_op jit(solution)/shard_map/ppermute | solution.py:596
  3.0 1.7 %shard_map.91.refs_4_ = bf16[672,256]{1,0:T(8,128)(2,1)} custom-call(bf16[2208,256]{1,0:T(8,128)(2,1)} %bitcast.14), custom_call_target="tpu_custom_call" | custom-call | tf_op jit(solution)/shard_map/pallas_call | solution.py:505
  4.7 1.6 %collective-permute-start.3 = (bf16[672,256]{1,0:T(8,128)(2,1)}, bf16[672,256]{1,0:T(8,128)(2,1)S(1)}, u32[]{:S(2)}, u32[]{:S(2)}) collective-permute-start(bf16[672,256]{1,0:T(8,128)(2,1)} %shard_map.91.refs_4_), channel_id=1, source_target_pairs={{0,1},{1,2},{2,3},{3,7},{7,6},{6,5},{5,4},{4,0},{8,9},{9,10},{10,1... | collective-permute-start | bytes 1032200 | tf_op jit(solution)/shard_map/ppermute | solution.py:592
  6.8 7.7 %collective-permute-done.3.refs_5_ = bf16[672,256]{1,0:T(8,128)(2,1)S(1)} collective-permute-done((bf16[672,256]{1,0:T(8,128)(2,1)}, bf16[672,256]{1,0:T(8,128)(2,1)S(1)}, u32[]{:S(2)}, u32[]{:S(2)}) %collective-permute-start.3) | collective-permute-done | bytes 344096 | tf_op jit(solution)/shard_map/ppermute | solution.py:592
  14.5 1.6 %collective-permute-start.4 = (bf16[672,256]{1,0:T(8,128)(2,1)S(1)}, bf16[672,256]{1,0:T(8,128)(2,1)S(1)}, u32[]{:S(2)}, u32[]{:S(2)}) collective-permute-start(bf16[672,256]{1,0:T(8,128)(2,1)S(1)} %collective-permute-done.3.refs_5_), channel_id=1, source_target_pairs={{0,1},{1,2},{2,3},{3,7},{7,6},{6,5},{5,4},{4,0},{8,9},{9,10},{10,1... | collective-permute-start | bytes 1032200 | tf_op jit(solution)/shard_map/ppermute | solution.py:592
  22.1 0.9 %shard_map.92 = (f32[2,4,640]{2,1,0:T(4,128)S(1)}, f32[2,640]{1,0:T(2,128)S(1)}, f32[2,8,128]{2,1,0:T(8,128)S(1)}, f32[2,8,512]{2,1,0:T(8,128)S(1)}, f32[2,512]{...) custom-call(s32[1,4]{1,0:T(1,128)S(1)} %copy-done.24, ...), custom_call_target="tpu_custom_call" | custom-call | flops 1000000000 | bytes 4194304 | tf_op jit(solution)/shard_map/pallas_call | solution.py:542
  24.4 1.6 %collective-permute-start.7 = (bf16[672,256]{1,0:T(8,128)(2,1)S(1)}, bf16[672,256]{1,0:T(8,128)(2,1)S(1)}, u32[]{:S(2)}, u32[]{:S(2)}) collective-permute-start(bf16[672,256]{1,0:T(8,128)(2,1)S(1)} %collective-permute-done.4.refs_7_), channel_id=1, source_target_pairs={{0,1},{1,2},{2,3},{3,7},{7,6},{6,5},{5,4},{4,0},{8,9},{9,10},{10,1... | collective-permute-start | bytes 1032200 | tf_op jit(solution)/shard_map/ppermute | solution.py:592
  26.5 1.2 %shard_map.93.refs_8_ = f32[512,768]{1,0:T(8,128)S(1)} custom-call(bf16[128,2048]{1,0:T(8,128)(2,1)S(1)} %bitcast.12, bf16[128,2048]{1,0:T(8,128)(2,1)S(1)} %collective-permute-done.refs_1_, bf16[128,2048]{1,0:T(8,128)(2,1)S(1)} %collective-permute-done.1.refs_2_, bf16[128,2048]{1,0:T(8,128)(2,1)S(1)} %collective-permute-done.2.refs_3_, ...), custom_call_target="tpu_custom_call" | custom-call | flops 1006632960 | bytes 8388608 | tf_op jit(solution)/shard_map/pallas_call | solution.py:519
  27.8 6.0 %collective-permute-done.7.refs_4_ = bf16[672,256]{1,0:T(8,128)(2,1)S(1)} collective-permute-done((bf16[672,256]{1,0:T(8,128)(2,1)S(1)}, bf16[672,256]{1,0:T(8,128)(2,1)S(1)}, u32[]{:S(2)}, u32[]{:S(2)}) %collective-permute-start.7) | collective-permute-done | bytes 344096 | tf_op jit(solution)/shard_map/ppermute | solution.py:592
  33.7 1.3 %collective-permute-done.8.refs_5_ = bf16[672,256]{1,0:T(8,128)(2,1)S(1)} collective-permute-done((bf16[672,256]{1,0:T(8,128)(2,1)S(1)}, bf16[672,256]{1,0:T(8,128)(2,1)S(1)}, u32[]{:S(2)}, u32[]{:S(2)}) %collective-permute-start.8) | collective-permute-done | bytes 344096 | tf_op jit(solution)/shard_map/ppermute | solution.py:592
  37.6 1.6 %collective-permute-start.9 = (bf16[336,256]{1,0:T(8,128)(2,1)}, bf16[336,256]{1,0:T(8,128)(2,1)S(1)}, u32[]{:S(2)}, u32[]{:S(2)}) collective-permute-start(bf16[336,256]{1,0:T(8,128)(2,1)} %slice.6), channel_id=1, source_target_pairs={{0,1},{1,2},{2,3},{3,7},{7,6},{6,5},{5,4},{4,0},{8,9},{9,10},{10,1... | collective-permute-start | bytes 516104 | tf_op jit(solution)/shard_map/ppermute | solution.py:592
  39.2 2.9 %collective-permute-done.10.refs_7_ = bf16[336,256]{1,0:T(8,128)(2,1)S(1)} collective-permute-done((bf16[336,256]{1,0:T(8,128)(2,1)}, bf16[336,256]{1,0:T(8,128)(2,1)S(1)}, u32[]{:S(2)}, u32[]{:S(2)}) %collective-permute-start.10) | collective-permute-done | bytes 172064 | tf_op jit(solution)/shard_map/ppermute | solution.py:592
  43.9 1.0 %copy-done.2 = bf16[128,2048]{1,0:T(8,128)(2,1)S(1)} copy-done((bf16[128,2048]{1,0:T(8,128)(2,1)S(1)}, bf16[128,2048]{1,0:T(8,128)(2,1)}, u32[]{:S(2)}) %copy-start.2) | copy-done | bytes 524312
  44.9 1.0 %copy-done.4 = bf16[128,2048]{1,0:T(8,128)(2,1)S(1)} copy-done((bf16[128,2048]{1,0:T(8,128)(2,1)S(1)}, bf16[128,2048]{1,0:T(8,128)(2,1)}, u32[]{:S(2)}) %copy-start.4) | copy-done | bytes 524312
  46.0 1.0 %copy-done.7 = bf16[672,256]{1,0:T(8,128)(2,1)S(1)} copy-done((bf16[672,256]{1,0:T(8,128)(2,1)S(1)}, bf16[672,256]{1,0:T(8,128)(2,1)}, u32[]{:S(2)}) %copy-start.7) | copy-done | bytes 344088
  47.0 1.0 %copy-done.9 = f32[2,4,128,128]{3,2,1,0:T(8,128)S(1)} copy-done((f32[2,4,128,128]{3,2,1,0:T(8,128)S(1)}, f32[2,4,128,128]{3,2,1,0:T(8,128)}, u32[]{:S(2)}) %copy-start.9) | copy-done | bytes 524312
  48.0 0.9 %copy-done.11 = bf16[2,128,512]{2,1,0:T(8,128)(2,1)S(1)} copy-done((bf16[2,128,512]{2,1,0:T(8,128)(2,1)S(1)}, bf16[2,128,512]{2,1,0:T(8,128)(2,1)}, u32[]{:S(2)}) %copy-start.11) | copy-done | bytes 262168
  49.0 0.9 %copy-done.13 = f32[3,128,128]{2,1,0:T(8,128)S(1)} copy-done((f32[3,128,128]{2,1,0:T(8,128)S(1)}, f32[3,128,128]{2,1,0:T(8,128)}, u32[]{:S(2)}) %copy-start.13) | copy-done | bytes 196632
  49.9 0.9 %copy-done.15 = bf16[336,256]{1,0:T(8,128)(2,1)S(1)} copy-done((bf16[336,256]{1,0:T(8,128)(2,1)S(1)}, bf16[336,256]{1,0:T(8,128)(2,1)}, u32[]{:S(2)}) %copy-start.15) | copy-done | bytes 172056
  50.8 0.9 %copy-done.17 = bf16[336,256]{1,0:T(8,128)(2,1)S(1)} copy-done((bf16[336,256]{1,0:T(8,128)(2,1)S(1)}, bf16[336,256]{1,0:T(8,128)(2,1)}, u32[]{:S(2)}) %copy-start.17) | copy-done | bytes 172056
  51.7 6.1 %shard_map.94 = (bf16[128,512]{1,0:T(8,128)(2,1)S(1)}, bf16[128,512]{1,0:T(8,128)(2,1)S(1)}, bf16[128,512]{1,0:T(8,128)(2,1)S(1)}, bf16[128,512]{1,0:T(8,128)(2,1)S(1)}) custom-call(bf16[128,2048]{1,0:T(8,128)(2,1)S(1)} %bitcast.13, bf16[128,2048]{1,0:T(8,128)(2,1)S(1)} %copy-done.2, bf16[128,2048]{1,0:T(8,128)(2,1)S(1)} %collective-permute-done.1.refs_2_, ...), custom_call_target="tpu_custom_call" | custom-call | tf_op jit(solution)/shard_map/pallas_call | solution.py:579
  58.3 1.5 %collective-permute-start.13 = (bf16[128,512]{1,0:T(8,128)(2,1)S(1)}, bf16[128,512]{1,0:T(8,128)(2,1)S(1)}, u32[]{:S(2)}, u32[]{:S(2)}) collective-permute-start(bf16[128,512]{1,0:T(8,128)(2,1)S(1)} %get-tuple-element.54), channel_id=1, source_target_pairs={{0,24},{8,16},{16,8},{24,0},{1,25},{9,17},{17,9},{25,1},{2,26},{10... | collective-permute-start | bytes 393224 | tf_op jit(solution)/shard_map/ppermute | solution.py:596
  59.9 4.4 %collective-permute-done.12 = bf16[128,512]{1,0:T(8,128)(2,1)S(1)} collective-permute-done((bf16[128,512]{1,0:T(8,128)(2,1)S(1)}, bf16[128,512]{1,0:T(8,128)(2,1)S(1)}, u32[]{:S(2)}, u32[]{:S(2)}) %collective-permute-start.12) | collective-permute-done | bytes 131104 | tf_op jit(solution)/shard_map/ppermute | solution.py:596
  64.3 1.9 %collective-permute-done.13 = bf16[128,512]{1,0:T(8,128)(2,1)S(1)} collective-permute-done((bf16[128,512]{1,0:T(8,128)(2,1)S(1)}, bf16[128,512]{1,0:T(8,128)(2,1)S(1)}, u32[]{:S(2)}, u32[]{:S(2)}) %collective-permute-start.13) | collective-permute-done | bytes 131104 | tf_op jit(solution)/shard_map/ppermute | solution.py:596
  (67 shorter events, 13.9 us)
Async XLA Ops:
  0.0 16.5 %collective-permute-start.1 = (bf16[128,2048]{1,0:T(8,128)(2,1)}, bf16[128,2048]{1,0:T(8,128)(2,1)S(1)}, u32[]{:S(2)}, u32[]{:S(2)}) collective-permute-start(bf16[128,2048]{1,0:T(8,128)(2,1)} %bitcast.10), channel_id=1, source_target_pairs={{0,16},{8,24},{16,0},{24,8},{1,17},{9,25},{17,1},{25,9},{2,18},{10... | collective-permute-start | bytes 1572872 | tf_op jit(solution)/shard_map/ppermute | solution.py:596
  4.7 21.8 %copy-start = (bf16[1,128,2048]{2,1,0:T(8,128)(2,1)S(1)}, bf16[1,128,2048]{2,1,0:T(8,128)(2,1)}, u32[]{:S(2)}) copy-start(bf16[1,128,2048]{2,1,0:T(8,128)(2,1)} %param.9) | copy-start | bytes 1572868
  4.7 21.8 %copy-start.5 = (bf16[672,256]{1,0:T(8,128)(2,1)S(1)}, bf16[672,256]{1,0:T(8,128)(2,1)}, u32[]{:S(2)}) copy-start(bf16[672,256]{1,0:T(8,128)(2,1)} %shard_map.91.refs_4_) | copy-start | bytes 1032196
  4.7 9.8 %collective-permute-start.3 = (bf16[672,256]{1,0:T(8,128)(2,1)}, bf16[672,256]{1,0:T(8,128)(2,1)S(1)}, u32[]{:S(2)}, u32[]{:S(2)}) collective-permute-start(bf16[672,256]{1,0:T(8,128)(2,1)} %shard_map.91.refs_4_), channel_id=1, source_target_pairs={{0,1},{1,2},{2,3},{3,7},{7,6},{6,5},{5,4},{4,0},{8,9},{9,10},{10,1... | collective-permute-start | bytes 1032200 | tf_op jit(solution)/shard_map/ppermute | solution.py:592
  6.4 9.7 %collective-permute-start.5 = (bf16[672,256]{1,0:T(8,128)(2,1)}, bf16[672,256]{1,0:T(8,128)(2,1)S(1)}, u32[]{:S(2)}, u32[]{:S(2)}) collective-permute-start(bf16[672,256]{1,0:T(8,128)(2,1)} %shard_map.91.refs_4_), channel_id=1, source_target_pairs={{0,4},{1,0},{2,1},{3,2},{7,3},{6,7},{5,6},{4,5},{8,12},{9,8},{10,9... | collective-permute-start | bytes 1032200 | tf_op jit(solution)/shard_map/ppermute | solution.py:592
  14.5 9.2 %collective-permute-start.4 = (bf16[672,256]{1,0:T(8,128)(2,1)S(1)}, bf16[672,256]{1,0:T(8,128)(2,1)S(1)}, u32[]{:S(2)}, u32[]{:S(2)}) collective-permute-start(bf16[672,256]{1,0:T(8,128)(2,1)S(1)} %collective-permute-done.3.refs_5_), channel_id=1, source_target_pairs={{0,1},{1,2},{2,3},{3,7},{7,6},{6,5},{5,4},{4,0},{8,9},{9,10},{10,1... | collective-permute-start | bytes 1032200 | tf_op jit(solution)/shard_map/ppermute | solution.py:592
  16.1 8.3 %collective-permute-start.6 = (bf16[672,256]{1,0:T(8,128)(2,1)S(1)}, bf16[672,256]{1,0:T(8,128)(2,1)S(1)}, u32[]{:S(2)}, u32[]{:S(2)}) collective-permute-start(bf16[672,256]{1,0:T(8,128)(2,1)S(1)} %collective-permute-done.5.refs_6_), channel_id=1, source_target_pairs={{0,4},{1,0},{2,1},{3,2},{7,3},{6,7},{5,6},{4,5},{8,12},{9,8},{10,9... | collective-permute-start | bytes 1032200 | tf_op jit(solution)/shard_map/ppermute | solution.py:592
  16.5 9.9 %collective-permute-start = (bf16[128,2048]{1,0:T(8,128)(2,1)}, bf16[128,2048]{1,0:T(8,128)(2,1)S(1)}, u32[]{:S(2)}, u32[]{:S(2)}) collective-permute-start(bf16[128,2048]{1,0:T(8,128)(2,1)} %bitcast.11), channel_id=1, source_target_pairs={{0,8},{8,0},{16,24},{24,16},{1,9},{9,1},{17,25},{25,17},{2,10},{10... | collective-permute-start | bytes 1572872 | tf_op jit(solution)/shard_map/ppermute | solution.py:596
  16.5 9.9 %collective-permute-start.2 = (bf16[128,2048]{1,0:T(8,128)(2,1)S(1)}, bf16[128,2048]{1,0:T(8,128)(2,1)S(1)}, u32[]{:S(2)}, u32[]{:S(2)}) collective-permute-start(bf16[128,2048]{1,0:T(8,128)(2,1)S(1)} %collective-permute-done.1.refs_2_), channel_id=1, source_target_pairs={{0,8},{8,0},{16,24},{24,16},{1,9},{9,1},{17,25},{25,17},{2,10},{10... | collective-permute-start | bytes 1572872 | tf_op jit(solution)/shard_map/ppermute | solution.py:596
  23.7 4.0 %copy-start.8 = (f32[2,4,128,128]{3,2,1,0:T(8,128)}, f32[2,4,128,128]{3,2,1,0:T(8,128)S(1)}, u32[]{:S(2)}) copy-start(f32[2,4,128,128]{3,2,1,0:T(8,128)S(1)} %get-tuple-element.49.refs_15_) | copy-start | bytes 1572868
  23.7 4.0 %copy-start.10 = (bf16[2,128,512]{2,1,0:T(8,128)(2,1)}, bf16[2,128,512]{2,1,0:T(8,128)(2,1)S(1)}, u32[]{:S(2)}) copy-start(bf16[2,128,512]{2,1,0:T(8,128)(2,1)S(1)} %get-tuple-element.48.refs_14_) | copy-start | bytes 786436
  24.4 9.3 %collective-permute-start.7 = (bf16[672,256]{1,0:T(8,128)(2,1)S(1)}, bf16[672,256]{1,0:T(8,128)(2,1)S(1)}, u32[]{:S(2)}, u32[]{:S(2)}) collective-permute-start(bf16[672,256]{1,0:T(8,128)(2,1)S(1)} %collective-permute-done.4.refs_7_), channel_id=1, source_target_pairs={{0,1},{1,2},{2,3},{3,7},{7,6},{6,5},{5,4},{4,0},{8,9},{9,10},{10,1... | collective-permute-start | bytes 1032200 | tf_op jit(solution)/shard_map/ppermute | solution.py:592
  26.0 9.0 %collective-permute-start.8 = (bf16[672,256]{1,0:T(8,128)(2,1)S(1)}, bf16[672,256]{1,0:T(8,128)(2,1)S(1)}, u32[]{:S(2)}, u32[]{:S(2)}) collective-permute-start(bf16[672,256]{1,0:T(8,128)(2,1)S(1)} %collective-permute-done.6.refs_8_), channel_id=1, source_target_pairs={{0,4},{1,0},{2,1},{3,2},{7,3},{6,7},{5,6},{4,5},{8,12},{9,8},{10,9... | collective-permute-start | bytes 1032200 | tf_op jit(solution)/shard_map/ppermute | solution.py:592
  26.5 1.3 %copy-start.1 = (bf16[128,2048]{1,0:T(8,128)(2,1)}, bf16[128,2048]{1,0:T(8,128)(2,1)S(1)}, u32[]{:S(2)}) copy-start(bf16[128,2048]{1,0:T(8,128)(2,1)S(1)} %collective-permute-done.refs_1_) | copy-start | bytes 1572868
  26.5 1.3 %copy-start.3 = (bf16[128,2048]{1,0:T(8,128)(2,1)}, bf16[128,2048]{1,0:T(8,128)(2,1)S(1)}, u32[]{:S(2)}) copy-start(bf16[128,2048]{1,0:T(8,128)(2,1)S(1)} %collective-permute-done.2.refs_3_) | copy-start | bytes 1572868
  36.5 5.6 %collective-permute-start.10 = (bf16[336,256]{1,0:T(8,128)(2,1)}, bf16[336,256]{1,0:T(8,128)(2,1)S(1)}, u32[]{:S(2)}, u32[]{:S(2)}) collective-permute-start(bf16[336,256]{1,0:T(8,128)(2,1)} %slice.7), channel_id=1, source_target_pairs={{0,4},{1,0},{2,1},{3,2},{7,3},{6,7},{5,6},{4,5},{8,12},{9,8},{10,9... | collective-permute-start | bytes 516104 | tf_op jit(solution)/shard_map/ppermute | solution.py:592
  37.6 5.6 %collective-permute-start.9 = (bf16[336,256]{1,0:T(8,128)(2,1)}, bf16[336,256]{1,0:T(8,128)(2,1)S(1)}, u32[]{:S(2)}, u32[]{:S(2)}) collective-permute-start(bf16[336,256]{1,0:T(8,128)(2,1)} %slice.6), channel_id=1, source_target_pairs={{0,1},{1,2},{2,3},{3,7},{7,6},{6,5},{5,4},{4,0},{8,9},{9,10},{10,1... | collective-permute-start | bytes 516104 | tf_op jit(solution)/shard_map/ppermute | solution.py:592
  43.9 1.0 %copy-start.2 = (bf16[128,2048]{1,0:T(8,128)(2,1)S(1)}, bf16[128,2048]{1,0:T(8,128)(2,1)}, u32[]{:S(2)}) copy-start(bf16[128,2048]{1,0:T(8,128)(2,1)} %copy-done.1) | copy-start | bytes 1572868
  44.9 1.0 %copy-start.4 = (bf16[128,2048]{1,0:T(8,128)(2,1)S(1)}, bf16[128,2048]{1,0:T(8,128)(2,1)}, u32[]{:S(2)}) copy-start(bf16[128,2048]{1,0:T(8,128)(2,1)} %copy-done.3) | copy-start | bytes 1572868
  47.0 1.0 %copy-start.9 = (f32[2,4,128,128]{3,2,1,0:T(8,128)S(1)}, f32[2,4,128,128]{3,2,1,0:T(8,128)}, u32[]{:S(2)}) copy-start(f32[2,4,128,128]{3,2,1,0:T(8,128)} %copy-done.8) | copy-start | bytes 1572868
  57.8 2.0 %collective-permute-start.11 = (bf16[128,512]{1,0:T(8,128)(2,1)S(1)}, bf16[128,512]{1,0:T(8,128)(2,1)S(1)}, u32[]{:S(2)}, u32[]{:S(2)}) collective-permute-start(bf16[128,512]{1,0:T(8,128)(2,1)S(1)} %get-tuple-element.52), channel_id=1, source_target_pairs={{0,8},{8,0},{16,24},{24,16},{1,9},{9,1},{17,25},{25,17},{2,10},{10... | collective-permute-start | bytes 393224 | tf_op jit(solution)/shard_map/ppermute | solution.py:596
  57.9 6.4 %collective-permute-start.12 = (bf16[128,512]{1,0:T(8,128)(2,1)S(1)}, bf16[128,512]{1,0:T(8,128)(2,1)S(1)}, u32[]{:S(2)}, u32[]{:S(2)}) collective-permute-start(bf16[128,512]{1,0:T(8,128)(2,1)S(1)} %get-tuple-element.53), channel_id=1, source_target_pairs={{0,16},{8,24},{16,0},{24,8},{1,17},{9,25},{17,1},{25,9},{2,18},{10... | collective-permute-start | bytes 393224 | tf_op jit(solution)/shard_map/ppermute | solution.py:596
  58.3 7.9 %collective-permute-start.13 = (bf16[128,512]{1,0:T(8,128)(2,1)S(1)}, bf16[128,512]{1,0:T(8,128)(2,1)S(1)}, u32[]{:S(2)}, u32[]{:S(2)}) collective-permute-start(bf16[128,512]{1,0:T(8,128)(2,1)S(1)} %get-tuple-element.54), channel_id=1, source_target_pairs={{0,24},{8,16},{16,8},{24,0},{1,25},{9,17},{17,9},{25,1},{2,26},{10... | collective-permute-start | bytes 393224 | tf_op jit(solution)/shard_map/ppermute | solution.py:596
  64.3 1.9 %copy-start.25 = (bf16[1,128,2048]{2,1,0:T(8,128)(2,1)}, bf16[1,128,2048]{2,1,0:T(8,128)(2,1)S(1)}, u32[]{:S(2)}) copy-start(bf16[1,128,2048]{2,1,0:T(8,128)(2,1)S(1)} %bitcast_dynamic-update-slice_fusion.1) | copy-start | bytes 1572868
  (16 other events, 12.5 us)

commit v6 on v4

--- a/solution.py
+++ b/solution.py
@@ -181,6 +181,7 @@
 SIDE = 256
 EDGE = 8
 GROUP = 32
+HEADER = 16
 
 
 def ring_order(count):
@@ -220,30 +221,97 @@
     return lax.dot_general(a, b, (((1,), (1,)), ((), ())), preferred_element_type=jnp.float32)
 
 
-def pack_kernel(columns, weight_in, own, sems):
-    at = pl.ds(pl.multiple_of(lax.axis_index("seq") * columns, columns), columns)
-    side_rows = own.shape[0] - columns
+def pack_kernel(columns, weight_in, own, side, sems):
+    seq = lax.axis_index("seq")
+    half = side.shape[0]
+    few = own.shape[0] - columns - half
+    mine = pl.multiple_of(INNER + seq % 2 * half, half)
+    other = pl.multiple_of(INNER + (1 - seq % 2) * half, half)
+    steps_at = pl.multiple_of(INNER + 2 * half + seq // 2 * few, few)
     copies = [
-        pltpu.make_async_copy(weight_in.at[at], own.at[pl.ds(0, columns)], sems.at[0]),
-        pltpu.make_async_copy(weight_in.at[pl.ds(INNER, side_rows)], own.at[pl.ds(columns, side_rows)], sems.at[1]),
+        (weight_in.at[pl.ds(pl.multiple_of(seq * columns, columns), columns)], own.at[pl.ds(0, columns)]),
+        (weight_in.at[pl.ds(mine, half)], own.at[pl.ds(columns, half)]),
+        (weight_in.at[pl.ds(steps_at, few)], own.at[pl.ds(columns + half, few)]),
+        (weight_in.at[pl.ds(other, half)], side),
     ]
+    copies = [pltpu.make_async_copy(a, b, sems.at[i]) for i, (a, b) in enumerate(copies)]
     for copy in copies:
         copy.start()
     for copy in copies:
         copy.wait()
 
 
-def early_kernel(heads, ring, ways, *refs):
-    count = len(ways)
-    pieces, refs = refs[:4], refs[4:]
-    weights, refs = refs[:count], refs[count:]
+def first_gather_kernel(columns, own, side, up, down, out, sent):
+    rows, depth = own.shape
+    half = side.shape[0]
+    other = columns + LANES
+    out[rows:, :] = jnp.zeros((out.shape[0] - rows, out.shape[1]), out.dtype)
+    for n, weight in enumerate((own, up, down)):
+        out[:rows, n * depth : (n + 1) * depth] = weight[...]
+    out[other : other + half, :depth] = side[...]
+    sent[:half, :] = up[columns : columns + half, :]
+    sent[half:, :] = down[columns : columns + half, :]
+
+
+def next_gather_kernel(columns, at, held, swapped, up, down, out, sent):
+    del held
+    rows, depth = up.shape
+    half = swapped.shape[0] // 2
+    other = columns + LANES
+    for n, weight in enumerate((up, down)):
+        out[:rows, (at + n) * depth : (at + n + 1) * depth] = weight[...]
+        out[other : other + half, (at + n - 2) * depth : (at + n - 1) * depth] = swapped[n * half : (n + 1) * half, :]
+    sent[:half, :] = up[columns : columns + half, :]
+    sent[half:, :] = down[columns : columns + half, :]
+
+
+def split_kernel(columns, up, down, up_part, down_part, sent, crossing):
+    cut = up_part.shape[0]
+    half = crossing.shape[0]
+    up_part[...] = up[:cut, :]
+    down_part[...] = down[cut:, :]
+    sent[:half, :] = up[columns : columns + half, :]
+    sent[half:, :] = down[columns : columns + half, :]
+    crossing[...] = down[columns : columns + half, :]
+
+
+def early_kernel(columns, ring, ways, first, *refs):
+    pieces = refs[:4]
+    gathered, swapped, table, partial, rest, rows_in, side = refs[4:]
+    length = rows_in.shape[0]
+    half, depth = swapped.shape[0] // 2, swapped.shape[1]
+    take_rows(pieces, ring, ways[:first], rows_in)
+    take_rows(pieces, ring, ways[first:], rest)
+    for n in range(columns // SIDE):
+        at = slice(n * SIDE, (n + 1) * SIDE)
+        partial[:length, at] = times_transposed(rows_in[...], gathered[at, :])
+    side[...] = gathered[columns:, :]
+    for n in range(2):
+        side[LANES : LANES + half, (first - 2 + n) * depth : (first - 1 + n) * depth] = swapped[n * half : (n + 1) * half, :]
+    partial[:length, columns:] = times_transposed(rows_in[...], side[...])
+    partial[length:, : table.shape[1]] = table[...]
+
+
+def second_kernel(columns, partial, rest, up, down, swapped, out, w_in):
+    rows, depth = up.shape
+    length = rest.shape[0]
+    half = swapped.shape[0] // 2
+    other = columns + LANES
+    w_in[rows:, :] = jnp.zeros((w_in.shape[0] - rows, w_in.shape[1]), jnp.bfloat16)
+    for n, weight in enumerate((up, down)):
+        w_in[:rows, n * depth : (n + 1) * depth] = weight[...]
+        w_in[other : other + half, n * depth : (n + 1) * depth] = swapped[n * half : (n + 1) * half, :]
+    for n in range(w_in.shape[0] // SIDE):
+        at = slice(n * SIDE, (n + 1) * SIDE)
+        out[:length, at] = partial[:length, at] + times_transposed(rest[:, : 2 * depth], w_in[at, :])
+    out[length:, :] = partial[length:, :]
+
+
+def prepare_kernel(heads, *refs):
     marks_in, conv_w_in, conv_b_in, step_bias_in, decay_in, skip_in, gain_in = refs[:7]
-    partial, conv_w, conv_b, per_lane, skips, gains, spread, barred, flags, refs = (*refs[7:16], refs[16:])
-    per_head, marks, rows_in, w_in, sems = refs
+    table, conv_w, conv_b, gains, per_head, marks, sems = refs[7:]
     seq = lax.axis_index("seq")
     columns = heads * HEAD_DIM
-    depth = weights[0].shape[1]
-    rows = weights[0].shape[0]
     own_lanes = pl.ds(pl.multiple_of(seq * columns, columns), columns)
     side_lanes = pl.ds(INNER, LANES)
     copies = [
@@ -260,13 +328,6 @@
     copies = [pltpu.make_async_copy(a, b, sems.at[i]) for i, (a, b) in enumerate(copies)]
     for copy in copies:
         copy.start()
-    take_rows(pieces, ring, ways, rows_in)
-    w_in[rows:, :] = jnp.zeros((w_in.shape[0] - rows, w_in.shape[1]), jnp.bfloat16)
-    for n in range(count):
-        w_in[:rows, n * depth : (n + 1) * depth] = weights[n][...]
-    for n in range(w_in.shape[0] // SIDE):
-        at = slice(n * SIDE, (n + 1) * SIDE)
-        partial[:, at] = times_transposed(rows_in[...], w_in[at, :])
     for copy in copies:
         copy.wait()
 
@@ -282,17 +343,18 @@
         value = jnp.where(lane[:1] < heads, both[0:1, :], behind[1:2, :])
         return jnp.where(lane[:1] < 2 * heads, value, 0.0)
 
+    for d in range(2):
+        table[d * KERNEL : (d + 1) * KERNEL, :] = conv_w[d]
+    table[8:10, :] = conv_b[...]
     for k in range(2):
         value = jnp.broadcast_to(own_heads(k), (8, LANES))
-        per_lane[k] = sum([pltpu.roll(value, g * GROUP, 1) for g in range(1, LANES // GROUP)], value)
-    at_row = lax.broadcasted_iota(jnp.int32, (LANES, columns), 0)
-    head = lax.broadcasted_iota(jnp.int32, (LANES, columns), 1) // HEAD_DIM
-    direct = jnp.broadcast_to(own_heads(2), (16, LANES))
+        value = sum([pltpu.roll(value, g * GROUP, 1) for g in range(1, LANES // GROUP)], value)
+        table[10 + k : 11 + k, :LANES] = value[:1]
+    direct = packed(jnp.broadcast_to(own_heads(2), (16, LANES)), 3, heads)
     for d in range(2):
-        hit = (at_row == head + d * heads) | (at_row == head + (d + 2) * heads) | (at_row == head + (d + 4) * heads)
-        spread[d] = jnp.where(hit, 1.0, 0.0).astype(jnp.bfloat16)
-        wide = jnp.dot(packed(direct, 3, heads), spread[d], preferred_element_type=jnp.float32)
-        skips[d] = wide[:8]
+        wide = jnp.dot(direct, head_columns(heads, d), preferred_element_type=jnp.float32)
+        table[12 + d : 13 + d, :columns] = wide[:1]
+    table[14:16, :columns] = gains[...]
 
     position = row + lane // GROUP * BLOCK
     here = position == marks[:, 0:1]
@@ -312,16 +374,18 @@
     chosen = jnp.where(row == wanted, 1.0, 0.0).astype(jnp.bfloat16)
     seen = jnp.dot(seen.astype(jnp.bfloat16), chosen, preferred_element_type=jnp.float32)
     last = jnp.where(backward_lane[:1], seen[:1], seen[BLOCK - 1 :])
-    flags[0] = jnp.where((seen == last) & head_lane, 1.0, 0.0)
-    flags[1] = jnp.where((seen == 0.0) & head_lane, 1.0, 0.0)
-    flags[2] = jnp.where((jnp.broadcast_to(last, (BLOCK, LANES)) == 0.0) & head_lane, 1.0, 0.0)
-    turned = seen.T
-    for b in range(LANES // GROUP):
-        for d in range(2):
-            ordered = (row >= lane) if d == 0 else (row <= lane)
-            at = b * GROUP + d * heads
-            allowed = ordered & (seen[:, at : at + 1] == turned[at : at + 1, :])
-            barred[d, b] = jnp.where(allowed, 0.0, -1e30)
+    table[HEADER:, 0:LANES] = jnp.where((seen == last) & head_lane, 1.0, 0.0)
+    table[HEADER:, LANES : 2 * LANES] = jnp.where((seen == 0.0) & head_lane, 1.0, 0.0)
+    last = jnp.broadcast_to(last, (BLOCK, LANES))
+    table[HEADER:, 2 * LANES : 3 * LANES] = jnp.where((last == 0.0) & head_lane, 1.0, 0.0)
+    table[HEADER:, 3 * LANES : 4 * LANES] = seen
+
+
+def head_columns(heads, d):
+    at_row = lax.broadcasted_iota(jnp.int32, (LANES, heads * HEAD_DIM), 0)
+    head = lax.broadcasted_iota(jnp.int32, (LANES, heads * HEAD_DIM), 1) // HEAD_DIM + d * heads
+    hit = (at_row == head) | (at_row == head + 2 * heads) | (at_row == head + 4 * heads)
+    return jnp.where(hit, 1.0, 0.0).astype(jnp.bfloat16)
 
 
 def packed(value, count, heads):
@@ -332,30 +396,28 @@
     return joined.astype(jnp.bfloat16)
 
 
-def mixer_kernel(heads, ring, ways, *refs):
-    count = len(ways)
-    pieces, refs = refs[:4], refs[4:]
-    weights, refs = refs[: count - 1], refs[count - 1 :]
-    ends, refs = refs[:2], refs[2:]
-    partial, conv_w, conv_b, per_lane, skips, gains, spread, barred, flags = refs[:9]
-    outs, refs = refs[9:13], refs[13:]
-    rows_in, w_in, padded, xs, cs, bs, widen_in, leads, tails, state, ys, mixed = refs
+def mixer_kernel(heads, partial, rest, up_end, down_end, far, *refs):
+    outs, refs = refs[:4], refs[4:]
+    w_end, padded, xs, cs, bs, widen_in, leads, tails, state, ys, mixed = refs
     seq = lax.axis_index("seq")
     columns = heads * HEAD_DIM
-    depth = weights[0].shape[1]
-    rows = weights[0].shape[0]
+    depth = up_end.shape[1]
+    cut, rows = up_end.shape[0], up_end.shape[0] + down_end.shape[0]
     chunks = columns // LANES
-    length = rows_in.shape[0]
+    length = rest.shape[0]
     blocks = length // BLOCK
-    cut = ends[0].shape[0]
     lane, row = lane_row()
 
-    take_rows(pieces, ring, ways, rows_in)
-    w_in[rows:, :] = jnp.zeros((w_in.shape[0] - rows, w_in.shape[1]), jnp.bfloat16)
-    for n in range(count - 1):
-        w_in[:rows, n * depth : (n + 1) * depth] = weights[n][...]
-    w_in[:cut, (count - 1) * depth :] = ends[0][...]
-    w_in[cut:rows, (count - 1) * depth :] = ends[1][...]
+    def table(first, last, lanes):
+        return partial[length + first : length + last, lanes]
+
+    w_end[:cut, :] = up_end[...]
+    w_end[cut:rows, :] = down_end[...]
+    half = far.shape[0]
+    other = columns + LANES
+    w_end[rows:other, :] = jnp.zeros((other - rows, depth), jnp.bfloat16)
+    w_end[other : other + half, :] = far[...]
+    w_end[other + half :, :] = jnp.zeros((w_end.shape[0] - other - half, depth), jnp.bfloat16)
     edge = jnp.zeros((EDGE, LANES), jnp.float32)
     for c in range(chunks + 1):
         padded[c, 0:EDGE, :] = edge
@@ -366,32 +428,39 @@
 
     def project_in(n):
         at = slice(n * SIDE, (n + 1) * SIDE)
-        out = partial[:, at] + times_transposed(rows_in[...], w_in[at, :])
-        return out.astype(jnp.bfloat16).astype(jnp.float32)
+        return times_transposed(rest[:, 2 * depth :], w_end[at, :])
+
+    def rounded(value):
+        return value.astype(jnp.bfloat16).astype(jnp.float32)
 
     def keep(c, value):
         for mask in range(4):
             padded[c, pl.ds(EDGE + places[mask], BLOCK), :] = value[mask * BLOCK : (mask + 1) * BLOCK, :]
 
     side_out = project_in(columns // SIDE)
-    keep(chunks, side_out[:, :LANES])
+    mine = rounded(side_out[:, :LANES] + partial[:length, columns:other])
+    others = rounded(side_out[:, LANES:] + partial[:length, other:])
+    even = jnp.broadcast_to(seq, mine.shape) % 2 == 0
+    low, high = jnp.where(even, mine, others), jnp.where(even, others, mine)
+    left = lax.broadcasted_iota(jnp.int32, mine.shape, 1) < half
+    keep(chunks, jnp.where(left, low, pltpu.roll(high, half, 1)))
     for n in range(columns // SIDE):
-        part_out = project_in(n)
+        part_out = rounded(project_in(n) + partial[:length, n * SIDE : (n + 1) * SIDE])
         for k in range(SIDE // LANES):
             keep(n * (SIDE // LANES) + k, part_out[:, k * LANES : (k + 1) * LANES])
 
     within = lane % GROUP
     head_lane = within < 2 * heads
     backward_lane = (within >= heads) & head_lane
-    to_first = lax.rem(LANES - seq * heads, LANES)
+    to_first = LANES - half - seq % 2 * heads
     raw = jnp.zeros((BLOCK, LANES), jnp.float32)
     for mask in range(4):
-        mine = pltpu.roll(side_out[mask * BLOCK : (mask + 1) * BLOCK, LANES:], to_first, 1)
-        mine = jnp.where(lane < heads, mine, 0.0)
-        raw = raw + pltpu.roll(mine + pltpu.roll(mine, heads, 1), (seq ^ mask) * GROUP, 1)
-    raw = raw + per_lane[0][:1]
+        own_steps = pltpu.roll(mine[mask * BLOCK : (mask + 1) * BLOCK, :], to_first, 1)
+        own_steps = jnp.where(lane < heads, own_steps, 0.0)
+        raw = raw + pltpu.roll(own_steps + pltpu.roll(own_steps, heads, 1), (seq ^ mask) * GROUP, 1)
+    raw = raw + table(10, 11, slice(0, LANES))
     step = jnp.maximum(raw, 0.0) + jnp.log1p(jnp.exp(-jnp.abs(raw)))
-    rate = -step * per_lane[1][:1]
+    rate = -step * table(11, 12, slice(0, LANES))
     two = jnp.concatenate(split_parts(rate, 2), axis=1)
     lower = jnp.where(row >= lane, 1.0, 0.0).astype(jnp.bfloat16)
     upper = jnp.where(row <= lane, 1.0, 0.0).astype(jnp.bfloat16)
@@ -399,9 +468,13 @@
     sums = sums[:, :LANES] + sums[:, LANES:]
     cum = jnp.where(backward_lane, sums[BLOCK:], sums[:BLOCK])
     last = jnp.where(backward_lane[:1], cum[:1], cum[BLOCK - 1 :])
+    flags = [table(HEADER, HEADER + BLOCK, slice(k * LANES, (k + 1) * LANES)) for k in range(4)]
     tail = flags[0] * jnp.exp(last - cum) * step
     lead = flags[1] * jnp.exp(cum)
     fade = flags[2][:8] * jnp.exp(jnp.broadcast_to(last, (8, LANES)))
+    seen = flags[3]
+    seen_turned = seen.T
+    spread = [head_columns(heads, d) for d in range(2)]
     shown = (jnp.log(step) - cum).T
     fades = []
     for b in range(blocks):
@@ -428,9 +501,10 @@
             taps = [padded[c, pl.ds(at + EDGE - 3 + k, short), :] for k in range(7)]
             lanes = slice(c * LANES, (c + 1) * LANES)
             for d in range(2):
-                acc = conv_b[d : d + 1, lanes] + conv_w[d, 0:1, lanes] * taps[0 if d == 0 else 6]
-                for k in range(1, KERNEL):
-                    acc = acc + conv_w[d, k : k + 1, lanes] * taps[k if d == 0 else 6 - k]
+                acc = table(8 + d, 9 + d, lanes)
+                for k in range(KERNEL):
+                    n = d * KERNEL + k
+                    acc = acc + table(n, n + 1, lanes) * taps[k if d == 0 else 6 - k]
                 half = 0.5 * acc
                 value = half + half * jnp.tanh(half)
                 if c < chunks:
@@ -454,7 +528,9 @@
             c_part = cs[d, at, :]
             b_part = bs[d, at, :]
             scores = times_transposed(c_part, b_part)
-            bar = barred[d, b]
+            ordered = (row >= lane) if d == 0 else (row <= lane)
+            n = b * GROUP + d * heads
+            bar = jnp.where(ordered & (seen[:, n : n + 1] == seen_turned[n : n + 1, :]), 0.0, -1e30)
             before = state[d]
             carried = jnp.dot(c_part, before.astype(jnp.bfloat16), preferred_element_type=jnp.float32)
             x_all = xs[d, at, :]
@@ -476,7 +552,7 @@
                 ys[d, at, lanes] = (
                     inner
                     + leads[d, at, lanes].astype(jnp.float32) * carried[:, lanes]
-                    + skips[d, :1, lanes] * x_part.astype(jnp.float32)
+                    + table(12 + d, 13 + d, lanes) * x_part.astype(jnp.float32)
                 )
 
     head_row = lax.broadcasted_iota(jnp.int32, (SIDE, SIDE), 0) // HEAD_DIM
@@ -488,7 +564,7 @@
         for d in range(2):
             y = ys[d, :, lanes]
             mean = jnp.dot((y * y).astype(jnp.bfloat16), same, preferred_element_type=jnp.float32)
-            both = both + y * lax.rsqrt(mean + 1e-05) * gains[d : d + 1, lanes]
+            both = both + y * lax.rsqrt(mean + 1e-05) * table(14 + d, 15 + d, lanes)
         mixed[:, lanes] = both.astype(jnp.bfloat16)
     for mask in range(4):
         outs[mask][...] = mixed[pl.ds(places[mask], BLOCK), :]
@@ -499,65 +575,86 @@
 ROOM = 24 * 1024 * 1024
 
 
+def call(kernel, shapes, scratch, *operands, space=IN_VMEM, aliases=None):
+    shapes = [jax.ShapeDtypeStruct(*one) for one in shapes]
+    return pl.pallas_call(
+        kernel,
+        out_shape=shapes,
+        in_specs=[space] * len(operands),
+        out_specs=[IN_VMEM] * len(shapes),
+        scratch_shapes=scratch,
+        input_output_aliases=aliases or {},
+        compiler_params=pltpu.CompilerParams(vmem_limit_bytes=ROOM),
+    )(*operands)
+
+
 def pack(weight, columns):
-    side_rows = weight.shape[0] - INNER
-    return pl.pallas_call(
-        functools.partial(pack_kernel, columns),
-        out_shape=jax.ShapeDtypeStruct((columns + side_rows, weight.shape[1]), weight.dtype),
-        in_specs=[IN_HBM],
-        out_specs=IN_VMEM,
-        scratch_shapes=[pltpu.SemaphoreType.DMA((2,))],
-        compiler_params=pltpu.CompilerParams(vmem_limit_bytes=ROOM),
-    )(weight)
-
-
-def early(heads, ring, ways, pieces, weights, params):
+    depth = weight.shape[1]
+    few = 2 * columns // HEAD_DIM
+    shapes = [((columns + STATE + few, depth), weight.dtype), ((STATE, depth), weight.dtype)]
+    scratch = [pltpu.SemaphoreType.DMA((4,))]
+    return call(functools.partial(pack_kernel, columns), shapes, scratch, weight, space=IN_HBM)
+
+
+def first_gather(columns, shape, own, side, up, down):
+    shapes = [(shape, own.dtype), ((2 * side.shape[0], side.shape[1]), own.dtype)]
+    return call(functools.partial(first_gather_kernel, columns), shapes, [], own, side, up, down)
+
+
+def next_gather(columns, at, held, swapped, up, down):
+    shapes = [(held.shape, held.dtype), (swapped.shape, held.dtype)]
+    kernel = functools.partial(next_gather_kernel, columns, at)
+    return call(kernel, shapes, [], held, swapped, up, down, aliases={0: 0})
+
+
+def split(columns, up, down):
+    rows, depth = up.shape
+    cut = rows // 32 * 16
+    shapes = [(cut, depth), (rows - cut, depth), (2 * STATE, depth), (STATE, depth)]
+    shapes = [(one, up.dtype) for one in shapes]
+    return call(functools.partial(split_kernel, columns), shapes, [], up, down)
+
+
+def prepare(heads, params):
+    columns = heads * HEAD_DIM
+    scratch = [
+        pltpu.VMEM((2, KERNEL, columns + LANES), jnp.float32),
+        pltpu.VMEM((2, columns + LANES), jnp.float32),
+        pltpu.VMEM((2, columns), jnp.float32),
+        pltpu.VMEM((3, 2, HEADS), jnp.float32),
+        pltpu.VMEM(params[0].shape, jnp.int32),
+        pltpu.SemaphoreType.DMA((9,)),
+    ]
+    shape = ((HEADER + BLOCK, columns + LANES), jnp.float32)
+    return call(functools.partial(prepare_kernel, heads), [shape], scratch, *params, space=IN_HBM)[0]
+
+
+def early(columns, ring, ways, pieces, gathered, swapped, table):
     length = pieces[0].shape[0] * len(pieces)
+    wide, known = gathered.shape
+    first = 2 * ring - 3
+    depth = known // first
+    shapes = [
+        ((length + table.shape[0], wide), jnp.float32),
+        ((length, depth * len(ways) - known), jnp.bfloat16),
+    ]
+    scratch = [pltpu.VMEM((length, known), jnp.bfloat16), pltpu.VMEM((SIDE, known), jnp.bfloat16)]
+    kernel = functools.partial(early_kernel, columns, ring, ways, first)
+    return call(kernel, shapes, scratch, *pieces, gathered, swapped, table)
+
+
+def second(columns, partial, rest, up, down, swapped):
+    scratch = [pltpu.VMEM((partial.shape[1], 2 * up.shape[1]), jnp.bfloat16)]
+    shapes = [(partial.shape, jnp.float32)]
+    return call(functools.partial(second_kernel, columns), shapes, scratch, partial, rest, up, down, swapped)[0]
+
+
+def mix(heads, count, partial, rest, *others):
     columns = heads * HEAD_DIM
-    depth = weights[0].shape[1]
-    blocks = length // BLOCK
-    wide = columns + SIDE
-    known = depth * len(ways)
-    shapes = [
-        ((length, wide), jnp.float32),
-        ((2, KERNEL, columns + LANES), jnp.float32),
-        ((2, columns + LANES), jnp.float32),
-        ((2, 8, LANES), jnp.float32),
-        ((2, 8, columns), jnp.float32),
-        ((2, columns), jnp.float32),
-        ((2, LANES, columns), jnp.bfloat16),
-        ((2, blocks, BLOCK, LANES), jnp.float32),
-        ((3, BLOCK, LANES), jnp.float32),
-    ]
-    return pl.pallas_call(
-        functools.partial(early_kernel, heads, ring, ways),
-        out_shape=[jax.ShapeDtypeStruct(*one) for one in shapes],
-        in_specs=[IN_VMEM] * (len(pieces) + len(weights)) + [IN_HBM] * len(params),
-        out_specs=[IN_VMEM] * len(shapes),
-        scratch_shapes=[
-            pltpu.VMEM((3, 2, HEADS), jnp.float32),
-            pltpu.VMEM(params[0].shape, jnp.int32),
-            pltpu.VMEM((length, known), jnp.bfloat16),
-            pltpu.VMEM((wide, known), jnp.bfloat16),
-            pltpu.SemaphoreType.DMA((9,)),
-        ],
-        cost_estimate=pl.CostEstimate(flops=2 * length * wide * known, bytes_accessed=8 * 1024 * 1024, transcendentals=0),
-        compiler_params=pltpu.CompilerParams(vmem_limit_bytes=ROOM),
-    )(*pieces, *weights, *params)
-
-
-def mix(heads, ring, ways, pieces, weights, ends, prepared):
-    section = pieces[0].shape[0]
-    columns = heads * HEAD_DIM
-    length = section * len(pieces)
-    depth = weights[0].shape[1]
-    chunks = columns // LANES
-    known = depth * len(ways)
-    operands = (*pieces, *weights, *ends, *prepared)
+    length = rest.shape[0]
     scratch = [
-        ((length, known), jnp.bfloat16),
-        ((columns + SIDE, known), jnp.bfloat16),
-        ((chunks + 1, length + 2 * EDGE, LANES), jnp.float32),
+        ((columns + SIDE, others[0].shape[1]), jnp.bfloat16),
+        ((columns // LANES + 1, length + 2 * EDGE, LANES), jnp.float32),
         ((2, length, columns), jnp.bfloat16),
         ((2, length, LANES), jnp.bfloat16),
         ((2, length, LANES), jnp.bfloat16),
@@ -568,20 +665,24 @@
         ((2, length, columns), jnp.float32),
         ((length, columns), jnp.bfloat16),
     ]
-    return pl.pallas_call(
-        functools.partial(mixer_kernel, heads, ring, ways),
-        out_shape=[jax.ShapeDtypeStruct((section, columns), jnp.bfloat16)] * len(pieces),
-        in_specs=[IN_VMEM] * len(operands),
-        out_specs=[IN_VMEM] * len(pieces),
-        scratch_shapes=[pltpu.VMEM(*one) for one in scratch],
-        compiler_params=pltpu.CompilerParams(vmem_limit_bytes=ROOM),
-    )(*operands)
+    shapes = [((length // count, columns), jnp.bfloat16)] * count
+    scratch = [pltpu.VMEM(*one) for one in scratch]
+    return call(functools.partial(mixer_kernel, heads), shapes, scratch, partial, rest, *others)
 
 
 def turn(value, way):
     order = ring_order(lax.axis_size("batch"))
     count = len(order)
     return lax.ppermute(value, ("fsdp", "batch"), [(order[i], order[(i + way) % count]) for i in range(count)])
+
+
+def turn_across(value, way):
+    order = ring_order(lax.axis_size("batch"))
+    count = len(order)
+    pairs = []
+    for s in range(lax.axis_size("seq")):
+        pairs += [(s * count + order[i], (s ^ 1) * count + order[(i + way) % count]) for i in range(count)]
+    return lax.ppermute(value, ("seq", "fsdp", "batch"), pairs)
 
 
 def swap(value, axis, mask):
@@ -594,24 +695,40 @@
     seq = lax.axis_index("seq")
     heads = HEADS // count
     columns = heads * HEAD_DIM
-    own = pack(in_weight.T, columns)
+    own, side = pack(in_weight.T, columns)
 
     ring = lax.axis_size("batch")
-    across = swap(tokens, "seq", 2)
+    late, _ = lax.optimization_barrier((tokens, own))
+    across = swap(late, "seq", 2)
     pieces = [tokens, swap(tokens, "seq", 1), across, swap(across, "seq", 1)]
-    weights, ways = [own], [0]
+    table = prepare(heads, (read_starts, conv_weight, conv_bias, dt_bias, decay, skip, norm_gain))
+    first = 2 * ring - 3
+    ways = [0]
     up = down = own
     for away in range(1, ring):
+        before = up, down
         up, down = turn(up, 1), turn(down, -1)
-        weights += [up, down]
         ways += [-away, away]
-    cut = own.shape[0] // 32 * 16
-    ends = [turn(up[:cut], 1), turn(down[cut:], -1)]
-    ways.append(ring)
-    params = (read_starts, conv_weight, conv_bias, dt_bias, decay, skip, norm_gain)
-    first = 2 * ring - 3
-    prepared = early(heads, ring, ways[:first], pieces, weights[:first], params)
-    results = mix(heads, ring, ways[first:], pieces, weights[first:], ends, prepared)
+        if away == 1:
+            beside = table
+        elif away == 2:
+            gathered, sent = first_gather(columns, (columns + SIDE, first * own.shape[1]), own, side, *before)
+            beside = swapped = swap(sent, "seq", 1)
+        elif away < ring - 1:
+            gathered, sent = next_gather(columns, 2 * away - 3, gathered, swapped, *before)
+            beside = swapped = swap(sent, "seq", 1)
+        else:
+            gathered, sent = next_gather(columns, 2 * away - 3, gathered, swapped, *before)
+            swapped = swap(sent, "seq", 1)
+            partial, rest = early(columns, ring, tuple(ways) + (ring,), pieces, gathered, swapped, table)
+            beside = partial
+        up, _ = lax.optimization_barrier((up, beside))
+        down, _ = lax.optimization_barrier((down, beside))
+    up_part, down_part, sent, crossing = split(columns, up, down)
+    ends = [turn(up_part, 1), turn(down_part, -1)]
+    far = turn_across(crossing, -1)
+    partial = second(columns, partial, rest, up, down, swap(sent, "seq", 1))
+    results = mix(heads, count, partial, rest, *ends, far)
     received = [results[0]] + [swap(results[mask], "seq", mask) for mask in range(1, count)]
     mixed = jnp.zeros((tokens.shape[0], INNER), jnp.bfloat16)
     for mask in range(count):

time: 57.5 us -> 53.1 us (0.923)
  waiting for transfers between devices: 24.4 us -> 18.9 us
  local copies, waits for them, and re-layouts: 9.92 us -> 7.03 us
  starting transfers between devices: 13.1 us -> 15.4 us
  Pallas kernels: 9.53 us -> 11.2 us
    ppermute x8, waiting for transfers between devices: 15.3 us -> 7.89 us  [turn(): lax.ppermute(value, ('fsdp', 'batch'), [(order[i], order[(i + way) % coun...]
    ppermute x6 -> x9, starting transfers between devices: 3.84 us -> 5.62 us  [swap(): lax.ppermute(value, axis, [(i, i ^ mask) for i in range(lax.axis_size(axi...]
    pallas_call x3 -> x8, Pallas kernels: 9.53 us -> 11.2 us  [call(): pl.pallas_call(kernel, out_shape=shapes, in_specs=[space] * len(operands)...]
    ppermute x0 -> x1, starting transfers between devices: none -> 1.69 us  [turn_across(): return lax.ppermute(value, ('seq', 'fsdp', 'batch'), pairs)]
    unnamed x32 -> x20, local copies, waits for them, and re-layouts: 7.81 us -> 6.27 us
    slice x2 -> x0, local copies, waits for them, and re-layouts: 1.35 us -> none  [on_heads(): ends = [turn(up[:cut], 1), turn(down[cut:], -1)]]
    ppermute x6 -> x9, waiting for transfers between devices: 9.11 us -> 10.3 us  [swap(): lax.ppermute(value, axis, [(i, i ^ mask) for i in range(lax.axis_size(axi...]
    ppermute x8, starting transfers between devices: 9.22 us -> 8.1 us  [turn(): lax.ppermute(value, ('fsdp', 'batch'), [(order[i], order[(i + way) % coun...]
  transfers between devices with their start and end apart: 14 -> 18, of which waited for: 6 -> 11; matrix products, arithmetic and copies ran while one was open for 3% -> 0% of each run, Pallas kernels for 4% -> 7%
where the time goes in v6:
time: 53.1 us; the launch traced here: 52.7 us
  waiting for transfers between devices  18.9 us (36%)
  starting transfers between devices  15.4 us (29%)
  Pallas kernels  11.2 us (21%)
  local copies, waits for them, and re-layouts  7.03 us (13%)
    pallas_call x8, Pallas kernels, call(): pl.pallas_call(kernel, out_shape=shapes, in_specs=[space] * len(operands)...  11.2 us
    ppermute x9, waiting for transfers between devices, swap(): lax.ppermute(value, axis, [(i, i ^ mask) for i in range(lax.axis_size(axi...  10.3 us
    ppermute x8, starting transfers between devices, turn(): lax.ppermute(value, ('fsdp', 'batch'), [(order[i], order[(i + way) % coun...  8.1 us
    ppermute x8, waiting for transfers between devices, turn(): lax.ppermute(value, ('fsdp', 'batch'), [(order[i], order[(i + way) % coun...  7.89 us
    unnamed x20, local copies, waits for them, and re-layouts  6.27 us
    ppermute x9, starting transfers between devices, swap(): lax.ppermute(value, axis, [(i, i ^ mask) for i in range(lax.axis_size(axi...  5.62 us
    ppermute x1, starting transfers between devices, turn_across(): return lax.ppermute(value, ('seq', 'fsdp', 'batch'), pairs)  1.69 us
  transfers between devices with their start and end apart: 18, of which 11 were waited for; matrix products, arithmetic and copies ran while one was open for 0% of the time, Pallas kernels for 7%

profile of v6, /device:TPU:0, one launch (start us, length us, event | category | flops | bytes accessed | tf_op | source)
XLA Modules:
  0.0 52.7 jit_solution(14362278760477392951)
XLA Ops:
  0.0 1.3 %copy-done = bf16[256,2208]{0,1:T(8,128)(2,1)S(1)} copy-done((bf16[256,2208]{0,1:T(8,128)(2,1)S(1)}, bf16[256,2208]{0,1:T(8,128)(2,1)}, u32[]{:S(2)}) %copy-start) | copy-done | bytes 1130520
  1.4 3.0 %collective-permute-start.1 = (bf16[128,2048]{1,0:T(8,128)(2,1)}, bf16[128,2048]{1,0:T(8,128)(2,1)S(1)}, u32[]{:S(2)}, u32[]{:S(2)}) collective-permute-start(bf16[128,2048]{1,0:T(8,128)(2,1)} %bitcast.11), channel_id=1, source_target_pairs={{0,16},{8,24},{16,0},{24,8},{1,17},{9,25},{17,1},{25,9},{2,18},{10... | collective-permute-start | bytes 1572872 | tf_op jit(solution)/shard_map/ppermute | solution.py:689
  4.5 1.5 %collective-permute-start.4 = (bf16[592,256]{1,0:T(8,128)(2,1)S(1)}, bf16[592,256]{1,0:T(8,128)(2,1)S(1)}, u32[]{:S(2)}, u32[]{:S(2)}) collective-permute-start(bf16[592,256]{1,0:T(8,128)(2,1)S(1)} %get-tuple-element.28.own), channel_id=1, source_target_pairs={{0,4},{1,0},{2,1},{3,2},{7,3},{6,7},{5,6},{4,5},{8,12},{9,8},{10,9... | collective-permute-start | bytes 909320 | tf_op jit(solution)/shard_map/ppermute | solution.py:676
  6.5 0.9 %copy-done.2 = f32[2,4,2176]{2,1,0:T(4,128)S(1)} copy-done((f32[2,4,2176]{2,1,0:T(4,128)S(1)}, f32[2,4,2176]{2,1,0:T(4,128)}, u32[]{:S(2)}) %copy-start.2) | copy-done | bytes 69656
  7.4 0.7 %copy-done.3 = f32[2,2176]{1,0:T(2,128)S(1)} copy-done((f32[2,2176]{1,0:T(2,128)S(1)}, f32[2,2176]{1,0:T(2,128)}, u32[]{:S(2)}) %copy-start.3) | copy-done | bytes 17432
  12.2 0.9 %collective-permute-done.4.down = bf16[592,256]{1,0:T(8,128)(2,1)S(1)} collective-permute-done((bf16[592,256]{1,0:T(8,128)(2,1)S(1)}, bf16[592,256]{1,0:T(8,128)(2,1)S(1)}, u32[]{:S(2)}, u32[]{:S(2)}) %collective-permute-start.4) | collective-permute-done | bytes 303136 | tf_op jit(solution)/shard_map/ppermute | solution.py:676
  13.1 1.5 %collective-permute-start.7 = (bf16[592,256]{1,0:T(8,128)(2,1)S(1)}, bf16[592,256]{1,0:T(8,128)(2,1)S(1)}, u32[]{:S(2)}, u32[]{:S(2)}) collective-permute-start(bf16[592,256]{1,0:T(8,128)(2,1)S(1)} %collective-permute-done.4.down), channel_id=1, source_target_pairs={{0,4},{1,0},{2,1},{3,2},{7,3},{6,7},{5,6},{4,5},{8,12},{9,8},{10,9... | collective-permute-start | bytes 909320 | tf_op jit(solution)/shard_map/ppermute | solution.py:676
  15.1 1.5 %collective-permute-done.1.refs_2_ = bf16[128,2048]{1,0:T(8,128)(2,1)S(1)} collective-permute-done((bf16[128,2048]{1,0:T(8,128)(2,1)}, bf16[128,2048]{1,0:T(8,128)(2,1)S(1)}, u32[]{:S(2)}, u32[]{:S(2)}) %collective-permute-start.1) | collective-permute-done | bytes 524320 | tf_op jit(solution)/shard_map/ppermute | solution.py:689
  17.3 1.3 %collective-permute-done.5.swapped = bf16[128,256]{1,0:T(8,128)(2,1)S(1)} collective-permute-done((bf16[128,256]{1,0:T(8,128)(2,1)S(1)}, bf16[128,256]{1,0:T(8,128)(2,1)S(1)}, u32[]{:S(2)}, u32[]{:S(2)}) %collective-permute-start.5) | collective-permute-done | bytes 65568 | tf_op jit(solution)/shard_map/ppermute | solution.py:689
  18.6 2.2 %collective-permute-done.7.down = bf16[592,256]{1,0:T(8,128)(2,1)S(1)} collective-permute-done((bf16[592,256]{1,0:T(8,128)(2,1)S(1)}, bf16[592,256]{1,0:T(8,128)(2,1)S(1)}, u32[]{:S(2)}, u32[]{:S(2)}) %collective-permute-start.7) | collective-permute-done | bytes 303136 | tf_op jit(solution)/shard_map/ppermute | solution.py:676
  20.8 1.5 %collective-permute-start.10 = (bf16[592,256]{1,0:T(8,128)(2,1)S(1)}, bf16[592,256]{1,0:T(8,128)(2,1)S(1)}, u32[]{:S(2)}, u32[]{:S(2)}) collective-permute-start(bf16[592,256]{1,0:T(8,128)(2,1)S(1)} %collective-permute-done.7.down), channel_id=1, source_target_pairs={{0,4},{1,0},{2,1},{3,2},{7,3},{6,7},{5,6},{4,5},{8,12},{9,8},{10,9... | collective-permute-start | bytes 909320 | tf_op jit(solution)/shard_map/ppermute | solution.py:676
  23.0 1.2 %collective-permute-done.8.refs_5_ = bf16[128,256]{1,0:T(8,128)(2,1)S(1)} collective-permute-done((bf16[128,256]{1,0:T(8,128)(2,1)S(1)}, bf16[128,256]{1,0:T(8,128)(2,1)S(1)}, u32[]{:S(2)}, u32[]{:S(2)}) %collective-permute-start.8) | collective-permute-done | bytes 65568 | tf_op jit(solution)/shard_map/ppermute | solution.py:689
  24.2 1.3 %shard_map.95 = (f32[656,768]{1,0:T(8,128)S(1)}, bf16[512,768]{1,0:T(8,128)(2,1)S(1)}) custom-call(bf16[128,2048]{1,0:T(8,128)(2,1)S(1)} %bitcast.13, bf16[128,2048]{1,0:T(8,128)(2,1)S(1)} %collective-permute-done.refs_1_, bf16[128,2048]{1,0:T(8,128)(2,1)S(1)} %collective-permute-done.1.refs_2_, bf16[128,2048]{1,0:T(8,128)(2,1)S(1)} %collective-permute-done.2.refs_3_, ...), custom_call_target="tpu_custom_call" | custom-call | tf_op jit(solution)/shard_map/pallas_call | solution.py:580
  25.5 2.3 %collective-permute-done.10.down = bf16[592,256]{1,0:T(8,128)(2,1)S(1)} collective-permute-done((bf16[592,256]{1,0:T(8,128)(2,1)S(1)}, bf16[592,256]{1,0:T(8,128)(2,1)S(1)}, u32[]{:S(2)}, u32[]{:S(2)}) %collective-permute-start.10) | collective-permute-done | bytes 303136 | tf_op jit(solution)/shard_map/ppermute | solution.py:676
  27.9 1.4 %collective-permute-done.9.up = bf16[592,256]{1,0:T(8,128)(2,1)S(1)} collective-permute-done((bf16[592,256]{1,0:T(8,128)(2,1)S(1)}, bf16[592,256]{1,0:T(8,128)(2,1)S(1)}, u32[]{:S(2)}, u32[]{:S(2)}) %collective-permute-start.9) | collective-permute-done | bytes 303136 | tf_op jit(solution)/shard_map/ppermute | solution.py:676
  29.3 0.8 %shard_map.96 = (bf16[288,256]{1,0:T(8,128)(2,1)}, bf16[304,256]{1,0:T(8,128)(2,1)}, bf16[128,256]{1,0:T(8,128)(2,1)}, bf16[64,256]{1,0:T(8,128)(2,1)}) custom-call(bf16[592,256]{1,0:T(8,128)(2,1)S(1)} %collective-permute-done.9.up, bf16[592,256]{1,0:T(8,128)(2,1)S(1)} %collective-permute-done.10.down), custom_call_target="tpu_custom_call" | custom-call | tf_op jit(solution)/shard_map/pallas_call | solution.py:580
  30.0 1.6 %collective-permute-start.13 = (bf16[304,256]{1,0:T(8,128)(2,1)}, bf16[304,256]{1,0:T(8,128)(2,1)}, u32[]{:S(2)}, u32[]{:S(2)}) collective-permute-start(bf16[304,256]{1,0:T(8,128)(2,1)} %get-tuple-element.45), channel_id=1, source_target_pairs={{0,4},{1,0},{2,1},{3,2},{7,3},{6,7},{5,6},{4,5},{8,12},{9,8},{10,9... | collective-permute-start | bytes 466952 | tf_op jit(solution)/shard_map/ppermute | solution.py:676
  32.1 1.7 %collective-permute-start.14 = (bf16[64,256]{1,0:T(8,128)(2,1)}, bf16[64,256]{1,0:T(8,128)(2,1)}, u32[]{:S(2)}, u32[]{:S(2)}) collective-permute-start(bf16[64,256]{1,0:T(8,128)(2,1)} %get-tuple-element.46), channel_id=1, source_target_pairs={{0,12},{1,8},{2,9},{3,10},{7,11},{6,15},{5,14},{4,13},{8,4},{9,0},... | collective-permute-start | bytes 98312 | tf_op jit(solution)/shard_map/ppermute | solution.py:685
  33.8 1.5 %shard_map.97.partial = f32[656,768]{1,0:T(8,128)S(1)} custom-call(f32[656,768]{1,0:T(8,128)S(1)} %get-tuple-element.39.partial, bf16[512,768]{1,0:T(8,128)(2,1)S(1)} %get-tuple-element.40.rest, bf16[592,256]{1,0:T(8,128)(2,1)S(1)} %collective-permute-done.9.up, bf16[592,256]{1,0:T(8,128)(2,1)S(1)} %collective-permute-done.10.down, ...), custom_call_target="tpu_custom_call" | custom-call | tf_op jit(solution)/shard_map/pallas_call | solution.py:580
  35.9 1.0 %collective-permute-done.12.up_end = bf16[288,256]{1,0:T(8,128)(2,1)S(1)} collective-permute-done((bf16[288,256]{1,0:T(8,128)(2,1)}, bf16[288,256]{1,0:T(8,128)(2,1)S(1)}, u32[]{:S(2)}, u32[]{:S(2)}) %collective-permute-start.12) | collective-permute-done | bytes 147488 | tf_op jit(solution)/shard_map/ppermute | solution.py:676
  37.0 6.7 %shard_map.98 = (bf16[128,512]{1,0:T(8,128)(2,1)S(1)}, bf16[128,512]{1,0:T(8,128)(2,1)S(1)}, bf16[128,512]{1,0:T(8,128)(2,1)S(1)}, bf16[128,512]{1,0:T(8,128)(2,1)S(1)}) custom-call(f32[656,768]{1,0:T(8,128)S(1)} %shard_map.97.partial, bf16[512,768]{1,0:T(8,128)(2,1)S(1)} %get-tuple-element.40.rest, bf16[288,256]{1,0:T(8,128)(2,1)S(1)} %collective-permute-done.12.up_end, ...), custom_call_target="tpu_custom_call" | custom-call | tf_op jit(solution)/shard_map/pallas_call | solution.py:580
  43.8 1.6 %collective-permute-start.16 = (bf16[128,512]{1,0:T(8,128)(2,1)S(1)}, bf16[128,512]{1,0:T(8,128)(2,1)S(1)}, u32[]{:S(2)}, u32[]{:S(2)}) collective-permute-start(bf16[128,512]{1,0:T(8,128)(2,1)S(1)} %get-tuple-element.49), channel_id=1, source_target_pairs={{0,16},{8,24},{16,0},{24,8},{1,17},{9,25},{17,1},{25,9},{2,18},{10... | collective-permute-start | bytes 393224 | tf_op jit(solution)/shard_map/ppermute | solution.py:689
  45.7 4.4 %collective-permute-done.16 = bf16[128,512]{1,0:T(8,128)(2,1)S(1)} collective-permute-done((bf16[128,512]{1,0:T(8,128)(2,1)S(1)}, bf16[128,512]{1,0:T(8,128)(2,1)S(1)}, u32[]{:S(2)}, u32[]{:S(2)}) %collective-permute-start.16) | collective-permute-done | bytes 131104 | tf_op jit(solution)/shard_map/ppermute | solution.py:689
  50.1 1.9 %collective-permute-done.17 = bf16[128,512]{1,0:T(8,128)(2,1)S(1)} collective-permute-done((bf16[128,512]{1,0:T(8,128)(2,1)S(1)}, bf16[128,512]{1,0:T(8,128)(2,1)S(1)}, u32[]{:S(2)}, u32[]{:S(2)}) %collective-permute-start.17) | collective-permute-done | bytes 131104 | tf_op jit(solution)/shard_map/ppermute | solution.py:689
  (45 shorter events, 8.9 us)
Async XLA Ops:
  0.0 1.3 %copy-start = (bf16[256,2208]{0,1:T(8,128)(2,1)S(1)}, bf16[256,2208]{0,1:T(8,128)(2,1)}, u32[]{:S(2)}) copy-start(bf16[256,2208]{0,1:T(8,128)(2,1)} %param.10) | copy-start | bytes 3391492
  1.4 22.8 %copy-start.1 = (bf16[1,128,2048]{2,1,0:T(8,128)(2,1)S(1)}, bf16[1,128,2048]{2,1,0:T(8,128)(2,1)}, u32[]{:S(2)}) copy-start(bf16[1,128,2048]{2,1,0:T(8,128)(2,1)} %param.9) | copy-start | bytes 1572868
  1.4 15.2 %collective-permute-start.1 = (bf16[128,2048]{1,0:T(8,128)(2,1)}, bf16[128,2048]{1,0:T(8,128)(2,1)S(1)}, u32[]{:S(2)}, u32[]{:S(2)}) collective-permute-start(bf16[128,2048]{1,0:T(8,128)(2,1)} %bitcast.11), channel_id=1, source_target_pairs={{0,16},{8,24},{16,0},{24,8},{1,17},{9,25},{17,1},{25,9},{2,18},{10... | collective-permute-start | bytes 1572872 | tf_op jit(solution)/shard_map/ppermute | solution.py:689
  4.5 8.6 %collective-permute-start.4 = (bf16[592,256]{1,0:T(8,128)(2,1)S(1)}, bf16[592,256]{1,0:T(8,128)(2,1)S(1)}, u32[]{:S(2)}, u32[]{:S(2)}) collective-permute-start(bf16[592,256]{1,0:T(8,128)(2,1)S(1)} %get-tuple-element.28.own), channel_id=1, source_target_pairs={{0,4},{1,0},{2,1},{3,2},{7,3},{6,7},{5,6},{4,5},{8,12},{9,8},{10,9... | collective-permute-start | bytes 909320 | tf_op jit(solution)/shard_map/ppermute | solution.py:676
  6.0 8.6 %collective-permute-start.3 = (bf16[592,256]{1,0:T(8,128)(2,1)S(1)}, bf16[592,256]{1,0:T(8,128)(2,1)S(1)}, u32[]{:S(2)}, u32[]{:S(2)}) collective-permute-start(bf16[592,256]{1,0:T(8,128)(2,1)S(1)} %get-tuple-element.28.own), channel_id=1, source_target_pairs={{0,1},{1,2},{2,3},{3,7},{7,6},{6,5},{5,4},{4,0},{8,9},{9,10},{10,1... | collective-permute-start | bytes 909320 | tf_op jit(solution)/shard_map/ppermute | solution.py:676
  6.5 0.9 %copy-start.2 = (f32[2,4,2176]{2,1,0:T(4,128)S(1)}, f32[2,4,2176]{2,1,0:T(4,128)}, u32[]{:S(2)}) copy-start(f32[2,4,2176]{2,1,0:T(4,128)} %refs_1_.1) | copy-start | bytes 208900
  7.4 0.7 %copy-start.3 = (f32[2,2176]{1,0:T(2,128)S(1)}, f32[2,2176]{1,0:T(2,128)}, u32[]{:S(2)}) copy-start(f32[2,2176]{1,0:T(2,128)} %refs_2_.1) | copy-start | bytes 52228
  8.1 0.7 %copy-start.4 = (f32[2,2048]{1,0:T(2,128)S(1)}, f32[2,2048]{1,0:T(2,128)}, u32[]{:S(2)}) copy-start(f32[2,2048]{1,0:T(2,128)} %refs_6_.1) | copy-start | bytes 49156
  13.1 7.7 %collective-permute-start.7 = (bf16[592,256]{1,0:T(8,128)(2,1)S(1)}, bf16[592,256]{1,0:T(8,128)(2,1)S(1)}, u32[]{:S(2)}, u32[]{:S(2)}) collective-permute-start(bf16[592,256]{1,0:T(8,128)(2,1)S(1)} %collective-permute-done.4.down), channel_id=1, source_target_pairs={{0,4},{1,0},{2,1},{3,2},{7,3},{6,7},{5,6},{4,5},{8,12},{9,8},{10,9... | collective-permute-start | bytes 909320 | tf_op jit(solution)/shard_map/ppermute | solution.py:676
  14.6 7.7 %collective-permute-start.6 = (bf16[592,256]{1,0:T(8,128)(2,1)S(1)}, bf16[592,256]{1,0:T(8,128)(2,1)S(1)}, u32[]{:S(2)}, u32[]{:S(2)}) collective-permute-start(bf16[592,256]{1,0:T(8,128)(2,1)S(1)} %collective-permute-done.3.up), channel_id=1, source_target_pairs={{0,1},{1,2},{2,3},{3,7},{7,6},{6,5},{5,4},{4,0},{8,9},{9,10},{10,1... | collective-permute-start | bytes 909320 | tf_op jit(solution)/shard_map/ppermute | solution.py:676
  15.1 7.9 %collective-permute-start = (bf16[128,2048]{1,0:T(8,128)(2,1)}, bf16[128,2048]{1,0:T(8,128)(2,1)S(1)}, u32[]{:S(2)}, u32[]{:S(2)}) collective-permute-start(bf16[128,2048]{1,0:T(8,128)(2,1)} %bitcast.12), channel_id=1, source_target_pairs={{0,8},{8,0},{16,24},{24,16},{1,9},{9,1},{17,25},{25,17},{2,10},{10... | collective-permute-start | bytes 1572872 | tf_op jit(solution)/shard_map/ppermute | solution.py:689
  16.6 7.7 %collective-permute-start.2 = (bf16[128,2048]{1,0:T(8,128)(2,1)S(1)}, bf16[128,2048]{1,0:T(8,128)(2,1)S(1)}, u32[]{:S(2)}, u32[]{:S(2)}) collective-permute-start(bf16[128,2048]{1,0:T(8,128)(2,1)S(1)} %collective-permute-done.1.refs_2_), channel_id=1, source_target_pairs={{0,8},{8,0},{16,24},{24,16},{1,9},{9,1},{17,25},{25,17},{2,10},{10... | collective-permute-start | bytes 1572872 | tf_op jit(solution)/shard_map/ppermute | solution.py:689
  16.7 1.9 %collective-permute-start.5 = (bf16[128,256]{1,0:T(8,128)(2,1)S(1)}, bf16[128,256]{1,0:T(8,128)(2,1)S(1)}, u32[]{:S(2)}, u32[]{:S(2)}) collective-permute-start(bf16[128,256]{1,0:T(8,128)(2,1)S(1)} %get-tuple-element.34), channel_id=1, source_target_pairs={{0,8},{8,0},{16,24},{24,16},{1,9},{9,1},{17,25},{25,17},{2,10},{10... | collective-permute-start | bytes 196616 | tf_op jit(solution)/shard_map/ppermute | solution.py:689
  20.8 7.0 %collective-permute-start.10 = (bf16[592,256]{1,0:T(8,128)(2,1)S(1)}, bf16[592,256]{1,0:T(8,128)(2,1)S(1)}, u32[]{:S(2)}, u32[]{:S(2)}) collective-permute-start(bf16[592,256]{1,0:T(8,128)(2,1)S(1)} %collective-permute-done.7.down), channel_id=1, source_target_pairs={{0,4},{1,0},{2,1},{3,2},{7,3},{6,7},{5,6},{4,5},{8,12},{9,8},{10,9... | collective-permute-start | bytes 909320 | tf_op jit(solution)/shard_map/ppermute | solution.py:676
  22.3 6.9 %collective-permute-start.9 = (bf16[592,256]{1,0:T(8,128)(2,1)S(1)}, bf16[592,256]{1,0:T(8,128)(2,1)S(1)}, u32[]{:S(2)}, u32[]{:S(2)}) collective-permute-start(bf16[592,256]{1,0:T(8,128)(2,1)S(1)} %collective-permute-done.6.up), channel_id=1, source_target_pairs={{0,1},{1,2},{2,3},{3,7},{7,6},{6,5},{5,4},{4,0},{8,9},{9,10},{10,1... | collective-permute-start | bytes 909320 | tf_op jit(solution)/shard_map/ppermute | solution.py:676
  22.9 1.3 %collective-permute-start.8 = (bf16[128,256]{1,0:T(8,128)(2,1)S(1)}, bf16[128,256]{1,0:T(8,128)(2,1)S(1)}, u32[]{:S(2)}, u32[]{:S(2)}) collective-permute-start(bf16[128,256]{1,0:T(8,128)(2,1)S(1)} %get-tuple-element.38), channel_id=1, source_target_pairs={{0,8},{8,0},{16,24},{24,16},{1,9},{9,1},{17,25},{25,17},{2,10},{10... | collective-permute-start | bytes 196616 | tf_op jit(solution)/shard_map/ppermute | solution.py:689
  30.0 6.9 %collective-permute-start.13 = (bf16[304,256]{1,0:T(8,128)(2,1)}, bf16[304,256]{1,0:T(8,128)(2,1)}, u32[]{:S(2)}, u32[]{:S(2)}) collective-permute-start(bf16[304,256]{1,0:T(8,128)(2,1)} %get-tuple-element.45), channel_id=1, source_target_pairs={{0,4},{1,0},{2,1},{3,2},{7,3},{6,7},{5,6},{4,5},{8,12},{9,8},{10,9... | collective-permute-start | bytes 466952 | tf_op jit(solution)/shard_map/ppermute | solution.py:676
  31.6 5.4 %collective-permute-start.12 = (bf16[288,256]{1,0:T(8,128)(2,1)}, bf16[288,256]{1,0:T(8,128)(2,1)S(1)}, u32[]{:S(2)}, u32[]{:S(2)}) collective-permute-start(bf16[288,256]{1,0:T(8,128)(2,1)} %get-tuple-element.44), channel_id=1, source_target_pairs={{0,1},{1,2},{2,3},{3,7},{7,6},{6,5},{5,4},{4,0},{8,9},{9,10},{10,1... | collective-permute-start | bytes 442376 | tf_op jit(solution)/shard_map/ppermute | solution.py:676
  32.1 1.7 %collective-permute-start.11 = (bf16[128,256]{1,0:T(8,128)(2,1)}, bf16[128,256]{1,0:T(8,128)(2,1)}, u32[]{:S(2)}, u32[]{:S(2)}) collective-permute-start(bf16[128,256]{1,0:T(8,128)(2,1)} %get-tuple-element.43), channel_id=1, source_target_pairs={{0,8},{8,0},{16,24},{24,16},{1,9},{9,1},{17,25},{25,17},{2,10},{10... | collective-permute-start | bytes 196616 | tf_op jit(solution)/shard_map/ppermute | solution.py:689
  32.1 3.9 %collective-permute-start.14 = (bf16[64,256]{1,0:T(8,128)(2,1)}, bf16[64,256]{1,0:T(8,128)(2,1)}, u32[]{:S(2)}, u32[]{:S(2)}) collective-permute-start(bf16[64,256]{1,0:T(8,128)(2,1)} %get-tuple-element.46), channel_id=1, source_target_pairs={{0,12},{1,8},{2,9},{3,10},{7,11},{6,15},{5,14},{4,13},{8,4},{9,0},... | collective-permute-start | bytes 98312 | tf_op jit(solution)/shard_map/ppermute | solution.py:685
  43.7 2.0 %collective-permute-start.15 = (bf16[128,512]{1,0:T(8,128)(2,1)S(1)}, bf16[128,512]{1,0:T(8,128)(2,1)S(1)}, u32[]{:S(2)}, u32[]{:S(2)}) collective-permute-start(bf16[128,512]{1,0:T(8,128)(2,1)S(1)} %get-tuple-element.48), channel_id=1, source_target_pairs={{0,8},{8,0},{16,24},{24,16},{1,9},{9,1},{17,25},{25,17},{2,10},{10... | collective-permute-start | bytes 393224 | tf_op jit(solution)/shard_map/ppermute | solution.py:689
  43.8 6.4 %collective-permute-start.16 = (bf16[128,512]{1,0:T(8,128)(2,1)S(1)}, bf16[128,512]{1,0:T(8,128)(2,1)S(1)}, u32[]{:S(2)}, u32[]{:S(2)}) collective-permute-start(bf16[128,512]{1,0:T(8,128)(2,1)S(1)} %get-tuple-element.49), channel_id=1, source_target_pairs={{0,16},{8,24},{16,0},{24,8},{1,17},{9,25},{17,1},{25,9},{2,18},{10... | collective-permute-start | bytes 393224 | tf_op jit(solution)/shard_map/ppermute | solution.py:689
  45.3 6.7 %collective-permute-start.17 = (bf16[128,512]{1,0:T(8,128)(2,1)S(1)}, bf16[128,512]{1,0:T(8,128)(2,1)S(1)}, u32[]{:S(2)}, u32[]{:S(2)}) collective-permute-start(bf16[128,512]{1,0:T(8,128)(2,1)S(1)} %get-tuple-element.50), channel_id=1, source_target_pairs={{0,24},{8,16},{16,8},{24,0},{1,25},{9,17},{17,9},{25,1},{2,26},{10... | collective-permute-start | bytes 393224 | tf_op jit(solution)/shard_map/ppermute | solution.py:689
  50.1 1.9 %copy-start.9 = (bf16[1,128,2048]{2,1,0:T(8,128)(2,1)}, bf16[1,128,2048]{2,1,0:T(8,128)(2,1)S(1)}, u32[]{:S(2)}) copy-start(bf16[1,128,2048]{2,1,0:T(8,128)(2,1)S(1)} %bitcast_dynamic-update-slice_fusion.1) | copy-start | bytes 1572868
  (4 other events, 2.7 us)

commit v7 on v6

--- a/solution.py
+++ b/solution.py
@@ -265,11 +265,8 @@
     sent[half:, :] = down[columns : columns + half, :]
 
 
-def split_kernel(columns, up, down, up_part, down_part, sent, crossing):
-    cut = up_part.shape[0]
+def split_kernel(columns, up, down, sent, crossing):
     half = crossing.shape[0]
-    up_part[...] = up[:cut, :]
-    down_part[...] = down[cut:, :]
     sent[:half, :] = up[columns : columns + half, :]
     sent[half:, :] = down[columns : columns + half, :]
     crossing[...] = down[columns : columns + half, :]
@@ -289,20 +286,30 @@
     for n in range(2):
         side[LANES : LANES + half, (first - 2 + n) * depth : (first - 1 + n) * depth] = swapped[n * half : (n + 1) * half, :]
     partial[:length, columns:] = times_transposed(rows_in[...], side[...])
-    partial[length:, : table.shape[1]] = table[...]
-
-
-def second_kernel(columns, partial, rest, up, down, swapped, out, w_in):
+    other = columns + LANES
+    partial[:BLOCK, other:] = partial[:BLOCK, other:] + pltpu.roll(table[HEADER:, :LANES], half, 1)
+    partial[length:, : table.shape[1]] = table[:HEADER, :]
+
+
+def second_kernel(columns, partial, rest, up, down, swapped, out, w_in, sems):
     rows, depth = up.shape
     length = rest.shape[0]
     half = swapped.shape[0] // 2
     other = columns + LANES
-    w_in[rows:, :] = jnp.zeros((w_in.shape[0] - rows, w_in.shape[1]), jnp.bfloat16)
+    copies = []
+    for n in range(2):
+        place = w_in.at[pl.ds(other, half), pl.ds(n * depth, depth)]
+        copies.append(pltpu.make_async_copy(swapped.at[pl.ds(n * half, half)], place, sems.at[n]))
+        copies[-1].start()
+    w_in[rows:other, :] = jnp.zeros((other - rows, w_in.shape[1]), jnp.bfloat16)
+    w_in[other + half :, :] = jnp.zeros((w_in.shape[0] - other - half, w_in.shape[1]), jnp.bfloat16)
     for n, weight in enumerate((up, down)):
         w_in[:rows, n * depth : (n + 1) * depth] = weight[...]
-        w_in[other : other + half, n * depth : (n + 1) * depth] = swapped[n * half : (n + 1) * half, :]
     for n in range(w_in.shape[0] // SIDE):
         at = slice(n * SIDE, (n + 1) * SIDE)
+        if n == columns // SIDE:
+            for copy in copies:
+                copy.wait()
         out[:length, at] = partial[:length, at] + times_transposed(rest[:, : 2 * depth], w_in[at, :])
     out[length:, :] = partial[length:, :]
 
@@ -373,12 +380,9 @@
     wanted = lane - within + 2 * heads + jnp.where(backward_lane, 1, 0)
     chosen = jnp.where(row == wanted, 1.0, 0.0).astype(jnp.bfloat16)
     seen = jnp.dot(seen.astype(jnp.bfloat16), chosen, preferred_element_type=jnp.float32)
-    last = jnp.where(backward_lane[:1], seen[:1], seen[BLOCK - 1 :])
-    table[HEADER:, 0:LANES] = jnp.where((seen == last) & head_lane, 1.0, 0.0)
-    table[HEADER:, LANES : 2 * LANES] = jnp.where((seen == 0.0) & head_lane, 1.0, 0.0)
-    last = jnp.broadcast_to(last, (BLOCK, LANES))
-    table[HEADER:, 2 * LANES : 3 * LANES] = jnp.where((last == 0.0) & head_lane, 1.0, 0.0)
-    table[HEADER:, 3 * LANES : 4 * LANES] = seen
+    chosen = (row == lane // 2 * GROUP + lane % 2 * heads) & (lane < 2 * LANES // GROUP)
+    chosen = jnp.where(chosen, 1.0, 0.0).astype(jnp.bfloat16)
+    table[HEADER:, :LANES] = jnp.dot(seen.astype(jnp.bfloat16), chosen, preferred_element_type=jnp.float32)
 
 
 def head_columns(heads, d):
@@ -411,12 +415,12 @@
     def table(first, last, lanes):
         return partial[length + first : length + last, lanes]
 
+    half = far.shape[0]
+    other = columns + LANES
     w_end[:cut, :] = up_end[...]
     w_end[cut:rows, :] = down_end[...]
-    half = far.shape[0]
-    other = columns + LANES
+    w_end[other : other + half, :] = far[...]
     w_end[rows:other, :] = jnp.zeros((other - rows, depth), jnp.bfloat16)
-    w_end[other : other + half, :] = far[...]
     w_end[other + half :, :] = jnp.zeros((w_end.shape[0] - other - half, depth), jnp.bfloat16)
     edge = jnp.zeros((EDGE, LANES), jnp.float32)
     for c in range(chunks + 1):
@@ -468,11 +472,14 @@
     sums = sums[:, :LANES] + sums[:, LANES:]
     cum = jnp.where(backward_lane, sums[BLOCK:], sums[:BLOCK])
     last = jnp.where(backward_lane[:1], cum[:1], cum[BLOCK - 1 :])
-    flags = [table(HEADER, HEADER + BLOCK, slice(k * LANES, (k + 1) * LANES)) for k in range(4)]
-    tail = flags[0] * jnp.exp(last - cum) * step
-    lead = flags[1] * jnp.exp(cum)
-    fade = flags[2][:8] * jnp.exp(jnp.broadcast_to(last, (8, LANES)))
-    seen = flags[3]
+    chosen = jnp.where(row == lane // GROUP * 2 + jnp.where(backward_lane, 1, 0), 1.0, 0.0).astype(jnp.bfloat16)
+    seen = pltpu.roll(partial[:BLOCK, other:], half, 1).astype(jnp.bfloat16)
+    seen = jnp.dot(seen, chosen, preferred_element_type=jnp.float32)
+    seen_last = jnp.where(backward_lane[:1], seen[:1], seen[BLOCK - 1 :])
+    tail = jnp.where(seen == seen_last, jnp.exp(last - cum) * step, 0.0)
+    lead = jnp.where(seen == 0.0, jnp.exp(cum), 0.0)
+    last, seen_last = jnp.broadcast_to(last, (8, LANES)), jnp.broadcast_to(seen_last, (8, LANES))
+    fade = jnp.where(seen_last == 0.0, jnp.exp(last), 0.0)
     seen_turned = seen.T
     spread = [head_columns(heads, d) for d in range(2)]
     shown = (jnp.log(step) - cum).T
@@ -575,12 +582,12 @@
 ROOM = 24 * 1024 * 1024
 
 
-def call(kernel, shapes, scratch, *operands, space=IN_VMEM, aliases=None):
+def call(kernel, shapes, scratch, *operands, space=IN_VMEM, apart=0, aliases=None):
     shapes = [jax.ShapeDtypeStruct(*one) for one in shapes]
     return pl.pallas_call(
         kernel,
         out_shape=shapes,
-        in_specs=[space] * len(operands),
+        in_specs=[space] * (len(operands) - apart) + [pl.BlockSpec(memory_space=pl.ANY)] * apart,
         out_specs=[IN_VMEM] * len(shapes),
         scratch_shapes=scratch,
         input_output_aliases=aliases or {},
@@ -609,8 +616,7 @@
 
 def split(columns, up, down):
     rows, depth = up.shape
-    cut = rows // 32 * 16
-    shapes = [(cut, depth), (rows - cut, depth), (2 * STATE, depth), (STATE, depth)]
+    shapes = [(2 * STATE, depth), (STATE, depth)]
     shapes = [(one, up.dtype) for one in shapes]
     return call(functools.partial(split_kernel, columns), shapes, [], up, down)
 
@@ -635,7 +641,7 @@
     first = 2 * ring - 3
     depth = known // first
     shapes = [
-        ((length + table.shape[0], wide), jnp.float32),
+        ((length + HEADER, wide), jnp.float32),
         ((length, depth * len(ways) - known), jnp.bfloat16),
     ]
     scratch = [pltpu.VMEM((length, known), jnp.bfloat16), pltpu.VMEM((SIDE, known), jnp.bfloat16)]
@@ -644,9 +650,9 @@
 
 
 def second(columns, partial, rest, up, down, swapped):
-    scratch = [pltpu.VMEM((partial.shape[1], 2 * up.shape[1]), jnp.bfloat16)]
-    shapes = [(partial.shape, jnp.float32)]
-    return call(functools.partial(second_kernel, columns), shapes, scratch, partial, rest, up, down, swapped)[0]
+    scratch = [pltpu.VMEM((partial.shape[1], 2 * up.shape[1]), jnp.bfloat16), pltpu.SemaphoreType.DMA((2,))]
+    operands = (partial, rest, up, down, swapped)
+    return call(functools.partial(second_kernel, columns), [(partial.shape, jnp.float32)], scratch, *operands, apart=1)[0]
 
 
 def mix(heads, count, partial, rest, *others):
@@ -724,8 +730,9 @@
             beside = partial
         up, _ = lax.optimization_barrier((up, beside))
         down, _ = lax.optimization_barrier((down, beside))
-    up_part, down_part, sent, crossing = split(columns, up, down)
-    ends = [turn(up_part, 1), turn(down_part, -1)]
+    cut = own.shape[0] // 32 * 16
+    ends = [turn(up[:cut], 1), turn(down[cut:], -1)]
+    sent, crossing = split(columns, up, down)
     far = turn_across(crossing, -1)
     partial = second(columns, partial, rest, up, down, swap(sent, "seq", 1))
     results = mix(heads, count, partial, rest, *ends, far)

time: 53.1 us -> 51.4 us (0.968)
  Pallas kernels: 11.2 us -> 9.32 us
  local copies, waits for them, and re-layouts: 7.03 us -> 8.36 us
  waiting for transfers between devices: 18.9 us -> 17.7 us
    pallas_call x8, Pallas kernels: 11.2 us -> 9.32 us  [call(): pl.pallas_call(kernel, out_shape=shapes, in_specs=[space] * (len(operands...]
    slice x0 -> x2, local copies, waits for them, and re-layouts: none -> 1.34 us  [on_heads(): ends = [turn(up[:cut], 1), turn(down[cut:], -1)]]
    ppermute x8, waiting for transfers between devices: 7.89 us -> 6.83 us  [turn(): lax.ppermute(value, ('fsdp', 'batch'), [(order[i], order[(i + way) % coun...]
  transfers between devices with their start and end apart: 18 -> 18, of which waited for: 11 -> 10; matrix products, arithmetic and copies ran while one was open for 0% -> 3% of each run, Pallas kernels for 7% -> 7%
where the time goes in v7:
time: 51.4 us; the launch traced here: 51.1 us
  waiting for transfers between devices  17.7 us (34%)
  starting transfers between devices  15.5 us (30%)
  Pallas kernels  9.32 us (18%)
  local copies, waits for them, and re-layouts  8.36 us (16%)
    ppermute x9, waiting for transfers between devices, swap(): lax.ppermute(value, axis, [(i, i ^ mask) for i in range(lax.axis_size(axi...  10.3 us
    pallas_call x8, Pallas kernels, call(): pl.pallas_call(kernel, out_shape=shapes, in_specs=[space] * (len(operands...  9.32 us
    ppermute x8, starting transfers between devices, turn(): lax.ppermute(value, ('fsdp', 'batch'), [(order[i], order[(i + way) % coun...  8.1 us
    ppermute x8, waiting for transfers between devices, turn(): lax.ppermute(value, ('fsdp', 'batch'), [(order[i], order[(i + way) % coun...  6.83 us
    unnamed x20, local copies, waits for them, and re-layouts  6.27 us
    ppermute x9, starting transfers between devices, swap(): lax.ppermute(value, axis, [(i, i ^ mask) for i in range(lax.axis_size(axi...  5.68 us
    ppermute x1, starting transfers between devices, turn_across(): return lax.ppermute(value, ('seq', 'fsdp', 'batch'), pairs)  1.76 us
    slice x2, local copies, waits for them, and re-layouts, on_heads(): ends = [turn(up[:cut], 1), turn(down[cut:], -1)]  1.34 us
  transfers between devices with their start and end apart: 18, of which 10 were waited for; matrix products, arithmetic and copies ran while one was open for 3% of the time, Pallas kernels for 7%

profile of v7, /device:TPU:0, one launch (start us, length us, event | category | flops | bytes accessed | tf_op | source)
XLA Modules:
  0.0 51.1 jit_solution(723343428248710662)
XLA Ops:
  0.0 1.3 %copy-done = bf16[256,2208]{0,1:T(8,128)(2,1)S(1)} copy-done((bf16[256,2208]{0,1:T(8,128)(2,1)S(1)}, bf16[256,2208]{0,1:T(8,128)(2,1)}, u32[]{:S(2)}) %copy-start) | copy-done | bytes 1130520
  1.4 3.0 %collective-permute-start.1 = (bf16[128,2048]{1,0:T(8,128)(2,1)}, bf16[128,2048]{1,0:T(8,128)(2,1)S(1)}, u32[]{:S(2)}, u32[]{:S(2)}) collective-permute-start(bf16[128,2048]{1,0:T(8,128)(2,1)} %bitcast.11), channel_id=1, source_target_pairs={{0,16},{8,24},{16,0},{24,8},{1,17},{9,25},{17,1},{25,9},{2,18},{10... | collective-permute-start | bytes 1572872 | tf_op jit(solution)/shard_map/ppermute | solution.py:695
  4.4 1.5 %collective-permute-start.4 = (bf16[592,256]{1,0:T(8,128)(2,1)S(1)}, bf16[592,256]{1,0:T(8,128)(2,1)S(1)}, u32[]{:S(2)}, u32[]{:S(2)}) collective-permute-start(bf16[592,256]{1,0:T(8,128)(2,1)S(1)} %get-tuple-element.26.own), channel_id=1, source_target_pairs={{0,4},{1,0},{2,1},{3,2},{7,3},{6,7},{5,6},{4,5},{8,12},{9,8},{10,9... | collective-permute-start | bytes 909320 | tf_op jit(solution)/shard_map/ppermute | solution.py:682
  6.5 0.9 %copy-done.2 = f32[2,4,2176]{2,1,0:T(4,128)S(1)} copy-done((f32[2,4,2176]{2,1,0:T(4,128)S(1)}, f32[2,4,2176]{2,1,0:T(4,128)}, u32[]{:S(2)}) %copy-start.2) | copy-done | bytes 69656
  7.4 0.7 %copy-done.3 = f32[2,2176]{1,0:T(2,128)S(1)} copy-done((f32[2,2176]{1,0:T(2,128)S(1)}, f32[2,2176]{1,0:T(2,128)}, u32[]{:S(2)}) %copy-start.3) | copy-done | bytes 17432
  8.1 0.7 %copy-done.4 = f32[2,2048]{1,0:T(2,128)S(1)} copy-done((f32[2,2048]{1,0:T(2,128)S(1)}, f32[2,2048]{1,0:T(2,128)}, u32[]{:S(2)}) %copy-start.4) | copy-done | bytes 16408
  11.5 0.8 %shard_map.92.refs_6_ = f32[144,640]{1,0:T(8,128)S(1)} custom-call(s32[1,4]{1,0:T(1,128)S(1)} %copy-done.8, f32[2,4,2176]{2,1,0:T(4,128)S(1)} %copy-done.2, f32[2,2176]{1,0:T(2,128)S(1)} %copy-done.3, f32[2,32]{1,0:T(2,128)S(1)} %copy-done.5, f32[2,32]{1,0:T(2,128)S(1)} %copy-done.6, f32[2,32]{1,0:T(2,128)S(1)} %copy-done.7, f32[2,2048]{1,0:T(2,128)S(1)} %copy-done.4), custom_call_target="tpu_custom_call" | custom-call | tf_op jit(solution)/shard_map/pallas_call | solution.py:587
  12.3 0.8 %collective-permute-done.4.down = bf16[592,256]{1,0:T(8,128)(2,1)S(1)} collective-permute-done((bf16[592,256]{1,0:T(8,128)(2,1)S(1)}, bf16[592,256]{1,0:T(8,128)(2,1)S(1)}, u32[]{:S(2)}, u32[]{:S(2)}) %collective-permute-start.4) | collective-permute-done | bytes 303136 | tf_op jit(solution)/shard_map/ppermute | solution.py:682
  13.1 1.5 %collective-permute-start.7 = (bf16[592,256]{1,0:T(8,128)(2,1)S(1)}, bf16[592,256]{1,0:T(8,128)(2,1)S(1)}, u32[]{:S(2)}, u32[]{:S(2)}) collective-permute-start(bf16[592,256]{1,0:T(8,128)(2,1)S(1)} %collective-permute-done.4.down), channel_id=1, source_target_pairs={{0,4},{1,0},{2,1},{3,2},{7,3},{6,7},{5,6},{4,5},{8,12},{9,8},{10,9... | collective-permute-start | bytes 909320 | tf_op jit(solution)/shard_map/ppermute | solution.py:682
  15.1 1.5 %collective-permute-done.1.refs_2_ = bf16[128,2048]{1,0:T(8,128)(2,1)S(1)} collective-permute-done((bf16[128,2048]{1,0:T(8,128)(2,1)}, bf16[128,2048]{1,0:T(8,128)(2,1)S(1)}, u32[]{:S(2)}, u32[]{:S(2)}) %collective-permute-start.1) | collective-permute-done | bytes 524320 | tf_op jit(solution)/shard_map/ppermute | solution.py:695
  17.3 1.3 %collective-permute-done.5.swapped = bf16[128,256]{1,0:T(8,128)(2,1)S(1)} collective-permute-done((bf16[128,256]{1,0:T(8,128)(2,1)S(1)}, bf16[128,256]{1,0:T(8,128)(2,1)S(1)}, u32[]{:S(2)}, u32[]{:S(2)}) %collective-permute-start.5) | collective-permute-done | bytes 65568 | tf_op jit(solution)/shard_map/ppermute | solution.py:695
  18.6 2.2 %collective-permute-done.7.down = bf16[592,256]{1,0:T(8,128)(2,1)S(1)} collective-permute-done((bf16[592,256]{1,0:T(8,128)(2,1)S(1)}, bf16[592,256]{1,0:T(8,128)(2,1)S(1)}, u32[]{:S(2)}, u32[]{:S(2)}) %collective-permute-start.7) | collective-permute-done | bytes 303136 | tf_op jit(solution)/shard_map/ppermute | solution.py:682
  20.8 1.5 %collective-permute-start.10 = (bf16[592,256]{1,0:T(8,128)(2,1)S(1)}, bf16[592,256]{1,0:T(8,128)(2,1)S(1)}, u32[]{:S(2)}, u32[]{:S(2)}) collective-permute-start(bf16[592,256]{1,0:T(8,128)(2,1)S(1)} %collective-permute-done.7.down), channel_id=1, source_target_pairs={{0,4},{1,0},{2,1},{3,2},{7,3},{6,7},{5,6},{4,5},{8,12},{9,8},{10,9... | collective-permute-start | bytes 909320 | tf_op jit(solution)/shard_map/ppermute | solution.py:682
  23.0 1.2 %collective-permute-done.8.refs_5_ = bf16[128,256]{1,0:T(8,128)(2,1)S(1)} collective-permute-done((bf16[128,256]{1,0:T(8,128)(2,1)S(1)}, bf16[128,256]{1,0:T(8,128)(2,1)S(1)}, u32[]{:S(2)}, u32[]{:S(2)}) %collective-permute-start.8) | collective-permute-done | bytes 65568 | tf_op jit(solution)/shard_map/ppermute | solution.py:695
  24.2 1.3 %shard_map.95 = (f32[528,768]{1,0:T(8,128)S(1)}, bf16[512,768]{1,0:T(8,128)(2,1)S(1)}) custom-call(bf16[128,2048]{1,0:T(8,128)(2,1)S(1)} %bitcast.13, bf16[128,2048]{1,0:T(8,128)(2,1)S(1)} %collective-permute-done.refs_1_, bf16[128,2048]{1,0:T(8,128)(2,1)S(1)} %collective-permute-done.1.refs_2_, bf16[128,2048]{1,0:T(8,128)(2,1)S(1)} %collective-permute-done.2.refs_3_, ...), custom_call_target="tpu_custom_call" | custom-call | tf_op jit(solution)/shard_map/pallas_call | solution.py:587
  25.5 2.3 %collective-permute-done.10.down = bf16[592,256]{1,0:T(8,128)(2,1)S(1)} collective-permute-done((bf16[592,256]{1,0:T(8,128)(2,1)S(1)}, bf16[592,256]{1,0:T(8,128)(2,1)S(1)}, u32[]{:S(2)}, u32[]{:S(2)}) %collective-permute-start.10) | collective-permute-done | bytes 303136 | tf_op jit(solution)/shard_map/ppermute | solution.py:682
  28.5 1.7 %collective-permute-start.13 = (bf16[304,256]{1,0:T(8,128)(2,1)}, bf16[304,256]{1,0:T(8,128)(2,1)S(1)}, u32[]{:S(2)}, u32[]{:S(2)}) collective-permute-start(bf16[304,256]{1,0:T(8,128)(2,1)} %slice.7), channel_id=1, source_target_pairs={{0,4},{1,0},{2,1},{3,2},{7,3},{6,7},{5,6},{4,5},{8,12},{9,8},{10,9... | collective-permute-start | bytes 466952 | tf_op jit(solution)/shard_map/ppermute | solution.py:682
  31.3 1.8 %collective-permute-start.14 = (bf16[64,256]{1,0:T(8,128)(2,1)S(1)}, bf16[64,256]{1,0:T(8,128)(2,1)S(1)}, u32[]{:S(2)}, u32[]{:S(2)}) collective-permute-start(bf16[64,256]{1,0:T(8,128)(2,1)S(1)} %get-tuple-element.42), channel_id=1, source_target_pairs={{0,12},{1,8},{2,9},{3,10},{7,11},{6,15},{5,14},{4,13},{8,4},{9,0},... | collective-permute-start | bytes 98312 | tf_op jit(solution)/shard_map/ppermute | solution.py:691
  33.1 1.1 %shard_map.97.partial = f32[528,768]{1,0:T(8,128)S(1)} custom-call(f32[528,768]{1,0:T(8,128)S(1)} %get-tuple-element.37.partial, bf16[512,768]{1,0:T(8,128)(2,1)S(1)} %get-tuple-element.38.rest, bf16[592,256]{1,0:T(8,128)(2,1)S(1)} %collective-permute-done.9.up, bf16[592,256]{1,0:T(8,128)(2,1)S(1)} %collective-permute-done.10.down, ...), custom_call_target="tpu_custom_call" | custom-call | tf_op jit(solution)/shard_map/pallas_call | solution.py:587
  34.8 1.5 %collective-permute-done.12.up_end = bf16[288,256]{1,0:T(8,128)(2,1)S(1)} collective-permute-done((bf16[288,256]{1,0:T(8,128)(2,1)}, bf16[288,256]{1,0:T(8,128)(2,1)S(1)}, u32[]{:S(2)}, u32[]{:S(2)}) %collective-permute-start.12) | collective-permute-done | bytes 147488 | tf_op jit(solution)/shard_map/ppermute | solution.py:682
  36.2 5.8 %shard_map.98 = (bf16[128,512]{1,0:T(8,128)(2,1)S(1)}, bf16[128,512]{1,0:T(8,128)(2,1)S(1)}, bf16[128,512]{1,0:T(8,128)(2,1)S(1)}, bf16[128,512]{1,0:T(8,128)(2,1)S(1)}) custom-call(f32[528,768]{1,0:T(8,128)S(1)} %shard_map.97.partial, bf16[512,768]{1,0:T(8,128)(2,1)S(1)} %get-tuple-element.38.rest, bf16[288,256]{1,0:T(8,128)(2,1)S(1)} %collective-permute-done.12.up_end, ...), custom_call_target="tpu_custom_call" | custom-call | tf_op jit(solution)/shard_map/pallas_call | solution.py:587
  42.1 1.6 %collective-permute-start.16 = (bf16[128,512]{1,0:T(8,128)(2,1)S(1)}, bf16[128,512]{1,0:T(8,128)(2,1)S(1)}, u32[]{:S(2)}, u32[]{:S(2)}) collective-permute-start(bf16[128,512]{1,0:T(8,128)(2,1)S(1)} %get-tuple-element.45), channel_id=1, source_target_pairs={{0,16},{8,24},{16,0},{24,8},{1,17},{9,25},{17,1},{25,9},{2,18},{10... | collective-permute-start | bytes 393224 | tf_op jit(solution)/shard_map/ppermute | solution.py:695
  44.1 4.4 %collective-permute-done.16 = bf16[128,512]{1,0:T(8,128)(2,1)S(1)} collective-permute-done((bf16[128,512]{1,0:T(8,128)(2,1)S(1)}, bf16[128,512]{1,0:T(8,128)(2,1)S(1)}, u32[]{:S(2)}, u32[]{:S(2)}) %collective-permute-start.16) | collective-permute-done | bytes 131104 | tf_op jit(solution)/shard_map/ppermute | solution.py:695
  48.5 1.9 %collective-permute-done.17 = bf16[128,512]{1,0:T(8,128)(2,1)S(1)} collective-permute-done((bf16[128,512]{1,0:T(8,128)(2,1)S(1)}, bf16[128,512]{1,0:T(8,128)(2,1)S(1)}, u32[]{:S(2)}, u32[]{:S(2)}) %collective-permute-start.17) | collective-permute-done | bytes 131104 | tf_op jit(solution)/shard_map/ppermute | solution.py:695
  (47 shorter events, 8.7 us)
Async XLA Ops:
  0.0 1.3 %copy-start = (bf16[256,2208]{0,1:T(8,128)(2,1)S(1)}, bf16[256,2208]{0,1:T(8,128)(2,1)}, u32[]{:S(2)}) copy-start(bf16[256,2208]{0,1:T(8,128)(2,1)} %param.10) | copy-start | bytes 3391492
  1.4 15.2 %collective-permute-start.1 = (bf16[128,2048]{1,0:T(8,128)(2,1)}, bf16[128,2048]{1,0:T(8,128)(2,1)S(1)}, u32[]{:S(2)}, u32[]{:S(2)}) collective-permute-start(bf16[128,2048]{1,0:T(8,128)(2,1)} %bitcast.11), channel_id=1, source_target_pairs={{0,16},{8,24},{16,0},{24,8},{1,17},{9,25},{17,1},{25,9},{2,18},{10... | collective-permute-start | bytes 1572872 | tf_op jit(solution)/shard_map/ppermute | solution.py:695
  4.4 8.6 %collective-permute-start.4 = (bf16[592,256]{1,0:T(8,128)(2,1)S(1)}, bf16[592,256]{1,0:T(8,128)(2,1)S(1)}, u32[]{:S(2)}, u32[]{:S(2)}) collective-permute-start(bf16[592,256]{1,0:T(8,128)(2,1)S(1)} %get-tuple-element.26.own), channel_id=1, source_target_pairs={{0,4},{1,0},{2,1},{3,2},{7,3},{6,7},{5,6},{4,5},{8,12},{9,8},{10,9... | collective-permute-start | bytes 909320 | tf_op jit(solution)/shard_map/ppermute | solution.py:682
  5.9 8.6 %collective-permute-start.3 = (bf16[592,256]{1,0:T(8,128)(2,1)S(1)}, bf16[592,256]{1,0:T(8,128)(2,1)S(1)}, u32[]{:S(2)}, u32[]{:S(2)}) collective-permute-start(bf16[592,256]{1,0:T(8,128)(2,1)S(1)} %get-tuple-element.26.own), channel_id=1, source_target_pairs={{0,1},{1,2},{2,3},{3,7},{7,6},{6,5},{5,4},{4,0},{8,9},{9,10},{10,1... | collective-permute-start | bytes 909320 | tf_op jit(solution)/shard_map/ppermute | solution.py:682
  6.5 0.9 %copy-start.2 = (f32[2,4,2176]{2,1,0:T(4,128)S(1)}, f32[2,4,2176]{2,1,0:T(4,128)}, u32[]{:S(2)}) copy-start(f32[2,4,2176]{2,1,0:T(4,128)} %refs_1_.1) | copy-start | bytes 208900
  7.4 0.7 %copy-start.3 = (f32[2,2176]{1,0:T(2,128)S(1)}, f32[2,2176]{1,0:T(2,128)}, u32[]{:S(2)}) copy-start(f32[2,2176]{1,0:T(2,128)} %refs_2_.1) | copy-start | bytes 52228
  8.1 0.7 %copy-start.4 = (f32[2,2048]{1,0:T(2,128)S(1)}, f32[2,2048]{1,0:T(2,128)}, u32[]{:S(2)}) copy-start(f32[2,2048]{1,0:T(2,128)} %refs_6_.1) | copy-start | bytes 49156
  13.1 7.7 %collective-permute-start.7 = (bf16[592,256]{1,0:T(8,128)(2,1)S(1)}, bf16[592,256]{1,0:T(8,128)(2,1)S(1)}, u32[]{:S(2)}, u32[]{:S(2)}) collective-permute-start(bf16[592,256]{1,0:T(8,128)(2,1)S(1)} %collective-permute-done.4.down), channel_id=1, source_target_pairs={{0,4},{1,0},{2,1},{3,2},{7,3},{6,7},{5,6},{4,5},{8,12},{9,8},{10,9... | collective-permute-start | bytes 909320 | tf_op jit(solution)/shard_map/ppermute | solution.py:682
  14.6 7.7 %collective-permute-start.6 = (bf16[592,256]{1,0:T(8,128)(2,1)S(1)}, bf16[592,256]{1,0:T(8,128)(2,1)S(1)}, u32[]{:S(2)}, u32[]{:S(2)}) collective-permute-start(bf16[592,256]{1,0:T(8,128)(2,1)S(1)} %collective-permute-done.3.up), channel_id=1, source_target_pairs={{0,1},{1,2},{2,3},{3,7},{7,6},{6,5},{5,4},{4,0},{8,9},{9,10},{10,1... | collective-permute-start | bytes 909320 | tf_op jit(solution)/shard_map/ppermute | solution.py:682
  15.1 7.9 %collective-permute-start = (bf16[128,2048]{1,0:T(8,128)(2,1)}, bf16[128,2048]{1,0:T(8,128)(2,1)S(1)}, u32[]{:S(2)}, u32[]{:S(2)}) collective-permute-start(bf16[128,2048]{1,0:T(8,128)(2,1)} %bitcast.12), channel_id=1, source_target_pairs={{0,8},{8,0},{16,24},{24,16},{1,9},{9,1},{17,25},{25,17},{2,10},{10... | collective-permute-start | bytes 1572872 | tf_op jit(solution)/shard_map/ppermute | solution.py:695
  16.6 7.6 %collective-permute-start.2 = (bf16[128,2048]{1,0:T(8,128)(2,1)S(1)}, bf16[128,2048]{1,0:T(8,128)(2,1)S(1)}, u32[]{:S(2)}, u32[]{:S(2)}) collective-permute-start(bf16[128,2048]{1,0:T(8,128)(2,1)S(1)} %collective-permute-done.1.refs_2_), channel_id=1, source_target_pairs={{0,8},{8,0},{16,24},{24,16},{1,9},{9,1},{17,25},{25,17},{2,10},{10... | collective-permute-start | bytes 1572872 | tf_op jit(solution)/shard_map/ppermute | solution.py:695
  16.6 7.6 %copy-start.1 = (bf16[1,128,2048]{2,1,0:T(8,128)(2,1)S(1)}, bf16[1,128,2048]{2,1,0:T(8,128)(2,1)}, u32[]{:S(2)}) copy-start(bf16[1,128,2048]{2,1,0:T(8,128)(2,1)} %param.9) | copy-start | bytes 1572868
  16.7 1.9 %collective-permute-start.5 = (bf16[128,256]{1,0:T(8,128)(2,1)S(1)}, bf16[128,256]{1,0:T(8,128)(2,1)S(1)}, u32[]{:S(2)}, u32[]{:S(2)}) collective-permute-start(bf16[128,256]{1,0:T(8,128)(2,1)S(1)} %get-tuple-element.32), channel_id=1, source_target_pairs={{0,8},{8,0},{16,24},{24,16},{1,9},{9,1},{17,25},{25,17},{2,10},{10... | collective-permute-start | bytes 196616 | tf_op jit(solution)/shard_map/ppermute | solution.py:695
  20.8 7.0 %collective-permute-start.10 = (bf16[592,256]{1,0:T(8,128)(2,1)S(1)}, bf16[592,256]{1,0:T(8,128)(2,1)S(1)}, u32[]{:S(2)}, u32[]{:S(2)}) collective-permute-start(bf16[592,256]{1,0:T(8,128)(2,1)S(1)} %collective-permute-done.7.down), channel_id=1, source_target_pairs={{0,4},{1,0},{2,1},{3,2},{7,3},{6,7},{5,6},{4,5},{8,12},{9,8},{10,9... | collective-permute-start | bytes 909320 | tf_op jit(solution)/shard_map/ppermute | solution.py:682
  22.3 7.9 %collective-permute-start.9 = (bf16[592,256]{1,0:T(8,128)(2,1)S(1)}, bf16[592,256]{1,0:T(8,128)(2,1)S(1)}, u32[]{:S(2)}, u32[]{:S(2)}) collective-permute-start(bf16[592,256]{1,0:T(8,128)(2,1)S(1)} %collective-permute-done.6.up), channel_id=1, source_target_pairs={{0,1},{1,2},{2,3},{3,7},{7,6},{6,5},{5,4},{4,0},{8,9},{9,10},{10,1... | collective-permute-start | bytes 909320 | tf_op jit(solution)/shard_map/ppermute | solution.py:682
  22.9 1.3 %collective-permute-start.8 = (bf16[128,256]{1,0:T(8,128)(2,1)S(1)}, bf16[128,256]{1,0:T(8,128)(2,1)S(1)}, u32[]{:S(2)}, u32[]{:S(2)}) collective-permute-start(bf16[128,256]{1,0:T(8,128)(2,1)S(1)} %get-tuple-element.36), channel_id=1, source_target_pairs={{0,8},{8,0},{16,24},{24,16},{1,9},{9,1},{17,25},{25,17},{2,10},{10... | collective-permute-start | bytes 196616 | tf_op jit(solution)/shard_map/ppermute | solution.py:695
  28.5 7.7 %collective-permute-start.13 = (bf16[304,256]{1,0:T(8,128)(2,1)}, bf16[304,256]{1,0:T(8,128)(2,1)S(1)}, u32[]{:S(2)}, u32[]{:S(2)}) collective-permute-start(bf16[304,256]{1,0:T(8,128)(2,1)} %slice.7), channel_id=1, source_target_pairs={{0,4},{1,0},{2,1},{3,2},{7,3},{6,7},{5,6},{4,5},{8,12},{9,8},{10,9... | collective-permute-start | bytes 466952 | tf_op jit(solution)/shard_map/ppermute | solution.py:682
  30.9 5.4 %collective-permute-start.12 = (bf16[288,256]{1,0:T(8,128)(2,1)}, bf16[288,256]{1,0:T(8,128)(2,1)S(1)}, u32[]{:S(2)}, u32[]{:S(2)}) collective-permute-start(bf16[288,256]{1,0:T(8,128)(2,1)} %slice.6), channel_id=1, source_target_pairs={{0,1},{1,2},{2,3},{3,7},{7,6},{6,5},{5,4},{4,0},{8,9},{9,10},{10,1... | collective-permute-start | bytes 442376 | tf_op jit(solution)/shard_map/ppermute | solution.py:682
  31.2 1.8 %collective-permute-start.11 = (bf16[128,256]{1,0:T(8,128)(2,1)S(1)}, bf16[128,256]{1,0:T(8,128)(2,1)S(1)}, u32[]{:S(2)}, u32[]{:S(2)}) collective-permute-start(bf16[128,256]{1,0:T(8,128)(2,1)S(1)} %get-tuple-element.41), channel_id=1, source_target_pairs={{0,8},{8,0},{16,24},{24,16},{1,9},{9,1},{17,25},{25,17},{2,10},{10... | collective-permute-start | bytes 196616 | tf_op jit(solution)/shard_map/ppermute | solution.py:695
  31.3 3.4 %collective-permute-start.14 = (bf16[64,256]{1,0:T(8,128)(2,1)S(1)}, bf16[64,256]{1,0:T(8,128)(2,1)S(1)}, u32[]{:S(2)}, u32[]{:S(2)}) collective-permute-start(bf16[64,256]{1,0:T(8,128)(2,1)S(1)} %get-tuple-element.42), channel_id=1, source_target_pairs={{0,12},{1,8},{2,9},{3,10},{7,11},{6,15},{5,14},{4,13},{8,4},{9,0},... | collective-permute-start | bytes 98312 | tf_op jit(solution)/shard_map/ppermute | solution.py:691
  42.0 2.0 %collective-permute-start.15 = (bf16[128,512]{1,0:T(8,128)(2,1)S(1)}, bf16[128,512]{1,0:T(8,128)(2,1)S(1)}, u32[]{:S(2)}, u32[]{:S(2)}) collective-permute-start(bf16[128,512]{1,0:T(8,128)(2,1)S(1)} %get-tuple-element.44), channel_id=1, source_target_pairs={{0,8},{8,0},{16,24},{24,16},{1,9},{9,1},{17,25},{25,17},{2,10},{10... | collective-permute-start | bytes 393224 | tf_op jit(solution)/shard_map/ppermute | solution.py:695
  42.1 6.4 %collective-permute-start.16 = (bf16[128,512]{1,0:T(8,128)(2,1)S(1)}, bf16[128,512]{1,0:T(8,128)(2,1)S(1)}, u32[]{:S(2)}, u32[]{:S(2)}) collective-permute-start(bf16[128,512]{1,0:T(8,128)(2,1)S(1)} %get-tuple-element.45), channel_id=1, source_target_pairs={{0,16},{8,24},{16,0},{24,8},{1,17},{9,25},{17,1},{25,9},{2,18},{10... | collective-permute-start | bytes 393224 | tf_op jit(solution)/shard_map/ppermute | solution.py:695
  43.7 6.7 %collective-permute-start.17 = (bf16[128,512]{1,0:T(8,128)(2,1)S(1)}, bf16[128,512]{1,0:T(8,128)(2,1)S(1)}, u32[]{:S(2)}, u32[]{:S(2)}) collective-permute-start(bf16[128,512]{1,0:T(8,128)(2,1)S(1)} %get-tuple-element.46), channel_id=1, source_target_pairs={{0,24},{8,16},{16,8},{24,0},{1,25},{9,17},{17,9},{25,1},{2,26},{10... | collective-permute-start | bytes 393224 | tf_op jit(solution)/shard_map/ppermute | solution.py:695
  48.5 1.9 %copy-start.9 = (bf16[1,128,2048]{2,1,0:T(8,128)(2,1)}, bf16[1,128,2048]{2,1,0:T(8,128)(2,1)S(1)}, u32[]{:S(2)}) copy-start(bf16[1,128,2048]{2,1,0:T(8,128)(2,1)S(1)} %bitcast_dynamic-update-slice_fusion.1) | copy-start | bytes 1572868
  (4 other events, 2.7 us)

commit v8 on v7

--- a/solution.py
+++ b/solution.py
@@ -502,65 +502,72 @@
 
     short = 64
 
-    def conv_rows(i, carry):
-        at = pl.multiple_of(i * short, short)
-        for c in range(chunks + 1):
-            taps = [padded[c, pl.ds(at + EDGE - 3 + k, short), :] for k in range(7)]
-            lanes = slice(c * LANES, (c + 1) * LANES)
-            for d in range(2):
-                acc = table(8 + d, 9 + d, lanes)
-                for k in range(KERNEL):
-                    n = d * KERNEL + k
-                    acc = acc + table(n, n + 1, lanes) * taps[k if d == 0 else 6 - k]
-                half = 0.5 * acc
-                value = half + half * jnp.tanh(half)
-                if c < chunks:
-                    xs[d, pl.ds(at, short), lanes] = value.astype(jnp.bfloat16)
-                else:
-                    high = lax.broadcasted_iota(jnp.int32, (short, LANES), 1) >= STATE
-                    cs[d, pl.ds(at, short), :] = jnp.where(high, value, 0.0).astype(jnp.bfloat16)
-                    bs[d, pl.ds(at, short), :] = jnp.where(
-                        high, pltpu.roll(value, STATE, 1), 0.0
-                    ).astype(jnp.bfloat16)
-        return carry
-
-    lax.fori_loop(0, length // short, conv_rows, 0)
+    def convolve(c, i):
+        at = i * short
+        taps = [padded[c, at + EDGE - 3 + k : at + EDGE - 3 + k + short, :] for k in range(7)]
+        rows_at = slice(at, at + short)
+        lanes = slice(c * LANES, (c + 1) * LANES)
+        for d in range(2):
+            acc = table(8 + d, 9 + d, lanes)
+            for k in range(KERNEL):
+                n = d * KERNEL + k
+                acc = acc + table(n, n + 1, lanes) * taps[k if d == 0 else 6 - k]
+            half = 0.5 * acc
+            value = half + half * jnp.tanh(half)
+            if c < chunks:
+                xs[d, rows_at, lanes] = value.astype(jnp.bfloat16)
+            else:
+                high = lax.broadcasted_iota(jnp.int32, (short, LANES), 1) >= STATE
+                cs[d, rows_at, :] = jnp.where(high, value, 0.0).astype(jnp.bfloat16)
+                bs[d, rows_at, :] = jnp.where(high, pltpu.roll(value, STATE, 1), 0.0).astype(jnp.bfloat16)
 
     group = SIDE // HEAD_DIM
     lane_head = lax.broadcasted_iota(jnp.int32, (BLOCK, SIDE), 1) // HEAD_DIM
-    for i in range(blocks):
-        for d in range(2):
-            b = i if d == 0 else blocks - 1 - i
-            at = slice(b * BLOCK, (b + 1) * BLOCK)
-            c_part = cs[d, at, :]
-            b_part = bs[d, at, :]
-            scores = times_transposed(c_part, b_part)
+    known = {}
+
+    def scan_block(q, d, b):
+        at = slice(b * BLOCK, (b + 1) * BLOCK)
+        lanes = slice(q * SIDE, (q + 1) * SIDE)
+        c_part = cs[d, at, :]
+        b_part = bs[d, at, :]
+        if (d, b) not in known:
             ordered = (row >= lane) if d == 0 else (row <= lane)
             n = b * GROUP + d * heads
             bar = jnp.where(ordered & (seen[:, n : n + 1] == seen_turned[n : n + 1, :]), 0.0, -1e30)
-            before = state[d]
-            carried = jnp.dot(c_part, before.astype(jnp.bfloat16), preferred_element_type=jnp.float32)
-            x_all = xs[d, at, :]
-            local_end = lax.dot_general(
-                b_part, tails[d, at, :] * x_all, (((0,), (0,)), ((), ())), preferred_element_type=jnp.float32
-            )
-            state[d] = fade_wide[d][b : b + 1] * before + local_end
-            for q in range(columns // SIDE):
-                some = []
-                for h in range(q * group, (q + 1) * group):
-                    n = b * GROUP + d * heads + h
-                    gap = cum[:, n : n + 1] + (shown[n : n + 1, :] + bar)
-                    some.append((jnp.exp(gap) * scores).astype(jnp.bfloat16))
-                lanes = slice(q * SIDE, (q + 1) * SIDE)
-                x_part = x_all[:, lanes]
-                none = jnp.zeros_like(x_part)
-                spaced = jnp.concatenate([jnp.where(lane_head == h, x_part, none) for h in range(group)], axis=0)
-                inner = jnp.dot(jnp.concatenate(some, axis=1), spaced, preferred_element_type=jnp.float32)
-                ys[d, at, lanes] = (
-                    inner
-                    + leads[d, at, lanes].astype(jnp.float32) * carried[:, lanes]
-                    + table(12 + d, 13 + d, lanes) * x_part.astype(jnp.float32)
-                )
+            known[d, b] = times_transposed(c_part, b_part), bar
+        scores, bar = known[d, b]
+        before = state[d, :, lanes]
+        carried = jnp.dot(c_part, before.astype(jnp.bfloat16), preferred_element_type=jnp.float32)
+        x_part = xs[d, at, lanes]
+        local_end = lax.dot_general(
+            b_part, tails[d, at, lanes] * x_part, (((0,), (0,)), ((), ())), preferred_element_type=jnp.float32
+        )
+        state[d, :, lanes] = fade_wide[d][b : b + 1, lanes] * before + local_end
+        some = []
+        for h in range(q * group, (q + 1) * group):
+            n = b * GROUP + d * heads + h
+            gap = cum[:, n : n + 1] + (shown[n : n + 1, :] + bar)
+            some.append((jnp.exp(gap) * scores).astype(jnp.bfloat16))
+        none = jnp.zeros_like(x_part)
+        spaced = jnp.concatenate([jnp.where(lane_head == h, x_part, none) for h in range(group)], axis=0)
+        inner = jnp.dot(jnp.concatenate(some, axis=1), spaced, preferred_element_type=jnp.float32)
+        ys[d, at, lanes] = (
+            inner
+            + leads[d, at, lanes].astype(jnp.float32) * carried
+            + table(12 + d, 13 + d, lanes) * x_part.astype(jnp.float32)
+        )
+
+    in_group = SIDE // LANES
+    for i in range(length // short):
+        for c in (chunks, *range(in_group)):
+            convolve(c, i)
+    for q in range(columns // SIDE):
+        for i in range(blocks):
+            for d in range(2):
+                scan_block(q, d, i if d == 0 else blocks - 1 - i)
+            for c in range((q + 1) * in_group, min((q + 2) * in_group, chunks)):
+                for part in range(BLOCK // short):
+                    convolve(c, i * (BLOCK // short) + part)
 
     head_row = lax.broadcasted_iota(jnp.int32, (SIDE, SIDE), 0) // HEAD_DIM
     head_col = lax.broadcasted_iota(jnp.int32, (SIDE, SIDE), 1) // HEAD_DIM

time: 51.4 us -> 50.6 us (0.984)
  Pallas kernels: 9.32 us -> 8.52 us
    pallas_call x8, Pallas kernels: 9.32 us -> 8.52 us  [call(): pl.pallas_call(kernel, out_shape=shapes, in_specs=[space] * (len(operands...]
where the time goes in v8:
time: 50.6 us; the launch traced here: 50.3 us
  waiting for transfers between devices  17.7 us (35%)
  starting transfers between devices  15.5 us (31%)
  Pallas kernels  8.52 us (17%)
  local copies, waits for them, and re-layouts  8.36 us (17%)
    ppermute x9, waiting for transfers between devices, swap(): lax.ppermute(value, axis, [(i, i ^ mask) for i in range(lax.axis_size(axi...  10.3 us
    pallas_call x8, Pallas kernels, call(): pl.pallas_call(kernel, out_shape=shapes, in_specs=[space] * (len(operands...  8.52 us
    ppermute x8, starting transfers between devices, turn(): lax.ppermute(value, ('fsdp', 'batch'), [(order[i], order[(i + way) % coun...  8.1 us
    ppermute x8, waiting for transfers between devices, turn(): lax.ppermute(value, ('fsdp', 'batch'), [(order[i], order[(i + way) % coun...  6.83 us
    unnamed x20, local copies, waits for them, and re-layouts  6.27 us
    ppermute x9, starting transfers between devices, swap(): lax.ppermute(value, axis, [(i, i ^ mask) for i in range(lax.axis_size(axi...  5.68 us
    ppermute x1, starting transfers between devices, turn_across(): return lax.ppermute(value, ('seq', 'fsdp', 'batch'), pairs)  1.76 us
    slice x2, local copies, waits for them, and re-layouts, on_heads(): ends = [turn(up[:cut], 1), turn(down[cut:], -1)]  1.34 us
  transfers between devices with their start and end apart: 18, of which 10 were waited for; matrix products, arithmetic and copies ran while one was open for 3% of the time, Pallas kernels for 7%

profile of v8, /device:TPU:0, one launch (start us, length us, event | category | flops | bytes accessed | tf_op | source)
XLA Modules:
  0.0 50.3 jit_solution(14705300231251923487)
XLA Ops:
  0.0 1.3 %copy-done = bf16[256,2208]{0,1:T(8,128)(2,1)S(1)} copy-done((bf16[256,2208]{0,1:T(8,128)(2,1)S(1)}, bf16[256,2208]{0,1:T(8,128)(2,1)}, u32[]{:S(2)}) %copy-start) | copy-done | bytes 1130520
  1.4 3.0 %collective-permute-start.1 = (bf16[128,2048]{1,0:T(8,128)(2,1)}, bf16[128,2048]{1,0:T(8,128)(2,1)S(1)}, u32[]{:S(2)}, u32[]{:S(2)}) collective-permute-start(bf16[128,2048]{1,0:T(8,128)(2,1)} %bitcast.11), channel_id=1, source_target_pairs={{0,16},{8,24},{16,0},{24,8},{1,17},{9,25},{17,1},{25,9},{2,18},{10... | collective-permute-start | bytes 1572872 | tf_op jit(solution)/shard_map/ppermute | solution.py:702
  4.4 1.5 %collective-permute-start.4 = (bf16[592,256]{1,0:T(8,128)(2,1)S(1)}, bf16[592,256]{1,0:T(8,128)(2,1)S(1)}, u32[]{:S(2)}, u32[]{:S(2)}) collective-permute-start(bf16[592,256]{1,0:T(8,128)(2,1)S(1)} %get-tuple-element.26.own), channel_id=1, source_target_pairs={{0,4},{1,0},{2,1},{3,2},{7,3},{6,7},{5,6},{4,5},{8,12},{9,8},{10,9... | collective-permute-start | bytes 909320 | tf_op jit(solution)/shard_map/ppermute | solution.py:689
  6.5 0.9 %copy-done.2 = f32[2,4,2176]{2,1,0:T(4,128)S(1)} copy-done((f32[2,4,2176]{2,1,0:T(4,128)S(1)}, f32[2,4,2176]{2,1,0:T(4,128)}, u32[]{:S(2)}) %copy-start.2) | copy-done | bytes 69656
  7.4 0.7 %copy-done.3 = f32[2,2176]{1,0:T(2,128)S(1)} copy-done((f32[2,2176]{1,0:T(2,128)S(1)}, f32[2,2176]{1,0:T(2,128)}, u32[]{:S(2)}) %copy-start.3) | copy-done | bytes 17432
  8.1 0.7 %copy-done.4 = f32[2,2048]{1,0:T(2,128)S(1)} copy-done((f32[2,2048]{1,0:T(2,128)S(1)}, f32[2,2048]{1,0:T(2,128)}, u32[]{:S(2)}) %copy-start.4) | copy-done | bytes 16408
  11.5 0.8 %shard_map.92.refs_6_ = f32[144,640]{1,0:T(8,128)S(1)} custom-call(s32[1,4]{1,0:T(1,128)S(1)} %copy-done.8, f32[2,4,2176]{2,1,0:T(4,128)S(1)} %copy-done.2, f32[2,2176]{1,0:T(2,128)S(1)} %copy-done.3, f32[2,32]{1,0:T(2,128)S(1)} %copy-done.5, f32[2,32]{1,0:T(2,128)S(1)} %copy-done.6, f32[2,32]{1,0:T(2,128)S(1)} %copy-done.7, f32[2,2048]{1,0:T(2,128)S(1)} %copy-done.4), custom_call_target="tpu_custom_call" | custom-call | tf_op jit(solution)/shard_map/pallas_call | solution.py:594
  12.3 0.8 %collective-permute-done.4.down = bf16[592,256]{1,0:T(8,128)(2,1)S(1)} collective-permute-done((bf16[592,256]{1,0:T(8,128)(2,1)S(1)}, bf16[592,256]{1,0:T(8,128)(2,1)S(1)}, u32[]{:S(2)}, u32[]{:S(2)}) %collective-permute-start.4) | collective-permute-done | bytes 303136 | tf_op jit(solution)/shard_map/ppermute | solution.py:689
  13.1 1.5 %collective-permute-start.7 = (bf16[592,256]{1,0:T(8,128)(2,1)S(1)}, bf16[592,256]{1,0:T(8,128)(2,1)S(1)}, u32[]{:S(2)}, u32[]{:S(2)}) collective-permute-start(bf16[592,256]{1,0:T(8,128)(2,1)S(1)} %collective-permute-done.4.down), channel_id=1, source_target_pairs={{0,4},{1,0},{2,1},{3,2},{7,3},{6,7},{5,6},{4,5},{8,12},{9,8},{10,9... | collective-permute-start | bytes 909320 | tf_op jit(solution)/shard_map/ppermute | solution.py:689
  15.1 1.5 %collective-permute-done.1.refs_2_ = bf16[128,2048]{1,0:T(8,128)(2,1)S(1)} collective-permute-done((bf16[128,2048]{1,0:T(8,128)(2,1)}, bf16[128,2048]{1,0:T(8,128)(2,1)S(1)}, u32[]{:S(2)}, u32[]{:S(2)}) %collective-permute-start.1) | collective-permute-done | bytes 524320 | tf_op jit(solution)/shard_map/ppermute | solution.py:702
  17.3 1.3 %collective-permute-done.5.swapped = bf16[128,256]{1,0:T(8,128)(2,1)S(1)} collective-permute-done((bf16[128,256]{1,0:T(8,128)(2,1)S(1)}, bf16[128,256]{1,0:T(8,128)(2,1)S(1)}, u32[]{:S(2)}, u32[]{:S(2)}) %collective-permute-start.5) | collective-permute-done | bytes 65568 | tf_op jit(solution)/shard_map/ppermute | solution.py:702
  18.6 2.2 %collective-permute-done.7.down = bf16[592,256]{1,0:T(8,128)(2,1)S(1)} collective-permute-done((bf16[592,256]{1,0:T(8,128)(2,1)S(1)}, bf16[592,256]{1,0:T(8,128)(2,1)S(1)}, u32[]{:S(2)}, u32[]{:S(2)}) %collective-permute-start.7) | collective-permute-done | bytes 303136 | tf_op jit(solution)/shard_map/ppermute | solution.py:689
  20.8 1.5 %collective-permute-start.10 = (bf16[592,256]{1,0:T(8,128)(2,1)S(1)}, bf16[592,256]{1,0:T(8,128)(2,1)S(1)}, u32[]{:S(2)}, u32[]{:S(2)}) collective-permute-start(bf16[592,256]{1,0:T(8,128)(2,1)S(1)} %collective-permute-done.7.down), channel_id=1, source_target_pairs={{0,4},{1,0},{2,1},{3,2},{7,3},{6,7},{5,6},{4,5},{8,12},{9,8},{10,9... | collective-permute-start | bytes 909320 | tf_op jit(solution)/shard_map/ppermute | solution.py:689
  23.0 1.2 %collective-permute-done.8.refs_5_ = bf16[128,256]{1,0:T(8,128)(2,1)S(1)} collective-permute-done((bf16[128,256]{1,0:T(8,128)(2,1)S(1)}, bf16[128,256]{1,0:T(8,128)(2,1)S(1)}, u32[]{:S(2)}, u32[]{:S(2)}) %collective-permute-start.8) | collective-permute-done | bytes 65568 | tf_op jit(solution)/shard_map/ppermute | solution.py:702
  24.2 1.3 %shard_map.95 = (f32[528,768]{1,0:T(8,128)S(1)}, bf16[512,768]{1,0:T(8,128)(2,1)S(1)}) custom-call(bf16[128,2048]{1,0:T(8,128)(2,1)S(1)} %bitcast.13, bf16[128,2048]{1,0:T(8,128)(2,1)S(1)} %collective-permute-done.refs_1_, bf16[128,2048]{1,0:T(8,128)(2,1)S(1)} %collective-permute-done.1.refs_2_, bf16[128,2048]{1,0:T(8,128)(2,1)S(1)} %collective-permute-done.2.refs_3_, ...), custom_call_target="tpu_custom_call" | custom-call | tf_op jit(solution)/shard_map/pallas_call | solution.py:594
  25.5 2.3 %collective-permute-done.10.down = bf16[592,256]{1,0:T(8,128)(2,1)S(1)} collective-permute-done((bf16[592,256]{1,0:T(8,128)(2,1)S(1)}, bf16[592,256]{1,0:T(8,128)(2,1)S(1)}, u32[]{:S(2)}, u32[]{:S(2)}) %collective-permute-start.10) | collective-permute-done | bytes 303136 | tf_op jit(solution)/shard_map/ppermute | solution.py:689
  28.5 1.7 %collective-permute-start.13 = (bf16[304,256]{1,0:T(8,128)(2,1)}, bf16[304,256]{1,0:T(8,128)(2,1)S(1)}, u32[]{:S(2)}, u32[]{:S(2)}) collective-permute-start(bf16[304,256]{1,0:T(8,128)(2,1)} %slice.7), channel_id=1, source_target_pairs={{0,4},{1,0},{2,1},{3,2},{7,3},{6,7},{5,6},{4,5},{8,12},{9,8},{10,9... | collective-permute-start | bytes 466952 | tf_op jit(solution)/shard_map/ppermute | solution.py:689
  31.3 1.8 %collective-permute-start.14 = (bf16[64,256]{1,0:T(8,128)(2,1)S(1)}, bf16[64,256]{1,0:T(8,128)(2,1)S(1)}, u32[]{:S(2)}, u32[]{:S(2)}) collective-permute-start(bf16[64,256]{1,0:T(8,128)(2,1)S(1)} %get-tuple-element.42), channel_id=1, source_target_pairs={{0,12},{1,8},{2,9},{3,10},{7,11},{6,15},{5,14},{4,13},{8,4},{9,0},... | collective-permute-start | bytes 98312 | tf_op jit(solution)/shard_map/ppermute | solution.py:698
  33.1 1.1 %shard_map.97.partial = f32[528,768]{1,0:T(8,128)S(1)} custom-call(f32[528,768]{1,0:T(8,128)S(1)} %get-tuple-element.37.partial, bf16[512,768]{1,0:T(8,128)(2,1)S(1)} %get-tuple-element.38.rest, bf16[592,256]{1,0:T(8,128)(2,1)S(1)} %collective-permute-done.9.up, bf16[592,256]{1,0:T(8,128)(2,1)S(1)} %collective-permute-done.10.down, ...), custom_call_target="tpu_custom_call" | custom-call | tf_op jit(solution)/shard_map/pallas_call | solution.py:594
  34.8 1.5 %collective-permute-done.12.up_end = bf16[288,256]{1,0:T(8,128)(2,1)S(1)} collective-permute-done((bf16[288,256]{1,0:T(8,128)(2,1)}, bf16[288,256]{1,0:T(8,128)(2,1)S(1)}, u32[]{:S(2)}, u32[]{:S(2)}) %collective-permute-start.12) | collective-permute-done | bytes 147488 | tf_op jit(solution)/shard_map/ppermute | solution.py:689
  36.2 5.0 %shard_map.98 = (bf16[128,512]{1,0:T(8,128)(2,1)S(1)}, bf16[128,512]{1,0:T(8,128)(2,1)S(1)}, bf16[128,512]{1,0:T(8,128)(2,1)S(1)}, bf16[128,512]{1,0:T(8,128)(2,1)S(1)}) custom-call(f32[528,768]{1,0:T(8,128)S(1)} %shard_map.97.partial, bf16[512,768]{1,0:T(8,128)(2,1)S(1)} %get-tuple-element.38.rest, bf16[288,256]{1,0:T(8,128)(2,1)S(1)} %collective-permute-done.12.up_end, ...), custom_call_target="tpu_custom_call" | custom-call | tf_op jit(solution)/shard_map/pallas_call | solution.py:594
  41.3 1.6 %collective-permute-start.16 = (bf16[128,512]{1,0:T(8,128)(2,1)S(1)}, bf16[128,512]{1,0:T(8,128)(2,1)S(1)}, u32[]{:S(2)}, u32[]{:S(2)}) collective-permute-start(bf16[128,512]{1,0:T(8,128)(2,1)S(1)} %get-tuple-element.45), channel_id=1, source_target_pairs={{0,16},{8,24},{16,0},{24,8},{1,17},{9,25},{17,1},{25,9},{2,18},{10... | collective-permute-start | bytes 393224 | tf_op jit(solution)/shard_map/ppermute | solution.py:702
  43.3 4.4 %collective-permute-done.16 = bf16[128,512]{1,0:T(8,128)(2,1)S(1)} collective-permute-done((bf16[128,512]{1,0:T(8,128)(2,1)S(1)}, bf16[128,512]{1,0:T(8,128)(2,1)S(1)}, u32[]{:S(2)}, u32[]{:S(2)}) %collective-permute-start.16) | collective-permute-done | bytes 131104 | tf_op jit(solution)/shard_map/ppermute | solution.py:702
  47.7 1.9 %collective-permute-done.17 = bf16[128,512]{1,0:T(8,128)(2,1)S(1)} collective-permute-done((bf16[128,512]{1,0:T(8,128)(2,1)S(1)}, bf16[128,512]{1,0:T(8,128)(2,1)S(1)}, u32[]{:S(2)}, u32[]{:S(2)}) %collective-permute-start.17) | collective-permute-done | bytes 131104 | tf_op jit(solution)/shard_map/ppermute | solution.py:702
  (47 shorter events, 8.7 us)
Async XLA Ops:
  0.0 1.3 %copy-start = (bf16[256,2208]{0,1:T(8,128)(2,1)S(1)}, bf16[256,2208]{0,1:T(8,128)(2,1)}, u32[]{:S(2)}) copy-start(bf16[256,2208]{0,1:T(8,128)(2,1)} %param.10) | copy-start | bytes 3391492
  1.4 15.2 %collective-permute-start.1 = (bf16[128,2048]{1,0:T(8,128)(2,1)}, bf16[128,2048]{1,0:T(8,128)(2,1)S(1)}, u32[]{:S(2)}, u32[]{:S(2)}) collective-permute-start(bf16[128,2048]{1,0:T(8,128)(2,1)} %bitcast.11), channel_id=1, source_target_pairs={{0,16},{8,24},{16,0},{24,8},{1,17},{9,25},{17,1},{25,9},{2,18},{10... | collective-permute-start | bytes 1572872 | tf_op jit(solution)/shard_map/ppermute | solution.py:702
  4.4 8.6 %collective-permute-start.4 = (bf16[592,256]{1,0:T(8,128)(2,1)S(1)}, bf16[592,256]{1,0:T(8,128)(2,1)S(1)}, u32[]{:S(2)}, u32[]{:S(2)}) collective-permute-start(bf16[592,256]{1,0:T(8,128)(2,1)S(1)} %get-tuple-element.26.own), channel_id=1, source_target_pairs={{0,4},{1,0},{2,1},{3,2},{7,3},{6,7},{5,6},{4,5},{8,12},{9,8},{10,9... | collective-permute-start | bytes 909320 | tf_op jit(solution)/shard_map/ppermute | solution.py:689
  5.9 8.6 %collective-permute-start.3 = (bf16[592,256]{1,0:T(8,128)(2,1)S(1)}, bf16[592,256]{1,0:T(8,128)(2,1)S(1)}, u32[]{:S(2)}, u32[]{:S(2)}) collective-permute-start(bf16[592,256]{1,0:T(8,128)(2,1)S(1)} %get-tuple-element.26.own), channel_id=1, source_target_pairs={{0,1},{1,2},{2,3},{3,7},{7,6},{6,5},{5,4},{4,0},{8,9},{9,10},{10,1... | collective-permute-start | bytes 909320 | tf_op jit(solution)/shard_map/ppermute | solution.py:689
  6.5 0.9 %copy-start.2 = (f32[2,4,2176]{2,1,0:T(4,128)S(1)}, f32[2,4,2176]{2,1,0:T(4,128)}, u32[]{:S(2)}) copy-start(f32[2,4,2176]{2,1,0:T(4,128)} %refs_1_.1) | copy-start | bytes 208900
  7.4 0.7 %copy-start.3 = (f32[2,2176]{1,0:T(2,128)S(1)}, f32[2,2176]{1,0:T(2,128)}, u32[]{:S(2)}) copy-start(f32[2,2176]{1,0:T(2,128)} %refs_2_.1) | copy-start | bytes 52228
  8.1 0.7 %copy-start.4 = (f32[2,2048]{1,0:T(2,128)S(1)}, f32[2,2048]{1,0:T(2,128)}, u32[]{:S(2)}) copy-start(f32[2,2048]{1,0:T(2,128)} %refs_6_.1) | copy-start | bytes 49156
  13.1 7.7 %collective-permute-start.7 = (bf16[592,256]{1,0:T(8,128)(2,1)S(1)}, bf16[592,256]{1,0:T(8,128)(2,1)S(1)}, u32[]{:S(2)}, u32[]{:S(2)}) collective-permute-start(bf16[592,256]{1,0:T(8,128)(2,1)S(1)} %collective-permute-done.4.down), channel_id=1, source_target_pairs={{0,4},{1,0},{2,1},{3,2},{7,3},{6,7},{5,6},{4,5},{8,12},{9,8},{10,9... | collective-permute-start | bytes 909320 | tf_op jit(solution)/shard_map/ppermute | solution.py:689
  14.6 7.7 %collective-permute-start.6 = (bf16[592,256]{1,0:T(8,128)(2,1)S(1)}, bf16[592,256]{1,0:T(8,128)(2,1)S(1)}, u32[]{:S(2)}, u32[]{:S(2)}) collective-permute-start(bf16[592,256]{1,0:T(8,128)(2,1)S(1)} %collective-permute-done.3.up), channel_id=1, source_target_pairs={{0,1},{1,2},{2,3},{3,7},{7,6},{6,5},{5,4},{4,0},{8,9},{9,10},{10,1... | collective-permute-start | bytes 909320 | tf_op jit(solution)/shard_map/ppermute | solution.py:689
  15.1 7.9 %collective-permute-start = (bf16[128,2048]{1,0:T(8,128)(2,1)}, bf16[128,2048]{1,0:T(8,128)(2,1)S(1)}, u32[]{:S(2)}, u32[]{:S(2)}) collective-permute-start(bf16[128,2048]{1,0:T(8,128)(2,1)} %bitcast.12), channel_id=1, source_target_pairs={{0,8},{8,0},{16,24},{24,16},{1,9},{9,1},{17,25},{25,17},{2,10},{10... | collective-permute-start | bytes 1572872 | tf_op jit(solution)/shard_map/ppermute | solution.py:702
  16.6 7.6 %collective-permute-start.2 = (bf16[128,2048]{1,0:T(8,128)(2,1)S(1)}, bf16[128,2048]{1,0:T(8,128)(2,1)S(1)}, u32[]{:S(2)}, u32[]{:S(2)}) collective-permute-start(bf16[128,2048]{1,0:T(8,128)(2,1)S(1)} %collective-permute-done.1.refs_2_), channel_id=1, source_target_pairs={{0,8},{8,0},{16,24},{24,16},{1,9},{9,1},{17,25},{25,17},{2,10},{10... | collective-permute-start | bytes 1572872 | tf_op jit(solution)/shard_map/ppermute | solution.py:702
  16.6 7.6 %copy-start.1 = (bf16[1,128,2048]{2,1,0:T(8,128)(2,1)S(1)}, bf16[1,128,2048]{2,1,0:T(8,128)(2,1)}, u32[]{:S(2)}) copy-start(bf16[1,128,2048]{2,1,0:T(8,128)(2,1)} %param.9) | copy-start | bytes 1572868
  16.7 1.9 %collective-permute-start.5 = (bf16[128,256]{1,0:T(8,128)(2,1)S(1)}, bf16[128,256]{1,0:T(8,128)(2,1)S(1)}, u32[]{:S(2)}, u32[]{:S(2)}) collective-permute-start(bf16[128,256]{1,0:T(8,128)(2,1)S(1)} %get-tuple-element.32), channel_id=1, source_target_pairs={{0,8},{8,0},{16,24},{24,16},{1,9},{9,1},{17,25},{25,17},{2,10},{10... | collective-permute-start | bytes 196616 | tf_op jit(solution)/shard_map/ppermute | solution.py:702
  20.8 7.0 %collective-permute-start.10 = (bf16[592,256]{1,0:T(8,128)(2,1)S(1)}, bf16[592,256]{1,0:T(8,128)(2,1)S(1)}, u32[]{:S(2)}, u32[]{:S(2)}) collective-permute-start(bf16[592,256]{1,0:T(8,128)(2,1)S(1)} %collective-permute-done.7.down), channel_id=1, source_target_pairs={{0,4},{1,0},{2,1},{3,2},{7,3},{6,7},{5,6},{4,5},{8,12},{9,8},{10,9... | collective-permute-start | bytes 909320 | tf_op jit(solution)/shard_map/ppermute | solution.py:689
  22.3 7.9 %collective-permute-start.9 = (bf16[592,256]{1,0:T(8,128)(2,1)S(1)}, bf16[592,256]{1,0:T(8,128)(2,1)S(1)}, u32[]{:S(2)}, u32[]{:S(2)}) collective-permute-start(bf16[592,256]{1,0:T(8,128)(2,1)S(1)} %collective-permute-done.6.up), channel_id=1, source_target_pairs={{0,1},{1,2},{2,3},{3,7},{7,6},{6,5},{5,4},{4,0},{8,9},{9,10},{10,1... | collective-permute-start | bytes 909320 | tf_op jit(solution)/shard_map/ppermute | solution.py:689
  22.9 1.3 %collective-permute-start.8 = (bf16[128,256]{1,0:T(8,128)(2,1)S(1)}, bf16[128,256]{1,0:T(8,128)(2,1)S(1)}, u32[]{:S(2)}, u32[]{:S(2)}) collective-permute-start(bf16[128,256]{1,0:T(8,128)(2,1)S(1)} %get-tuple-element.36), channel_id=1, source_target_pairs={{0,8},{8,0},{16,24},{24,16},{1,9},{9,1},{17,25},{25,17},{2,10},{10... | collective-permute-start | bytes 196616 | tf_op jit(solution)/shard_map/ppermute | solution.py:702
  28.5 7.7 %collective-permute-start.13 = (bf16[304,256]{1,0:T(8,128)(2,1)}, bf16[304,256]{1,0:T(8,128)(2,1)S(1)}, u32[]{:S(2)}, u32[]{:S(2)}) collective-permute-start(bf16[304,256]{1,0:T(8,128)(2,1)} %slice.7), channel_id=1, source_target_pairs={{0,4},{1,0},{2,1},{3,2},{7,3},{6,7},{5,6},{4,5},{8,12},{9,8},{10,9... | collective-permute-start | bytes 466952 | tf_op jit(solution)/shard_map/ppermute | solution.py:689
  30.9 5.4 %collective-permute-start.12 = (bf16[288,256]{1,0:T(8,128)(2,1)}, bf16[288,256]{1,0:T(8,128)(2,1)S(1)}, u32[]{:S(2)}, u32[]{:S(2)}) collective-permute-start(bf16[288,256]{1,0:T(8,128)(2,1)} %slice.6), channel_id=1, source_target_pairs={{0,1},{1,2},{2,3},{3,7},{7,6},{6,5},{5,4},{4,0},{8,9},{9,10},{10,1... | collective-permute-start | bytes 442376 | tf_op jit(solution)/shard_map/ppermute | solution.py:689
  31.2 1.8 %collective-permute-start.11 = (bf16[128,256]{1,0:T(8,128)(2,1)S(1)}, bf16[128,256]{1,0:T(8,128)(2,1)S(1)}, u32[]{:S(2)}, u32[]{:S(2)}) collective-permute-start(bf16[128,256]{1,0:T(8,128)(2,1)S(1)} %get-tuple-element.41), channel_id=1, source_target_pairs={{0,8},{8,0},{16,24},{24,16},{1,9},{9,1},{17,25},{25,17},{2,10},{10... | collective-permute-start | bytes 196616 | tf_op jit(solution)/shard_map/ppermute | solution.py:702
  31.3 3.4 %collective-permute-start.14 = (bf16[64,256]{1,0:T(8,128)(2,1)S(1)}, bf16[64,256]{1,0:T(8,128)(2,1)S(1)}, u32[]{:S(2)}, u32[]{:S(2)}) collective-permute-start(bf16[64,256]{1,0:T(8,128)(2,1)S(1)} %get-tuple-element.42), channel_id=1, source_target_pairs={{0,12},{1,8},{2,9},{3,10},{7,11},{6,15},{5,14},{4,13},{8,4},{9,0},... | collective-permute-start | bytes 98312 | tf_op jit(solution)/shard_map/ppermute | solution.py:698
  41.3 2.0 %collective-permute-start.15 = (bf16[128,512]{1,0:T(8,128)(2,1)S(1)}, bf16[128,512]{1,0:T(8,128)(2,1)S(1)}, u32[]{:S(2)}, u32[]{:S(2)}) collective-permute-start(bf16[128,512]{1,0:T(8,128)(2,1)S(1)} %get-tuple-element.44), channel_id=1, source_target_pairs={{0,8},{8,0},{16,24},{24,16},{1,9},{9,1},{17,25},{25,17},{2,10},{10... | collective-permute-start | bytes 393224 | tf_op jit(solution)/shard_map/ppermute | solution.py:702
  41.3 6.4 %collective-permute-start.16 = (bf16[128,512]{1,0:T(8,128)(2,1)S(1)}, bf16[128,512]{1,0:T(8,128)(2,1)S(1)}, u32[]{:S(2)}, u32[]{:S(2)}) collective-permute-start(bf16[128,512]{1,0:T(8,128)(2,1)S(1)} %get-tuple-element.45), channel_id=1, source_target_pairs={{0,16},{8,24},{16,0},{24,8},{1,17},{9,25},{17,1},{25,9},{2,18},{10... | collective-permute-start | bytes 393224 | tf_op jit(solution)/shard_map/ppermute | solution.py:702
  42.9 6.7 %collective-permute-start.17 = (bf16[128,512]{1,0:T(8,128)(2,1)S(1)}, bf16[128,512]{1,0:T(8,128)(2,1)S(1)}, u32[]{:S(2)}, u32[]{:S(2)}) collective-permute-start(bf16[128,512]{1,0:T(8,128)(2,1)S(1)} %get-tuple-element.46), channel_id=1, source_target_pairs={{0,24},{8,16},{16,8},{24,0},{1,25},{9,17},{17,9},{25,1},{2,26},{10... | collective-permute-start | bytes 393224 | tf_op jit(solution)/shard_map/ppermute | solution.py:702
  47.7 1.9 %copy-start.9 = (bf16[1,128,2048]{2,1,0:T(8,128)(2,1)}, bf16[1,128,2048]{2,1,0:T(8,128)(2,1)S(1)}, u32[]{:S(2)}) copy-start(bf16[1,128,2048]{2,1,0:T(8,128)(2,1)S(1)} %bitcast_dynamic-update-slice_fusion.1) | copy-start | bytes 1572868
  (4 other events, 2.7 us)

commit v9 on v8

--- a/solution.py
+++ b/solution.py
@@ -737,7 +737,7 @@
             beside = partial
         up, _ = lax.optimization_barrier((up, beside))
         down, _ = lax.optimization_barrier((down, beside))
-    cut = own.shape[0] // 32 * 16
+    cut = own.shape[0] * 2 // 5 // 16 * 16
     ends = [turn(up[:cut], 1), turn(down[cut:], -1)]
     sent, crossing = split(columns, up, down)
     far = turn_across(crossing, -1)

time: 50.6 us -> 50.3 us (level)
  no operation moved by 1% of the time
where the time goes in v9:
time: 50.3 us; the launch traced here: 49.9 us
  waiting for transfers between devices  17.3 us (34%)
  starting transfers between devices  15.5 us (31%)
  Pallas kernels  8.52 us (17%)
  local copies, waits for them, and re-layouts  8.37 us (17%)
    ppermute x9, waiting for transfers between devices, swap(): lax.ppermute(value, axis, [(i, i ^ mask) for i in range(lax.axis_size(axi...  10.3 us
    pallas_call x8, Pallas kernels, call(): pl.pallas_call(kernel, out_shape=shapes, in_specs=[space] * (len(operands...  8.52 us
    ppermute x8, starting transfers between devices, turn(): lax.ppermute(value, ('fsdp', 'batch'), [(order[i], order[(i + way) % coun...  8.1 us
    ppermute x8, waiting for transfers between devices, turn(): lax.ppermute(value, ('fsdp', 'batch'), [(order[i], order[(i + way) % coun...  6.48 us
    unnamed x20, local copies, waits for them, and re-layouts  6.27 us
    ppermute x9, starting transfers between devices, swap(): lax.ppermute(value, axis, [(i, i ^ mask) for i in range(lax.axis_size(axi...  5.68 us
    ppermute x1, starting transfers between devices, turn_across(): return lax.ppermute(value, ('seq', 'fsdp', 'batch'), pairs)  1.76 us
    slice x2, local copies, waits for them, and re-layouts, on_heads(): ends = [turn(up[:cut], 1), turn(down[cut:], -1)]  1.35 us
  transfers between devices with their start and end apart: 18, of which 10 were waited for; matrix products, arithmetic and copies ran while one was open for 3% of the time, Pallas kernels for 7%

profile of v9, /device:TPU:0, one launch (start us, length us, event | category | flops | bytes accessed | tf_op | source)
XLA Modules:
  0.0 49.9 jit_solution(5026774750866718820)
XLA Ops:
  0.0 1.3 %copy-done = bf16[256,2208]{0,1:T(8,128)(2,1)S(1)} copy-done((bf16[256,2208]{0,1:T(8,128)(2,1)S(1)}, bf16[256,2208]{0,1:T(8,128)(2,1)}, u32[]{:S(2)}) %copy-start) | copy-done | bytes 1130520
  1.4 3.0 %collective-permute-start.1 = (bf16[128,2048]{1,0:T(8,128)(2,1)}, bf16[128,2048]{1,0:T(8,128)(2,1)S(1)}, u32[]{:S(2)}, u32[]{:S(2)}) collective-permute-start(bf16[128,2048]{1,0:T(8,128)(2,1)} %bitcast.11), channel_id=1, source_target_pairs={{0,16},{8,24},{16,0},{24,8},{1,17},{9,25},{17,1},{25,9},{2,18},{10... | collective-permute-start | bytes 1572872 | tf_op jit(solution)/shard_map/ppermute | solution.py:702
  4.4 1.5 %collective-permute-start.4 = (bf16[592,256]{1,0:T(8,128)(2,1)S(1)}, bf16[592,256]{1,0:T(8,128)(2,1)S(1)}, u32[]{:S(2)}, u32[]{:S(2)}) collective-permute-start(bf16[592,256]{1,0:T(8,128)(2,1)S(1)} %get-tuple-element.26.own), channel_id=1, source_target_pairs={{0,4},{1,0},{2,1},{3,2},{7,3},{6,7},{5,6},{4,5},{8,12},{9,8},{10,9... | collective-permute-start | bytes 909320 | tf_op jit(solution)/shard_map/ppermute | solution.py:689
  6.5 0.9 %copy-done.2 = f32[2,4,2176]{2,1,0:T(4,128)S(1)} copy-done((f32[2,4,2176]{2,1,0:T(4,128)S(1)}, f32[2,4,2176]{2,1,0:T(4,128)}, u32[]{:S(2)}) %copy-start.2) | copy-done | bytes 69656
  7.4 0.7 %copy-done.3 = f32[2,2176]{1,0:T(2,128)S(1)} copy-done((f32[2,2176]{1,0:T(2,128)S(1)}, f32[2,2176]{1,0:T(2,128)}, u32[]{:S(2)}) %copy-start.3) | copy-done | bytes 17432
  8.1 0.7 %copy-done.4 = f32[2,2048]{1,0:T(2,128)S(1)} copy-done((f32[2,2048]{1,0:T(2,128)S(1)}, f32[2,2048]{1,0:T(2,128)}, u32[]{:S(2)}) %copy-start.4) | copy-done | bytes 16408
  11.5 0.8 %shard_map.92.refs_6_ = f32[144,640]{1,0:T(8,128)S(1)} custom-call(s32[1,4]{1,0:T(1,128)S(1)} %copy-done.8, f32[2,4,2176]{2,1,0:T(4,128)S(1)} %copy-done.2, f32[2,2176]{1,0:T(2,128)S(1)} %copy-done.3, f32[2,32]{1,0:T(2,128)S(1)} %copy-done.5, f32[2,32]{1,0:T(2,128)S(1)} %copy-done.6, f32[2,32]{1,0:T(2,128)S(1)} %copy-done.7, f32[2,2048]{1,0:T(2,128)S(1)} %copy-done.4), custom_call_target="tpu_custom_call" | custom-call | tf_op jit(solution)/shard_map/pallas_call | solution.py:594
  12.3 0.8 %collective-permute-done.4.down = bf16[592,256]{1,0:T(8,128)(2,1)S(1)} collective-permute-done((bf16[592,256]{1,0:T(8,128)(2,1)S(1)}, bf16[592,256]{1,0:T(8,128)(2,1)S(1)}, u32[]{:S(2)}, u32[]{:S(2)}) %collective-permute-start.4) | collective-permute-done | bytes 303136 | tf_op jit(solution)/shard_map/ppermute | solution.py:689
  13.1 1.5 %collective-permute-start.7 = (bf16[592,256]{1,0:T(8,128)(2,1)S(1)}, bf16[592,256]{1,0:T(8,128)(2,1)S(1)}, u32[]{:S(2)}, u32[]{:S(2)}) collective-permute-start(bf16[592,256]{1,0:T(8,128)(2,1)S(1)} %collective-permute-done.4.down), channel_id=1, source_target_pairs={{0,4},{1,0},{2,1},{3,2},{7,3},{6,7},{5,6},{4,5},{8,12},{9,8},{10,9... | collective-permute-start | bytes 909320 | tf_op jit(solution)/shard_map/ppermute | solution.py:689
  15.1 1.5 %collective-permute-done.1.refs_2_ = bf16[128,2048]{1,0:T(8,128)(2,1)S(1)} collective-permute-done((bf16[128,2048]{1,0:T(8,128)(2,1)}, bf16[128,2048]{1,0:T(8,128)(2,1)S(1)}, u32[]{:S(2)}, u32[]{:S(2)}) %collective-permute-start.1) | collective-permute-done | bytes 524320 | tf_op jit(solution)/shard_map/ppermute | solution.py:702
  17.3 1.3 %collective-permute-done.5.swapped = bf16[128,256]{1,0:T(8,128)(2,1)S(1)} collective-permute-done((bf16[128,256]{1,0:T(8,128)(2,1)S(1)}, bf16[128,256]{1,0:T(8,128)(2,1)S(1)}, u32[]{:S(2)}, u32[]{:S(2)}) %collective-permute-start.5) | collective-permute-done | bytes 65568 | tf_op jit(solution)/shard_map/ppermute | solution.py:702
  18.6 2.2 %collective-permute-done.7.down = bf16[592,256]{1,0:T(8,128)(2,1)S(1)} collective-permute-done((bf16[592,256]{1,0:T(8,128)(2,1)S(1)}, bf16[592,256]{1,0:T(8,128)(2,1)S(1)}, u32[]{:S(2)}, u32[]{:S(2)}) %collective-permute-start.7) | collective-permute-done | bytes 303136 | tf_op jit(solution)/shard_map/ppermute | solution.py:689
  20.8 1.5 %collective-permute-start.10 = (bf16[592,256]{1,0:T(8,128)(2,1)S(1)}, bf16[592,256]{1,0:T(8,128)(2,1)S(1)}, u32[]{:S(2)}, u32[]{:S(2)}) collective-permute-start(bf16[592,256]{1,0:T(8,128)(2,1)S(1)} %collective-permute-done.7.down), channel_id=1, source_target_pairs={{0,4},{1,0},{2,1},{3,2},{7,3},{6,7},{5,6},{4,5},{8,12},{9,8},{10,9... | collective-permute-start | bytes 909320 | tf_op jit(solution)/shard_map/ppermute | solution.py:689
  23.0 1.2 %collective-permute-done.8.refs_5_ = bf16[128,256]{1,0:T(8,128)(2,1)S(1)} collective-permute-done((bf16[128,256]{1,0:T(8,128)(2,1)S(1)}, bf16[128,256]{1,0:T(8,128)(2,1)S(1)}, u32[]{:S(2)}, u32[]{:S(2)}) %collective-permute-start.8) | collective-permute-done | bytes 65568 | tf_op jit(solution)/shard_map/ppermute | solution.py:702
  24.2 1.3 %shard_map.95 = (f32[528,768]{1,0:T(8,128)S(1)}, bf16[512,768]{1,0:T(8,128)(2,1)S(1)}) custom-call(bf16[128,2048]{1,0:T(8,128)(2,1)S(1)} %bitcast.13, bf16[128,2048]{1,0:T(8,128)(2,1)S(1)} %collective-permute-done.refs_1_, bf16[128,2048]{1,0:T(8,128)(2,1)S(1)} %collective-permute-done.1.refs_2_, bf16[128,2048]{1,0:T(8,128)(2,1)S(1)} %collective-permute-done.2.refs_3_, ...), custom_call_target="tpu_custom_call" | custom-call | tf_op jit(solution)/shard_map/pallas_call | solution.py:594
  25.5 2.3 %collective-permute-done.10.down = bf16[592,256]{1,0:T(8,128)(2,1)S(1)} collective-permute-done((bf16[592,256]{1,0:T(8,128)(2,1)S(1)}, bf16[592,256]{1,0:T(8,128)(2,1)S(1)}, u32[]{:S(2)}, u32[]{:S(2)}) %collective-permute-start.10) | collective-permute-done | bytes 303136 | tf_op jit(solution)/shard_map/ppermute | solution.py:689
  28.6 1.7 %collective-permute-start.13 = (bf16[368,256]{1,0:T(8,128)(2,1)}, bf16[368,256]{1,0:T(8,128)(2,1)S(1)}, u32[]{:S(2)}, u32[]{:S(2)}) collective-permute-start(bf16[368,256]{1,0:T(8,128)(2,1)} %slice.7), channel_id=1, source_target_pairs={{0,4},{1,0},{2,1},{3,2},{7,3},{6,7},{5,6},{4,5},{8,12},{9,8},{10,9... | collective-permute-start | bytes 565256 | tf_op jit(solution)/shard_map/ppermute | solution.py:689
  31.3 1.8 %collective-permute-start.14 = (bf16[64,256]{1,0:T(8,128)(2,1)S(1)}, bf16[64,256]{1,0:T(8,128)(2,1)S(1)}, u32[]{:S(2)}, u32[]{:S(2)}) collective-permute-start(bf16[64,256]{1,0:T(8,128)(2,1)S(1)} %get-tuple-element.42), channel_id=1, source_target_pairs={{0,12},{1,8},{2,9},{3,10},{7,11},{6,15},{5,14},{4,13},{8,4},{9,0},... | collective-permute-start | bytes 98312 | tf_op jit(solution)/shard_map/ppermute | solution.py:698
  33.1 1.1 %shard_map.97.partial = f32[528,768]{1,0:T(8,128)S(1)} custom-call(f32[528,768]{1,0:T(8,128)S(1)} %get-tuple-element.37.partial, bf16[512,768]{1,0:T(8,128)(2,1)S(1)} %get-tuple-element.38.rest, bf16[592,256]{1,0:T(8,128)(2,1)S(1)} %collective-permute-done.9.up, bf16[592,256]{1,0:T(8,128)(2,1)S(1)} %collective-permute-done.10.down, ...), custom_call_target="tpu_custom_call" | custom-call | tf_op jit(solution)/shard_map/pallas_call | solution.py:594
  34.8 1.1 %collective-permute-done.12.up_end = bf16[224,256]{1,0:T(8,128)(2,1)S(1)} collective-permute-done((bf16[224,256]{1,0:T(8,128)(2,1)}, bf16[224,256]{1,0:T(8,128)(2,1)S(1)}, u32[]{:S(2)}, u32[]{:S(2)}) %collective-permute-start.12) | collective-permute-done | bytes 114720 | tf_op jit(solution)/shard_map/ppermute | solution.py:689
  35.9 5.0 %shard_map.98 = (bf16[128,512]{1,0:T(8,128)(2,1)S(1)}, bf16[128,512]{1,0:T(8,128)(2,1)S(1)}, bf16[128,512]{1,0:T(8,128)(2,1)S(1)}, bf16[128,512]{1,0:T(8,128)(2,1)S(1)}) custom-call(f32[528,768]{1,0:T(8,128)S(1)} %shard_map.97.partial, bf16[512,768]{1,0:T(8,128)(2,1)S(1)} %get-tuple-element.38.rest, bf16[224,256]{1,0:T(8,128)(2,1)S(1)} %collective-permute-done.12.up_end, ...), custom_call_target="tpu_custom_call" | custom-call | tf_op jit(solution)/shard_map/pallas_call | solution.py:594
  41.0 1.6 %collective-permute-start.16 = (bf16[128,512]{1,0:T(8,128)(2,1)S(1)}, bf16[128,512]{1,0:T(8,128)(2,1)S(1)}, u32[]{:S(2)}, u32[]{:S(2)}) collective-permute-start(bf16[128,512]{1,0:T(8,128)(2,1)S(1)} %get-tuple-element.45), channel_id=1, source_target_pairs={{0,16},{8,24},{16,0},{24,8},{1,17},{9,25},{17,1},{25,9},{2,18},{10... | collective-permute-start | bytes 393224 | tf_op jit(solution)/shard_map/ppermute | solution.py:702
  43.0 4.4 %collective-permute-done.16 = bf16[128,512]{1,0:T(8,128)(2,1)S(1)} collective-permute-done((bf16[128,512]{1,0:T(8,128)(2,1)S(1)}, bf16[128,512]{1,0:T(8,128)(2,1)S(1)}, u32[]{:S(2)}, u32[]{:S(2)}) %collective-permute-start.16) | collective-permute-done | bytes 131104 | tf_op jit(solution)/shard_map/ppermute | solution.py:702
  47.4 1.9 %collective-permute-done.17 = bf16[128,512]{1,0:T(8,128)(2,1)S(1)} collective-permute-done((bf16[128,512]{1,0:T(8,128)(2,1)S(1)}, bf16[128,512]{1,0:T(8,128)(2,1)S(1)}, u32[]{:S(2)}, u32[]{:S(2)}) %collective-permute-start.17) | collective-permute-done | bytes 131104 | tf_op jit(solution)/shard_map/ppermute | solution.py:702
  (47 shorter events, 8.7 us)
Async XLA Ops:
  0.0 1.3 %copy-start = (bf16[256,2208]{0,1:T(8,128)(2,1)S(1)}, bf16[256,2208]{0,1:T(8,128)(2,1)}, u32[]{:S(2)}) copy-start(bf16[256,2208]{0,1:T(8,128)(2,1)} %param.10) | copy-start | bytes 3391492
  1.4 15.2 %collective-permute-start.1 = (bf16[128,2048]{1,0:T(8,128)(2,1)}, bf16[128,2048]{1,0:T(8,128)(2,1)S(1)}, u32[]{:S(2)}, u32[]{:S(2)}) collective-permute-start(bf16[128,2048]{1,0:T(8,128)(2,1)} %bitcast.11), channel_id=1, source_target_pairs={{0,16},{8,24},{16,0},{24,8},{1,17},{9,25},{17,1},{25,9},{2,18},{10... | collective-permute-start | bytes 1572872 | tf_op jit(solution)/shard_map/ppermute | solution.py:702
  4.4 8.6 %collective-permute-start.4 = (bf16[592,256]{1,0:T(8,128)(2,1)S(1)}, bf16[592,256]{1,0:T(8,128)(2,1)S(1)}, u32[]{:S(2)}, u32[]{:S(2)}) collective-permute-start(bf16[592,256]{1,0:T(8,128)(2,1)S(1)} %get-tuple-element.26.own), channel_id=1, source_target_pairs={{0,4},{1,0},{2,1},{3,2},{7,3},{6,7},{5,6},{4,5},{8,12},{9,8},{10,9... | collective-permute-start | bytes 909320 | tf_op jit(solution)/shard_map/ppermute | solution.py:689
  5.9 8.6 %collective-permute-start.3 = (bf16[592,256]{1,0:T(8,128)(2,1)S(1)}, bf16[592,256]{1,0:T(8,128)(2,1)S(1)}, u32[]{:S(2)}, u32[]{:S(2)}) collective-permute-start(bf16[592,256]{1,0:T(8,128)(2,1)S(1)} %get-tuple-element.26.own), channel_id=1, source_target_pairs={{0,1},{1,2},{2,3},{3,7},{7,6},{6,5},{5,4},{4,0},{8,9},{9,10},{10,1... | collective-permute-start | bytes 909320 | tf_op jit(solution)/shard_map/ppermute | solution.py:689
  6.5 0.9 %copy-start.2 = (f32[2,4,2176]{2,1,0:T(4,128)S(1)}, f32[2,4,2176]{2,1,0:T(4,128)}, u32[]{:S(2)}) copy-start(f32[2,4,2176]{2,1,0:T(4,128)} %refs_1_.1) | copy-start | bytes 208900
  7.4 0.7 %copy-start.3 = (f32[2,2176]{1,0:T(2,128)S(1)}, f32[2,2176]{1,0:T(2,128)}, u32[]{:S(2)}) copy-start(f32[2,2176]{1,0:T(2,128)} %refs_2_.1) | copy-start | bytes 52228
  8.1 0.7 %copy-start.4 = (f32[2,2048]{1,0:T(2,128)S(1)}, f32[2,2048]{1,0:T(2,128)}, u32[]{:S(2)}) copy-start(f32[2,2048]{1,0:T(2,128)} %refs_6_.1) | copy-start | bytes 49156
  13.1 7.7 %collective-permute-start.7 = (bf16[592,256]{1,0:T(8,128)(2,1)S(1)}, bf16[592,256]{1,0:T(8,128)(2,1)S(1)}, u32[]{:S(2)}, u32[]{:S(2)}) collective-permute-start(bf16[592,256]{1,0:T(8,128)(2,1)S(1)} %collective-permute-done.4.down), channel_id=1, source_target_pairs={{0,4},{1,0},{2,1},{3,2},{7,3},{6,7},{5,6},{4,5},{8,12},{9,8},{10,9... | collective-permute-start | bytes 909320 | tf_op jit(solution)/shard_map/ppermute | solution.py:689
  14.6 7.7 %collective-permute-start.6 = (bf16[592,256]{1,0:T(8,128)(2,1)S(1)}, bf16[592,256]{1,0:T(8,128)(2,1)S(1)}, u32[]{:S(2)}, u32[]{:S(2)}) collective-permute-start(bf16[592,256]{1,0:T(8,128)(2,1)S(1)} %collective-permute-done.3.up), channel_id=1, source_target_pairs={{0,1},{1,2},{2,3},{3,7},{7,6},{6,5},{5,4},{4,0},{8,9},{9,10},{10,1... | collective-permute-start | bytes 909320 | tf_op jit(solution)/shard_map/ppermute | solution.py:689
  15.1 7.9 %collective-permute-start = (bf16[128,2048]{1,0:T(8,128)(2,1)}, bf16[128,2048]{1,0:T(8,128)(2,1)S(1)}, u32[]{:S(2)}, u32[]{:S(2)}) collective-permute-start(bf16[128,2048]{1,0:T(8,128)(2,1)} %bitcast.12), channel_id=1, source_target_pairs={{0,8},{8,0},{16,24},{24,16},{1,9},{9,1},{17,25},{25,17},{2,10},{10... | collective-permute-start | bytes 1572872 | tf_op jit(solution)/shard_map/ppermute | solution.py:702
  16.6 7.6 %collective-permute-start.2 = (bf16[128,2048]{1,0:T(8,128)(2,1)S(1)}, bf16[128,2048]{1,0:T(8,128)(2,1)S(1)}, u32[]{:S(2)}, u32[]{:S(2)}) collective-permute-start(bf16[128,2048]{1,0:T(8,128)(2,1)S(1)} %collective-permute-done.1.refs_2_), channel_id=1, source_target_pairs={{0,8},{8,0},{16,24},{24,16},{1,9},{9,1},{17,25},{25,17},{2,10},{10... | collective-permute-start | bytes 1572872 | tf_op jit(solution)/shard_map/ppermute | solution.py:702
  16.6 7.6 %copy-start.1 = (bf16[1,128,2048]{2,1,0:T(8,128)(2,1)S(1)}, bf16[1,128,2048]{2,1,0:T(8,128)(2,1)}, u32[]{:S(2)}) copy-start(bf16[1,128,2048]{2,1,0:T(8,128)(2,1)} %param.9) | copy-start | bytes 1572868
  16.7 1.9 %collective-permute-start.5 = (bf16[128,256]{1,0:T(8,128)(2,1)S(1)}, bf16[128,256]{1,0:T(8,128)(2,1)S(1)}, u32[]{:S(2)}, u32[]{:S(2)}) collective-permute-start(bf16[128,256]{1,0:T(8,128)(2,1)S(1)} %get-tuple-element.32), channel_id=1, source_target_pairs={{0,8},{8,0},{16,24},{24,16},{1,9},{9,1},{17,25},{25,17},{2,10},{10... | collective-permute-start | bytes 196616 | tf_op jit(solution)/shard_map/ppermute | solution.py:702
  20.8 7.0 %collective-permute-start.10 = (bf16[592,256]{1,0:T(8,128)(2,1)S(1)}, bf16[592,256]{1,0:T(8,128)(2,1)S(1)}, u32[]{:S(2)}, u32[]{:S(2)}) collective-permute-start(bf16[592,256]{1,0:T(8,128)(2,1)S(1)} %collective-permute-done.7.down), channel_id=1, source_target_pairs={{0,4},{1,0},{2,1},{3,2},{7,3},{6,7},{5,6},{4,5},{8,12},{9,8},{10,9... | collective-permute-start | bytes 909320 | tf_op jit(solution)/shard_map/ppermute | solution.py:689
  22.3 7.9 %collective-permute-start.9 = (bf16[592,256]{1,0:T(8,128)(2,1)S(1)}, bf16[592,256]{1,0:T(8,128)(2,1)S(1)}, u32[]{:S(2)}, u32[]{:S(2)}) collective-permute-start(bf16[592,256]{1,0:T(8,128)(2,1)S(1)} %collective-permute-done.6.up), channel_id=1, source_target_pairs={{0,1},{1,2},{2,3},{3,7},{7,6},{6,5},{5,4},{4,0},{8,9},{9,10},{10,1... | collective-permute-start | bytes 909320 | tf_op jit(solution)/shard_map/ppermute | solution.py:689
  22.9 1.3 %collective-permute-start.8 = (bf16[128,256]{1,0:T(8,128)(2,1)S(1)}, bf16[128,256]{1,0:T(8,128)(2,1)S(1)}, u32[]{:S(2)}, u32[]{:S(2)}) collective-permute-start(bf16[128,256]{1,0:T(8,128)(2,1)S(1)} %get-tuple-element.36), channel_id=1, source_target_pairs={{0,8},{8,0},{16,24},{24,16},{1,9},{9,1},{17,25},{25,17},{2,10},{10... | collective-permute-start | bytes 196616 | tf_op jit(solution)/shard_map/ppermute | solution.py:702
  28.6 7.3 %collective-permute-start.13 = (bf16[368,256]{1,0:T(8,128)(2,1)}, bf16[368,256]{1,0:T(8,128)(2,1)S(1)}, u32[]{:S(2)}, u32[]{:S(2)}) collective-permute-start(bf16[368,256]{1,0:T(8,128)(2,1)} %slice.7), channel_id=1, source_target_pairs={{0,4},{1,0},{2,1},{3,2},{7,3},{6,7},{5,6},{4,5},{8,12},{9,8},{10,9... | collective-permute-start | bytes 565256 | tf_op jit(solution)/shard_map/ppermute | solution.py:689
  30.9 5.0 %collective-permute-start.12 = (bf16[224,256]{1,0:T(8,128)(2,1)}, bf16[224,256]{1,0:T(8,128)(2,1)S(1)}, u32[]{:S(2)}, u32[]{:S(2)}) collective-permute-start(bf16[224,256]{1,0:T(8,128)(2,1)} %slice.6), channel_id=1, source_target_pairs={{0,1},{1,2},{2,3},{3,7},{7,6},{6,5},{5,4},{4,0},{8,9},{9,10},{10,1... | collective-permute-start | bytes 344072 | tf_op jit(solution)/shard_map/ppermute | solution.py:689
  31.3 1.8 %collective-permute-start.11 = (bf16[128,256]{1,0:T(8,128)(2,1)S(1)}, bf16[128,256]{1,0:T(8,128)(2,1)S(1)}, u32[]{:S(2)}, u32[]{:S(2)}) collective-permute-start(bf16[128,256]{1,0:T(8,128)(2,1)S(1)} %get-tuple-element.41), channel_id=1, source_target_pairs={{0,8},{8,0},{16,24},{24,16},{1,9},{9,1},{17,25},{25,17},{2,10},{10... | collective-permute-start | bytes 196616 | tf_op jit(solution)/shard_map/ppermute | solution.py:702
  31.3 3.4 %collective-permute-start.14 = (bf16[64,256]{1,0:T(8,128)(2,1)S(1)}, bf16[64,256]{1,0:T(8,128)(2,1)S(1)}, u32[]{:S(2)}, u32[]{:S(2)}) collective-permute-start(bf16[64,256]{1,0:T(8,128)(2,1)S(1)} %get-tuple-element.42), channel_id=1, source_target_pairs={{0,12},{1,8},{2,9},{3,10},{7,11},{6,15},{5,14},{4,13},{8,4},{9,0},... | collective-permute-start | bytes 98312 | tf_op jit(solution)/shard_map/ppermute | solution.py:698
  40.9 2.0 %collective-permute-start.15 = (bf16[128,512]{1,0:T(8,128)(2,1)S(1)}, bf16[128,512]{1,0:T(8,128)(2,1)S(1)}, u32[]{:S(2)}, u32[]{:S(2)}) collective-permute-start(bf16[128,512]{1,0:T(8,128)(2,1)S(1)} %get-tuple-element.44), channel_id=1, source_target_pairs={{0,8},{8,0},{16,24},{24,16},{1,9},{9,1},{17,25},{25,17},{2,10},{10... | collective-permute-start | bytes 393224 | tf_op jit(solution)/shard_map/ppermute | solution.py:702
  41.0 6.4 %collective-permute-start.16 = (bf16[128,512]{1,0:T(8,128)(2,1)S(1)}, bf16[128,512]{1,0:T(8,128)(2,1)S(1)}, u32[]{:S(2)}, u32[]{:S(2)}) collective-permute-start(bf16[128,512]{1,0:T(8,128)(2,1)S(1)} %get-tuple-element.45), channel_id=1, source_target_pairs={{0,16},{8,24},{16,0},{24,8},{1,17},{9,25},{17,1},{25,9},{2,18},{10... | collective-permute-start | bytes 393224 | tf_op jit(solution)/shard_map/ppermute | solution.py:702
  42.6 6.7 %collective-permute-start.17 = (bf16[128,512]{1,0:T(8,128)(2,1)S(1)}, bf16[128,512]{1,0:T(8,128)(2,1)S(1)}, u32[]{:S(2)}, u32[]{:S(2)}) collective-permute-start(bf16[128,512]{1,0:T(8,128)(2,1)S(1)} %get-tuple-element.46), channel_id=1, source_target_pairs={{0,24},{8,16},{16,8},{24,0},{1,25},{9,17},{17,9},{25,1},{2,26},{10... | collective-permute-start | bytes 393224 | tf_op jit(solution)/shard_map/ppermute | solution.py:702
  47.4 1.9 %copy-start.9 = (bf16[1,128,2048]{2,1,0:T(8,128)(2,1)}, bf16[1,128,2048]{2,1,0:T(8,128)(2,1)S(1)}, u32[]{:S(2)}) copy-start(bf16[1,128,2048]{2,1,0:T(8,128)(2,1)S(1)} %bitcast_dynamic-update-slice_fusion.1) | copy-start | bytes 1572868
  (4 other events, 2.7 us)

commit v10 on v9

--- a/solution.py
+++ b/solution.py
@@ -482,7 +482,7 @@
     fade = jnp.where(seen_last == 0.0, jnp.exp(last), 0.0)
     seen_turned = seen.T
     spread = [head_columns(heads, d) for d in range(2)]
-    shown = (jnp.log(step) - cum).T
+    shown, step_turned = (-cum).T, step.T
     fades = []
     for b in range(blocks):
         for k, value in enumerate((lead, tail)):
@@ -547,7 +547,7 @@
         for h in range(q * group, (q + 1) * group):
             n = b * GROUP + d * heads + h
             gap = cum[:, n : n + 1] + (shown[n : n + 1, :] + bar)
-            some.append((jnp.exp(gap) * scores).astype(jnp.bfloat16))
+            some.append((jnp.exp(gap) * scores * step_turned[n : n + 1, :]).astype(jnp.bfloat16))
         none = jnp.zeros_like(x_part)
         spaced = jnp.concatenate([jnp.where(lane_head == h, x_part, none) for h in range(group)], axis=0)
         inner = jnp.dot(jnp.concatenate(some, axis=1), spaced, preferred_element_type=jnp.float32)
@@ -763,7 +763,7 @@
         P(),
     )
     out_specs = P(("fsdp", "batch"), "seq", None)
-    by_heads = mesh.shape["seq"] == 4 and mesh.shape["fsdp"] == 2
+    by_heads = mesh.shape["seq"] == 4 and mesh.shape["fsdp"] == 2 and mesh.shape["batch"] > 3
 
     def mixer(hidden, *rest):
         whole = by_heads and hidden.shape[1] == mesh.shape["seq"] * BLOCK

time: 50.3 us -> 50.4 us (level)
  no operation moved by 1% of the time
where the time goes in v10:
time: 50.4 us; the launch traced here: 50 us
  waiting for transfers between devices  17.3 us (34%)
  starting transfers between devices  15.5 us (31%)
  Pallas kernels  8.64 us (17%)
  local copies, waits for them, and re-layouts  8.37 us (17%)
    ppermute x9, waiting for transfers between devices, swap(): lax.ppermute(value, axis, [(i, i ^ mask) for i in range(lax.axis_size(axi...  10.3 us
    pallas_call x8, Pallas kernels, call(): pl.pallas_call(kernel, out_shape=shapes, in_specs=[space] * (len(operands...  8.64 us
    ppermute x8, starting transfers between devices, turn(): lax.ppermute(value, ('fsdp', 'batch'), [(order[i], order[(i + way) % coun...  8.1 us
    ppermute x8, waiting for transfers between devices, turn(): lax.ppermute(value, ('fsdp', 'batch'), [(order[i], order[(i + way) % coun...  6.48 us
    unnamed x20, local copies, waits for them, and re-layouts  6.27 us
    ppermute x9, starting transfers between devices, swap(): lax.ppermute(value, axis, [(i, i ^ mask) for i in range(lax.axis_size(axi...  5.68 us
    ppermute x1, starting transfers between devices, turn_across(): return lax.ppermute(value, ('seq', 'fsdp', 'batch'), pairs)  1.76 us
    slice x2, local copies, waits for them, and re-layouts, on_heads(): ends = [turn(up[:cut], 1), turn(down[cut:], -1)]  1.35 us
  transfers between devices with their start and end apart: 18, of which 10 were waited for; matrix products, arithmetic and copies ran while one was open for 3% of the time, Pallas kernels for 7%

profile of v10, /device:TPU:0, one launch (start us, length us, event | category | flops | bytes accessed | tf_op | source)
XLA Modules:
  0.0 50.0 jit_solution(8436217999253670755)
XLA Ops:
  0.0 1.3 %copy-done = bf16[256,2208]{0,1:T(8,128)(2,1)S(1)} copy-done((bf16[256,2208]{0,1:T(8,128)(2,1)S(1)}, bf16[256,2208]{0,1:T(8,128)(2,1)}, u32[]{:S(2)}) %copy-start) | copy-done | bytes 1130520
  1.4 3.0 %collective-permute-start.1 = (bf16[128,2048]{1,0:T(8,128)(2,1)}, bf16[128,2048]{1,0:T(8,128)(2,1)S(1)}, u32[]{:S(2)}, u32[]{:S(2)}) collective-permute-start(bf16[128,2048]{1,0:T(8,128)(2,1)} %bitcast.11), channel_id=1, source_target_pairs={{0,16},{8,24},{16,0},{24,8},{1,17},{9,25},{17,1},{25,9},{2,18},{10... | collective-permute-start | bytes 1572872 | tf_op jit(solution)/shard_map/ppermute | solution.py:702
  4.4 1.5 %collective-permute-start.4 = (bf16[592,256]{1,0:T(8,128)(2,1)S(1)}, bf16[592,256]{1,0:T(8,128)(2,1)S(1)}, u32[]{:S(2)}, u32[]{:S(2)}) collective-permute-start(bf16[592,256]{1,0:T(8,128)(2,1)S(1)} %get-tuple-element.26.own), channel_id=1, source_target_pairs={{0,4},{1,0},{2,1},{3,2},{7,3},{6,7},{5,6},{4,5},{8,12},{9,8},{10,9... | collective-permute-start | bytes 909320 | tf_op jit(solution)/shard_map/ppermute | solution.py:689
  6.5 0.9 %copy-done.2 = f32[2,4,2176]{2,1,0:T(4,128)S(1)} copy-done((f32[2,4,2176]{2,1,0:T(4,128)S(1)}, f32[2,4,2176]{2,1,0:T(4,128)}, u32[]{:S(2)}) %copy-start.2) | copy-done | bytes 69656
  7.4 0.7 %copy-done.3 = f32[2,2176]{1,0:T(2,128)S(1)} copy-done((f32[2,2176]{1,0:T(2,128)S(1)}, f32[2,2176]{1,0:T(2,128)}, u32[]{:S(2)}) %copy-start.3) | copy-done | bytes 17432
  8.1 0.7 %copy-done.4 = f32[2,2048]{1,0:T(2,128)S(1)} copy-done((f32[2,2048]{1,0:T(2,128)S(1)}, f32[2,2048]{1,0:T(2,128)}, u32[]{:S(2)}) %copy-start.4) | copy-done | bytes 16408
  11.5 0.8 %shard_map.92.refs_6_ = f32[144,640]{1,0:T(8,128)S(1)} custom-call(s32[1,4]{1,0:T(1,128)S(1)} %copy-done.8, f32[2,4,2176]{2,1,0:T(4,128)S(1)} %copy-done.2, f32[2,2176]{1,0:T(2,128)S(1)} %copy-done.3, f32[2,32]{1,0:T(2,128)S(1)} %copy-done.5, f32[2,32]{1,0:T(2,128)S(1)} %copy-done.6, f32[2,32]{1,0:T(2,128)S(1)} %copy-done.7, f32[2,2048]{1,0:T(2,128)S(1)} %copy-done.4), custom_call_target="tpu_custom_call" | custom-call | tf_op jit(solution)/shard_map/pallas_call | solution.py:594
  12.3 0.8 %collective-permute-done.4.down = bf16[592,256]{1,0:T(8,128)(2,1)S(1)} collective-permute-done((bf16[592,256]{1,0:T(8,128)(2,1)S(1)}, bf16[592,256]{1,0:T(8,128)(2,1)S(1)}, u32[]{:S(2)}, u32[]{:S(2)}) %collective-permute-start.4) | collective-permute-done | bytes 303136 | tf_op jit(solution)/shard_map/ppermute | solution.py:689
  13.1 1.5 %collective-permute-start.7 = (bf16[592,256]{1,0:T(8,128)(2,1)S(1)}, bf16[592,256]{1,0:T(8,128)(2,1)S(1)}, u32[]{:S(2)}, u32[]{:S(2)}) collective-permute-start(bf16[592,256]{1,0:T(8,128)(2,1)S(1)} %collective-permute-done.4.down), channel_id=1, source_target_pairs={{0,4},{1,0},{2,1},{3,2},{7,3},{6,7},{5,6},{4,5},{8,12},{9,8},{10,9... | collective-permute-start | bytes 909320 | tf_op jit(solution)/shard_map/ppermute | solution.py:689
  15.1 1.5 %collective-permute-done.1.refs_2_ = bf16[128,2048]{1,0:T(8,128)(2,1)S(1)} collective-permute-done((bf16[128,2048]{1,0:T(8,128)(2,1)}, bf16[128,2048]{1,0:T(8,128)(2,1)S(1)}, u32[]{:S(2)}, u32[]{:S(2)}) %collective-permute-start.1) | collective-permute-done | bytes 524320 | tf_op jit(solution)/shard_map/ppermute | solution.py:702
  17.3 1.3 %collective-permute-done.5.swapped = bf16[128,256]{1,0:T(8,128)(2,1)S(1)} collective-permute-done((bf16[128,256]{1,0:T(8,128)(2,1)S(1)}, bf16[128,256]{1,0:T(8,128)(2,1)S(1)}, u32[]{:S(2)}, u32[]{:S(2)}) %collective-permute-start.5) | collective-permute-done | bytes 65568 | tf_op jit(solution)/shard_map/ppermute | solution.py:702
  18.6 2.2 %collective-permute-done.7.down = bf16[592,256]{1,0:T(8,128)(2,1)S(1)} collective-permute-done((bf16[592,256]{1,0:T(8,128)(2,1)S(1)}, bf16[592,256]{1,0:T(8,128)(2,1)S(1)}, u32[]{:S(2)}, u32[]{:S(2)}) %collective-permute-start.7) | collective-permute-done | bytes 303136 | tf_op jit(solution)/shard_map/ppermute | solution.py:689
  20.8 1.5 %collective-permute-start.10 = (bf16[592,256]{1,0:T(8,128)(2,1)S(1)}, bf16[592,256]{1,0:T(8,128)(2,1)S(1)}, u32[]{:S(2)}, u32[]{:S(2)}) collective-permute-start(bf16[592,256]{1,0:T(8,128)(2,1)S(1)} %collective-permute-done.7.down), channel_id=1, source_target_pairs={{0,4},{1,0},{2,1},{3,2},{7,3},{6,7},{5,6},{4,5},{8,12},{9,8},{10,9... | collective-permute-start | bytes 909320 | tf_op jit(solution)/shard_map/ppermute | solution.py:689
  23.0 1.2 %collective-permute-done.8.refs_5_ = bf16[128,256]{1,0:T(8,128)(2,1)S(1)} collective-permute-done((bf16[128,256]{1,0:T(8,128)(2,1)S(1)}, bf16[128,256]{1,0:T(8,128)(2,1)S(1)}, u32[]{:S(2)}, u32[]{:S(2)}) %collective-permute-start.8) | collective-permute-done | bytes 65568 | tf_op jit(solution)/shard_map/ppermute | solution.py:702
  24.2 1.3 %shard_map.95 = (f32[528,768]{1,0:T(8,128)S(1)}, bf16[512,768]{1,0:T(8,128)(2,1)S(1)}) custom-call(bf16[128,2048]{1,0:T(8,128)(2,1)S(1)} %bitcast.13, bf16[128,2048]{1,0:T(8,128)(2,1)S(1)} %collective-permute-done.refs_1_, bf16[128,2048]{1,0:T(8,128)(2,1)S(1)} %collective-permute-done.1.refs_2_, bf16[128,2048]{1,0:T(8,128)(2,1)S(1)} %collective-permute-done.2.refs_3_, ...), custom_call_target="tpu_custom_call" | custom-call | tf_op jit(solution)/shard_map/pallas_call | solution.py:594
  25.5 2.3 %collective-permute-done.10.down = bf16[592,256]{1,0:T(8,128)(2,1)S(1)} collective-permute-done((bf16[592,256]{1,0:T(8,128)(2,1)S(1)}, bf16[592,256]{1,0:T(8,128)(2,1)S(1)}, u32[]{:S(2)}, u32[]{:S(2)}) %collective-permute-start.10) | collective-permute-done | bytes 303136 | tf_op jit(solution)/shard_map/ppermute | solution.py:689
  28.6 1.7 %collective-permute-start.13 = (bf16[368,256]{1,0:T(8,128)(2,1)}, bf16[368,256]{1,0:T(8,128)(2,1)S(1)}, u32[]{:S(2)}, u32[]{:S(2)}) collective-permute-start(bf16[368,256]{1,0:T(8,128)(2,1)} %slice.7), channel_id=1, source_target_pairs={{0,4},{1,0},{2,1},{3,2},{7,3},{6,7},{5,6},{4,5},{8,12},{9,8},{10,9... | collective-permute-start | bytes 565256 | tf_op jit(solution)/shard_map/ppermute | solution.py:689
  31.3 1.8 %collective-permute-start.14 = (bf16[64,256]{1,0:T(8,128)(2,1)S(1)}, bf16[64,256]{1,0:T(8,128)(2,1)S(1)}, u32[]{:S(2)}, u32[]{:S(2)}) collective-permute-start(bf16[64,256]{1,0:T(8,128)(2,1)S(1)} %get-tuple-element.42), channel_id=1, source_target_pairs={{0,12},{1,8},{2,9},{3,10},{7,11},{6,15},{5,14},{4,13},{8,4},{9,0},... | collective-permute-start | bytes 98312 | tf_op jit(solution)/shard_map/ppermute | solution.py:698
  33.1 1.1 %shard_map.97.partial = f32[528,768]{1,0:T(8,128)S(1)} custom-call(f32[528,768]{1,0:T(8,128)S(1)} %get-tuple-element.37.partial, bf16[512,768]{1,0:T(8,128)(2,1)S(1)} %get-tuple-element.38.rest, bf16[592,256]{1,0:T(8,128)(2,1)S(1)} %collective-permute-done.9.up, bf16[592,256]{1,0:T(8,128)(2,1)S(1)} %collective-permute-done.10.down, ...), custom_call_target="tpu_custom_call" | custom-call | tf_op jit(solution)/shard_map/pallas_call | solution.py:594
  34.8 1.1 %collective-permute-done.12.up_end = bf16[224,256]{1,0:T(8,128)(2,1)S(1)} collective-permute-done((bf16[224,256]{1,0:T(8,128)(2,1)}, bf16[224,256]{1,0:T(8,128)(2,1)S(1)}, u32[]{:S(2)}, u32[]{:S(2)}) %collective-permute-start.12) | collective-permute-done | bytes 114720 | tf_op jit(solution)/shard_map/ppermute | solution.py:689
  35.9 5.1 %shard_map.98 = (bf16[128,512]{1,0:T(8,128)(2,1)S(1)}, bf16[128,512]{1,0:T(8,128)(2,1)S(1)}, bf16[128,512]{1,0:T(8,128)(2,1)S(1)}, bf16[128,512]{1,0:T(8,128)(2,1)S(1)}) custom-call(f32[528,768]{1,0:T(8,128)S(1)} %shard_map.97.partial, bf16[512,768]{1,0:T(8,128)(2,1)S(1)} %get-tuple-element.38.rest, bf16[224,256]{1,0:T(8,128)(2,1)S(1)} %collective-permute-done.12.up_end, ...), custom_call_target="tpu_custom_call" | custom-call | tf_op jit(solution)/shard_map/pallas_call | solution.py:594
  41.1 1.6 %collective-permute-start.16 = (bf16[128,512]{1,0:T(8,128)(2,1)S(1)}, bf16[128,512]{1,0:T(8,128)(2,1)S(1)}, u32[]{:S(2)}, u32[]{:S(2)}) collective-permute-start(bf16[128,512]{1,0:T(8,128)(2,1)S(1)} %get-tuple-element.45), channel_id=1, source_target_pairs={{0,16},{8,24},{16,0},{24,8},{1,17},{9,25},{17,1},{25,9},{2,18},{10... | collective-permute-start | bytes 393224 | tf_op jit(solution)/shard_map/ppermute | solution.py:702
  43.1 4.4 %collective-permute-done.16 = bf16[128,512]{1,0:T(8,128)(2,1)S(1)} collective-permute-done((bf16[128,512]{1,0:T(8,128)(2,1)S(1)}, bf16[128,512]{1,0:T(8,128)(2,1)S(1)}, u32[]{:S(2)}, u32[]{:S(2)}) %collective-permute-start.16) | collective-permute-done | bytes 131104 | tf_op jit(solution)/shard_map/ppermute | solution.py:702
  47.5 1.9 %collective-permute-done.17 = bf16[128,512]{1,0:T(8,128)(2,1)S(1)} collective-permute-done((bf16[128,512]{1,0:T(8,128)(2,1)S(1)}, bf16[128,512]{1,0:T(8,128)(2,1)S(1)}, u32[]{:S(2)}, u32[]{:S(2)}) %collective-permute-start.17) | collective-permute-done | bytes 131104 | tf_op jit(solution)/shard_map/ppermute | solution.py:702
  (47 shorter events, 8.7 us)
Async XLA Ops:
  0.0 1.3 %copy-start = (bf16[256,2208]{0,1:T(8,128)(2,1)S(1)}, bf16[256,2208]{0,1:T(8,128)(2,1)}, u32[]{:S(2)}) copy-start(bf16[256,2208]{0,1:T(8,128)(2,1)} %param.10) | copy-start | bytes 3391492
  1.4 15.2 %collective-permute-start.1 = (bf16[128,2048]{1,0:T(8,128)(2,1)}, bf16[128,2048]{1,0:T(8,128)(2,1)S(1)}, u32[]{:S(2)}, u32[]{:S(2)}) collective-permute-start(bf16[128,2048]{1,0:T(8,128)(2,1)} %bitcast.11), channel_id=1, source_target_pairs={{0,16},{8,24},{16,0},{24,8},{1,17},{9,25},{17,1},{25,9},{2,18},{10... | collective-permute-start | bytes 1572872 | tf_op jit(solution)/shard_map/ppermute | solution.py:702
  4.4 8.6 %collective-permute-start.4 = (bf16[592,256]{1,0:T(8,128)(2,1)S(1)}, bf16[592,256]{1,0:T(8,128)(2,1)S(1)}, u32[]{:S(2)}, u32[]{:S(2)}) collective-permute-start(bf16[592,256]{1,0:T(8,128)(2,1)S(1)} %get-tuple-element.26.own), channel_id=1, source_target_pairs={{0,4},{1,0},{2,1},{3,2},{7,3},{6,7},{5,6},{4,5},{8,12},{9,8},{10,9... | collective-permute-start | bytes 909320 | tf_op jit(solution)/shard_map/ppermute | solution.py:689
  5.9 8.6 %collective-permute-start.3 = (bf16[592,256]{1,0:T(8,128)(2,1)S(1)}, bf16[592,256]{1,0:T(8,128)(2,1)S(1)}, u32[]{:S(2)}, u32[]{:S(2)}) collective-permute-start(bf16[592,256]{1,0:T(8,128)(2,1)S(1)} %get-tuple-element.26.own), channel_id=1, source_target_pairs={{0,1},{1,2},{2,3},{3,7},{7,6},{6,5},{5,4},{4,0},{8,9},{9,10},{10,1... | collective-permute-start | bytes 909320 | tf_op jit(solution)/shard_map/ppermute | solution.py:689
  6.5 0.9 %copy-start.2 = (f32[2,4,2176]{2,1,0:T(4,128)S(1)}, f32[2,4,2176]{2,1,0:T(4,128)}, u32[]{:S(2)}) copy-start(f32[2,4,2176]{2,1,0:T(4,128)} %refs_1_.1) | copy-start | bytes 208900
  7.4 0.7 %copy-start.3 = (f32[2,2176]{1,0:T(2,128)S(1)}, f32[2,2176]{1,0:T(2,128)}, u32[]{:S(2)}) copy-start(f32[2,2176]{1,0:T(2,128)} %refs_2_.1) | copy-start | bytes 52228
  8.1 0.7 %copy-start.4 = (f32[2,2048]{1,0:T(2,128)S(1)}, f32[2,2048]{1,0:T(2,128)}, u32[]{:S(2)}) copy-start(f32[2,2048]{1,0:T(2,128)} %refs_6_.1) | copy-start | bytes 49156
  13.1 7.7 %collective-permute-start.7 = (bf16[592,256]{1,0:T(8,128)(2,1)S(1)}, bf16[592,256]{1,0:T(8,128)(2,1)S(1)}, u32[]{:S(2)}, u32[]{:S(2)}) collective-permute-start(bf16[592,256]{1,0:T(8,128)(2,1)S(1)} %collective-permute-done.4.down), channel_id=1, source_target_pairs={{0,4},{1,0},{2,1},{3,2},{7,3},{6,7},{5,6},{4,5},{8,12},{9,8},{10,9... | collective-permute-start | bytes 909320 | tf_op jit(solution)/shard_map/ppermute | solution.py:689
  14.6 7.7 %collective-permute-start.6 = (bf16[592,256]{1,0:T(8,128)(2,1)S(1)}, bf16[592,256]{1,0:T(8,128)(2,1)S(1)}, u32[]{:S(2)}, u32[]{:S(2)}) collective-permute-start(bf16[592,256]{1,0:T(8,128)(2,1)S(1)} %collective-permute-done.3.up), channel_id=1, source_target_pairs={{0,1},{1,2},{2,3},{3,7},{7,6},{6,5},{5,4},{4,0},{8,9},{9,10},{10,1... | collective-permute-start | bytes 909320 | tf_op jit(solution)/shard_map/ppermute | solution.py:689
  15.1 7.9 %collective-permute-start = (bf16[128,2048]{1,0:T(8,128)(2,1)}, bf16[128,2048]{1,0:T(8,128)(2,1)S(1)}, u32[]{:S(2)}, u32[]{:S(2)}) collective-permute-start(bf16[128,2048]{1,0:T(8,128)(2,1)} %bitcast.12), channel_id=1, source_target_pairs={{0,8},{8,0},{16,24},{24,16},{1,9},{9,1},{17,25},{25,17},{2,10},{10... | collective-permute-start | bytes 1572872 | tf_op jit(solution)/shard_map/ppermute | solution.py:702
  16.6 7.6 %collective-permute-start.2 = (bf16[128,2048]{1,0:T(8,128)(2,1)S(1)}, bf16[128,2048]{1,0:T(8,128)(2,1)S(1)}, u32[]{:S(2)}, u32[]{:S(2)}) collective-permute-start(bf16[128,2048]{1,0:T(8,128)(2,1)S(1)} %collective-permute-done.1.refs_2_), channel_id=1, source_target_pairs={{0,8},{8,0},{16,24},{24,16},{1,9},{9,1},{17,25},{25,17},{2,10},{10... | collective-permute-start | bytes 1572872 | tf_op jit(solution)/shard_map/ppermute | solution.py:702
  16.6 7.6 %copy-start.1 = (bf16[1,128,2048]{2,1,0:T(8,128)(2,1)S(1)}, bf16[1,128,2048]{2,1,0:T(8,128)(2,1)}, u32[]{:S(2)}) copy-start(bf16[1,128,2048]{2,1,0:T(8,128)(2,1)} %param.9) | copy-start | bytes 1572868
  16.7 1.9 %collective-permute-start.5 = (bf16[128,256]{1,0:T(8,128)(2,1)S(1)}, bf16[128,256]{1,0:T(8,128)(2,1)S(1)}, u32[]{:S(2)}, u32[]{:S(2)}) collective-permute-start(bf16[128,256]{1,0:T(8,128)(2,1)S(1)} %get-tuple-element.32), channel_id=1, source_target_pairs={{0,8},{8,0},{16,24},{24,16},{1,9},{9,1},{17,25},{25,17},{2,10},{10... | collective-permute-start | bytes 196616 | tf_op jit(solution)/shard_map/ppermute | solution.py:702
  20.8 7.0 %collective-permute-start.10 = (bf16[592,256]{1,0:T(8,128)(2,1)S(1)}, bf16[592,256]{1,0:T(8,128)(2,1)S(1)}, u32[]{:S(2)}, u32[]{:S(2)}) collective-permute-start(bf16[592,256]{1,0:T(8,128)(2,1)S(1)} %collective-permute-done.7.down), channel_id=1, source_target_pairs={{0,4},{1,0},{2,1},{3,2},{7,3},{6,7},{5,6},{4,5},{8,12},{9,8},{10,9... | collective-permute-start | bytes 909320 | tf_op jit(solution)/shard_map/ppermute | solution.py:689
  22.3 7.9 %collective-permute-start.9 = (bf16[592,256]{1,0:T(8,128)(2,1)S(1)}, bf16[592,256]{1,0:T(8,128)(2,1)S(1)}, u32[]{:S(2)}, u32[]{:S(2)}) collective-permute-start(bf16[592,256]{1,0:T(8,128)(2,1)S(1)} %collective-permute-done.6.up), channel_id=1, source_target_pairs={{0,1},{1,2},{2,3},{3,7},{7,6},{6,5},{5,4},{4,0},{8,9},{9,10},{10,1... | collective-permute-start | bytes 909320 | tf_op jit(solution)/shard_map/ppermute | solution.py:689
  22.9 1.3 %collective-permute-start.8 = (bf16[128,256]{1,0:T(8,128)(2,1)S(1)}, bf16[128,256]{1,0:T(8,128)(2,1)S(1)}, u32[]{:S(2)}, u32[]{:S(2)}) collective-permute-start(bf16[128,256]{1,0:T(8,128)(2,1)S(1)} %get-tuple-element.36), channel_id=1, source_target_pairs={{0,8},{8,0},{16,24},{24,16},{1,9},{9,1},{17,25},{25,17},{2,10},{10... | collective-permute-start | bytes 196616 | tf_op jit(solution)/shard_map/ppermute | solution.py:702
  28.6 7.3 %collective-permute-start.13 = (bf16[368,256]{1,0:T(8,128)(2,1)}, bf16[368,256]{1,0:T(8,128)(2,1)S(1)}, u32[]{:S(2)}, u32[]{:S(2)}) collective-permute-start(bf16[368,256]{1,0:T(8,128)(2,1)} %slice.7), channel_id=1, source_target_pairs={{0,4},{1,0},{2,1},{3,2},{7,3},{6,7},{5,6},{4,5},{8,12},{9,8},{10,9... | collective-permute-start | bytes 565256 | tf_op jit(solution)/shard_map/ppermute | solution.py:689
  30.9 5.0 %collective-permute-start.12 = (bf16[224,256]{1,0:T(8,128)(2,1)}, bf16[224,256]{1,0:T(8,128)(2,1)S(1)}, u32[]{:S(2)}, u32[]{:S(2)}) collective-permute-start(bf16[224,256]{1,0:T(8,128)(2,1)} %slice.6), channel_id=1, source_target_pairs={{0,1},{1,2},{2,3},{3,7},{7,6},{6,5},{5,4},{4,0},{8,9},{9,10},{10,1... | collective-permute-start | bytes 344072 | tf_op jit(solution)/shard_map/ppermute | solution.py:689
  31.3 1.8 %collective-permute-start.11 = (bf16[128,256]{1,0:T(8,128)(2,1)S(1)}, bf16[128,256]{1,0:T(8,128)(2,1)S(1)}, u32[]{:S(2)}, u32[]{:S(2)}) collective-permute-start(bf16[128,256]{1,0:T(8,128)(2,1)S(1)} %get-tuple-element.41), channel_id=1, source_target_pairs={{0,8},{8,0},{16,24},{24,16},{1,9},{9,1},{17,25},{25,17},{2,10},{10... | collective-permute-start | bytes 196616 | tf_op jit(solution)/shard_map/ppermute | solution.py:702
  31.3 3.4 %collective-permute-start.14 = (bf16[64,256]{1,0:T(8,128)(2,1)S(1)}, bf16[64,256]{1,0:T(8,128)(2,1)S(1)}, u32[]{:S(2)}, u32[]{:S(2)}) collective-permute-start(bf16[64,256]{1,0:T(8,128)(2,1)S(1)} %get-tuple-element.42), channel_id=1, source_target_pairs={{0,12},{1,8},{2,9},{3,10},{7,11},{6,15},{5,14},{4,13},{8,4},{9,0},... | collective-permute-start | bytes 98312 | tf_op jit(solution)/shard_map/ppermute | solution.py:698
  41.0 2.0 %collective-permute-start.15 = (bf16[128,512]{1,0:T(8,128)(2,1)S(1)}, bf16[128,512]{1,0:T(8,128)(2,1)S(1)}, u32[]{:S(2)}, u32[]{:S(2)}) collective-permute-start(bf16[128,512]{1,0:T(8,128)(2,1)S(1)} %get-tuple-element.44), channel_id=1, source_target_pairs={{0,8},{8,0},{16,24},{24,16},{1,9},{9,1},{17,25},{25,17},{2,10},{10... | collective-permute-start | bytes 393224 | tf_op jit(solution)/shard_map/ppermute | solution.py:702
  41.1 6.4 %collective-permute-start.16 = (bf16[128,512]{1,0:T(8,128)(2,1)S(1)}, bf16[128,512]{1,0:T(8,128)(2,1)S(1)}, u32[]{:S(2)}, u32[]{:S(2)}) collective-permute-start(bf16[128,512]{1,0:T(8,128)(2,1)S(1)} %get-tuple-element.45), channel_id=1, source_target_pairs={{0,16},{8,24},{16,0},{24,8},{1,17},{9,25},{17,1},{25,9},{2,18},{10... | collective-permute-start | bytes 393224 | tf_op jit(solution)/shard_map/ppermute | solution.py:702
  42.7 6.7 %collective-permute-start.17 = (bf16[128,512]{1,0:T(8,128)(2,1)S(1)}, bf16[128,512]{1,0:T(8,128)(2,1)S(1)}, u32[]{:S(2)}, u32[]{:S(2)}) collective-permute-start(bf16[128,512]{1,0:T(8,128)(2,1)S(1)} %get-tuple-element.46), channel_id=1, source_target_pairs={{0,24},{8,16},{16,8},{24,0},{1,25},{9,17},{17,9},{25,1},{2,26},{10... | collective-permute-start | bytes 393224 | tf_op jit(solution)/shard_map/ppermute | solution.py:702
  47.5 1.9 %copy-start.9 = (bf16[1,128,2048]{2,1,0:T(8,128)(2,1)}, bf16[1,128,2048]{2,1,0:T(8,128)(2,1)S(1)}, u32[]{:S(2)}) copy-start(bf16[1,128,2048]{2,1,0:T(8,128)(2,1)S(1)} %bitcast_dynamic-update-slice_fusion.1) | copy-start | bytes 1572868
  (4 other events, 2.7 us)

commit v11 on v10

--- a/solution.py
+++ b/solution.py
@@ -621,6 +621,14 @@
     return call(kernel, shapes, [], held, swapped, up, down, aliases={0: 0})
 
 
+def take_kernel(value, out):
+    out[...] = value[: out.shape[0], :]
+
+
+def take(value, rows):
+    return call(take_kernel, [((rows, value.shape[1]), value.dtype)], [], value)[0]
+
+
 def split(columns, up, down):
     rows, depth = up.shape
     shapes = [(2 * STATE, depth), (STATE, depth)]
@@ -738,7 +746,7 @@
         up, _ = lax.optimization_barrier((up, beside))
         down, _ = lax.optimization_barrier((down, beside))
     cut = own.shape[0] * 2 // 5 // 16 * 16
-    ends = [turn(up[:cut], 1), turn(down[cut:], -1)]
+    ends = [turn(take(up, cut), 1), turn(down[cut:], -1)]
     sent, crossing = split(columns, up, down)
     far = turn_across(crossing, -1)
     partial = second(columns, partial, rest, up, down, swap(sent, "seq", 1))

time: 50.4 us -> 49.4 us (0.980)
  waiting for transfers between devices: 17.3 us -> 16.2 us
  local copies, waits for them, and re-layouts: 8.37 us -> 7.71 us
  Pallas kernels: 8.64 us -> 9.28 us
    ppermute x8, waiting for transfers between devices: 6.48 us -> 5.46 us  [turn(): lax.ppermute(value, ('fsdp', 'batch'), [(order[i], order[(i + way) % coun...]
    slice x2 -> x1, local copies, waits for them, and re-layouts: 1.35 us -> 0.69 us  [on_heads(): ends = [turn(take(up, cut), 1), turn(down[cut:], -1)]]
    pallas_call x8 -> x9, Pallas kernels: 8.64 us -> 9.28 us  [call(): pl.pallas_call(kernel, out_shape=shapes, in_specs=[space] * (len(operands...]
  transfers between devices with their start and end apart: 18 -> 18, of which waited for: 10 -> 10; matrix products, arithmetic and copies ran while one was open for 3% -> 2% of each run, Pallas kernels for 7% -> 8%
where the time goes in v11:
time: 49.4 us; the launch traced here: 49 us
  waiting for transfers between devices  16.2 us (33%)
  starting transfers between devices  15.7 us (32%)
  Pallas kernels  9.28 us (19%)
  local copies, waits for them, and re-layouts  7.71 us (16%)
    ppermute x9, waiting for transfers between devices, swap(): lax.ppermute(value, axis, [(i, i ^ mask) for i in range(lax.axis_size(axi...  9.9 us
    pallas_call x9, Pallas kernels, call(): pl.pallas_call(kernel, out_shape=shapes, in_specs=[space] * (len(operands...  9.28 us
    ppermute x8, starting transfers between devices, turn(): lax.ppermute(value, ('fsdp', 'batch'), [(order[i], order[(i + way) % coun...  8.16 us
    unnamed x20, local copies, waits for them, and re-layouts  6.27 us
    ppermute x9, starting transfers between devices, swap(): lax.ppermute(value, axis, [(i, i ^ mask) for i in range(lax.axis_size(axi...  5.74 us
    ppermute x8, waiting for transfers between devices, turn(): lax.ppermute(value, ('fsdp', 'batch'), [(order[i], order[(i + way) % coun...  5.46 us
    ppermute x1, starting transfers between devices, turn_across(): return lax.ppermute(value, ('seq', 'fsdp', 'batch'), pairs)  1.77 us
  transfers between devices with their start and end apart: 18, of which 10 were waited for; matrix products, arithmetic and copies ran while one was open for 2% of the time, Pallas kernels for 8%

profile of v11, /device:TPU:0, one launch (start us, length us, event | category | flops | bytes accessed | tf_op | source)
XLA Modules:
  0.0 49.0 jit_solution(18274457046802558712)
XLA Ops:
  0.0 1.3 %copy-done = bf16[256,2208]{0,1:T(8,128)(2,1)S(1)} copy-done((bf16[256,2208]{0,1:T(8,128)(2,1)S(1)}, bf16[256,2208]{0,1:T(8,128)(2,1)}, u32[]{:S(2)}) %copy-start) | copy-done | bytes 1130520
  1.4 3.0 %collective-permute-start.1 = (bf16[128,2048]{1,0:T(8,128)(2,1)}, bf16[128,2048]{1,0:T(8,128)(2,1)S(1)}, u32[]{:S(2)}, u32[]{:S(2)}) collective-permute-start(bf16[128,2048]{1,0:T(8,128)(2,1)} %bitcast.11), channel_id=1, source_target_pairs={{0,16},{8,24},{16,0},{24,8},{1,17},{9,25},{17,1},{25,9},{2,18},{10... | collective-permute-start | bytes 1572872 | tf_op jit(solution)/shard_map/ppermute | solution.py:710
  4.4 1.5 %collective-permute-start.4 = (bf16[592,256]{1,0:T(8,128)(2,1)S(1)}, bf16[592,256]{1,0:T(8,128)(2,1)S(1)}, u32[]{:S(2)}, u32[]{:S(2)}) collective-permute-start(bf16[592,256]{1,0:T(8,128)(2,1)S(1)} %get-tuple-element.26.own), channel_id=1, source_target_pairs={{0,4},{1,0},{2,1},{3,2},{7,3},{6,7},{5,6},{4,5},{8,12},{9,8},{10,9... | collective-permute-start | bytes 909320 | tf_op jit(solution)/shard_map/ppermute | solution.py:697
  6.5 0.9 %copy-done.2 = f32[2,4,2176]{2,1,0:T(4,128)S(1)} copy-done((f32[2,4,2176]{2,1,0:T(4,128)S(1)}, f32[2,4,2176]{2,1,0:T(4,128)}, u32[]{:S(2)}) %copy-start.2) | copy-done | bytes 69656
  7.4 0.7 %copy-done.3 = f32[2,2176]{1,0:T(2,128)S(1)} copy-done((f32[2,2176]{1,0:T(2,128)S(1)}, f32[2,2176]{1,0:T(2,128)}, u32[]{:S(2)}) %copy-start.3) | copy-done | bytes 17432
  8.1 0.7 %copy-done.4 = f32[2,2048]{1,0:T(2,128)S(1)} copy-done((f32[2,2048]{1,0:T(2,128)S(1)}, f32[2,2048]{1,0:T(2,128)}, u32[]{:S(2)}) %copy-start.4) | copy-done | bytes 16408
  11.5 0.8 %shard_map.92.refs_6_ = f32[144,640]{1,0:T(8,128)S(1)} custom-call(s32[1,4]{1,0:T(1,128)S(1)} %copy-done.8, f32[2,4,2176]{2,1,0:T(4,128)S(1)} %copy-done.2, f32[2,2176]{1,0:T(2,128)S(1)} %copy-done.3, f32[2,32]{1,0:T(2,128)S(1)} %copy-done.5, f32[2,32]{1,0:T(2,128)S(1)} %copy-done.6, f32[2,32]{1,0:T(2,128)S(1)} %copy-done.7, f32[2,2048]{1,0:T(2,128)S(1)} %copy-done.4), custom_call_target="tpu_custom_call" | custom-call | tf_op jit(solution)/shard_map/pallas_call | solution.py:594
  12.3 0.8 %collective-permute-done.4.down = bf16[592,256]{1,0:T(8,128)(2,1)S(1)} collective-permute-done((bf16[592,256]{1,0:T(8,128)(2,1)S(1)}, bf16[592,256]{1,0:T(8,128)(2,1)S(1)}, u32[]{:S(2)}, u32[]{:S(2)}) %collective-permute-start.4) | collective-permute-done | bytes 303136 | tf_op jit(solution)/shard_map/ppermute | solution.py:697
  13.1 1.5 %collective-permute-start.7 = (bf16[592,256]{1,0:T(8,128)(2,1)S(1)}, bf16[592,256]{1,0:T(8,128)(2,1)S(1)}, u32[]{:S(2)}, u32[]{:S(2)}) collective-permute-start(bf16[592,256]{1,0:T(8,128)(2,1)S(1)} %collective-permute-done.4.down), channel_id=1, source_target_pairs={{0,4},{1,0},{2,1},{3,2},{7,3},{6,7},{5,6},{4,5},{8,12},{9,8},{10,9... | collective-permute-start | bytes 909320 | tf_op jit(solution)/shard_map/ppermute | solution.py:697
  15.1 1.5 %collective-permute-done.1.refs_2_ = bf16[128,2048]{1,0:T(8,128)(2,1)S(1)} collective-permute-done((bf16[128,2048]{1,0:T(8,128)(2,1)}, bf16[128,2048]{1,0:T(8,128)(2,1)S(1)}, u32[]{:S(2)}, u32[]{:S(2)}) %collective-permute-start.1) | collective-permute-done | bytes 524320 | tf_op jit(solution)/shard_map/ppermute | solution.py:710
  17.3 1.3 %collective-permute-done.5.swapped = bf16[128,256]{1,0:T(8,128)(2,1)S(1)} collective-permute-done((bf16[128,256]{1,0:T(8,128)(2,1)S(1)}, bf16[128,256]{1,0:T(8,128)(2,1)S(1)}, u32[]{:S(2)}, u32[]{:S(2)}) %collective-permute-start.5) | collective-permute-done | bytes 65568 | tf_op jit(solution)/shard_map/ppermute | solution.py:710
  18.6 2.2 %collective-permute-done.7.down = bf16[592,256]{1,0:T(8,128)(2,1)S(1)} collective-permute-done((bf16[592,256]{1,0:T(8,128)(2,1)S(1)}, bf16[592,256]{1,0:T(8,128)(2,1)S(1)}, u32[]{:S(2)}, u32[]{:S(2)}) %collective-permute-start.7) | collective-permute-done | bytes 303136 | tf_op jit(solution)/shard_map/ppermute | solution.py:697
  20.8 1.5 %collective-permute-start.10 = (bf16[592,256]{1,0:T(8,128)(2,1)S(1)}, bf16[592,256]{1,0:T(8,128)(2,1)S(1)}, u32[]{:S(2)}, u32[]{:S(2)}) collective-permute-start(bf16[592,256]{1,0:T(8,128)(2,1)S(1)} %collective-permute-done.7.down), channel_id=1, source_target_pairs={{0,4},{1,0},{2,1},{3,2},{7,3},{6,7},{5,6},{4,5},{8,12},{9,8},{10,9... | collective-permute-start | bytes 909320 | tf_op jit(solution)/shard_map/ppermute | solution.py:697
  23.0 1.2 %collective-permute-done.8.refs_5_ = bf16[128,256]{1,0:T(8,128)(2,1)S(1)} collective-permute-done((bf16[128,256]{1,0:T(8,128)(2,1)S(1)}, bf16[128,256]{1,0:T(8,128)(2,1)S(1)}, u32[]{:S(2)}, u32[]{:S(2)}) %collective-permute-start.8) | collective-permute-done | bytes 65568 | tf_op jit(solution)/shard_map/ppermute | solution.py:710
  24.2 1.3 %shard_map.95 = (f32[528,768]{1,0:T(8,128)S(1)}, bf16[512,768]{1,0:T(8,128)(2,1)S(1)}) custom-call(bf16[128,2048]{1,0:T(8,128)(2,1)S(1)} %bitcast.13, bf16[128,2048]{1,0:T(8,128)(2,1)S(1)} %collective-permute-done.refs_1_, bf16[128,2048]{1,0:T(8,128)(2,1)S(1)} %collective-permute-done.1.refs_2_, bf16[128,2048]{1,0:T(8,128)(2,1)S(1)} %collective-permute-done.2.refs_3_, ...), custom_call_target="tpu_custom_call" | custom-call | tf_op jit(solution)/shard_map/pallas_call | solution.py:594
  25.5 2.3 %collective-permute-done.10.down = bf16[592,256]{1,0:T(8,128)(2,1)S(1)} collective-permute-done((bf16[592,256]{1,0:T(8,128)(2,1)S(1)}, bf16[592,256]{1,0:T(8,128)(2,1)S(1)}, u32[]{:S(2)}, u32[]{:S(2)}) %collective-permute-start.10) | collective-permute-done | bytes 303136 | tf_op jit(solution)/shard_map/ppermute | solution.py:697
  28.6 1.7 %collective-permute-start.13 = (bf16[368,256]{1,0:T(8,128)(2,1)}, bf16[368,256]{1,0:T(8,128)(2,1)S(1)}, u32[]{:S(2)}, u32[]{:S(2)}) collective-permute-start(bf16[368,256]{1,0:T(8,128)(2,1)} %slice.3), channel_id=1, source_target_pairs={{0,4},{1,0},{2,1},{3,2},{7,3},{6,7},{5,6},{4,5},{8,12},{9,8},{10,9... | collective-permute-start | bytes 565256 | tf_op jit(solution)/shard_map/ppermute | solution.py:697
  31.3 1.8 %collective-permute-start.14 = (bf16[64,256]{1,0:T(8,128)(2,1)}, bf16[64,256]{1,0:T(8,128)(2,1)S(1)}, u32[]{:S(2)}, u32[]{:S(2)}) collective-permute-start(bf16[64,256]{1,0:T(8,128)(2,1)} %get-tuple-element.42), channel_id=1, source_target_pairs={{0,12},{1,8},{2,9},{3,10},{7,11},{6,15},{5,14},{4,13},{8,4},{9,0},... | collective-permute-start | bytes 98312 | tf_op jit(solution)/shard_map/ppermute | solution.py:706
  33.1 1.1 %shard_map.97.partial = f32[528,768]{1,0:T(8,128)S(1)} custom-call(f32[528,768]{1,0:T(8,128)S(1)} %get-tuple-element.37.partial, bf16[512,768]{1,0:T(8,128)(2,1)S(1)} %get-tuple-element.38.rest, bf16[592,256]{1,0:T(8,128)(2,1)S(1)} %collective-permute-done.9.up.value, bf16[592,256]{1,0:T(8,128)(2,1)S(1)} %collective-permute-done.10.down, ...), custom_call_target="tpu_custom_call" | custom-call | tf_op jit(solution)/shard_map/pallas_call | solution.py:594
  34.2 0.8 %collective-permute-done.14.far = bf16[64,256]{1,0:T(8,128)(2,1)S(1)} collective-permute-done((bf16[64,256]{1,0:T(8,128)(2,1)}, bf16[64,256]{1,0:T(8,128)(2,1)S(1)}, u32[]{:S(2)}, u32[]{:S(2)}) %collective-permute-start.14) | collective-permute-done | bytes 32800 | tf_op jit(solution)/shard_map/ppermute | solution.py:706
  35.1 5.1 %shard_map.99 = (bf16[128,512]{1,0:T(8,128)(2,1)S(1)}, bf16[128,512]{1,0:T(8,128)(2,1)S(1)}, bf16[128,512]{1,0:T(8,128)(2,1)S(1)}, bf16[128,512]{1,0:T(8,128)(2,1)S(1)}) custom-call(f32[528,768]{1,0:T(8,128)S(1)} %shard_map.97.partial, bf16[512,768]{1,0:T(8,128)(2,1)S(1)} %get-tuple-element.38.rest, bf16[224,256]{1,0:T(8,128)(2,1)S(1)} %collective-permute-done.12.up_end, ...), custom_call_target="tpu_custom_call" | custom-call | tf_op jit(solution)/shard_map/pallas_call | solution.py:594
  40.6 1.7 %collective-permute-start.16 = (bf16[128,512]{1,0:T(8,128)(2,1)S(1)}, bf16[128,512]{1,0:T(8,128)(2,1)S(1)}, u32[]{:S(2)}, u32[]{:S(2)}) collective-permute-start(bf16[128,512]{1,0:T(8,128)(2,1)S(1)} %get-tuple-element.45), channel_id=1, source_target_pairs={{0,16},{8,24},{16,0},{24,8},{1,17},{9,25},{17,1},{25,9},{2,18},{10... | collective-permute-start | bytes 393224 | tf_op jit(solution)/shard_map/ppermute | solution.py:710
  42.4 4.5 %collective-permute-done.16 = bf16[128,512]{1,0:T(8,128)(2,1)S(1)} collective-permute-done((bf16[128,512]{1,0:T(8,128)(2,1)S(1)}, bf16[128,512]{1,0:T(8,128)(2,1)S(1)}, u32[]{:S(2)}, u32[]{:S(2)}) %collective-permute-start.16) | collective-permute-done | bytes 131104 | tf_op jit(solution)/shard_map/ppermute | solution.py:710
  46.9 1.4 %collective-permute-done.17 = bf16[128,512]{1,0:T(8,128)(2,1)S(1)} collective-permute-done((bf16[128,512]{1,0:T(8,128)(2,1)S(1)}, bf16[128,512]{1,0:T(8,128)(2,1)S(1)}, u32[]{:S(2)}, u32[]{:S(2)}) %collective-permute-start.17) | collective-permute-done | bytes 131104 | tf_op jit(solution)/shard_map/ppermute | solution.py:710
  (47 shorter events, 8.2 us)
Async XLA Ops:
  0.0 1.3 %copy-start = (bf16[256,2208]{0,1:T(8,128)(2,1)S(1)}, bf16[256,2208]{0,1:T(8,128)(2,1)}, u32[]{:S(2)}) copy-start(bf16[256,2208]{0,1:T(8,128)(2,1)} %param.10) | copy-start | bytes 3391492
  1.4 15.2 %collective-permute-start.1 = (bf16[128,2048]{1,0:T(8,128)(2,1)}, bf16[128,2048]{1,0:T(8,128)(2,1)S(1)}, u32[]{:S(2)}, u32[]{:S(2)}) collective-permute-start(bf16[128,2048]{1,0:T(8,128)(2,1)} %bitcast.11), channel_id=1, source_target_pairs={{0,16},{8,24},{16,0},{24,8},{1,17},{9,25},{17,1},{25,9},{2,18},{10... | collective-permute-start | bytes 1572872 | tf_op jit(solution)/shard_map/ppermute | solution.py:710
  4.4 8.6 %collective-permute-start.4 = (bf16[592,256]{1,0:T(8,128)(2,1)S(1)}, bf16[592,256]{1,0:T(8,128)(2,1)S(1)}, u32[]{:S(2)}, u32[]{:S(2)}) collective-permute-start(bf16[592,256]{1,0:T(8,128)(2,1)S(1)} %get-tuple-element.26.own), channel_id=1, source_target_pairs={{0,4},{1,0},{2,1},{3,2},{7,3},{6,7},{5,6},{4,5},{8,12},{9,8},{10,9... | collective-permute-start | bytes 909320 | tf_op jit(solution)/shard_map/ppermute | solution.py:697
  5.9 8.6 %collective-permute-start.3 = (bf16[592,256]{1,0:T(8,128)(2,1)S(1)}, bf16[592,256]{1,0:T(8,128)(2,1)S(1)}, u32[]{:S(2)}, u32[]{:S(2)}) collective-permute-start(bf16[592,256]{1,0:T(8,128)(2,1)S(1)} %get-tuple-element.26.own), channel_id=1, source_target_pairs={{0,1},{1,2},{2,3},{3,7},{7,6},{6,5},{5,4},{4,0},{8,9},{9,10},{10,1... | collective-permute-start | bytes 909320 | tf_op jit(solution)/shard_map/ppermute | solution.py:697
  6.5 0.9 %copy-start.2 = (f32[2,4,2176]{2,1,0:T(4,128)S(1)}, f32[2,4,2176]{2,1,0:T(4,128)}, u32[]{:S(2)}) copy-start(f32[2,4,2176]{2,1,0:T(4,128)} %refs_1_.1) | copy-start | bytes 208900
  7.4 0.7 %copy-start.3 = (f32[2,2176]{1,0:T(2,128)S(1)}, f32[2,2176]{1,0:T(2,128)}, u32[]{:S(2)}) copy-start(f32[2,2176]{1,0:T(2,128)} %refs_2_.1) | copy-start | bytes 52228
  8.1 0.7 %copy-start.4 = (f32[2,2048]{1,0:T(2,128)S(1)}, f32[2,2048]{1,0:T(2,128)}, u32[]{:S(2)}) copy-start(f32[2,2048]{1,0:T(2,128)} %refs_6_.1) | copy-start | bytes 49156
  13.1 7.7 %collective-permute-start.7 = (bf16[592,256]{1,0:T(8,128)(2,1)S(1)}, bf16[592,256]{1,0:T(8,128)(2,1)S(1)}, u32[]{:S(2)}, u32[]{:S(2)}) collective-permute-start(bf16[592,256]{1,0:T(8,128)(2,1)S(1)} %collective-permute-done.4.down), channel_id=1, source_target_pairs={{0,4},{1,0},{2,1},{3,2},{7,3},{6,7},{5,6},{4,5},{8,12},{9,8},{10,9... | collective-permute-start | bytes 909320 | tf_op jit(solution)/shard_map/ppermute | solution.py:697
  14.6 7.7 %collective-permute-start.6 = (bf16[592,256]{1,0:T(8,128)(2,1)S(1)}, bf16[592,256]{1,0:T(8,128)(2,1)S(1)}, u32[]{:S(2)}, u32[]{:S(2)}) collective-permute-start(bf16[592,256]{1,0:T(8,128)(2,1)S(1)} %collective-permute-done.3.up), channel_id=1, source_target_pairs={{0,1},{1,2},{2,3},{3,7},{7,6},{6,5},{5,4},{4,0},{8,9},{9,10},{10,1... | collective-permute-start | bytes 909320 | tf_op jit(solution)/shard_map/ppermute | solution.py:697
  15.1 7.9 %collective-permute-start = (bf16[128,2048]{1,0:T(8,128)(2,1)}, bf16[128,2048]{1,0:T(8,128)(2,1)S(1)}, u32[]{:S(2)}, u32[]{:S(2)}) collective-permute-start(bf16[128,2048]{1,0:T(8,128)(2,1)} %bitcast.12), channel_id=1, source_target_pairs={{0,8},{8,0},{16,24},{24,16},{1,9},{9,1},{17,25},{25,17},{2,10},{10... | collective-permute-start | bytes 1572872 | tf_op jit(solution)/shard_map/ppermute | solution.py:710
  16.6 7.6 %collective-permute-start.2 = (bf16[128,2048]{1,0:T(8,128)(2,1)S(1)}, bf16[128,2048]{1,0:T(8,128)(2,1)S(1)}, u32[]{:S(2)}, u32[]{:S(2)}) collective-permute-start(bf16[128,2048]{1,0:T(8,128)(2,1)S(1)} %collective-permute-done.1.refs_2_), channel_id=1, source_target_pairs={{0,8},{8,0},{16,24},{24,16},{1,9},{9,1},{17,25},{25,17},{2,10},{10... | collective-permute-start | bytes 1572872 | tf_op jit(solution)/shard_map/ppermute | solution.py:710
  16.6 7.6 %copy-start.1 = (bf16[1,128,2048]{2,1,0:T(8,128)(2,1)S(1)}, bf16[1,128,2048]{2,1,0:T(8,128)(2,1)}, u32[]{:S(2)}) copy-start(bf16[1,128,2048]{2,1,0:T(8,128)(2,1)} %param.9) | copy-start | bytes 1572868
  16.7 1.9 %collective-permute-start.5 = (bf16[128,256]{1,0:T(8,128)(2,1)S(1)}, bf16[128,256]{1,0:T(8,128)(2,1)S(1)}, u32[]{:S(2)}, u32[]{:S(2)}) collective-permute-start(bf16[128,256]{1,0:T(8,128)(2,1)S(1)} %get-tuple-element.32), channel_id=1, source_target_pairs={{0,8},{8,0},{16,24},{24,16},{1,9},{9,1},{17,25},{25,17},{2,10},{10... | collective-permute-start | bytes 196616 | tf_op jit(solution)/shard_map/ppermute | solution.py:710
  20.8 7.0 %collective-permute-start.10 = (bf16[592,256]{1,0:T(8,128)(2,1)S(1)}, bf16[592,256]{1,0:T(8,128)(2,1)S(1)}, u32[]{:S(2)}, u32[]{:S(2)}) collective-permute-start(bf16[592,256]{1,0:T(8,128)(2,1)S(1)} %collective-permute-done.7.down), channel_id=1, source_target_pairs={{0,4},{1,0},{2,1},{3,2},{7,3},{6,7},{5,6},{4,5},{8,12},{9,8},{10,9... | collective-permute-start | bytes 909320 | tf_op jit(solution)/shard_map/ppermute | solution.py:697
  22.3 7.9 %collective-permute-start.9 = (bf16[592,256]{1,0:T(8,128)(2,1)S(1)}, bf16[592,256]{1,0:T(8,128)(2,1)S(1)}, u32[]{:S(2)}, u32[]{:S(2)}) collective-permute-start(bf16[592,256]{1,0:T(8,128)(2,1)S(1)} %collective-permute-done.6.up), channel_id=1, source_target_pairs={{0,1},{1,2},{2,3},{3,7},{7,6},{6,5},{5,4},{4,0},{8,9},{9,10},{10,1... | collective-permute-start | bytes 909320 | tf_op jit(solution)/shard_map/ppermute | solution.py:697
  22.9 1.3 %collective-permute-start.8 = (bf16[128,256]{1,0:T(8,128)(2,1)S(1)}, bf16[128,256]{1,0:T(8,128)(2,1)S(1)}, u32[]{:S(2)}, u32[]{:S(2)}) collective-permute-start(bf16[128,256]{1,0:T(8,128)(2,1)S(1)} %get-tuple-element.36), channel_id=1, source_target_pairs={{0,8},{8,0},{16,24},{24,16},{1,9},{9,1},{17,25},{25,17},{2,10},{10... | collective-permute-start | bytes 196616 | tf_op jit(solution)/shard_map/ppermute | solution.py:710
  28.6 6.5 %collective-permute-start.13 = (bf16[368,256]{1,0:T(8,128)(2,1)}, bf16[368,256]{1,0:T(8,128)(2,1)S(1)}, u32[]{:S(2)}, u32[]{:S(2)}) collective-permute-start(bf16[368,256]{1,0:T(8,128)(2,1)} %slice.3), channel_id=1, source_target_pairs={{0,4},{1,0},{2,1},{3,2},{7,3},{6,7},{5,6},{4,5},{8,12},{9,8},{10,9... | collective-permute-start | bytes 565256 | tf_op jit(solution)/shard_map/ppermute | solution.py:697
  30.2 4.8 %collective-permute-start.12 = (bf16[224,256]{1,0:T(8,128)(2,1)S(1)}, bf16[224,256]{1,0:T(8,128)(2,1)S(1)}, u32[]{:S(2)}, u32[]{:S(2)}) collective-permute-start(bf16[224,256]{1,0:T(8,128)(2,1)S(1)} %shard_map.98), channel_id=1, source_target_pairs={{0,1},{1,2},{2,3},{3,7},{7,6},{6,5},{5,4},{4,0},{8,9},{9,10},{10,1... | collective-permute-start | bytes 344072 | tf_op jit(solution)/shard_map/ppermute | solution.py:697
  31.3 1.8 %collective-permute-start.11 = (bf16[128,256]{1,0:T(8,128)(2,1)}, bf16[128,256]{1,0:T(8,128)(2,1)S(1)}, u32[]{:S(2)}, u32[]{:S(2)}) collective-permute-start(bf16[128,256]{1,0:T(8,128)(2,1)} %get-tuple-element.41), channel_id=1, source_target_pairs={{0,8},{8,0},{16,24},{24,16},{1,9},{9,1},{17,25},{25,17},{2,10},{10... | collective-permute-start | bytes 196616 | tf_op jit(solution)/shard_map/ppermute | solution.py:710
  31.3 3.7 %collective-permute-start.14 = (bf16[64,256]{1,0:T(8,128)(2,1)}, bf16[64,256]{1,0:T(8,128)(2,1)S(1)}, u32[]{:S(2)}, u32[]{:S(2)}) collective-permute-start(bf16[64,256]{1,0:T(8,128)(2,1)} %get-tuple-element.42), channel_id=1, source_target_pairs={{0,12},{1,8},{2,9},{3,10},{7,11},{6,15},{5,14},{4,13},{8,4},{9,0},... | collective-permute-start | bytes 98312 | tf_op jit(solution)/shard_map/ppermute | solution.py:706
  40.2 2.1 %collective-permute-start.15 = (bf16[128,512]{1,0:T(8,128)(2,1)S(1)}, bf16[128,512]{1,0:T(8,128)(2,1)S(1)}, u32[]{:S(2)}, u32[]{:S(2)}) collective-permute-start(bf16[128,512]{1,0:T(8,128)(2,1)S(1)} %get-tuple-element.44), channel_id=1, source_target_pairs={{0,8},{8,0},{16,24},{24,16},{1,9},{9,1},{17,25},{25,17},{2,10},{10... | collective-permute-start | bytes 393224 | tf_op jit(solution)/shard_map/ppermute | solution.py:710
  40.6 6.3 %collective-permute-start.16 = (bf16[128,512]{1,0:T(8,128)(2,1)S(1)}, bf16[128,512]{1,0:T(8,128)(2,1)S(1)}, u32[]{:S(2)}, u32[]{:S(2)}) collective-permute-start(bf16[128,512]{1,0:T(8,128)(2,1)S(1)} %get-tuple-element.45), channel_id=1, source_target_pairs={{0,16},{8,24},{16,0},{24,8},{1,17},{9,25},{17,1},{25,9},{2,18},{10... | collective-permute-start | bytes 393224 | tf_op jit(solution)/shard_map/ppermute | solution.py:710
  42.3 6.0 %collective-permute-start.17 = (bf16[128,512]{1,0:T(8,128)(2,1)S(1)}, bf16[128,512]{1,0:T(8,128)(2,1)S(1)}, u32[]{:S(2)}, u32[]{:S(2)}) collective-permute-start(bf16[128,512]{1,0:T(8,128)(2,1)S(1)} %get-tuple-element.46), channel_id=1, source_target_pairs={{0,24},{8,16},{16,8},{24,0},{1,25},{9,17},{17,9},{25,1},{2,26},{10... | collective-permute-start | bytes 393224 | tf_op jit(solution)/shard_map/ppermute | solution.py:710
  46.9 1.4 %copy-start.9 = (bf16[1,128,2048]{2,1,0:T(8,128)(2,1)}, bf16[1,128,2048]{2,1,0:T(8,128)(2,1)S(1)}, u32[]{:S(2)}) copy-start(bf16[1,128,2048]{2,1,0:T(8,128)(2,1)S(1)} %bitcast_dynamic-update-slice_fusion.1) | copy-start | bytes 1572868
  (4 other events, 2.7 us)

commit v12 on v11

--- a/solution.py
+++ b/solution.py
@@ -721,7 +721,8 @@
     ring = lax.axis_size("batch")
     late, _ = lax.optimization_barrier((tokens, own))
     across = swap(late, "seq", 2)
-    pieces = [tokens, swap(tokens, "seq", 1), across, swap(across, "seq", 1)]
+    hc = swap(tokens, "seq", 1)
+    hyc = swap(across, "seq", 1)
     table = prepare(heads, (read_starts, conv_weight, conv_bias, dt_bias, decay, skip, norm_gain))
     first = 2 * ring - 3
     ways = [0]
@@ -731,7 +732,7 @@
         up, down = turn(up, 1), turn(down, -1)
         ways += [-away, away]
         if away == 1:
-            beside = table
+            continue
         elif away == 2:
             gathered, sent = first_gather(columns, (columns + SIDE, first * own.shape[1]), own, side, *before)
             beside = swapped = swap(sent, "seq", 1)
@@ -741,6 +742,7 @@
         else:
             gathered, sent = next_gather(columns, 2 * away - 3, gathered, swapped, *before)
             swapped = swap(sent, "seq", 1)
+            pieces = [tokens, hc, across, hyc]
             partial, rest = early(columns, ring, tuple(ways) + (ring,), pieces, gathered, swapped, table)
             beside = partial
         up, _ = lax.optimization_barrier((up, beside))

time: 49.4 us -> 49.2 us (level)
  local copies, waits for them, and re-layouts: 7.71 us -> 2.74 us
  waiting for transfers between devices: 16.2 us -> 21 us
    ppermute x8, waiting for transfers between devices: 5.46 us -> 11.3 us  [turn(): lax.ppermute(value, ('fsdp', 'batch'), [(order[i], order[(i + way) % coun...]
    unnamed x20, local copies, waits for them, and re-layouts: 6.27 us -> 1.3 us
    ppermute x9, waiting for transfers between devices: 9.9 us -> 8.92 us  [swap(): lax.ppermute(value, axis, [(i, i ^ mask) for i in range(lax.axis_size(axi...]
where the time goes in v12:
time: 49.2 us; the launch traced here: 49 us
  waiting for transfers between devices  21 us (43%)
  starting transfers between devices  15.7 us (32%)
  Pallas kernels  9.32 us (19%)
  local copies, waits for them, and re-layouts  2.74 us (6%)
    ppermute x8, waiting for transfers between devices, turn(): lax.ppermute(value, ('fsdp', 'batch'), [(order[i], order[(i + way) % coun...  11.3 us
    pallas_call x9, Pallas kernels, call(): pl.pallas_call(kernel, out_shape=shapes, in_specs=[space] * (len(operands...  9.32 us
    ppermute x9, waiting for transfers between devices, swap(): lax.ppermute(value, axis, [(i, i ^ mask) for i in range(lax.axis_size(axi...  8.92 us
    ppermute x8, starting transfers between devices, turn(): lax.ppermute(value, ('fsdp', 'batch'), [(order[i], order[(i + way) % coun...  8.16 us
    ppermute x9, starting transfers between devices, swap(): lax.ppermute(value, axis, [(i, i ^ mask) for i in range(lax.axis_size(axi...  5.73 us
    ppermute x1, starting transfers between devices, turn_across(): return lax.ppermute(value, ('seq', 'fsdp', 'batch'), pairs)  1.77 us
    unnamed x20, local copies, waits for them, and re-layouts  1.3 us
  transfers between devices with their start and end apart: 18, of which 10 were waited for; matrix products, arithmetic and copies ran while one was open for 2% of the time, Pallas kernels for 8%

profile of v12, /device:TPU:0, one launch (start us, length us, event | category | flops | bytes accessed | tf_op | source)
XLA Modules:
  0.0 49.0 jit_solution(6105962541011605524)
XLA Ops:
  0.0 1.3 %copy-done = bf16[256,2208]{0,1:T(8,128)(2,1)S(1)} copy-done((bf16[256,2208]{0,1:T(8,128)(2,1)S(1)}, bf16[256,2208]{0,1:T(8,128)(2,1)}, u32[]{:S(2)}) %copy-start) | copy-done | bytes 1130520
  1.4 3.0 %collective-permute-start.1 = (bf16[128,2048]{1,0:T(8,128)(2,1)}, bf16[128,2048]{1,0:T(8,128)(2,1)S(1)}, u32[]{:S(2)}, u32[]{:S(2)}) collective-permute-start(bf16[128,2048]{1,0:T(8,128)(2,1)} %bitcast.11), channel_id=1, source_target_pairs={{0,16},{8,24},{16,0},{24,8},{1,17},{9,25},{17,1},{25,9},{2,18},{10... | collective-permute-start | bytes 1572872 | tf_op jit(solution)/shard_map/ppermute | solution.py:710
  4.4 1.5 %collective-permute-start.4 = (bf16[592,256]{1,0:T(8,128)(2,1)S(1)}, bf16[592,256]{1,0:T(8,128)(2,1)S(1)}, u32[]{:S(2)}, u32[]{:S(2)}) collective-permute-start(bf16[592,256]{1,0:T(8,128)(2,1)S(1)} %get-tuple-element.24.own), channel_id=1, source_target_pairs={{0,4},{1,0},{2,1},{3,2},{7,3},{6,7},{5,6},{4,5},{8,12},{9,8},{10,9... | collective-permute-start | bytes 909320 | tf_op jit(solution)/shard_map/ppermute | solution.py:697
  6.5 6.6 %collective-permute-done.4.down = bf16[592,256]{1,0:T(8,128)(2,1)S(1)} collective-permute-done((bf16[592,256]{1,0:T(8,128)(2,1)S(1)}, bf16[592,256]{1,0:T(8,128)(2,1)S(1)}, u32[]{:S(2)}, u32[]{:S(2)}) %collective-permute-start.4) | collective-permute-done | bytes 303136 | tf_op jit(solution)/shard_map/ppermute | solution.py:697
  13.1 1.5 %collective-permute-start.7 = (bf16[592,256]{1,0:T(8,128)(2,1)S(1)}, bf16[592,256]{1,0:T(8,128)(2,1)S(1)}, u32[]{:S(2)}, u32[]{:S(2)}) collective-permute-start(bf16[592,256]{1,0:T(8,128)(2,1)S(1)} %collective-permute-done.4.down), channel_id=1, source_target_pairs={{0,4},{1,0},{2,1},{3,2},{7,3},{6,7},{5,6},{4,5},{8,12},{9,8},{10,9... | collective-permute-start | bytes 909320 | tf_op jit(solution)/shard_map/ppermute | solution.py:697
  15.1 1.5 %collective-permute-done.1.refs_2_ = bf16[128,2048]{1,0:T(8,128)(2,1)S(1)} collective-permute-done((bf16[128,2048]{1,0:T(8,128)(2,1)}, bf16[128,2048]{1,0:T(8,128)(2,1)S(1)}, u32[]{:S(2)}, u32[]{:S(2)}) %collective-permute-start.1) | collective-permute-done | bytes 524320 | tf_op jit(solution)/shard_map/ppermute | solution.py:710
  16.8 0.6 %collective-permute-start.5 = (bf16[128,256]{1,0:T(8,128)(2,1)S(1)}, bf16[128,256]{1,0:T(8,128)(2,1)S(1)}, u32[]{:S(2)}, u32[]{:S(2)}) collective-permute-start(bf16[128,256]{1,0:T(8,128)(2,1)S(1)} %get-tuple-element.28), channel_id=1, source_target_pairs={{0,8},{8,0},{16,24},{24,16},{1,9},{9,1},{17,25},{25,17},{2,10},{10... | collective-permute-start | bytes 196616 | tf_op jit(solution)/shard_map/ppermute | solution.py:710
  17.3 1.3 %collective-permute-done.5.swapped = bf16[128,256]{1,0:T(8,128)(2,1)S(1)} collective-permute-done((bf16[128,256]{1,0:T(8,128)(2,1)S(1)}, bf16[128,256]{1,0:T(8,128)(2,1)S(1)}, u32[]{:S(2)}, u32[]{:S(2)}) %collective-permute-start.5) | collective-permute-done | bytes 65568 | tf_op jit(solution)/shard_map/ppermute | solution.py:710
  18.6 2.2 %collective-permute-done.7.down = bf16[592,256]{1,0:T(8,128)(2,1)S(1)} collective-permute-done((bf16[592,256]{1,0:T(8,128)(2,1)S(1)}, bf16[592,256]{1,0:T(8,128)(2,1)S(1)}, u32[]{:S(2)}, u32[]{:S(2)}) %collective-permute-start.7) | collective-permute-done | bytes 303136 | tf_op jit(solution)/shard_map/ppermute | solution.py:697
  20.8 1.5 %collective-permute-start.10 = (bf16[592,256]{1,0:T(8,128)(2,1)S(1)}, bf16[592,256]{1,0:T(8,128)(2,1)S(1)}, u32[]{:S(2)}, u32[]{:S(2)}) collective-permute-start(bf16[592,256]{1,0:T(8,128)(2,1)S(1)} %collective-permute-done.7.down), channel_id=1, source_target_pairs={{0,4},{1,0},{2,1},{3,2},{7,3},{6,7},{5,6},{4,5},{8,12},{9,8},{10,9... | collective-permute-start | bytes 909320 | tf_op jit(solution)/shard_map/ppermute | solution.py:697
  23.1 0.8 %shard_map.94.refs_6_ = f32[144,640]{1,0:T(8,128)S(1)} custom-call(s32[1,4]{1,0:T(1,128)S(1)} %copy-done.8, f32[2,4,2176]{2,1,0:T(4,128)S(1)} %copy-done.2, f32[2,2176]{1,0:T(2,128)S(1)} %copy-done.3, f32[2,32]{1,0:T(2,128)S(1)} %copy-done.5, f32[2,32]{1,0:T(2,128)S(1)} %copy-done.6, f32[2,32]{1,0:T(2,128)S(1)} %copy-done.7, f32[2,2048]{1,0:T(2,128)S(1)} %copy-done.4), custom_call_target="tpu_custom_call" | custom-call | tf_op jit(solution)/shard_map/pallas_call | solution.py:594
  24.2 1.3 %shard_map.95 = (f32[528,768]{1,0:T(8,128)S(1)}, bf16[512,768]{1,0:T(8,128)(2,1)S(1)}) custom-call(bf16[128,2048]{1,0:T(8,128)(2,1)S(1)} %bitcast.13, bf16[128,2048]{1,0:T(8,128)(2,1)S(1)} %collective-permute-done.refs_1_, bf16[128,2048]{1,0:T(8,128)(2,1)S(1)} %collective-permute-done.1.refs_2_, bf16[128,2048]{1,0:T(8,128)(2,1)S(1)} %collective-permute-done.2.refs_3_, ...), custom_call_target="tpu_custom_call" | custom-call | tf_op jit(solution)/shard_map/pallas_call | solution.py:594
  25.5 2.3 %collective-permute-done.10.down = bf16[592,256]{1,0:T(8,128)(2,1)S(1)} collective-permute-done((bf16[592,256]{1,0:T(8,128)(2,1)S(1)}, bf16[592,256]{1,0:T(8,128)(2,1)S(1)}, u32[]{:S(2)}, u32[]{:S(2)}) %collective-permute-start.10) | collective-permute-done | bytes 303136 | tf_op jit(solution)/shard_map/ppermute | solution.py:697
  27.9 0.7 %slice.3 = bf16[368,256]{1,0:T(8,128)(2,1)} slice(bf16[592,256]{1,0:T(8,128)(2,1)S(1)} %collective-permute-done.10.down), slice={[224:592], [0:256]} | slice | bytes 376832 | tf_op jit(solution)/shard_map/slice | solution.py:751
  28.6 1.7 %collective-permute-start.13 = (bf16[368,256]{1,0:T(8,128)(2,1)}, bf16[368,256]{1,0:T(8,128)(2,1)S(1)}, u32[]{:S(2)}, u32[]{:S(2)}) collective-permute-start(bf16[368,256]{1,0:T(8,128)(2,1)} %slice.3), channel_id=1, source_target_pairs={{0,4},{1,0},{2,1},{3,2},{7,3},{6,7},{5,6},{4,5},{8,12},{9,8},{10,9... | collective-permute-start | bytes 565256 | tf_op jit(solution)/shard_map/ppermute | solution.py:697
  30.7 0.6 %shard_map.96 = (bf16[128,256]{1,0:T(8,128)(2,1)}, bf16[64,256]{1,0:T(8,128)(2,1)}) custom-call(bf16[592,256]{1,0:T(8,128)(2,1)S(1)} %collective-permute-done.9.up.value, bf16[592,256]{1,0:T(8,128)(2,1)S(1)} %collective-permute-done.10.down), custom_call_target="tpu_custom_call" | custom-call | tf_op jit(solution)/shard_map/pallas_call | solution.py:594
  31.3 1.8 %collective-permute-start.14 = (bf16[64,256]{1,0:T(8,128)(2,1)}, bf16[64,256]{1,0:T(8,128)(2,1)S(1)}, u32[]{:S(2)}, u32[]{:S(2)}) collective-permute-start(bf16[64,256]{1,0:T(8,128)(2,1)} %get-tuple-element.38), channel_id=1, source_target_pairs={{0,12},{1,8},{2,9},{3,10},{7,11},{6,15},{5,14},{4,13},{8,4},{9,0},... | collective-permute-start | bytes 98312 | tf_op jit(solution)/shard_map/ppermute | solution.py:706
  33.1 1.1 %shard_map.97.partial = f32[528,768]{1,0:T(8,128)S(1)} custom-call(f32[528,768]{1,0:T(8,128)S(1)} %get-tuple-element.33.partial, bf16[512,768]{1,0:T(8,128)(2,1)S(1)} %get-tuple-element.34.rest, bf16[592,256]{1,0:T(8,128)(2,1)S(1)} %collective-permute-done.9.up.value, bf16[592,256]{1,0:T(8,128)(2,1)S(1)} %collective-permute-done.10.down, ...), custom_call_target="tpu_custom_call" | custom-call | tf_op jit(solution)/shard_map/pallas_call | solution.py:594
  34.2 0.8 %collective-permute-done.14.far = bf16[64,256]{1,0:T(8,128)(2,1)S(1)} collective-permute-done((bf16[64,256]{1,0:T(8,128)(2,1)}, bf16[64,256]{1,0:T(8,128)(2,1)S(1)}, u32[]{:S(2)}, u32[]{:S(2)}) %collective-permute-start.14) | collective-permute-done | bytes 32800 | tf_op jit(solution)/shard_map/ppermute | solution.py:706
  35.1 5.1 %shard_map.99 = (bf16[128,512]{1,0:T(8,128)(2,1)S(1)}, bf16[128,512]{1,0:T(8,128)(2,1)S(1)}, bf16[128,512]{1,0:T(8,128)(2,1)S(1)}, bf16[128,512]{1,0:T(8,128)(2,1)S(1)}) custom-call(f32[528,768]{1,0:T(8,128)S(1)} %shard_map.97.partial, bf16[512,768]{1,0:T(8,128)(2,1)S(1)} %get-tuple-element.34.rest, bf16[224,256]{1,0:T(8,128)(2,1)S(1)} %collective-permute-done.12.up_end, ...), custom_call_target="tpu_custom_call" | custom-call | tf_op jit(solution)/shard_map/pallas_call | solution.py:594
  40.6 1.7 %collective-permute-start.16 = (bf16[128,512]{1,0:T(8,128)(2,1)S(1)}, bf16[128,512]{1,0:T(8,128)(2,1)S(1)}, u32[]{:S(2)}, u32[]{:S(2)}) collective-permute-start(bf16[128,512]{1,0:T(8,128)(2,1)S(1)} %get-tuple-element.41), channel_id=1, source_target_pairs={{0,16},{8,24},{16,0},{24,8},{1,17},{9,25},{17,1},{25,9},{2,18},{10... | collective-permute-start | bytes 393224 | tf_op jit(solution)/shard_map/ppermute | solution.py:710
  42.4 4.5 %collective-permute-done.16 = bf16[128,512]{1,0:T(8,128)(2,1)S(1)} collective-permute-done((bf16[128,512]{1,0:T(8,128)(2,1)S(1)}, bf16[128,512]{1,0:T(8,128)(2,1)S(1)}, u32[]{:S(2)}, u32[]{:S(2)}) %collective-permute-start.16) | collective-permute-done | bytes 131104 | tf_op jit(solution)/shard_map/ppermute | solution.py:710
  46.9 1.4 %collective-permute-done.17 = bf16[128,512]{1,0:T(8,128)(2,1)S(1)} collective-permute-done((bf16[128,512]{1,0:T(8,128)(2,1)S(1)}, bf16[128,512]{1,0:T(8,128)(2,1)S(1)}, u32[]{:S(2)}, u32[]{:S(2)}) %collective-permute-start.17) | collective-permute-done | bytes 131104 | tf_op jit(solution)/shard_map/ppermute | solution.py:710
  48.3 0.7 %bitcast_dynamic-update-slice_fusion = bf16[1,128,2048]{2,1,0:T(8,128)(2,1)} fusion(bf16[1,128,2048]{2,1,0:T(8,128)(2,1)} %copy-done.9, s32[]{:T(128)S(6)} %select_n.15, bf16[128,512]{1,0:T(8,128)(2,1)S(1)} %collective-permute-done.17), kind=kLoop, calls=%fused_computation | loop fusion | bytes 262148 | tf_op jit(solution)/shard_map/dynamic_update_slice | solution.py:759
  (47 shorter events, 3.3 us)
Async XLA Ops:
  1.4 15.2 %collective-permute-start.1 = (bf16[128,2048]{1,0:T(8,128)(2,1)}, bf16[128,2048]{1,0:T(8,128)(2,1)S(1)}, u32[]{:S(2)}, u32[]{:S(2)}) collective-permute-start(bf16[128,2048]{1,0:T(8,128)(2,1)} %bitcast.11), channel_id=1, source_target_pairs={{0,16},{8,24},{16,0},{24,8},{1,17},{9,25},{17,1},{25,9},{2,18},{10... | collective-permute-start | bytes 1572872 | tf_op jit(solution)/shard_map/ppermute | solution.py:710
  4.4 8.6 %collective-permute-start.4 = (bf16[592,256]{1,0:T(8,128)(2,1)S(1)}, bf16[592,256]{1,0:T(8,128)(2,1)S(1)}, u32[]{:S(2)}, u32[]{:S(2)}) collective-permute-start(bf16[592,256]{1,0:T(8,128)(2,1)S(1)} %get-tuple-element.24.own), channel_id=1, source_target_pairs={{0,4},{1,0},{2,1},{3,2},{7,3},{6,7},{5,6},{4,5},{8,12},{9,8},{10,9... | collective-permute-start | bytes 909320 | tf_op jit(solution)/shard_map/ppermute | solution.py:697
  5.9 8.6 %collective-permute-start.3 = (bf16[592,256]{1,0:T(8,128)(2,1)S(1)}, bf16[592,256]{1,0:T(8,128)(2,1)S(1)}, u32[]{:S(2)}, u32[]{:S(2)}) collective-permute-start(bf16[592,256]{1,0:T(8,128)(2,1)S(1)} %get-tuple-element.24.own), channel_id=1, source_target_pairs={{0,1},{1,2},{2,3},{3,7},{7,6},{6,5},{5,4},{4,0},{8,9},{9,10},{10,1... | collective-permute-start | bytes 909320 | tf_op jit(solution)/shard_map/ppermute | solution.py:697
  13.1 7.7 %collective-permute-start.7 = (bf16[592,256]{1,0:T(8,128)(2,1)S(1)}, bf16[592,256]{1,0:T(8,128)(2,1)S(1)}, u32[]{:S(2)}, u32[]{:S(2)}) collective-permute-start(bf16[592,256]{1,0:T(8,128)(2,1)S(1)} %collective-permute-done.4.down), channel_id=1, source_target_pairs={{0,4},{1,0},{2,1},{3,2},{7,3},{6,7},{5,6},{4,5},{8,12},{9,8},{10,9... | collective-permute-start | bytes 909320 | tf_op jit(solution)/shard_map/ppermute | solution.py:697
  14.6 7.7 %collective-permute-start.6 = (bf16[592,256]{1,0:T(8,128)(2,1)S(1)}, bf16[592,256]{1,0:T(8,128)(2,1)S(1)}, u32[]{:S(2)}, u32[]{:S(2)}) collective-permute-start(bf16[592,256]{1,0:T(8,128)(2,1)S(1)} %collective-permute-done.3.up), channel_id=1, source_target_pairs={{0,1},{1,2},{2,3},{3,7},{7,6},{6,5},{5,4},{4,0},{8,9},{9,10},{10,1... | collective-permute-start | bytes 909320 | tf_op jit(solution)/shard_map/ppermute | solution.py:697
  15.1 8.8 %collective-permute-start = (bf16[128,2048]{1,0:T(8,128)(2,1)}, bf16[128,2048]{1,0:T(8,128)(2,1)S(1)}, u32[]{:S(2)}, u32[]{:S(2)}) collective-permute-start(bf16[128,2048]{1,0:T(8,128)(2,1)} %bitcast.12), channel_id=1, source_target_pairs={{0,8},{8,0},{16,24},{24,16},{1,9},{9,1},{17,25},{25,17},{2,10},{10... | collective-permute-start | bytes 1572872 | tf_op jit(solution)/shard_map/ppermute | solution.py:710
  16.6 7.6 %collective-permute-start.2 = (bf16[128,2048]{1,0:T(8,128)(2,1)S(1)}, bf16[128,2048]{1,0:T(8,128)(2,1)S(1)}, u32[]{:S(2)}, u32[]{:S(2)}) collective-permute-start(bf16[128,2048]{1,0:T(8,128)(2,1)S(1)} %collective-permute-done.1.refs_2_), channel_id=1, source_target_pairs={{0,8},{8,0},{16,24},{24,16},{1,9},{9,1},{17,25},{25,17},{2,10},{10... | collective-permute-start | bytes 1572872 | tf_op jit(solution)/shard_map/ppermute | solution.py:710
  16.6 6.4 %copy-start.4 = (f32[2,2048]{1,0:T(2,128)S(1)}, f32[2,2048]{1,0:T(2,128)}, u32[]{:S(2)}) copy-start(f32[2,2048]{1,0:T(2,128)} %refs_6_.1) | copy-start | bytes 49156
  16.6 6.4 %copy-start.5 = (f32[2,32]{1,0:T(2,128)S(1)}, f32[2,32]{1,0:T(2,128)}, u32[]{:S(2)}) copy-start(f32[2,32]{1,0:T(2,128)} %refs_3_.1) | copy-start | bytes 772
  16.6 6.4 %copy-start.6 = (f32[2,32]{1,0:T(2,128)S(1)}, f32[2,32]{1,0:T(2,128)}, u32[]{:S(2)}) copy-start(f32[2,32]{1,0:T(2,128)} %refs_4_.1) | copy-start | bytes 772
  16.6 6.4 %copy-start.7 = (f32[2,32]{1,0:T(2,128)S(1)}, f32[2,32]{1,0:T(2,128)}, u32[]{:S(2)}) copy-start(f32[2,32]{1,0:T(2,128)} %refs_5_.1) | copy-start | bytes 772
  16.6 6.4 %copy-start.8 = (s32[1,4]{1,0:T(1,128)S(1)}, s32[1,4]{1,0:T(1,128)}, u32[]{:S(2)}) copy-start(s32[1,4]{1,0:T(1,128)} %refs_0_.1) | copy-start | bytes 52
  16.7 7.5 %copy-start.1 = (bf16[1,128,2048]{2,1,0:T(8,128)(2,1)S(1)}, bf16[1,128,2048]{2,1,0:T(8,128)(2,1)}, u32[]{:S(2)}) copy-start(bf16[1,128,2048]{2,1,0:T(8,128)(2,1)} %param.9) | copy-start | bytes 1572868
  16.8 1.8 %collective-permute-start.5 = (bf16[128,256]{1,0:T(8,128)(2,1)S(1)}, bf16[128,256]{1,0:T(8,128)(2,1)S(1)}, u32[]{:S(2)}, u32[]{:S(2)}) collective-permute-start(bf16[128,256]{1,0:T(8,128)(2,1)S(1)} %get-tuple-element.28), channel_id=1, source_target_pairs={{0,8},{8,0},{16,24},{24,16},{1,9},{9,1},{17,25},{25,17},{2,10},{10... | collective-permute-start | bytes 196616 | tf_op jit(solution)/shard_map/ppermute | solution.py:710
  20.8 7.0 %collective-permute-start.10 = (bf16[592,256]{1,0:T(8,128)(2,1)S(1)}, bf16[592,256]{1,0:T(8,128)(2,1)S(1)}, u32[]{:S(2)}, u32[]{:S(2)}) collective-permute-start(bf16[592,256]{1,0:T(8,128)(2,1)S(1)} %collective-permute-done.7.down), channel_id=1, source_target_pairs={{0,4},{1,0},{2,1},{3,2},{7,3},{6,7},{5,6},{4,5},{8,12},{9,8},{10,9... | collective-permute-start | bytes 909320 | tf_op jit(solution)/shard_map/ppermute | solution.py:697
  22.3 7.9 %collective-permute-start.9 = (bf16[592,256]{1,0:T(8,128)(2,1)S(1)}, bf16[592,256]{1,0:T(8,128)(2,1)S(1)}, u32[]{:S(2)}, u32[]{:S(2)}) collective-permute-start(bf16[592,256]{1,0:T(8,128)(2,1)S(1)} %collective-permute-done.6.up), channel_id=1, source_target_pairs={{0,1},{1,2},{2,3},{3,7},{7,6},{6,5},{5,4},{4,0},{8,9},{9,10},{10,1... | collective-permute-start | bytes 909320 | tf_op jit(solution)/shard_map/ppermute | solution.py:697
  22.9 1.3 %collective-permute-start.8 = (bf16[128,256]{1,0:T(8,128)(2,1)S(1)}, bf16[128,256]{1,0:T(8,128)(2,1)S(1)}, u32[]{:S(2)}, u32[]{:S(2)}) collective-permute-start(bf16[128,256]{1,0:T(8,128)(2,1)S(1)} %get-tuple-element.32), channel_id=1, source_target_pairs={{0,8},{8,0},{16,24},{24,16},{1,9},{9,1},{17,25},{25,17},{2,10},{10... | collective-permute-start | bytes 196616 | tf_op jit(solution)/shard_map/ppermute | solution.py:710
  28.6 6.5 %collective-permute-start.13 = (bf16[368,256]{1,0:T(8,128)(2,1)}, bf16[368,256]{1,0:T(8,128)(2,1)S(1)}, u32[]{:S(2)}, u32[]{:S(2)}) collective-permute-start(bf16[368,256]{1,0:T(8,128)(2,1)} %slice.3), channel_id=1, source_target_pairs={{0,4},{1,0},{2,1},{3,2},{7,3},{6,7},{5,6},{4,5},{8,12},{9,8},{10,9... | collective-permute-start | bytes 565256 | tf_op jit(solution)/shard_map/ppermute | solution.py:697
  30.2 4.8 %collective-permute-start.12 = (bf16[224,256]{1,0:T(8,128)(2,1)S(1)}, bf16[224,256]{1,0:T(8,128)(2,1)S(1)}, u32[]{:S(2)}, u32[]{:S(2)}) collective-permute-start(bf16[224,256]{1,0:T(8,128)(2,1)S(1)} %shard_map.98), channel_id=1, source_target_pairs={{0,1},{1,2},{2,3},{3,7},{7,6},{6,5},{5,4},{4,0},{8,9},{9,10},{10,1... | collective-permute-start | bytes 344072 | tf_op jit(solution)/shard_map/ppermute | solution.py:697
  31.3 1.8 %collective-permute-start.11 = (bf16[128,256]{1,0:T(8,128)(2,1)}, bf16[128,256]{1,0:T(8,128)(2,1)S(1)}, u32[]{:S(2)}, u32[]{:S(2)}) collective-permute-start(bf16[128,256]{1,0:T(8,128)(2,1)} %get-tuple-element.37), channel_id=1, source_target_pairs={{0,8},{8,0},{16,24},{24,16},{1,9},{9,1},{17,25},{25,17},{2,10},{10... | collective-permute-start | bytes 196616 | tf_op jit(solution)/shard_map/ppermute | solution.py:710
  31.3 3.7 %collective-permute-start.14 = (bf16[64,256]{1,0:T(8,128)(2,1)}, bf16[64,256]{1,0:T(8,128)(2,1)S(1)}, u32[]{:S(2)}, u32[]{:S(2)}) collective-permute-start(bf16[64,256]{1,0:T(8,128)(2,1)} %get-tuple-element.38), channel_id=1, source_target_pairs={{0,12},{1,8},{2,9},{3,10},{7,11},{6,15},{5,14},{4,13},{8,4},{9,0},... | collective-permute-start | bytes 98312 | tf_op jit(solution)/shard_map/ppermute | solution.py:706
  40.2 2.1 %collective-permute-start.15 = (bf16[128,512]{1,0:T(8,128)(2,1)S(1)}, bf16[128,512]{1,0:T(8,128)(2,1)S(1)}, u32[]{:S(2)}, u32[]{:S(2)}) collective-permute-start(bf16[128,512]{1,0:T(8,128)(2,1)S(1)} %get-tuple-element.40), channel_id=1, source_target_pairs={{0,8},{8,0},{16,24},{24,16},{1,9},{9,1},{17,25},{25,17},{2,10},{10... | collective-permute-start | bytes 393224 | tf_op jit(solution)/shard_map/ppermute | solution.py:710
  40.6 6.3 %collective-permute-start.16 = (bf16[128,512]{1,0:T(8,128)(2,1)S(1)}, bf16[128,512]{1,0:T(8,128)(2,1)S(1)}, u32[]{:S(2)}, u32[]{:S(2)}) collective-permute-start(bf16[128,512]{1,0:T(8,128)(2,1)S(1)} %get-tuple-element.41), channel_id=1, source_target_pairs={{0,16},{8,24},{16,0},{24,8},{1,17},{9,25},{17,1},{25,9},{2,18},{10... | collective-permute-start | bytes 393224 | tf_op jit(solution)/shard_map/ppermute | solution.py:710
  42.3 6.0 %collective-permute-start.17 = (bf16[128,512]{1,0:T(8,128)(2,1)S(1)}, bf16[128,512]{1,0:T(8,128)(2,1)S(1)}, u32[]{:S(2)}, u32[]{:S(2)}) collective-permute-start(bf16[128,512]{1,0:T(8,128)(2,1)S(1)} %get-tuple-element.42), channel_id=1, source_target_pairs={{0,24},{8,16},{16,8},{24,0},{1,25},{9,17},{17,9},{25,1},{2,26},{10... | collective-permute-start | bytes 393224 | tf_op jit(solution)/shard_map/ppermute | solution.py:710
  (4 other events, 15.4 us)
